TPU v7x, 256 devices: a whole 4x4x8 slice. The times are simulated.
256 devices in a mesh: tile: 32 (over y, z_lo, x), ens: 8 (over z_hi, core).
Axes of the slice: x: 4, y: 4, z: 8 (z_hi: 4, z_lo: 2; z = z_hi * 2 + z_lo), core: 2. Of those that a mesh axis runs over, the one named last changes fastest.
Arguments:
- network_conditions: bfloat16 [8, 96, 8, 8, 256], P('ens', 'tile'), may hold values from -6 to 6
- subsequent_targets: bfloat16 [8, 96, 8, 8, 256], P('ens', 'tile'), may hold values from -6 to 6
- w_first: bfloat16 [3, 3, 256, 256], replicated, may hold values from -0.125 to 0.125
- w_second: bfloat16 [3, 3, 256, 256], replicated, may hold values from -0.125 to 0.125
- tile_links: int32 [96, 16], P('tile'), may hold values from -1 to 383, as said below
Outputs:
- layer_prognosis: bfloat16 [8, 96, 8, 8, 256], P('ens', 'tile')
- condition_derivative: float32 [8, 96, 8, 8, 256], P('ens', 'tile')
- initial_kernel_slope: float32 [3, 3, 256, 256], replicated
- latter_kernel_slope: float32 [3, 3, 256, 256], replicated
Inputs may be any that keep to these rules, and one draw needn't show every extreme that they name: tile_links describes a cubed sphere of 6 faces of 4 x 4 tiles. The tiles are numbered face by face: face q holds tiles q * 4 * 4 to (q + 1) * 4 * 4 - 1, in row-major order of its 4 x 4 grid, and which cube face is face q is drawn. Row p: columns 0 to 3 name the tile beyond the north, east, south and west edge of tile p; columns 4 to 7 hold e + 4 f, where e is the edge of that tile that touches tile p and f is 1 when the cells along the two edges run opposite ways, else 0; columns 8 to 11 hold 4 m + k for the corners 0 to 3, tile m lying diagonally across with its corner k at the same point, or -1 where only three tiles meet; columns 12 to 15 hold the number of tiles meeting at those corners, 3 or 4. The relation is symmetric: the tile beyond edge e of p names p beyond its edge given by column 4+e, with the same f, and likewise for corners.
All inputs are finite; a program needn't handle non-finite values.
Results may differ from a plain program's by a relative error of at most 0.0034.
Values may be sent and summed in bfloat16 or wider, within the bound.
No kernel may reach another device: no remote copies, remote signals or barrier semaphores. Data moves between devices by JAX's collectives and lax.ppermute only.
A program may use at most 64 MiB of HBM per device.

v0:
```python
import math

import jax
import jax.numpy as jnp
from jax import lax
from jax.experimental import pallas as pl
from jax.experimental.pallas import tpu as pltpu
from jax.sharding import PartitionSpec as P

tanh_scale = 0.7978845608028654
cubic_term = 0.044715
layout_names = ("NHWC", "HWIO", "NHWC")
slot_rows = 32


def gelu_value(inputs):
    return (
        0.5
        * inputs
        * (1.0 + jnp.tanh(tanh_scale * (inputs + cubic_term * inputs * inputs * inputs)))
    )


def gelu_slope(inputs):
    tangent = jnp.tanh(tanh_scale * (inputs + cubic_term * inputs * inputs * inputs))
    return 0.5 * (1.0 + tangent) + 0.5 * inputs * (1.0 - tangent * tangent) * tanh_scale * (
        1.0 + 3.0 * cubic_term * inputs * inputs
    )


def rim_frame(values):
    length = values.shape[1]
    edge_cells = jnp.stack(
        [values[:, 0], values[:, :, length - 1], values[:, length - 1], values[:, :, 0]], axis=1
    )
    corner_cells = jnp.stack(
        [
            values[:, 0, 0],
            values[:, 0, length - 1],
            values[:, length - 1, length - 1],
            values[:, length - 1, 0],
        ],
        axis=1,
    )
    return (edge_cells, corner_cells)


def routes(tile_links):
    number = tile_links.shape[0]
    here = lax.axis_index("tile")
    strips = 4 * number

    def rows_of(tile, side, valid, base, width, local_base):
        device = tile // number
        source = (tile % number) * 4 + side
        near = (device[:, None] == device[None, :]) & valid[None, :]
        order = jnp.arange(strips)
        send_rank = jnp.sum(near & (order[None, :] < order[:, None]), axis=1)
        take_rank = jnp.sum(near & (source[None, :] < source[:, None]), axis=1)
        own = device == here
        send = jnp.where(own | ~valid, -width, device * slot_rows + base + send_rank * width)
        take = jnp.where(
            own,
            local_base + source * width,
            device * slot_rows + base + take_rank * width,
        )
        return send, jnp.where(valid, take, -width)

    across = tile_links[:, 8:12].reshape(-1)
    code = tile_links[:, 4:8].reshape(-1)
    total = lax.axis_size("tile") * slot_rows
    always = jnp.ones((strips,), bool)
    send_edge, take_edge = rows_of(
        tile_links[:, 0:4].reshape(-1), code % 4, always, 0, 8, total
    )
    send_corner, take_corner = rows_of(
        jnp.maximum(across, 0) // 4, jnp.maximum(across, 0) % 4, across >= 0, 24, 1, total + 8 * strips
    )
    step = jnp.arange(8)
    forward = send_edge[:, None] + step[None, :]
    backward = take_edge[:, None] + jnp.where((code // 4 == 1)[:, None], 7 - step, step)
    send_rows = jnp.concatenate([forward.reshape(-1), send_corner])
    take_rows = jnp.concatenate([backward.reshape(-1), take_corner])
    cells = 9 * strips
    pack = (jnp.arange(total)[:, None] == send_rows[None, :]).astype(jnp.bfloat16)
    unpack = (take_rows[:, None] == jnp.arange(total + cells)[None, :]).astype(jnp.bfloat16)
    return pack, unpack


def move_frames(edge_cells, corner_cells, pack, unpack):
    number, _, length, channels = edge_cells.shape
    frame = jnp.concatenate(
        [edge_cells.reshape(-1, channels), corner_cells.reshape(-1, channels)], axis=0
    )
    sent = jnp.dot(pack, frame, preferred_element_type=jnp.float32).astype(jnp.bfloat16)
    got = lax.all_to_all(sent, "tile", 0, 0, tiled=True)
    out = jnp.dot(
        unpack, jnp.concatenate([got, frame], axis=0), preferred_element_type=jnp.float32
    ).astype(jnp.bfloat16)
    strips = 4 * number * length
    return (
        out[:strips].reshape(number, 4, length, channels),
        out[strips:].reshape(number, 4, channels),
    )


sizes = {"x": 4, "y": 4, "z": 8, "core": 2}


def place_of(x, y, z, core):
    return ((y * 2 + z % 2) * 4 + x) * 8 + (z // 2) * 2 + core


def shifted(values, axis, by):
    pairs = []
    for x in range(4):
        for y in range(4):
            for z in range(8):
                for core in range(2):
                    at = {"x": x, "y": y, "z": z, "core": core}
                    to = dict(at)
                    to[axis] = (at[axis] + by) % sizes[axis]
                    pairs.append((place_of(**at), place_of(**to)))
    return lax.ppermute(values, ("tile", "ens"), pairs)


def coordinates():
    tile = lax.axis_index("tile")
    ens = lax.axis_index("ens")
    return {
        "x": tile % 4,
        "y": tile // 8,
        "z": (ens // 2) * 2 + (tile // 4) % 2,
        "core": ens % 2,
    }


def pool_halves(values, where, pick):
    lanes = values.shape[-1] // 2
    low, high = values[..., :lanes], values[..., lanes:]
    parts = []
    for k in range(4):
        part = jnp.where(pick((where["x"] + k) % 4) == 0, low, high)
        parts.append(shifted(part, "x", k) if k else part)
    return parts


def slope_kernel(core_ref, *refs):
    pads, grads = refs[:4], refs[4:8]
    kept_ref, sent_ref, wide, total = refs[8:]
    for n in range(4):
        wide[3 * n : 3 * n + 3] = pads[n][...].astype(jnp.float32)
    flat = jnp.concatenate(
        [g[...].astype(jnp.float32).reshape(192, 128) for g in grads], axis=0
    ).astype(jnp.bfloat16)
    low = core_ref[0] == 0
    for across in range(3):
        columns = wide[:, :, across : across + 8, :]
        for down in range(3):
            window = columns[:, down : down + 8].reshape(768, 128).astype(jnp.bfloat16)
            out = lax.dot_general(
                window, flat, (((0,), (0,)), ((), ())), preferred_element_type=jnp.float32
            )
            tap = (3 * down + across) * 64
            total[0, tap : tap + 64] = jnp.where(low, out[:64], out[64:])
            total[1, tap : tap + 64] = jnp.where(low, out[64:], out[:64])
    for j in range(32):
        kept_ref[j] = total[0, 18 * j : 18 * j + 18]
        sent_ref[j] = total[1, 18 * j : 18 * j + 18]


def slope_terms(pads, grads, where):
    shape = jax.ShapeDtypeStruct((32, 18, 128), jnp.float32)
    vmem = pl.BlockSpec(memory_space=pltpu.VMEM)
    kept, sent = pl.pallas_call(
        slope_kernel,
        out_shape=(shape, shape),
        in_specs=[pl.BlockSpec(memory_space=pltpu.SMEM)] + [vmem] * 8,
        out_specs=(vmem, vmem),
        scratch_shapes=[
            pltpu.VMEM((12, 10, 10, 128), jnp.float32),
            pltpu.VMEM((2, 576, 128), jnp.float32),
        ],
        compiler_params=pltpu.CompilerParams(vmem_limit_bytes=40 * 2**20),
        cost_estimate=pl.CostEstimate(
            flops=2 * 9 * 768 * 128 * 128, bytes_accessed=2000000, transcendentals=0
        ),
        name="slope_terms",
    )(jnp.reshape(where["core"], (1,)), *pads, *grads)
    return kept + shifted(sent, "core", 1)


def spread_kernel(x_ref, *refs):
    parts = refs[:8]
    first_ref, second_ref, total = refs[8:]
    x, core = x_ref[0], x_ref[1]
    for k in range(4):
        quarter = lax.rem(x + 4 - k, 4)
        column = pl.multiple_of(lax.rem(quarter, 2) * 128, 128)
        for other in range(2):
            side = core if other == 0 else 1 - core
            row = pl.multiple_of((quarter // 2) * 128 + side * 64, 64)
            for j in range(32):
                piece = parts[4 * other + k][j].astype(jnp.float32)
                total[0, 18 * j : 18 * j + 18] = piece[:18]
                total[1, 18 * j : 18 * j + 18] = piece[18:36]
            first_ref[:, pl.ds(row, 64), pl.ds(column, 128)] = total[0].reshape(9, 64, 128)
            second_ref[:, pl.ds(row, 64), pl.ds(column, 128)] = total[1].reshape(9, 64, 128)


def spread_slopes(parts, where):
    shape = jax.ShapeDtypeStruct((9, 256, 256), jnp.float32)
    vmem = pl.BlockSpec(memory_space=pltpu.VMEM)
    return pl.pallas_call(
        spread_kernel,
        out_shape=(shape, shape),
        in_specs=[pl.BlockSpec(memory_space=pltpu.SMEM)] + [vmem] * 8,
        out_specs=(vmem, vmem),
        scratch_shapes=[pltpu.VMEM((2, 576, 128), jnp.float32)],
        compiler_params=pltpu.CompilerParams(vmem_limit_bytes=40 * 2**20),
        cost_estimate=pl.CostEstimate(flops=1000, bytes_accessed=7000000, transcendentals=0),
        name="spread_slopes",
    )(jnp.stack([where["x"], where["core"]]), *parts)


def plane_groups():
    return [
        [place_of(x, y, z, core) for y in range(4) for z in range(8)]
        for x in range(4)
        for core in range(2)
    ]


def plane_exchange(values):
    return lax.all_to_all(
        values, ("tile", "ens"), 0, 0, axis_index_groups=plane_groups(), tiled=True
    )


def finish_slopes(first, second, scale, where):
    terms = plane_exchange(jnp.concatenate([first, second], axis=-1))
    mine = jnp.sum(terms, axis=0) * scale
    mine = jnp.concatenate([mine[:, :128], mine[:, 128:]], axis=0).astype(jnp.bfloat16)
    plane = plane_exchange(jnp.broadcast_to(mine[None], (32,) + mine.shape))
    own = [plane] + [shifted(plane, "x", k) for k in range(1, 4)]
    other = [shifted(part, "core", 1) for part in own]
    return spread_slopes(own + other, where)


def with_ghosts(values, ghost_rows, ghost_corners, tile_links):
    length = values.shape[1]
    widened = ghost_rows.astype(jnp.float32)
    meeting = tile_links[:, 12:16]
    blended = jnp.stack(
        [
            0.5 * (widened[:, 0, 0] + widened[:, 3, 0]),
            0.5 * (widened[:, 0, length - 1] + widened[:, 1, 0]),
            0.5 * (widened[:, 1, length - 1] + widened[:, 2, length - 1]),
            0.5 * (widened[:, 2, 0] + widened[:, 3, length - 1]),
        ],
        axis=1,
    )
    corner = jnp.where(
        (meeting == 4)[:, :, None], ghost_corners.astype(jnp.float32), blended
    ).astype(values.dtype)
    middle = jnp.concatenate(
        [ghost_rows[:, 3][:, :, None], values, ghost_rows[:, 1][:, :, None]], axis=2
    )
    top_row = jnp.concatenate(
        [corner[:, 0][:, None], ghost_rows[:, 0], corner[:, 1][:, None]], axis=1
    )
    bottom = jnp.concatenate(
        [corner[:, 3][:, None], ghost_rows[:, 2], corner[:, 2][:, None]], axis=1
    )
    return jnp.concatenate([top_row[:, None], middle, bottom[:, None]], axis=1)


def ghost_grads(full, tile_links):
    length = full.shape[1] - 2
    meeting = tile_links[:, 12:16]
    corners = jnp.stack(
        [
            full[:, 0, 0],
            full[:, 0, length + 1],
            full[:, length + 1, length + 1],
            full[:, length + 1, 0],
        ],
        axis=1,
    )
    half_corner = jnp.where((meeting == 3)[:, :, None], 0.5 * corners, jnp.zeros_like(corners))
    north_row = (
        full[:, 0, 1 : length + 1]
        .at[:, 0]
        .add(half_corner[:, 0])
        .at[:, length - 1]
        .add(half_corner[:, 1])
    )
    east_column = (
        full[:, 1 : length + 1, length + 1]
        .at[:, 0]
        .add(half_corner[:, 1])
        .at[:, length - 1]
        .add(half_corner[:, 2])
    )
    south_row = (
        full[:, length + 1, 1 : length + 1]
        .at[:, length - 1]
        .add(half_corner[:, 2])
        .at[:, 0]
        .add(half_corner[:, 3])
    )
    west_column = (
        full[:, 1 : length + 1, 0]
        .at[:, 0]
        .add(half_corner[:, 0])
        .at[:, length - 1]
        .add(half_corner[:, 3])
    )
    edge_cells = jnp.stack([north_row, east_column, south_row, west_column], axis=1).astype(
        jnp.bfloat16
    )
    kept = jnp.where((meeting == 4)[:, :, None], corners, jnp.zeros_like(corners)).astype(
        jnp.bfloat16
    )
    return (edge_cells, kept)


def add_returns(full, ghost_rows, ghost_corners):
    length = full.shape[1] - 2
    interior = full[:, 1 : length + 1, 1 : length + 1]
    ghost_rows = ghost_rows.astype(jnp.float32)
    ghost_corners = ghost_corners.astype(jnp.float32)
    interior = interior.at[:, 0, :].add(ghost_rows[:, 0])
    interior = interior.at[:, :, length - 1].add(ghost_rows[:, 1])
    interior = interior.at[:, length - 1, :].add(ghost_rows[:, 2])
    interior = interior.at[:, :, 0].add(ghost_rows[:, 3])
    interior = interior.at[:, 0, 0].add(ghost_corners[:, 0])
    interior = interior.at[:, 0, length - 1].add(ghost_corners[:, 1])
    interior = interior.at[:, length - 1, length - 1].add(ghost_corners[:, 2])
    interior = interior.at[:, length - 1, 0].add(ghost_corners[:, 3])
    return interior


def convolve(padded, kernel):
    return lax.conv_general_dilated(
        padded,
        kernel,
        (1, 1),
        "VALID",
        dimension_numbers=layout_names,
        preferred_element_type=jnp.float32,
    )


def spread_back(gradient, kernel):
    turned_kernel = jnp.transpose(kernel[::-1, ::-1], (0, 1, 3, 2))
    return lax.conv_general_dilated(
        gradient,
        turned_kernel,
        (1, 1),
        ((2, 2), (2, 2)),
        dimension_numbers=layout_names,
        preferred_element_type=jnp.float32,
    )


def per_device(network_conditions, subsequent_targets, w_first, w_second, tile_links):
    field_here = network_conditions[0]
    goal_here = subsequent_targets[0]
    number = field_here.shape[0]
    length = field_here.shape[1]
    gradient_scale = 1.0 / math.sqrt(
        lax.axis_size("ens") * lax.axis_size("tile") * number * length * length
    )
    pack, unpack = routes(tile_links)
    edge_cells, corner_cells = rim_frame(field_here)
    ghost_rows, ghost_corners = move_frames(edge_cells, corner_cells, pack, unpack)
    field_pad = with_ghosts(field_here, ghost_rows, ghost_corners, tile_links)
    where = coordinates()
    field_parts = pool_halves(field_pad, where, lambda x: x // 2)
    pre_first = convolve(field_pad, w_first)
    hidden = gelu_value(pre_first).astype(jnp.bfloat16)
    edge_cells, corner_cells = rim_frame(hidden)
    ghost_rows, ghost_corners = move_frames(edge_cells, corner_cells, pack, unpack)
    hidden_pad = with_ghosts(hidden, ghost_rows, ghost_corners, tile_links)
    pre_second = convolve(hidden_pad, w_second)
    estimated_states = field_here.astype(jnp.float32) + pre_second
    layer_prognosis = estimated_states.astype(jnp.bfloat16)
    misfit = estimated_states - goal_here.astype(jnp.float32)
    misfit_low = misfit.astype(jnp.bfloat16)
    closing_terms = slope_terms(
        pool_halves(hidden_pad, where, lambda x: x // 2),
        pool_halves(misfit_low, where, lambda x: x % 2),
        where,
    )
    spread = spread_back(misfit_low, w_second)
    edge_cells, corner_cells = ghost_grads(spread, tile_links)
    ghost_rows, ghost_corners = move_frames(edge_cells, corner_cells, pack, unpack)
    hidden_grad = add_returns(spread, ghost_rows, ghost_corners)
    first_low = (hidden_grad * gelu_slope(pre_first)).astype(jnp.bfloat16)
    opening_terms = slope_terms(
        field_parts, pool_halves(first_low, where, lambda x: x % 2), where
    )
    slopes = finish_slopes(opening_terms, closing_terms, gradient_scale, where)
    spread = spread_back(first_low, w_first)
    edge_cells, corner_cells = ghost_grads(spread, tile_links)
    ghost_rows, ghost_corners = move_frames(edge_cells, corner_cells, pack, unpack)
    condition_derivative = misfit + add_returns(spread, ghost_rows, ghost_corners)
    return (
        layer_prognosis[None],
        condition_derivative[None],
        slopes[0].reshape(w_first.shape),
        slopes[1].reshape(w_second.shape),
    )


def solution(mesh):
    return jax.shard_map(
        per_device,
        mesh=mesh,
        in_specs=(
            P("ens", "tile", None, None, None),
            P("ens", "tile", None, None, None),
            P(),
            P(),
            P("tile", None),
        ),
        out_specs=(
            P("ens", "tile", None, None, None),
            P("ens", "tile", None, None, None),
            P(),
            P(),
        ),
        check_vma=False,
    )
```

profile of v0, /device:TPU:1, one launch (start us, length us, event | category | flops | bytes accessed | tf_op | source)
XLA Modules:
  0.0 191.7 jit_solution(9804225951800223849)
XLA Ops:
  3.9 1.0 fusion.125
  6.4 1.1 convolution_convert_fusion.3
  7.5 9.2 %all-to-all-start = ((bf16[32,32,256]{2,1,0:T(8,128)(2,1)}), bf16[32,32,256]{2,1,0:T(8,128)(2,1)S(1)}, u32[]{:S(2)}, u32[]{:S(2)}) async-start(bf16[32,32,256]{2,1,0:T(8,128)(2,1)} %bitcast.4), calls=%async_computation | async-start | bytes 1048576 | tf_op jit(solution)/shard_map/all_to_all | solution.py:96
  17.0 9.6 %all-to-all-done = bf16[32,32,256]{2,1,0:T(8,128)(2,1)S(1)} async-done(((bf16[32,32,256]{2,1,0:T(8,128)(2,1)}), bf16[32,32,256]{2,1,0:T(8,128)(2,1)S(1)}, u32[]{:S(2)}, u32[]{:S(2)}) %all-to-all-start) | async-done | bytes 524320 | tf_op jit(solution)/shard_map/all_to_all | solution.py:96
  29.1 1.1 convolution_convert_fusion.2
  30.2 5.9 %all-to-all-start.1 = ((bf16[32,32,256]{2,1,0:T(8,128)(2,1)}), bf16[32,32,256]{2,1,0:T(8,128)(2,1)}, u32[]{:S(2)}, u32[]{:S(2)}) async-start(bf16[32,32,256]{2,1,0:T(8,128)(2,1)} %bitcast.20), calls=%async_computation.1 | async-start | bytes 1048576 | tf_op jit(solution)/shard_map/all_to_all | solution.py:96
  36.3 9.5 %all-to-all-done.1 = bf16[32,32,256]{2,1,0:T(8,128)(2,1)} async-done(((bf16[32,32,256]{2,1,0:T(8,128)(2,1)}), bf16[32,32,256]{2,1,0:T(8,128)(2,1)}, u32[]{:S(2)}, u32[]{:S(2)}) %all-to-all-start.1) | async-done | bytes 524320 | tf_op jit(solution)/shard_map/all_to_all | solution.py:96
  45.8 1.3 convolution_convert_fusion.6
  47.6 1.5 fusion.28
  49.2 1.0 fusion.39
  50.2 1.1 fusion.42
  51.8 1.1 convolution_convert_fusion.1
  52.9 5.9 %all-to-all-start.2 = ((bf16[32,32,256]{2,1,0:T(8,128)(2,1)}), bf16[32,32,256]{2,1,0:T(8,128)(2,1)}, u32[]{:S(2)}, u32[]{:S(2)}) async-start(bf16[32,32,256]{2,1,0:T(8,128)(2,1)} %bitcast.56), calls=%async_computation.2 | async-start | bytes 1048576 | tf_op jit(solution)/shard_map/all_to_all | solution.py:96
  61.2 2.4 %collective-permute-start.2 = (bf16[3,10,10,128]{3,2,1,0:T(8,128)(2,1)}, bf16[3,10,10,128]{3,2,1,0:T(8,128)(2,1)S(1)}, u32[]{:S(2)}, u32[]{:S(2)}) collective-permute-start(bf16[3,10,10,128]{3,2,1,0:T(8,128)(2,1)} %get-tuple-element.434), channel_id=1, source_target_pairs={{0,24},{1,25},{32,56},{33,57},{2,26},{3,27},{34,58},{35,59},{4,28}... | collective-permute-start | bytes 230408 | tf_op jit(solution)/shard_map/ppermute | solution.py:124
  64.4 4.0 %all-to-all-done.2 = bf16[32,32,256]{2,1,0:T(8,128)(2,1)} async-done(((bf16[32,32,256]{2,1,0:T(8,128)(2,1)}), bf16[32,32,256]{2,1,0:T(8,128)(2,1)}, u32[]{:S(2)}, u32[]{:S(2)}) %all-to-all-start.2) | async-done | bytes 524320 | tf_op jit(solution)/shard_map/all_to_all | solution.py:96
  68.4 1.3 convolution_convert_fusion.5
  70.3 1.9 broadcast_select_fusion.17
  72.1 1.3 scatter-add.129
  73.6 1.1 fusion.38
  74.7 1.2 fusion.40
  77.0 1.1 convolution_convert_fusion
  78.1 5.8 %all-to-all-start.3 = ((bf16[32,32,256]{2,1,0:T(8,128)(2,1)}), bf16[32,32,256]{2,1,0:T(8,128)(2,1)S(1)}, u32[]{:S(2)}, u32[]{:S(2)}) async-start(bf16[32,32,256]{2,1,0:T(8,128)(2,1)} %bitcast.90), calls=%async_computation.3 | async-start | bytes 1048576 | tf_op jit(solution)/shard_map/all_to_all | solution.py:96
  83.9 2.5 %collective-permute-start.12 = (bf16[3,8,8,128]{3,2,1,0:T(8,128)(2,1)S(1)}, bf16[3,8,8,128]{3,2,1,0:T(8,128)(2,1)S(1)}, u32[]{:S(2)}, u32[]{:S(2)}) collective-permute-start(bf16[3,8,8,128]{3,2,1,0:T(8,128)(2,1)S(1)} %get-tuple-element.446), channel_id=1, source_target_pairs={{0,24},{1,25},{32,56},{33,57},{2,26},{3,27},{34,58},{35,59},{4,28}... | collective-permute-start | bytes 147464 | tf_op jit(solution)/shard_map/ppermute | solution.py:124
  87.7 1.6 collective-permute-start
  89.9 5.3 %collective-permute-start.9 = (bf16[3,10,10,128]{3,2,1,0:T(8,128)(2,1)S(1)}, bf16[3,10,10,128]{3,2,1,0:T(8,128)(2,1)S(1)}, u32[]{:S(2)}, u32[]{:S(2)}) collective-permute-start(bf16[3,10,10,128]{3,2,1,0:T(8,128)(2,1)S(1)} %get-tuple-element.438), channel_id=1, source_target_pairs={{0,24},{1,25},{32,56},{33,57},{2,26},{3,27},{34,58},{35,59},{4,28}... | collective-permute-start | bytes 230408 | tf_op jit(solution)/shard_map/ppermute | solution.py:124
  96.5 2.7 %collective-permute-done.9.refs_3_ = bf16[3,10,10,128]{3,2,1,0:T(8,128)(2,1)S(1)} collective-permute-done((bf16[3,10,10,128]{3,2,1,0:T(8,128)(2,1)S(1)}, bf16[3,10,10,128]{3,2,1,0:T(8,128)(2,1)S(1)}, u32[]{:S(2)}, u32[]{:S(2)}) %collective-permute-start.9) | collective-permute-done | bytes 76832 | tf_op jit(solution)/shard_map/ppermute | solution.py:124
  99.2 3.4 %collective-permute-start.5 = (bf16[3,8,8,128]{3,2,1,0:T(8,128)(2,1)}, bf16[3,8,8,128]{3,2,1,0:T(8,128)(2,1)S(1)}, u32[]{:S(2)}, u32[]{:S(2)}) collective-permute-start(bf16[3,8,8,128]{3,2,1,0:T(8,128)(2,1)} %get-tuple-element.442), channel_id=1, source_target_pairs={{0,24},{1,25},{32,56},{33,57},{2,26},{3,27},{34,58},{35,59},{4,28}... | collective-permute-start | bytes 147464 | tf_op jit(solution)/shard_map/ppermute | solution.py:124
  103.9 2.9 %collective-permute-start.13 = (f32[32,18,128]{2,1,0:T(8,128)S(1)}, f32[32,18,128]{2,1,0:T(8,128)S(1)}, u32[]{:S(2)}, u32[]{:S(2)}) collective-permute-start(f32[32,18,128]{2,1,0:T(8,128)S(1)} %get-tuple-element.397), channel_id=1, source_target_pairs={{0,1},{1,0},{32,33},{33,32},{2,3},{3,2},{34,35},{35,34},{4,5},{5,4... | collective-permute-start | bytes 884744 | tf_op jit(solution)/shard_map/ppermute | solution.py:124
  108.4 4.0 %collective-permute-start.6 = (f32[32,18,128]{2,1,0:T(8,128)S(1)}, f32[32,18,128]{2,1,0:T(8,128)S(1)}, u32[]{:S(2)}, u32[]{:S(2)}) collective-permute-start(f32[32,18,128]{2,1,0:T(8,128)S(1)} %get-tuple-element.395), channel_id=1, source_target_pairs={{0,1},{1,0},{32,33},{33,32},{2,3},{3,2},{34,35},{35,34},{4,5},{5,4... | collective-permute-start | bytes 884744 | tf_op jit(solution)/shard_map/ppermute | solution.py:124
  112.4 1.3 collective-permute-done.6
  114.7 10.1 %all-to-all-start.4 = ((f32[32,18,256]{2,1,0:T(8,128)}), f32[32,18,256]{2,1,0:T(8,128)S(1)}, u32[]{:S(2)}, u32[]{:S(2)}) async-start(f32[32,18,256]{2,1,0:T(8,128)} %pad_maximum_fusion), calls=%async_computation.4 | async-start | bytes 1572864 | tf_op jit(solution)/shard_map/all_to_all | solution.py:235
  126.5 1.7 scatter-add.146
  128.2 1.3 fusion.58
  130.5 13.1 %all-to-all-done.4 = f32[32,18,256]{2,1,0:T(8,128)S(1)} async-done(((f32[32,18,256]{2,1,0:T(8,128)}), f32[32,18,256]{2,1,0:T(8,128)S(1)}, u32[]{:S(2)}, u32[]{:S(2)}) %all-to-all-start.4) | async-done | bytes 589856 | tf_op jit(solution)/shard_map/all_to_all | solution.py:235
  144.5 8.9 %all-to-all-start.5 = ((bf16[32,36,128]{2,1,0:T(8,128)(2,1)}), bf16[32,36,128]{2,1,0:T(8,128)(2,1)S(1)}, u32[]{:S(2)}, u32[]{:S(2)}) async-start(bf16[32,36,128]{2,1,0:T(8,128)(2,1)} %broadcast_in_dim.121), calls=%async_computation.5 | async-start | bytes 655360 | tf_op jit(solution)/shard_map/all_to_all | solution.py:235
  153.4 1.7 scatter-add.150
  156.5 1.4 scatter-add.154
  157.8 5.6 %all-to-all-done.5.refs_0_ = bf16[32,36,128]{2,1,0:T(8,128)(2,1)S(1)} async-done(((bf16[32,36,128]{2,1,0:T(8,128)(2,1)}), bf16[32,36,128]{2,1,0:T(8,128)(2,1)S(1)}, u32[]{:S(2)}, u32[]{:S(2)}) %all-to-all-start.5) | async-done | bytes 294944 | tf_op jit(solution)/shard_map/all_to_all | solution.py:235
  164.9 2.6 %broadcast_select_fusion.16 = f32[3,1,1,256]{3,1,2,0:T(1,128)S(1)} fusion(pred[]{:T(512)} %and_reduce_fusion, f32[3,8,8,256]{3,1,2,0:T(8,128)} %scatter-add.154, s32[]{:T(128)} %bitcast.64, s32[]{:T(128)} %bitcast.65, f32[3,4,256]{2,1,0:T(4,128)S(1)} %reshape.1601), kind=kLoop, calls=%fused_computation.165 | loop fusion | flops 1536 | bytes 9225 | tf_op jit(solution)/shard_map/select.61
  167.5 2.6 %scatter-add.155 = f32[3,8,8,256]{3,1,2,0:T(8,128)} dynamic-update-slice(f32[3,8,8,256]{3,1,2,0:T(8,128)} %scatter-add.154, f32[3,1,1,256]{3,1,2,0:T(1,128)S(1)} %broadcast_select_fusion.16, s32[]{:T(128)} %constant.949.clone.1, s32[]{:T(128)} %bitcast.64, s32[]{:T(128)} %bitcast.65, s32[]{:T(128)} %constant.949.clone.1) | dynamic-update-slice | bytes 6148 | tf_op jit(solution)/shard_map/scatter-add | solution.py:338
  170.8 1.4 scatter-add.156
  172.2 5.0 %collective-permute-start.17 = (bf16[32,36,128]{2,1,0:T(8,128)(2,1)S(1)}, bf16[32,36,128]{2,1,0:T(8,128)(2,1)S(1)}, u32[]{:S(2)}, u32[]{:S(2)}) collective-permute-start(bf16[32,36,128]{2,1,0:T(8,128)(2,1)S(1)} %all-to-all-done.5.refs_0_), channel_id=1, source_target_pairs={{0,1},{1,0},{32,33},{33,32},{2,3},{3,2},{34,35},{35,34},{4,5},{5,4... | collective-permute-start | bytes 884744 | tf_op jit(solution)/shard_map/ppermute | solution.py:124
  177.2 1.5 collective-permute-start.19
  179.6 2.5 %collective-permute-start.18 = (bf16[32,36,128]{2,1,0:T(8,128)(2,1)S(1)}, bf16[32,36,128]{2,1,0:T(8,128)(2,1)}, u32[]{:S(2)}, u32[]{:S(2)}) collective-permute-start(bf16[32,36,128]{2,1,0:T(8,128)(2,1)S(1)} %collective-permute-done.14.refs_1_), channel_id=1, source_target_pairs={{0,1},{1,0},{32,33},{33,32},{2,3},{3,2},{34,35},{35,34},{4,5},{5,4... | collective-permute-start | bytes 884744 | tf_op jit(solution)/shard_map/ppermute | solution.py:124
  182.8 1.7 copy.325
  184.5 1.4 scatter-add.159
  185.8 1.9 add_bitcast_fusion
  187.7 3.9 %spread_slopes.1 = (f32[9,256,256]{2,1,0:T(8,128)}, f32[9,256,256]{2,1,0:T(8,128)}) custom-call(s32[2]{0:T(128)S(1)} %pad_add_fusion.2.x_ref, bf16[32,36,128]{2,1,0:T(8,128)(2,1)S(1)} %all-to-all-done.5.refs_0_, bf16[32,36,128]{2,1,0:T(8,128)(2,1)S(1)} %collective-permute-done.14.refs_1_, bf16[32,36,128]{2,1,0:T(8,128)(2,1)S(1)} %collective-permute-done.15.refs_2_, ...), custom_call_target="tpu_custom_call" | custom-call | flops 1000 | bytes 7000000 | tf_op jit(solution)/shard_map/spread_slopes/pallas_call | solution.py:214
  (220 shorter events, 28.3 us)
Async XLA Ops:
  0.6 47.0 %copy-start = (bf16[3,3,256,256]{3,2,1,0:T(8,128)(2,1)S(1)}, bf16[3,3,256,256]{3,2,1,0:T(8,128)(2,1)}, u32[]{:S(2)}) copy-start(bf16[3,3,256,256]{3,2,1,0:T(8,128)(2,1)} %param.72) | copy-start | bytes 3538948
  7.5 19.1 %all-to-all-start = ((bf16[32,32,256]{2,1,0:T(8,128)(2,1)}), bf16[32,32,256]{2,1,0:T(8,128)(2,1)S(1)}, u32[]{:S(2)}, u32[]{:S(2)}) async-start(bf16[32,32,256]{2,1,0:T(8,128)(2,1)} %bitcast.4), calls=%async_computation | async-start | bytes 1048576 | tf_op jit(solution)/shard_map/all_to_all | solution.py:96
  26.6 0.9 copy-start.1
  26.6 1.3 copy-start.2
  28.8 20.3 %copy-start.3 = (f32[3,8,8,256]{3,0,2,1:T(4,128)}, f32[3,8,8,256]{3,0,2,1:T(4,128)S(1)}, u32[]{:S(2)}) copy-start(f32[3,8,8,256]{3,0,2,1:T(4,128)S(1)} %fusion.30) | copy-start | bytes 589828
  30.2 15.6 %all-to-all-start.1 = ((bf16[32,32,256]{2,1,0:T(8,128)(2,1)}), bf16[32,32,256]{2,1,0:T(8,128)(2,1)}, u32[]{:S(2)}, u32[]{:S(2)}) async-start(bf16[32,32,256]{2,1,0:T(8,128)(2,1)} %bitcast.20), calls=%async_computation.1 | async-start | bytes 1048576 | tf_op jit(solution)/shard_map/all_to_all | solution.py:96
  47.6 1.6 copy-start.4
  47.6 1.6 copy-start.6
  51.6 8.1 %copy-start.8 = (s32[4]{0:T(128)S(1)}, s32[4]{0:T(128)}, u32[]{:S(2)}) copy-start(s32[4]{0:T(128)} %constant.967.clone.1) | copy-start | bytes 52
  52.9 15.5 %all-to-all-start.2 = ((bf16[32,32,256]{2,1,0:T(8,128)(2,1)}), bf16[32,32,256]{2,1,0:T(8,128)(2,1)}, u32[]{:S(2)}, u32[]{:S(2)}) async-start(bf16[32,32,256]{2,1,0:T(8,128)(2,1)} %bitcast.56), calls=%async_computation.2 | async-start | bytes 1048576 | tf_op jit(solution)/shard_map/all_to_all | solution.py:96
  61.2 26.4 %collective-permute-start.2 = (bf16[3,10,10,128]{3,2,1,0:T(8,128)(2,1)}, bf16[3,10,10,128]{3,2,1,0:T(8,128)(2,1)S(1)}, u32[]{:S(2)}, u32[]{:S(2)}) collective-permute-start(bf16[3,10,10,128]{3,2,1,0:T(8,128)(2,1)} %get-tuple-element.434), channel_id=1, source_target_pairs={{0,24},{1,25},{32,56},{33,57},{2,26},{3,27},{34,58},{35,59},{4,28}... | collective-permute-start | bytes 230408 | tf_op jit(solution)/shard_map/ppermute | solution.py:124
  63.6 40.3 %collective-permute-start.1 = (bf16[3,10,10,128]{3,2,1,0:T(8,128)(2,1)}, bf16[3,10,10,128]{3,2,1,0:T(8,128)(2,1)S(1)}, u32[]{:S(2)}, u32[]{:S(2)}) collective-permute-start(bf16[3,10,10,128]{3,2,1,0:T(8,128)(2,1)} %get-tuple-element.435), channel_id=1, source_target_pairs={{0,16},{1,17},{32,48},{33,49},{2,18},{3,19},{34,50},{35,51},{4,20}... | collective-permute-start | bytes 230408 | tf_op jit(solution)/shard_map/ppermute | solution.py:124
  76.9 10.8 %copy-start.5 = (bf16[3,10,10,256]{3,2,1,0:T(8,128)(2,1)S(1)}, bf16[3,10,10,256]{3,2,1,0:T(8,128)(2,1)}, u32[]{:S(2)}) copy-start(bf16[3,10,10,256]{3,2,1,0:T(8,128)(2,1)} %copy-done.4) | copy-start | bytes 460804
  78.1 36.6 %all-to-all-start.3 = ((bf16[32,32,256]{2,1,0:T(8,128)(2,1)}), bf16[32,32,256]{2,1,0:T(8,128)(2,1)S(1)}, u32[]{:S(2)}, u32[]{:S(2)}) async-start(bf16[32,32,256]{2,1,0:T(8,128)(2,1)} %bitcast.90), calls=%async_computation.3 | async-start | bytes 1048576 | tf_op jit(solution)/shard_map/all_to_all | solution.py:96
  83.9 5.9 %collective-permute-start.12 = (bf16[3,8,8,128]{3,2,1,0:T(8,128)(2,1)S(1)}, bf16[3,8,8,128]{3,2,1,0:T(8,128)(2,1)S(1)}, u32[]{:S(2)}, u32[]{:S(2)}) collective-permute-start(bf16[3,8,8,128]{3,2,1,0:T(8,128)(2,1)S(1)} %get-tuple-element.446), channel_id=1, source_target_pairs={{0,24},{1,25},{32,56},{33,57},{2,26},{3,27},{34,58},{35,59},{4,28}... | collective-permute-start | bytes 147464 | tf_op jit(solution)/shard_map/ppermute | solution.py:124
  86.5 8.7 %collective-permute-start.11 = (bf16[3,8,8,128]{3,2,1,0:T(8,128)(2,1)S(1)}, bf16[3,8,8,128]{3,2,1,0:T(8,128)(2,1)S(1)}, u32[]{:S(2)}, u32[]{:S(2)}) collective-permute-start(bf16[3,8,8,128]{3,2,1,0:T(8,128)(2,1)S(1)} %get-tuple-element.447), channel_id=1, source_target_pairs={{0,16},{1,17},{32,48},{33,49},{2,18},{3,19},{34,50},{35,51},{4,20}... | collective-permute-start | bytes 147464 | tf_op jit(solution)/shard_map/ppermute | solution.py:124
  87.0 8.2 %collective-permute-start.10 = (bf16[3,8,8,128]{3,2,1,0:T(8,128)(2,1)S(1)}, bf16[3,8,8,128]{3,2,1,0:T(8,128)(2,1)S(1)}, u32[]{:S(2)}, u32[]{:S(2)}) collective-permute-start(bf16[3,8,8,128]{3,2,1,0:T(8,128)(2,1)S(1)} %get-tuple-element.449), channel_id=1, source_target_pairs={{0,8},{1,9},{32,40},{33,41},{2,10},{3,11},{34,42},{35,43},{4,12},{... | collective-permute-start | bytes 147464 | tf_op jit(solution)/shard_map/ppermute | solution.py:124
  87.7 19.2 %collective-permute-start = (bf16[3,10,10,128]{3,2,1,0:T(8,128)(2,1)}, bf16[3,10,10,128]{3,2,1,0:T(8,128)(2,1)S(1)}, u32[]{:S(2)}, u32[]{:S(2)}) collective-permute-start(bf16[3,10,10,128]{3,2,1,0:T(8,128)(2,1)} %get-tuple-element.437), channel_id=1, source_target_pairs={{0,8},{1,9},{32,40},{33,41},{2,10},{3,11},{34,42},{35,43},{4,12},{... | collective-permute-start | bytes 230408 | tf_op jit(solution)/shard_map/ppermute | solution.py:124
  89.9 9.3 %collective-permute-start.9 = (bf16[3,10,10,128]{3,2,1,0:T(8,128)(2,1)S(1)}, bf16[3,10,10,128]{3,2,1,0:T(8,128)(2,1)S(1)}, u32[]{:S(2)}, u32[]{:S(2)}) collective-permute-start(bf16[3,10,10,128]{3,2,1,0:T(8,128)(2,1)S(1)} %get-tuple-element.438), channel_id=1, source_target_pairs={{0,24},{1,25},{32,56},{33,57},{2,26},{3,27},{34,58},{35,59},{4,28}... | collective-permute-start | bytes 230408 | tf_op jit(solution)/shard_map/ppermute | solution.py:124
  95.2 7.4 %collective-permute-start.8 = (bf16[3,10,10,128]{3,2,1,0:T(8,128)(2,1)S(1)}, bf16[3,10,10,128]{3,2,1,0:T(8,128)(2,1)S(1)}, u32[]{:S(2)}, u32[]{:S(2)}) collective-permute-start(bf16[3,10,10,128]{3,2,1,0:T(8,128)(2,1)S(1)} %get-tuple-element.439), channel_id=1, source_target_pairs={{0,16},{1,17},{32,48},{33,49},{2,18},{3,19},{34,50},{35,51},{4,20}... | collective-permute-start | bytes 230408 | tf_op jit(solution)/shard_map/ppermute | solution.py:124
  95.2 7.4 %collective-permute-start.7 = (bf16[3,10,10,128]{3,2,1,0:T(8,128)(2,1)S(1)}, bf16[3,10,10,128]{3,2,1,0:T(8,128)(2,1)S(1)}, u32[]{:S(2)}, u32[]{:S(2)}) collective-permute-start(bf16[3,10,10,128]{3,2,1,0:T(8,128)(2,1)S(1)} %get-tuple-element.441), channel_id=1, source_target_pairs={{0,8},{1,9},{32,40},{33,41},{2,10},{3,11},{34,42},{35,43},{4,12},{... | collective-permute-start | bytes 230408 | tf_op jit(solution)/shard_map/ppermute | solution.py:124
  99.2 7.7 %collective-permute-start.5 = (bf16[3,8,8,128]{3,2,1,0:T(8,128)(2,1)}, bf16[3,8,8,128]{3,2,1,0:T(8,128)(2,1)S(1)}, u32[]{:S(2)}, u32[]{:S(2)}) collective-permute-start(bf16[3,8,8,128]{3,2,1,0:T(8,128)(2,1)} %get-tuple-element.442), channel_id=1, source_target_pairs={{0,24},{1,25},{32,56},{33,57},{2,26},{3,27},{34,58},{35,59},{4,28}... | collective-permute-start | bytes 147464 | tf_op jit(solution)/shard_map/ppermute | solution.py:124
  102.6 4.8 %collective-permute-start.4 = (bf16[3,8,8,128]{3,2,1,0:T(8,128)(2,1)}, bf16[3,8,8,128]{3,2,1,0:T(8,128)(2,1)S(1)}, u32[]{:S(2)}, u32[]{:S(2)}) collective-permute-start(bf16[3,8,8,128]{3,2,1,0:T(8,128)(2,1)} %get-tuple-element.443), channel_id=1, source_target_pairs={{0,16},{1,17},{32,48},{33,49},{2,18},{3,19},{34,50},{35,51},{4,20}... | collective-permute-start | bytes 147464 | tf_op jit(solution)/shard_map/ppermute | solution.py:124
  102.6 5.0 %collective-permute-start.3 = (bf16[3,8,8,128]{3,2,1,0:T(8,128)(2,1)}, bf16[3,8,8,128]{3,2,1,0:T(8,128)(2,1)S(1)}, u32[]{:S(2)}, u32[]{:S(2)}) collective-permute-start(bf16[3,8,8,128]{3,2,1,0:T(8,128)(2,1)} %get-tuple-element.445), channel_id=1, source_target_pairs={{0,8},{1,9},{32,40},{33,41},{2,10},{3,11},{34,42},{35,43},{4,12},{... | collective-permute-start | bytes 147464 | tf_op jit(solution)/shard_map/ppermute | solution.py:124
  103.9 8.4 %collective-permute-start.13 = (f32[32,18,128]{2,1,0:T(8,128)S(1)}, f32[32,18,128]{2,1,0:T(8,128)S(1)}, u32[]{:S(2)}, u32[]{:S(2)}) collective-permute-start(f32[32,18,128]{2,1,0:T(8,128)S(1)} %get-tuple-element.397), channel_id=1, source_target_pairs={{0,1},{1,0},{32,33},{33,32},{2,3},{3,2},{34,35},{35,34},{4,5},{5,4... | collective-permute-start | bytes 884744 | tf_op jit(solution)/shard_map/ppermute | solution.py:124
  108.4 5.4 %collective-permute-start.6 = (f32[32,18,128]{2,1,0:T(8,128)S(1)}, f32[32,18,128]{2,1,0:T(8,128)S(1)}, u32[]{:S(2)}, u32[]{:S(2)}) collective-permute-start(f32[32,18,128]{2,1,0:T(8,128)S(1)} %get-tuple-element.395), channel_id=1, source_target_pairs={{0,1},{1,0},{32,33},{33,32},{2,3},{3,2},{34,35},{35,34},{4,5},{5,4... | collective-permute-start | bytes 884744 | tf_op jit(solution)/shard_map/ppermute | solution.py:124
  114.7 28.9 %all-to-all-start.4 = ((f32[32,18,256]{2,1,0:T(8,128)}), f32[32,18,256]{2,1,0:T(8,128)S(1)}, u32[]{:S(2)}, u32[]{:S(2)}) async-start(f32[32,18,256]{2,1,0:T(8,128)} %pad_maximum_fusion), calls=%async_computation.4 | async-start | bytes 1572864 | tf_op jit(solution)/shard_map/all_to_all | solution.py:235
  125.7 0.8 copy-start.7
  144.5 18.9 %all-to-all-start.5 = ((bf16[32,36,128]{2,1,0:T(8,128)(2,1)}), bf16[32,36,128]{2,1,0:T(8,128)(2,1)S(1)}, u32[]{:S(2)}, u32[]{:S(2)}) async-start(bf16[32,36,128]{2,1,0:T(8,128)(2,1)} %broadcast_in_dim.121), calls=%async_computation.5 | async-start | bytes 655360 | tf_op jit(solution)/shard_map/all_to_all | solution.py:235
  163.4 13.8 %collective-permute-start.16 = (bf16[32,36,128]{2,1,0:T(8,128)(2,1)S(1)}, bf16[32,36,128]{2,1,0:T(8,128)(2,1)S(1)}, u32[]{:S(2)}, u32[]{:S(2)}) collective-permute-start(bf16[32,36,128]{2,1,0:T(8,128)(2,1)S(1)} %all-to-all-done.5.refs_0_), channel_id=1, source_target_pairs={{0,24},{1,25},{32,56},{33,57},{2,26},{3,27},{34,58},{35,59},{4,28}... | collective-permute-start | bytes 884744 | tf_op jit(solution)/shard_map/ppermute | solution.py:124
  163.4 13.8 %collective-permute-start.15 = (bf16[32,36,128]{2,1,0:T(8,128)(2,1)S(1)}, bf16[32,36,128]{2,1,0:T(8,128)(2,1)S(1)}, u32[]{:S(2)}, u32[]{:S(2)}) collective-permute-start(bf16[32,36,128]{2,1,0:T(8,128)(2,1)S(1)} %all-to-all-done.5.refs_0_), channel_id=1, source_target_pairs={{0,16},{1,17},{32,48},{33,49},{2,18},{3,19},{34,50},{35,51},{4,20}... | collective-permute-start | bytes 884744 | tf_op jit(solution)/shard_map/ppermute | solution.py:124
  164.2 15.4 %collective-permute-start.14 = (bf16[32,36,128]{2,1,0:T(8,128)(2,1)S(1)}, bf16[32,36,128]{2,1,0:T(8,128)(2,1)S(1)}, u32[]{:S(2)}, u32[]{:S(2)}) collective-permute-start(bf16[32,36,128]{2,1,0:T(8,128)(2,1)S(1)} %all-to-all-done.5.refs_0_), channel_id=1, source_target_pairs={{0,8},{1,9},{32,40},{33,41},{2,10},{3,11},{34,42},{35,43},{4,12},{... | collective-permute-start | bytes 884744 | tf_op jit(solution)/shard_map/ppermute | solution.py:124
  172.2 15.5 %collective-permute-start.17 = (bf16[32,36,128]{2,1,0:T(8,128)(2,1)S(1)}, bf16[32,36,128]{2,1,0:T(8,128)(2,1)S(1)}, u32[]{:S(2)}, u32[]{:S(2)}) collective-permute-start(bf16[32,36,128]{2,1,0:T(8,128)(2,1)S(1)} %all-to-all-done.5.refs_0_), channel_id=1, source_target_pairs={{0,1},{1,0},{32,33},{33,32},{2,3},{3,2},{34,35},{35,34},{4,5},{5,4... | collective-permute-start | bytes 884744 | tf_op jit(solution)/shard_map/ppermute | solution.py:124
  177.2 10.5 %collective-permute-start.20 = (bf16[32,36,128]{2,1,0:T(8,128)(2,1)S(1)}, bf16[32,36,128]{2,1,0:T(8,128)(2,1)S(1)}, u32[]{:S(2)}, u32[]{:S(2)}) collective-permute-start(bf16[32,36,128]{2,1,0:T(8,128)(2,1)S(1)} %collective-permute-done.16.refs_3_), channel_id=1, source_target_pairs={{0,1},{1,0},{32,33},{33,32},{2,3},{3,2},{34,35},{35,34},{4,5},{5,4... | collective-permute-start | bytes 884744 | tf_op jit(solution)/shard_map/ppermute | solution.py:124
  177.2 10.5 %collective-permute-start.19 = (bf16[32,36,128]{2,1,0:T(8,128)(2,1)S(1)}, bf16[32,36,128]{2,1,0:T(8,128)(2,1)S(1)}, u32[]{:S(2)}, u32[]{:S(2)}) collective-permute-start(bf16[32,36,128]{2,1,0:T(8,128)(2,1)S(1)} %collective-permute-done.15.refs_2_), channel_id=1, source_target_pairs={{0,1},{1,0},{32,33},{33,32},{2,3},{3,2},{34,35},{35,34},{4,5},{5,4... | collective-permute-start | bytes 884744 | tf_op jit(solution)/shard_map/ppermute | solution.py:124
  179.6 8.1 %collective-permute-start.18 = (bf16[32,36,128]{2,1,0:T(8,128)(2,1)S(1)}, bf16[32,36,128]{2,1,0:T(8,128)(2,1)}, u32[]{:S(2)}, u32[]{:S(2)}) collective-permute-start(bf16[32,36,128]{2,1,0:T(8,128)(2,1)S(1)} %collective-permute-done.14.refs_1_), channel_id=1, source_target_pairs={{0,1},{1,0},{32,33},{33,32},{2,3},{3,2},{34,35},{35,34},{4,5},{5,4... | collective-permute-start | bytes 884744 | tf_op jit(solution)/shard_map/ppermute | solution.py:124
where the time goes:
time: 195 us; the launch traced here: 192 us
  starting transfers between devices  81.2 us (42%)
  waiting for transfers between devices  48.2 us (25%)
  local copies, waits for them, and re-layouts  22.3 us (11%)
  other arithmetic  20.3 us (10%)
  matrix products  12.3 us (6%)
  Pallas kernels  5.47 us (3%)
    ppermute x21, starting transfers between devices, shifted(): return lax.ppermute(values, ('tile', 'ens'), pairs)  35.4 us
    all_to_all x4, starting transfers between devices, move_frames(): got = lax.all_to_all(sent, 'tile', 0, 0, tiled=True)  26.8 us
    all_to_all x4, waiting for transfers between devices, move_frames(): got = lax.all_to_all(sent, 'tile', 0, 0, tiled=True)  23.2 us
    all_to_all x2, starting transfers between devices, plane_exchange(): lax.all_to_all(values, ('tile', 'ens'), 0, 0, axis_index_groups=plane_gro...  19 us
    all_to_all x2, waiting for transfers between devices, plane_exchange(): lax.all_to_all(values, ('tile', 'ens'), 0, 0, axis_index_groups=plane_gro...  18.7 us
    ppermute x21, waiting for transfers between devices, shifted(): return lax.ppermute(values, ('tile', 'ens'), pairs)  6.32 us
    another operation x13, other arithmetic  5.32 us
    dot_general x4, matrix products, move_frames(): jnp.dot(pack, frame, preferred_element_type=jnp.float32)  4.36 us
  transfers between devices with their start and end apart: 27, of which 11 were waited for; matrix products, arithmetic and copies ran while one was open for 19% of the time, Pallas kernels for 1%

commit v1 on v0

v1 whole, which is shorter than its diff:
```python
import math

import jax
import jax.numpy as jnp
from jax import lax
from jax.experimental import pallas as pl
from jax.experimental.pallas import tpu as pltpu
from jax.sharding import PartitionSpec as P

tanh_scale = 0.7978845608028654
cubic_term = 0.044715
slot_rows = 32
send_rows = 1024
bf16, f32 = jnp.bfloat16, jnp.float32


def gelu_value(inputs):
    return (
        0.5
        * inputs
        * (1.0 + jnp.tanh(tanh_scale * (inputs + cubic_term * inputs * inputs * inputs)))
    )


def gelu_slope(inputs):
    tangent = jnp.tanh(tanh_scale * (inputs + cubic_term * inputs * inputs * inputs))
    return 0.5 * (1.0 + tangent) + 0.5 * inputs * (1.0 - tangent * tangent) * tanh_scale * (
        1.0 + 3.0 * cubic_term * inputs * inputs
    )


sizes = {"x": 4, "y": 4, "z": 8, "core": 2}


def place_of(x, y, z, core):
    return ((y * 2 + z % 2) * 4 + x) * 8 + (z // 2) * 2 + core


def shifted(values, axis, by):
    pairs = []
    for x in range(4):
        for y in range(4):
            for z in range(8):
                for core in range(2):
                    at = {"x": x, "y": y, "z": z, "core": core}
                    to = dict(at)
                    to[axis] = (at[axis] + by) % sizes[axis]
                    pairs.append((place_of(**at), place_of(**to)))
    return lax.ppermute(values, ("tile", "ens"), pairs)


def coordinates():
    tile = lax.axis_index("tile")
    ens = lax.axis_index("ens")
    return {
        "x": tile % 4,
        "y": tile // 8,
        "z": (ens // 2) * 2 + (tile // 4) % 2,
        "core": ens % 2,
    }


edge_starts = ((0, 3), (0, 1), (1, 2), (2, 3))
corner_ends = ((0, 0), (7, 0), (7, 7), (0, 7))
corner_cells = ((0, 0), (0, 1), (1, 1), (1, 0))
strips = [(tile, edge) for tile in range(3) for edge in range(4)]


def edge_slices(tile, edge, low, high):
    inner = slice(1, 9)
    return (
        (tile, low, inner),
        (tile, inner, high),
        (tile, high, inner),
        (tile, inner, low),
    )[edge]


def corner_at(corner, low, high):
    down, across = corner_cells[corner]
    return (high if down else low), (high if across else low)


def take_frame(grid, frame, links, low, high, kept):
    for i, (tile, edge) in enumerate(strips):
        frame[8 * i : 8 * i + 8] = grid[edge_slices(tile, edge, low, high)]
    for tile in range(3):
        for corner in range(4):
            row, column = corner_at(corner, low, high)
            cell = grid[tile, row, column : column + 1, :]
            if kept:
                cell = jnp.where(links[tile, 12 + corner] == 4, cell, 0.0)
            at = 96 + 4 * tile + corner
            frame[at : at + 1] = cell
    frame[108:128] = jnp.zeros((20, 256), f32)


def fill_ghosts(grid, got, links):
    for i, (tile, edge) in enumerate(strips):
        grid[edge_slices(tile, edge, 0, 9)] = got[8 * i : 8 * i + 8]
    for tile in range(3):
        for corner in range(4):
            row, column = corner_at(corner, 0, 9)
            at = 96 + 4 * tile + corner
            beside = [
                8 * (4 * tile + edge) + end
                for edge, end in zip(edge_starts[corner], corner_ends[corner])
            ]
            blend = 0.5 * (got[beside[0] : beside[0] + 1] + got[beside[1] : beside[1] + 1])
            grid[tile, row, column : column + 1, :] = jnp.where(
                links[tile, 12 + corner] == 4, got[at : at + 1], blend
            )


def split_corners(grid, links):
    for tile in range(3):
        for corner in range(4):
            row, column = corner_at(corner, 0, 9)
            near_row, near_column = corner_at(corner, 1, 8)
            cell = grid[tile, row, column : column + 1, :]
            half = jnp.where(links[tile, 12 + corner] == 3, 0.5 * cell, 0.0)
            grid[tile, row, near_column : near_column + 1, :] += half
            grid[tile, near_row, column : column + 1, :] += half


def add_returns(grid, got):
    for i, (tile, edge) in enumerate(strips):
        grid[edge_slices(tile, edge, 1, 8)] += got[8 * i : 8 * i + 8]
    for tile in range(3):
        for corner in range(4):
            row, column = corner_at(corner, 1, 8)
            at = 96 + 4 * tile + corner
            grid[tile, row, column : column + 1, :] += got[at : at + 1]


def pack_frame(pack_ref, frame, frame_ref, sent_ref):
    cells = frame[...].astype(bf16)
    frame_ref[...] = cells
    sent_ref[...] = jnp.dot(pack_ref[...], cells, preferred_element_type=f32).astype(bf16)


def unpack_frame(unpack_ref, recv_ref, frame_ref, got):
    got[...] = jnp.dot(
        unpack_ref[:, :send_rows], recv_ref[...], preferred_element_type=f32
    ) + jnp.dot(unpack_ref[:, send_rows:], frame_ref[...], preferred_element_type=f32)


def convolve(grid, weights):
    total = jnp.zeros((192, 256), f32)
    for across in range(3):
        columns = grid[:, :, across : across + 8, :]
        for down in range(3):
            window = columns[:, down : down + 8].reshape(192, 256).astype(bf16)
            total += jnp.dot(window, weights[3 * down + across], preferred_element_type=f32)
    return total


def spread_back(gradient, weights, grid, column):
    grid[...] = jnp.zeros_like(grid)
    for across in range(3):
        column[...] = jnp.zeros_like(column)
        for down in range(3):
            part = lax.dot_general(
                gradient,
                weights[3 * down + across],
                (((1,), (1,)), ((), ())),
                preferred_element_type=f32,
            )
            column[:, down : down + 8] += part.reshape(3, 8, 8, 256)
        grid[:, :, across : across + 8, :] += column[...]


def halves(place, flat, pick):
    for k in range(4):
        quarter = lax.rem(place[1] + k, 4)
        side = quarter // 2 if pick == 0 else lax.rem(quarter, 2)
        yield k, jnp.where(side == 0, flat[:, :128], flat[:, 128:]).astype(bf16)


def flatten_grid(grid, flat):
    flat[300:304] = jnp.zeros((4, 256), f32)
    for tile in range(3):
        for row in range(10):
            at = 100 * tile + 10 * row
            flat[at : at + 10] = grid[tile, row]


def route_kernel(links, place, field_ref, pack_ref, unpack_ref, frame_ref, sent_ref, grid, frame):
    here = place[0]

    def rows_of(tiles, sides, valid, base, width, local_base):
        device = [tile // 3 for tile in tiles]
        source = [lax.rem(tile, 3) * 4 + side for tile, side in zip(tiles, sides)]
        out = []
        for i in range(12):
            send_rank = take_rank = jnp.int32(0)
            for j in range(12):
                near = (device[j] == device[i]) & valid[j]
                if j < i:
                    send_rank += jnp.where(near, width, 0)
                if j != i:
                    take_rank += jnp.where(near & (source[j] < source[i]), width, 0)
            first = device[i] * slot_rows + base
            own = device[i] == here
            send = jnp.where(own | ~valid[i], -1000, first + send_rank)
            take = jnp.where(own, local_base + source[i] * width, first + take_rank)
            out.append((send, jnp.where(valid[i], take, -1000)))
        return out

    codes = [links[tile, 4 + edge] for tile, edge in strips]
    edges = rows_of(
        [links[tile, edge] for tile, edge in strips],
        [lax.rem(code, 4) for code in codes],
        [links[tile, edge] >= 0 for tile, edge in strips],
        0,
        8,
        send_rows,
    )
    across = [links[tile, 8 + corner] for tile, corner in strips]
    corners = rows_of(
        [jnp.maximum(c, 0) // 4 for c in across],
        [lax.rem(jnp.maximum(c, 0), 4) for c in across],
        [c >= 0 for c in across],
        24,
        1,
        send_rows + 96,
    )
    lane = lax.broadcasted_iota(jnp.int32, (8, 128), 1)
    row = lax.broadcasted_iota(jnp.int32, (128, 128), 0)
    send = jnp.full((8, 128), -1000, jnp.int32)
    take = jnp.full((128, 128), -1000, jnp.int32)
    for i in range(12):
        send = jnp.where(lane // 8 == i, edges[i][0] + lane % 8, send)
        send = jnp.where(lane == 96 + i, corners[i][0], send)
        turned = codes[i] // 4 == 1
        step = jnp.where(turned, 7 - row % 8, row % 8)
        take = jnp.where(row // 8 == i, edges[i][1] + step, take)
        take = jnp.where(row == 96 + i, corners[i][1], take)
    slot = lax.broadcasted_iota(jnp.int32, (send_rows, 128), 0)
    pack_ref[...] = jnp.where(slot == send[:1], 1.0, 0.0).astype(bf16)
    column = lax.broadcasted_iota(jnp.int32, (128, 128), 1)
    for m in range(9):
        unpack_ref[:, 128 * m : 128 * m + 128] = jnp.where(
            take == column + 128 * m, 1.0, 0.0
        ).astype(bf16)
    grid[:, 1:9, 1:9, :] = field_ref[...].astype(f32)
    take_frame(grid, frame, links, 1, 8, False)
    pack_frame(pack_ref, frame, frame_ref, sent_ref)


def first_kernel(
    links, place, field_ref, recv_ref, old_ref, pack_ref, unpack_ref, weights,
    hidden_ref, pre_ref, frame_ref, sent_ref, part0, part1, part2, part3,
    grid, frame, got, flat,
):
    unpack_frame(unpack_ref, recv_ref, old_ref, got)
    grid[:, 1:9, 1:9, :] = field_ref[...].astype(f32)
    fill_ghosts(grid, got, links)
    pre_first = convolve(grid, weights)
    pre_ref[...] = pre_first
    hidden = gelu_value(pre_first).astype(bf16)
    hidden_ref[...] = hidden
    flatten_grid(grid, flat)
    grid[:, 1:9, 1:9, :] = hidden.astype(f32).reshape(3, 8, 8, 256)
    take_frame(grid, frame, links, 1, 8, False)
    pack_frame(pack_ref, frame, frame_ref, sent_ref)
    parts = (part0, part1, part2, part3)
    for k, half in halves(place, flat, 0):
        parts[k][...] = half


def second_kernel(
    links, place, field_ref, goal_ref, hidden_ref, recv_ref, old_ref, pack_ref, unpack_ref, weights,
    held0, held1, held2,
    state_ref, misfit_ref, inner_ref, frame_ref, sent_ref, part0, part1, part2, part3,
    grid, frame, got, flat, column,
):
    unpack_frame(unpack_ref, recv_ref, old_ref, got)
    grid[:, 1:9, 1:9, :] = hidden_ref[...].astype(f32).reshape(3, 8, 8, 256)
    fill_ghosts(grid, got, links)
    states = field_ref[...].astype(f32).reshape(192, 256) + convolve(grid, weights)
    state_ref[...] = states.reshape(3, 8, 8, 256).astype(bf16)
    misfit = states - goal_ref[...].astype(f32).reshape(192, 256)
    misfit_ref[...] = misfit
    low = misfit.astype(bf16)
    flatten_grid(grid, flat)
    spread_back(low, weights, grid, column)
    split_corners(grid, links)
    take_frame(grid, frame, links, 0, 9, True)
    pack_frame(pack_ref, frame, frame_ref, sent_ref)
    inner_ref[...] = grid[:, 1:9, 1:9, :]
    parts = (part0, part1, part2, part3)
    for k, half in halves(place, flat, 0):
        parts[k][:304] = half
    for k, half in halves(place, low.astype(f32), 1):
        parts[k][304:] = half


def third_kernel(
    links, place, inner_ref, pre_ref, recv_ref, old_ref, pack_ref, unpack_ref, weights, held,
    last_ref, frame_ref, sent_ref, part0, part1, part2, part3,
    grid, frame, got, column,
):
    unpack_frame(unpack_ref, recv_ref, old_ref, got)
    grid[:, 1:9, 1:9, :] = inner_ref[...]
    add_returns(grid, got)
    hidden_grad = grid[:, 1:9, 1:9, :].reshape(192, 256)
    low = (hidden_grad * gelu_slope(pre_ref[...])).astype(bf16)
    parts = (part0, part1, part2, part3)
    for k, half in halves(place, low.astype(f32), 1):
        parts[k][...] = half
    spread_back(low, weights, grid, column)
    split_corners(grid, links)
    take_frame(grid, frame, links, 0, 9, True)
    pack_frame(pack_ref, frame, frame_ref, sent_ref)
    last_ref[...] = grid[:, 1:9, 1:9, :]


def last_kernel(last_ref, misfit_ref, recv_ref, old_ref, unpack_ref, out_ref, grid, got):
    unpack_frame(unpack_ref, recv_ref, old_ref, got)
    grid[:, 1:9, 1:9, :] = last_ref[...] + misfit_ref[...].reshape(3, 8, 8, 256)
    add_returns(grid, got)
    out_ref[...] = grid[:, 1:9, 1:9, :]


vmem = pl.BlockSpec(memory_space=pltpu.VMEM)
smem = pl.BlockSpec(memory_space=pltpu.SMEM)
left = pl.BlockSpec(memory_space=pl.ANY)
grid_shape = pltpu.VMEM((3, 10, 10, 256), f32)
frame_shape = pltpu.VMEM((128, 256), f32)
flat_shape = pltpu.VMEM((304, 256), f32)
column_shape = pltpu.VMEM((3, 10, 8, 256), f32)


def like(*shape, dtype=bf16):
    return jax.ShapeDtypeStruct(shape, dtype)


def run(kernel, name, args, specs, outs, scratch, flops):
    return pl.pallas_call(
        kernel,
        out_shape=outs,
        in_specs=specs,
        out_specs=jax.tree.map(lambda _: vmem, outs),
        scratch_shapes=scratch,
        compiler_params=pltpu.CompilerParams(vmem_limit_bytes=40 * 2**20),
        cost_estimate=pl.CostEstimate(flops=flops, bytes_accessed=3000000, transcendentals=0),
        name=name,
    )(*args)


def slope_kernel(split, place, *refs):
    count = 4 if split else 8
    parts = refs[:count]
    kept_ref, sent_ref, flat, wide, total = refs[count:]
    grads = []
    for n in range(4):
        flat[304 * n : 304 * n + 304] = parts[n][:304].astype(f32)
        grads.append(parts[n][304:] if split else parts[4 + n][...])
    grads = jnp.concatenate(grads, axis=0)
    low = place[2] == 0
    for across in range(3):
        for n in range(4):
            for tile in range(3):
                for row in range(10):
                    at = 304 * n + 100 * tile + 10 * row + across
                    wide[3 * n + tile, row] = flat[at : at + 8]
        for down in range(3):
            window = wide[:, down : down + 8].reshape(768, 128).astype(bf16)
            out = lax.dot_general(
                window, grads, (((0,), (0,)), ((), ())), preferred_element_type=f32
            )
            tap = (3 * down + across) * 64
            total[0, tap : tap + 64] = jnp.where(low, out[:64], out[64:])
            total[1, tap : tap + 64] = jnp.where(low, out[64:], out[:64])
    for j in range(32):
        kept_ref[j] = total[0, 18 * j : 18 * j + 18]
        sent_ref[j] = total[1, 18 * j : 18 * j + 18]


def slope_terms(parts, place, split):
    shape = like(32, 18, 128, dtype=f32)

    def kernel(*refs):
        slope_kernel(split, *refs)

    return run(
        kernel,
        "slope_terms",
        (place, *parts),
        [smem] + [vmem] * len(parts),
        (shape, shape),
        [
            pltpu.VMEM((1216, 128), f32),
            pltpu.VMEM((12, 10, 8, 128), f32),
            pltpu.VMEM((2, 576, 128), f32),
        ],
        2 * 9 * 768 * 128 * 128,
    )


def ring(parts, axis):
    return [shifted(part, axis, k) if k else part for k, part in enumerate(parts)]


def spread_kernel(place, *refs):
    parts = refs[:8]
    first_ref, second_ref, total = refs[8:]
    x, core = place[1], place[2]
    for k in range(4):
        quarter = lax.rem(x + 4 - k, 4)
        column = pl.multiple_of(lax.rem(quarter, 2) * 128, 128)
        for other in range(2):
            side = core if other == 0 else 1 - core
            row = pl.multiple_of((quarter // 2) * 128 + side * 64, 64)
            for j in range(32):
                piece = parts[4 * other + k][j].astype(jnp.float32)
                total[0, 18 * j : 18 * j + 18] = piece[:18]
                total[1, 18 * j : 18 * j + 18] = piece[18:36]
            first_ref[:, pl.ds(row, 64), pl.ds(column, 128)] = total[0].reshape(9, 64, 128)
            second_ref[:, pl.ds(row, 64), pl.ds(column, 128)] = total[1].reshape(9, 64, 128)


def spread_slopes(parts, place):
    shape = like(9, 256, 256, dtype=f32)
    return run(
        spread_kernel,
        "spread_slopes",
        (place, *parts),
        [smem] + [vmem] * 8,
        (shape, shape),
        [pltpu.VMEM((2, 576, 128), f32)],
        1000,
    )


def plane_groups():
    return [
        [place_of(x, y, z, core) for y in range(4) for z in range(8)]
        for x in range(4)
        for core in range(2)
    ]


def plane_exchange(values):
    return lax.all_to_all(
        values, ("tile", "ens"), 0, 0, axis_index_groups=plane_groups(), tiled=True
    )


def finish_slopes(first, second, scale, place):
    terms = plane_exchange(jnp.concatenate([first, second], axis=-1))
    mine = jnp.sum(terms, axis=0) * scale
    mine = jnp.concatenate([mine[:, :128], mine[:, 128:]], axis=0).astype(jnp.bfloat16)
    plane = plane_exchange(jnp.broadcast_to(mine[None], (32,) + mine.shape))
    own = [plane] + [shifted(plane, "x", k) for k in range(1, 4)]
    other = [shifted(part, "core", 1) for part in own]
    return spread_slopes(own + other, place)


def exchange(values):
    return lax.all_to_all(values, "tile", 0, 0, tiled=True)


def per_device(network_conditions, subsequent_targets, w_first, w_second, tile_links):
    field, goal = network_conditions[0], subsequent_targets[0]
    first_weights, second_weights = w_first.reshape(9, 256, 256), w_second.reshape(9, 256, 256)
    scale = 1.0 / math.sqrt(lax.axis_size("ens") * lax.axis_size("tile") * 192)
    where = coordinates()
    place = jnp.stack([lax.axis_index("tile"), where["x"], where["core"]])
    frame_like, sent_like, rows_like = like(128, 256), like(send_rows, 256), like(192, 256)
    inner_like = like(3, 8, 8, 256, dtype=f32)
    conv_flops = 2 * 9 * 192 * 256 * 256

    pack, unpack, frame, sent = run(
        route_kernel,
        "routes",
        (tile_links, place, field),
        [smem, smem, vmem],
        (like(send_rows, 128), like(128, send_rows + 128), frame_like, sent_like),
        [grid_shape, frame_shape],
        2 * send_rows * 128 * 256,
    )
    recv = exchange(sent)
    hidden, pre_first, frame, sent, *parts = run(
        first_kernel,
        "first_layer",
        (tile_links, place, field, recv, frame, pack, unpack, first_weights),
        [smem, smem] + [vmem] * 6,
        (rows_like, like(192, 256, dtype=f32), frame_like, sent_like) + (like(304, 128),) * 4,
        [grid_shape, frame_shape, frame_shape, flat_shape],
        conv_flops,
    )
    recv = exchange(sent)
    field_parts = ring(parts, "x")
    states, misfit, inner, frame, sent, *parts = run(
        second_kernel,
        "second_layer",
        (
            tile_links, place, field, goal, hidden, recv, frame, pack, unpack, second_weights,
            *field_parts[1:],
        ),
        [smem, smem] + [vmem] * 8 + [left] * 3,
        (like(3, 8, 8, 256), like(192, 256, dtype=f32), inner_like, frame_like, sent_like)
        + (like(496, 128),) * 4,
        [grid_shape, frame_shape, frame_shape, flat_shape, column_shape],
        2 * conv_flops,
    )
    recv = exchange(sent)
    closing, sent_closing = slope_terms(ring(parts, "x"), place, True)
    last, frame, sent, *parts = run(
        third_kernel,
        "first_gradient",
        (tile_links, place, inner, pre_first, recv, frame, pack, unpack, first_weights, closing),
        [smem, smem] + [vmem] * 7 + [left],
        (inner_like, frame_like, sent_like) + (like(192, 128),) * 4,
        [grid_shape, frame_shape, frame_shape, column_shape],
        conv_flops,
    )
    recv = exchange(sent)
    opening, sent_opening = slope_terms(field_parts + ring(parts, "x"), place, False)
    condition_derivative = run(
        last_kernel,
        "last_gradient",
        (last, misfit, recv, frame, unpack),
        [vmem] * 5,
        inner_like,
        [grid_shape, frame_shape],
        1000,
    )
    slopes = finish_slopes(
        opening + shifted(sent_opening, "core", 1),
        closing + shifted(sent_closing, "core", 1),
        scale,
        place,
    )
    return (
        states[None],
        condition_derivative[None],
        slopes[0].reshape(w_first.shape),
        slopes[1].reshape(w_second.shape),
    )


def solution(mesh):
    return jax.shard_map(
        per_device,
        mesh=mesh,
        in_specs=(
            P("ens", "tile", None, None, None),
            P("ens", "tile", None, None, None),
            P(),
            P(),
            P("tile", None),
        ),
        out_specs=(
            P("ens", "tile", None, None, None),
            P("ens", "tile", None, None, None),
            P(),
            P(),
        ),
        check_vma=False,
    )
```

time: 195 us -> 192 us (0.985)
  blocking collectives: 0 us -> 66.4 us
  starting transfers between devices: 81.2 us -> 52.5 us
  waiting for transfers between devices: 48.2 us -> 26.7 us
  other arithmetic: 20.3 us -> 0.29 us
  matrix products: 12.3 us -> 0 us
  Pallas kernels: 5.47 us -> 17.4 us
  local copies, waits for them, and re-layouts: 22.3 us -> 26.5 us
    all_to_all x0 -> x3, blocking collectives: none -> 66.4 us  [the longest x2 47.4 us: plane_exchange(): lax.all_to_all(values, ('tile', 'ens'), 0, 0, axis_index_groups=plane_gro...]
    all_to_all x6 -> x3, waiting for transfers between devices: 41.9 us -> 0.01 us  [exchange(): return lax.all_to_all(values, 'tile', 0, 0, tiled=True)]
    all_to_all x6 -> x3, starting transfers between devices: 45.8 us -> 20.5 us  [exchange(): return lax.all_to_all(values, 'tile', 0, 0, tiled=True)]
    unnamed x38 -> x86, local copies, waits for them, and re-layouts: 2.09 us -> 26.4 us
    ppermute x21 -> x18, waiting for transfers between devices: 6.32 us -> 26.6 us  [shifted(): return lax.ppermute(values, ('tile', 'ens'), pairs)]
    scatter-add x15 -> x0, local copies, waits for them, and re-layouts: 14 us -> none  [the longest x2 3.89 us: add_returns(): interior = interior.at[:, 0, length - 1].add(ghost_corners[:, 1])]
    pallas_call x3 -> x8, Pallas kernels: 5.47 us -> 17.4 us  [run(): pl.pallas_call(kernel, out_shape=outs, in_specs=specs, out_specs=jax.tree...]
    dot_general x8 -> x0, matrix products: 7.57 us -> none  [the longest x4 4.36 us: move_frames(): jnp.dot(pack, frame, preferred_element_type=jnp.float32)]
  transfers between devices with their start and end apart: 27 -> 21, of which waited for: 11 -> 8; matrix products, arithmetic and copies ran while one was open for 19% -> 0% of each run, Pallas kernels for 1% -> 2%
where the time goes in v1:
time: 192 us; the launch traced here: 191 us
  blocking collectives  66.4 us (35%)
  starting transfers between devices  52.5 us (27%)
  waiting for transfers between devices  26.7 us (14%)
  local copies, waits for them, and re-layouts  26.5 us (14%)
  Pallas kernels  17.4 us (9%)
    all_to_all x2, blocking collectives, plane_exchange(): lax.all_to_all(values, ('tile', 'ens'), 0, 0, axis_index_groups=plane_gro...  47.4 us
    ppermute x18, starting transfers between devices, shifted(): return lax.ppermute(values, ('tile', 'ens'), pairs)  32 us
    ppermute x18, waiting for transfers between devices, shifted(): return lax.ppermute(values, ('tile', 'ens'), pairs)  26.6 us
    unnamed x86, local copies, waits for them, and re-layouts  26.4 us
    all_to_all x3, starting transfers between devices, exchange(): return lax.all_to_all(values, 'tile', 0, 0, tiled=True)  20.5 us
    all_to_all x1, blocking collectives, exchange(): return lax.all_to_all(values, 'tile', 0, 0, tiled=True)  18.9 us
    pallas_call x8, Pallas kernels, run(): pl.pallas_call(kernel, out_shape=outs, in_specs=specs, out_specs=jax.tree...  17.4 us
  transfers between devices with their start and end apart: 21, of which 8 were waited for; matrix products, arithmetic and copies ran while one was open for 0% of the time, Pallas kernels for 2%

profile of v1, /device:TPU:1, one launch (start us, length us, event | category | flops | bytes accessed | tf_op | source)
XLA Modules:
  0.0 190.6 jit_solution(2595444824599951931)
XLA Ops:
  0.7 0.9 copy-done.4
  2.3 2.1 %routes.1 = (bf16[1024,128]{1,0:T(8,128)(2,1)S(1)}, bf16[128,1152]{1,0:T(8,128)(2,1)S(1)}, bf16[128,256]{1,0:T(8,128)(2,1)S(1)}, bf16[1024,256]{1,0:T(8,128)(2,1)S(1)}) custom-call(s32[3,16]{1,0:T(4,128)S(1)} %copy-done.31, s32[3]{0:T(128)S(1)} %pad_add_fusion.place.refs_0_, bf16[3,8,8,256]{3,2,1,0:T(8,128)(2,1)S(1)} %bitcast.28), custom_call_target="tpu_custom_call" | custom-call | flops 67108864 | bytes 3000000 | tf_op jit(solution)/shard_map/routes/pallas_call | solution.py:340
  4.5 18.9 %all_to_all.54 = bf16[32,32,256]{2,1,0:T(8,128)(2,1)S(1)} all-to-all(bf16[32,32,256]{2,1,0:T(8,128)(2,1)S(1)} %bitcast.27), channel_id=1, replica_groups=mesh['tile'=32,'ens'=8] {'tile'}, dimensions={0} | all-to-all | bytes 1048576 | tf_op jit(solution)/shard_map/all_to_all | solution.py:462
  23.4 1.3 copy-done
  24.7 0.9 copy-done.5
  26.2 2.7 %first_layer.1 = (bf16[192,256]{1,0:T(8,128)(2,1)S(1)}, f32[192,256]{1,0:T(8,128)S(1)}, bf16[128,256]{1,0:T(8,128)(2,1)S(1)}, bf16[1024,256]{1,0:T(8,128)(2,1)},...) custom-call(s32[3,16]{1,0:T(4,128)S(1)} %copy-done.32, ...), custom_call_target="tpu_custom_call" | custom-call | flops 226492416 | bytes 3000000 | tf_op jit(solution)/shard_map/first_layer/pallas_call | solution.py:340
  31.5 5.8 %all-to-all-start.1 = ((bf16[32,32,256]{2,1,0:T(8,128)(2,1)}), bf16[32,32,256]{2,1,0:T(8,128)(2,1)S(1)}, u32[]{:S(2)}, u32[]{:S(2)}) async-start(bf16[32,32,256]{2,1,0:T(8,128)(2,1)} %bitcast.8), calls=%async_computation.1 | async-start | bytes 1048576 | tf_op jit(solution)/shard_map/all_to_all | solution.py:462
  37.3 1.3 collective-permute-start
  38.6 2.4 %collective-permute-start.1 = (bf16[304,128]{1,0:T(8,128)(2,1)S(1)}, bf16[304,128]{1,0:T(8,128)(2,1)S(1)}, u32[]{:S(2)}, u32[]{:S(2)}) collective-permute-start(bf16[304,128]{1,0:T(8,128)(2,1)S(1)} %get-tuple-element.46), channel_id=1, source_target_pairs={{0,16},{1,17},{32,48},{33,49},{2,18},{3,19},{34,50},{35,51},{4,20}... | collective-permute-start | bytes 233480 | tf_op jit(solution)/shard_map/ppermute | solution.py:49
  41.0 1.2 collective-permute-start.2
  42.2 5.4 %collective-permute-done.held0.refs_2_ = bf16[304,128]{1,0:T(8,128)(2,1)S(1)} collective-permute-done((bf16[304,128]{1,0:T(8,128)(2,1)S(1)}, bf16[304,128]{1,0:T(8,128)(2,1)S(1)}, u32[]{:S(2)}, u32[]{:S(2)}) %collective-permute-start) | collective-permute-done | bytes 77856 | tf_op jit(solution)/shard_map/ppermute | solution.py:49
  50.0 0.9 copy-done.15
  50.9 0.9 copy-done.17
  51.8 0.9 copy-done.19
  52.7 0.9 copy-done.22
  53.6 0.9 copy-done.25
  54.5 0.8 copy-done.30
  55.3 2.8 %second_layer.1 = (bf16[3,8,8,256]{3,2,1,0:T(8,128)(2,1)}, f32[192,256]{1,0:T(8,128)S(1)}, f32[3,8,8,256]{3,2,1,0:T(8,128)S(1)}, bf16[128,256]{1,0:T(8,128)(2,1)...) custom-call(s32[3,16]{1,0:T(4,128)S(1)} %copy-done.33, ...), custom_call_target="tpu_custom_call" | custom-call | flops 452984832 | bytes 3000000 | tf_op jit(solution)/shard_map/second_layer/pallas_call | solution.py:340
  63.5 5.9 %all-to-all-start.2 = ((bf16[32,32,256]{2,1,0:T(8,128)(2,1)}), bf16[32,32,256]{2,1,0:T(8,128)(2,1)S(1)}, u32[]{:S(2)}, u32[]{:S(2)}) async-start(bf16[32,32,256]{2,1,0:T(8,128)(2,1)} %bitcast.26), calls=%async_computation.2 | async-start | bytes 1048576 | tf_op jit(solution)/shard_map/all_to_all | solution.py:462
  69.5 1.3 collective-permute-start.3
  70.8 2.4 %collective-permute-start.4 = (bf16[496,128]{1,0:T(8,128)(2,1)}, bf16[496,128]{1,0:T(8,128)(2,1)S(1)}, u32[]{:S(2)}, u32[]{:S(2)}) collective-permute-start(bf16[496,128]{1,0:T(8,128)(2,1)} %copy-done.39), channel_id=1, source_target_pairs={{0,16},{1,17},{32,48},{33,49},{2,18},{3,19},{34,50},{35,51},{4,20}... | collective-permute-start | bytes 380936 | tf_op jit(solution)/shard_map/ppermute | solution.py:49
  73.2 1.2 collective-permute-start.5
  74.3 7.0 %collective-permute-done.3.refs_2_ = bf16[496,128]{1,0:T(8,128)(2,1)S(1)} collective-permute-done((bf16[496,128]{1,0:T(8,128)(2,1)}, bf16[496,128]{1,0:T(8,128)(2,1)S(1)}, u32[]{:S(2)}, u32[]{:S(2)}) %collective-permute-start.3) | collective-permute-done | bytes 127008 | tf_op jit(solution)/shard_map/ppermute | solution.py:49
  81.3 0.9 collective-permute-done.4.refs_3_
  82.3 0.9 copy-done.37
  83.2 1.3 slope_terms.2
  85.2 0.9 copy-done.8
  86.2 0.9 copy-done.10
  87.9 2.7 %first_gradient.1 = (f32[3,8,8,256]{3,2,1,0:T(8,128)S(1)}, bf16[128,256]{1,0:T(8,128)(2,1)S(1)}, bf16[1024,256]{1,0:T(8,128)(2,1)}, bf16[192,128]{1,0:T(8,128)(2...) custom-call(s32[3,16]{1,0:T(4,128)S(1)} %copy-done.33, ...), custom_call_target="tpu_custom_call" | custom-call | flops 226492416 | bytes 3000000 | tf_op jit(solution)/shard_map/first_gradient/pallas_call | solution.py:340
  91.3 1.9 collective-permute-start.6
  93.2 2.0 %collective-permute-start.7 = (bf16[192,128]{1,0:T(8,128)(2,1)S(1)}, bf16[192,128]{1,0:T(8,128)(2,1)S(1)}, u32[]{:S(2)}, u32[]{:S(2)}) collective-permute-start(bf16[192,128]{1,0:T(8,128)(2,1)S(1)} %get-tuple-element.65), channel_id=1, source_target_pairs={{0,16},{1,17},{32,48},{33,49},{2,18},{3,19},{34,50},{35,51},{4,20}... | collective-permute-start | bytes 147464 | tf_op jit(solution)/shard_map/ppermute | solution.py:49
  95.8 2.3 %collective-permute-start.10 = (f32[32,18,128]{2,1,0:T(8,128)S(1)}, f32[32,18,128]{2,1,0:T(8,128)S(1)}, u32[]{:S(2)}, u32[]{:S(2)}) collective-permute-start(f32[32,18,128]{2,1,0:T(8,128)S(1)} %copy-done.35), channel_id=1, source_target_pairs={{0,1},{1,0},{32,33},{33,32},{2,3},{3,2},{34,35},{35,34},{4,5},{5,4... | collective-permute-start | bytes 884744 | tf_op jit(solution)/shard_map/ppermute | solution.py:49
  98.4 1.3 slope_terms.3
  99.8 2.4 %collective-permute-start.9 = (f32[32,18,128]{2,1,0:T(8,128)S(1)}, f32[32,18,128]{2,1,0:T(8,128)S(1)}, u32[]{:S(2)}, u32[]{:S(2)}) collective-permute-start(f32[32,18,128]{2,1,0:T(8,128)S(1)} %get-tuple-element.68), channel_id=1, source_target_pairs={{0,1},{1,0},{32,33},{33,32},{2,3},{3,2},{34,35},{35,34},{4,5},{5,4... | collective-permute-start | bytes 884744 | tf_op jit(solution)/shard_map/ppermute | solution.py:49
  102.2 1.3 collective-permute-done.9
  103.6 28.8 %all_to_all.55 = f32[32,18,256]{2,1,0:T(8,128)S(1)} all-to-all(f32[32,18,256]{2,1,0:T(8,128)S(1)} %pad_maximum_fusion), channel_id=1, replica_groups={{0,32,2,34,4,36,6,38,64,96,66,98,68,100,70,102,128,160,130,162,132,164,..., dimensions={0} | all-to-all | bytes 1179648 | tf_op jit(solution)/shard_map/all_to_all | solution.py:446
  132.5 18.7 %all_to_all.56.refs_0_ = bf16[32,36,128]{2,1,0:T(8,128)(2,1)S(1)} all-to-all(bf16[32,36,128]{2,1,0:T(8,128)(2,1)S(1)} %broadcast_in_dim.14), channel_id=1, replica_groups={{0,32,2,34,4,36,6,38,64,96,66,98,68,100,70,102,128,160,130,162,132,164,..., dimensions={0} | all-to-all | bytes 589824 | tf_op jit(solution)/shard_map/all_to_all | solution.py:446
  151.2 8.8 %all-to-all-start.3 = ((bf16[32,32,256]{2,1,0:T(8,128)(2,1)}), bf16[32,32,256]{2,1,0:T(8,128)(2,1)S(1)}, u32[]{:S(2)}, u32[]{:S(2)}) async-start(bf16[32,32,256]{2,1,0:T(8,128)(2,1)} %bitcast.14), calls=%async_computation.3 | async-start | bytes 1048576 | tf_op jit(solution)/shard_map/all_to_all | solution.py:462
  160.0 2.5 %collective-permute-start.13 = (bf16[32,36,128]{2,1,0:T(8,128)(2,1)S(1)}, bf16[32,36,128]{2,1,0:T(8,128)(2,1)S(1)}, u32[]{:S(2)}, u32[]{:S(2)}) collective-permute-start(bf16[32,36,128]{2,1,0:T(8,128)(2,1)S(1)} %all_to_all.56.refs_0_), channel_id=1, source_target_pairs={{0,24},{1,25},{32,56},{33,57},{2,26},{3,27},{34,58},{35,59},{4,28}... | collective-permute-start | bytes 884744 | tf_op jit(solution)/shard_map/ppermute | solution.py:49
  163.6 3.2 %collective-permute-start.14 = (bf16[32,36,128]{2,1,0:T(8,128)(2,1)S(1)}, bf16[32,36,128]{2,1,0:T(8,128)(2,1)S(1)}, u32[]{:S(2)}, u32[]{:S(2)}) collective-permute-start(bf16[32,36,128]{2,1,0:T(8,128)(2,1)S(1)} %all_to_all.56.refs_0_), channel_id=1, source_target_pairs={{0,1},{1,0},{32,33},{33,32},{2,3},{3,2},{34,35},{35,34},{4,5},{5,4... | collective-permute-start | bytes 884744 | tf_op jit(solution)/shard_map/ppermute | solution.py:49
  166.8 7.0 %collective-permute-done.13.refs_3_ = bf16[32,36,128]{2,1,0:T(8,128)(2,1)S(1)} collective-permute-done((bf16[32,36,128]{2,1,0:T(8,128)(2,1)S(1)}, bf16[32,36,128]{2,1,0:T(8,128)(2,1)S(1)}, u32[]{:S(2)}, u32[]{:S(2)}) %collective-permute-start.13) | collective-permute-done | bytes 294944 | tf_op jit(solution)/shard_map/ppermute | solution.py:49
  173.8 3.1 %collective-permute-start.17 = (bf16[32,36,128]{2,1,0:T(8,128)(2,1)S(1)}, bf16[32,36,128]{2,1,0:T(8,128)(2,1)S(1)}, u32[]{:S(2)}, u32[]{:S(2)}) collective-permute-start(bf16[32,36,128]{2,1,0:T(8,128)(2,1)S(1)} %collective-permute-done.13.refs_3_), channel_id=1, source_target_pairs={{0,1},{1,0},{32,33},{33,32},{2,3},{3,2},{34,35},{35,34},{4,5},{5,4... | collective-permute-start | bytes 884744 | tf_op jit(solution)/shard_map/ppermute | solution.py:49
  177.0 2.2 %collective-permute-start.16 = (bf16[32,36,128]{2,1,0:T(8,128)(2,1)S(1)}, bf16[32,36,128]{2,1,0:T(8,128)(2,1)S(1)}, u32[]{:S(2)}, u32[]{:S(2)}) collective-permute-start(bf16[32,36,128]{2,1,0:T(8,128)(2,1)S(1)} %collective-permute-done.12.refs_2_), channel_id=1, source_target_pairs={{0,1},{1,0},{32,33},{33,32},{2,3},{3,2},{34,35},{35,34},{4,5},{5,4... | collective-permute-start | bytes 884744 | tf_op jit(solution)/shard_map/ppermute | solution.py:49
  179.2 4.2 %collective-permute-done.11.refs_1_ = bf16[32,36,128]{2,1,0:T(8,128)(2,1)S(1)} collective-permute-done((bf16[32,36,128]{2,1,0:T(8,128)(2,1)S(1)}, bf16[32,36,128]{2,1,0:T(8,128)(2,1)S(1)}, u32[]{:S(2)}, u32[]{:S(2)}) %collective-permute-start.11) | collective-permute-done | bytes 294944 | tf_op jit(solution)/shard_map/ppermute | solution.py:49
  184.2 0.9 copy-done.12
  185.1 0.9 copy-done.14
  186.0 1.0 last_gradient.1
  187.1 3.5 %spread_slopes.1 = (f32[9,256,256]{2,1,0:T(8,128)}, f32[9,256,256]{2,1,0:T(8,128)}) custom-call(s32[3]{0:T(128)S(1)} %pad_add_fusion.place.refs_0_, bf16[32,36,128]{2,1,0:T(8,128)(2,1)S(1)} %all_to_all.56.refs_0_, bf16[32,36,128]{2,1,0:T(8,128)(2,1)S(1)} %collective-permute-done.11.refs_1_, bf16[32,36,128]{2,1,0:T(8,128)(2,1)S(1)} %collective-permute-done.12.refs_2_, ...), custom_call_target="tpu_custom_call" | custom-call | flops 1000 | bytes 3000000 | tf_op jit(solution)/shard_map/spread_slopes/pallas_call | solution.py:340
  (100 shorter events, 17.3 us)
Async XLA Ops:
  0.7 0.9 copy-start.4
  1.6 0.7 copy-start.31
  2.3 47.7 %copy-start.2 = (bf16[3,3,256,256]{3,2,1,0:T(8,128)(2,1)S(1)}, bf16[3,3,256,256]{3,2,1,0:T(8,128)(2,1)}, u32[]{:S(2)}) copy-start(bf16[3,3,256,256]{3,2,1,0:T(8,128)(2,1)} %param.8) | copy-start | bytes 3538948
  2.3 47.7 %copy-start.6 = (bf16[1,3,8,8,256]{4,3,2,1,0:T(8,128)(2,1)S(1)}, bf16[1,3,8,8,256]{4,3,2,1,0:T(8,128)(2,1)}, u32[]{:S(2)}) copy-start(bf16[1,3,8,8,256]{4,3,2,1,0:T(8,128)(2,1)} %param.5) | copy-start | bytes 294916
  2.3 47.7 %copy-start.33 = (s32[3,16]{1,0:T(4,128)S(1)}, s32[3,16]{1,0:T(4,128)}, u32[]{:S(2)}) copy-start(s32[3,16]{1,0:T(4,128)} %links.7) | copy-start | bytes 580
  23.4 1.3 copy-start
  24.6 0.9 copy-start.5
  31.5 18.5 %all-to-all-start.1 = ((bf16[32,32,256]{2,1,0:T(8,128)(2,1)}), bf16[32,32,256]{2,1,0:T(8,128)(2,1)S(1)}, u32[]{:S(2)}, u32[]{:S(2)}) async-start(bf16[32,32,256]{2,1,0:T(8,128)(2,1)} %bitcast.8), calls=%async_computation.1 | async-start | bytes 1048576 | tf_op jit(solution)/shard_map/all_to_all | solution.py:462
  37.3 10.3 %collective-permute-start = (bf16[304,128]{1,0:T(8,128)(2,1)S(1)}, bf16[304,128]{1,0:T(8,128)(2,1)S(1)}, u32[]{:S(2)}, u32[]{:S(2)}) collective-permute-start(bf16[304,128]{1,0:T(8,128)(2,1)S(1)} %get-tuple-element.45), channel_id=1, source_target_pairs={{0,8},{1,9},{32,40},{33,41},{2,10},{3,11},{34,42},{35,43},{4,12},{... | collective-permute-start | bytes 233480 | tf_op jit(solution)/shard_map/ppermute | solution.py:49
  38.6 10.2 %collective-permute-start.1 = (bf16[304,128]{1,0:T(8,128)(2,1)S(1)}, bf16[304,128]{1,0:T(8,128)(2,1)S(1)}, u32[]{:S(2)}, u32[]{:S(2)}) collective-permute-start(bf16[304,128]{1,0:T(8,128)(2,1)S(1)} %get-tuple-element.46), channel_id=1, source_target_pairs={{0,16},{1,17},{32,48},{33,49},{2,18},{3,19},{34,50},{35,51},{4,20}... | collective-permute-start | bytes 233480 | tf_op jit(solution)/shard_map/ppermute | solution.py:49
  41.0 8.4 %collective-permute-start.2 = (bf16[304,128]{1,0:T(8,128)(2,1)S(1)}, bf16[304,128]{1,0:T(8,128)(2,1)S(1)}, u32[]{:S(2)}, u32[]{:S(2)}) collective-permute-start(bf16[304,128]{1,0:T(8,128)(2,1)S(1)} %get-tuple-element.47), channel_id=1, source_target_pairs={{0,24},{1,25},{32,56},{33,57},{2,26},{3,27},{34,58},{35,59},{4,28}... | collective-permute-start | bytes 233480 | tf_op jit(solution)/shard_map/ppermute | solution.py:49
  50.0 0.9 copy-start.15
  50.9 0.9 copy-start.17
  51.8 0.9 copy-start.19
  52.7 0.9 copy-start.22
  53.6 0.9 copy-start.25
  54.5 0.8 copy-start.30
  55.3 29.9 %copy-start.1 = (bf16[3,3,256,256]{3,2,1,0:T(8,128)(2,1)S(1)}, bf16[3,3,256,256]{3,2,1,0:T(8,128)(2,1)}, u32[]{:S(2)}) copy-start(bf16[3,3,256,256]{3,2,1,0:T(8,128)(2,1)} %param.7) | copy-start | bytes 3538948
  58.1 0.8 copy-start.3
  63.5 34.9 %copy-start.20 = (bf16[304,128]{1,0:T(8,128)(2,1)S(1)}, bf16[304,128]{1,0:T(8,128)(2,1)}, u32[]{:S(2)}) copy-start(bf16[304,128]{1,0:T(8,128)(2,1)} %copy-done.18) | copy-start | bytes 233476
  63.5 34.9 %copy-start.23 = (bf16[304,128]{1,0:T(8,128)(2,1)S(1)}, bf16[304,128]{1,0:T(8,128)(2,1)}, u32[]{:S(2)}) copy-start(bf16[304,128]{1,0:T(8,128)(2,1)} %copy-done.21) | copy-start | bytes 233476
  63.5 34.9 %copy-start.26 = (bf16[304,128]{1,0:T(8,128)(2,1)S(1)}, bf16[304,128]{1,0:T(8,128)(2,1)}, u32[]{:S(2)}) copy-start(bf16[304,128]{1,0:T(8,128)(2,1)} %copy-done.24) | copy-start | bytes 233476
  63.5 34.9 %copy-start.42 = (bf16[304,128]{1,0:T(8,128)(2,1)S(1)}, bf16[304,128]{1,0:T(8,128)(2,1)}, u32[]{:S(2)}) copy-start(bf16[304,128]{1,0:T(8,128)(2,1)} %copy-done.41) | copy-start | bytes 233476
  63.5 21.7 %all-to-all-start.2 = ((bf16[32,32,256]{2,1,0:T(8,128)(2,1)}), bf16[32,32,256]{2,1,0:T(8,128)(2,1)S(1)}, u32[]{:S(2)}, u32[]{:S(2)}) async-start(bf16[32,32,256]{2,1,0:T(8,128)(2,1)} %bitcast.26), calls=%async_computation.2 | async-start | bytes 1048576 | tf_op jit(solution)/shard_map/all_to_all | solution.py:462
  69.5 11.9 %collective-permute-start.3 = (bf16[496,128]{1,0:T(8,128)(2,1)}, bf16[496,128]{1,0:T(8,128)(2,1)S(1)}, u32[]{:S(2)}, u32[]{:S(2)}) collective-permute-start(bf16[496,128]{1,0:T(8,128)(2,1)} %copy-done.40), channel_id=1, source_target_pairs={{0,8},{1,9},{32,40},{33,41},{2,10},{3,11},{34,42},{35,43},{4,12},{... | collective-permute-start | bytes 380936 | tf_op jit(solution)/shard_map/ppermute | solution.py:49
  70.8 11.5 %collective-permute-start.4 = (bf16[496,128]{1,0:T(8,128)(2,1)}, bf16[496,128]{1,0:T(8,128)(2,1)S(1)}, u32[]{:S(2)}, u32[]{:S(2)}) collective-permute-start(bf16[496,128]{1,0:T(8,128)(2,1)} %copy-done.39), channel_id=1, source_target_pairs={{0,16},{1,17},{32,48},{33,49},{2,18},{3,19},{34,50},{35,51},{4,20}... | collective-permute-start | bytes 380936 | tf_op jit(solution)/shard_map/ppermute | solution.py:49
  73.2 9.1 %collective-permute-start.5 = (bf16[496,128]{1,0:T(8,128)(2,1)}, bf16[496,128]{1,0:T(8,128)(2,1)S(1)}, u32[]{:S(2)}, u32[]{:S(2)}) collective-permute-start(bf16[496,128]{1,0:T(8,128)(2,1)} %copy-done.38), channel_id=1, source_target_pairs={{0,24},{1,25},{32,56},{33,57},{2,26},{3,27},{34,58},{35,59},{4,28}... | collective-permute-start | bytes 380936 | tf_op jit(solution)/shard_map/ppermute | solution.py:49
  82.3 0.9 copy-start.37
  84.5 0.7 copy-start.34
  85.2 0.9 copy-start.8
  86.2 0.9 copy-start.10
  87.1 0.8 copy-start.28
  87.9 7.8 %copy-start.35 = (f32[32,18,128]{2,1,0:T(8,128)S(1)}, f32[32,18,128]{2,1,0:T(8,128)}, u32[]{:S(2)}) copy-start(f32[32,18,128]{2,1,0:T(8,128)} %copy-done.34) | copy-start | bytes 884740
  91.3 6.8 %collective-permute-start.6 = (bf16[192,128]{1,0:T(8,128)(2,1)S(1)}, bf16[192,128]{1,0:T(8,128)(2,1)S(1)}, u32[]{:S(2)}, u32[]{:S(2)}) collective-permute-start(bf16[192,128]{1,0:T(8,128)(2,1)S(1)} %get-tuple-element.64), channel_id=1, source_target_pairs={{0,8},{1,9},{32,40},{33,41},{2,10},{3,11},{34,42},{35,43},{4,12},{... | collective-permute-start | bytes 147464 | tf_op jit(solution)/shard_map/ppermute | solution.py:49
  93.2 5.0 %collective-permute-start.7 = (bf16[192,128]{1,0:T(8,128)(2,1)S(1)}, bf16[192,128]{1,0:T(8,128)(2,1)S(1)}, u32[]{:S(2)}, u32[]{:S(2)}) collective-permute-start(bf16[192,128]{1,0:T(8,128)(2,1)S(1)} %get-tuple-element.65), channel_id=1, source_target_pairs={{0,16},{1,17},{32,48},{33,49},{2,18},{3,19},{34,50},{35,51},{4,20}... | collective-permute-start | bytes 147464 | tf_op jit(solution)/shard_map/ppermute | solution.py:49
  95.2 3.2 %collective-permute-start.8 = (bf16[192,128]{1,0:T(8,128)(2,1)S(1)}, bf16[192,128]{1,0:T(8,128)(2,1)S(1)}, u32[]{:S(2)}, u32[]{:S(2)}) collective-permute-start(bf16[192,128]{1,0:T(8,128)(2,1)S(1)} %get-tuple-element.66), channel_id=1, source_target_pairs={{0,24},{1,25},{32,56},{33,57},{2,26},{3,27},{34,58},{35,59},{4,28}... | collective-permute-start | bytes 147464 | tf_op jit(solution)/shard_map/ppermute | solution.py:49
  95.8 6.4 %collective-permute-start.10 = (f32[32,18,128]{2,1,0:T(8,128)S(1)}, f32[32,18,128]{2,1,0:T(8,128)S(1)}, u32[]{:S(2)}, u32[]{:S(2)}) collective-permute-start(f32[32,18,128]{2,1,0:T(8,128)S(1)} %copy-done.35), channel_id=1, source_target_pairs={{0,1},{1,0},{32,33},{33,32},{2,3},{3,2},{34,35},{35,34},{4,5},{5,4... | collective-permute-start | bytes 884744 | tf_op jit(solution)/shard_map/ppermute | solution.py:49
  99.8 3.7 %collective-permute-start.9 = (f32[32,18,128]{2,1,0:T(8,128)S(1)}, f32[32,18,128]{2,1,0:T(8,128)S(1)}, u32[]{:S(2)}, u32[]{:S(2)}) collective-permute-start(f32[32,18,128]{2,1,0:T(8,128)S(1)} %get-tuple-element.68), channel_id=1, source_target_pairs={{0,1},{1,0},{32,33},{33,32},{2,3},{3,2},{34,35},{35,34},{4,5},{5,4... | collective-permute-start | bytes 884744 | tf_op jit(solution)/shard_map/ppermute | solution.py:49
  151.2 33.0 %all-to-all-start.3 = ((bf16[32,32,256]{2,1,0:T(8,128)(2,1)}), bf16[32,32,256]{2,1,0:T(8,128)(2,1)S(1)}, u32[]{:S(2)}, u32[]{:S(2)}) async-start(bf16[32,32,256]{2,1,0:T(8,128)(2,1)} %bitcast.14), calls=%async_computation.3 | async-start | bytes 1048576 | tf_op jit(solution)/shard_map/all_to_all | solution.py:462
  160.0 13.9 %collective-permute-start.13 = (bf16[32,36,128]{2,1,0:T(8,128)(2,1)S(1)}, bf16[32,36,128]{2,1,0:T(8,128)(2,1)S(1)}, u32[]{:S(2)}, u32[]{:S(2)}) collective-permute-start(bf16[32,36,128]{2,1,0:T(8,128)(2,1)S(1)} %all_to_all.56.refs_0_), channel_id=1, source_target_pairs={{0,24},{1,25},{32,56},{33,57},{2,26},{3,27},{34,58},{35,59},{4,28}... | collective-permute-start | bytes 884744 | tf_op jit(solution)/shard_map/ppermute | solution.py:49
  162.5 14.5 %collective-permute-start.12 = (bf16[32,36,128]{2,1,0:T(8,128)(2,1)S(1)}, bf16[32,36,128]{2,1,0:T(8,128)(2,1)S(1)}, u32[]{:S(2)}, u32[]{:S(2)}) collective-permute-start(bf16[32,36,128]{2,1,0:T(8,128)(2,1)S(1)} %all_to_all.56.refs_0_), channel_id=1, source_target_pairs={{0,16},{1,17},{32,48},{33,49},{2,18},{3,19},{34,50},{35,51},{4,20}... | collective-permute-start | bytes 884744 | tf_op jit(solution)/shard_map/ppermute | solution.py:49
  163.1 20.3 %collective-permute-start.11 = (bf16[32,36,128]{2,1,0:T(8,128)(2,1)S(1)}, bf16[32,36,128]{2,1,0:T(8,128)(2,1)S(1)}, u32[]{:S(2)}, u32[]{:S(2)}) collective-permute-start(bf16[32,36,128]{2,1,0:T(8,128)(2,1)S(1)} %all_to_all.56.refs_0_), channel_id=1, source_target_pairs={{0,8},{1,9},{32,40},{33,41},{2,10},{3,11},{34,42},{35,43},{4,12},{... | collective-permute-start | bytes 884744 | tf_op jit(solution)/shard_map/ppermute | solution.py:49
  163.6 23.4 %collective-permute-start.14 = (bf16[32,36,128]{2,1,0:T(8,128)(2,1)S(1)}, bf16[32,36,128]{2,1,0:T(8,128)(2,1)S(1)}, u32[]{:S(2)}, u32[]{:S(2)}) collective-permute-start(bf16[32,36,128]{2,1,0:T(8,128)(2,1)S(1)} %all_to_all.56.refs_0_), channel_id=1, source_target_pairs={{0,1},{1,0},{32,33},{33,32},{2,3},{3,2},{34,35},{35,34},{4,5},{5,4... | collective-permute-start | bytes 884744 | tf_op jit(solution)/shard_map/ppermute | solution.py:49
  173.8 13.2 %collective-permute-start.17 = (bf16[32,36,128]{2,1,0:T(8,128)(2,1)S(1)}, bf16[32,36,128]{2,1,0:T(8,128)(2,1)S(1)}, u32[]{:S(2)}, u32[]{:S(2)}) collective-permute-start(bf16[32,36,128]{2,1,0:T(8,128)(2,1)S(1)} %collective-permute-done.13.refs_3_), channel_id=1, source_target_pairs={{0,1},{1,0},{32,33},{33,32},{2,3},{3,2},{34,35},{35,34},{4,5},{5,4... | collective-permute-start | bytes 884744 | tf_op jit(solution)/shard_map/ppermute | solution.py:49
  177.0 10.1 %collective-permute-start.16 = (bf16[32,36,128]{2,1,0:T(8,128)(2,1)S(1)}, bf16[32,36,128]{2,1,0:T(8,128)(2,1)S(1)}, u32[]{:S(2)}, u32[]{:S(2)}) collective-permute-start(bf16[32,36,128]{2,1,0:T(8,128)(2,1)S(1)} %collective-permute-done.12.refs_2_), channel_id=1, source_target_pairs={{0,1},{1,0},{32,33},{33,32},{2,3},{3,2},{34,35},{35,34},{4,5},{5,4... | collective-permute-start | bytes 884744 | tf_op jit(solution)/shard_map/ppermute | solution.py:49
  183.4 3.7 %collective-permute-start.15 = (bf16[32,36,128]{2,1,0:T(8,128)(2,1)S(1)}, bf16[32,36,128]{2,1,0:T(8,128)(2,1)S(1)}, u32[]{:S(2)}, u32[]{:S(2)}) collective-permute-start(bf16[32,36,128]{2,1,0:T(8,128)(2,1)S(1)} %collective-permute-done.11.refs_1_), channel_id=1, source_target_pairs={{0,1},{1,0},{32,33},{33,32},{2,3},{3,2},{34,35},{35,34},{4,5},{5,4... | collective-permute-start | bytes 884744 | tf_op jit(solution)/shard_map/ppermute | solution.py:49
  184.2 0.9 copy-start.12
  185.1 0.9 copy-start.14
  (16 other events, 10.4 us)

commit v2 on v1

--- a/solution.py
+++ b/solution.py
@@ -1,3 +1,4 @@
+import itertools
 import math
 
 import jax
@@ -243,7 +244,7 @@
         unpack_ref[:, 128 * m : 128 * m + 128] = jnp.where(
             take == column + 128 * m, 1.0, 0.0
         ).astype(bf16)
-    grid[:, 1:9, 1:9, :] = field_ref[...].astype(f32)
+    grid[:, 1:9, 1:9, :] = field_ref[...].astype(f32).reshape(3, 8, 8, 256)
     take_frame(grid, frame, links, 1, 8, False)
     pack_frame(pack_ref, frame, frame_ref, sent_ref)
 
@@ -254,7 +255,7 @@
     grid, frame, got, flat,
 ):
     unpack_frame(unpack_ref, recv_ref, old_ref, got)
-    grid[:, 1:9, 1:9, :] = field_ref[...].astype(f32)
+    grid[:, 1:9, 1:9, :] = field_ref[...].astype(f32).reshape(3, 8, 8, 256)
     fill_ghosts(grid, got, links)
     pre_first = convolve(grid, weights)
     pre_ref[...] = pre_first
@@ -278,9 +279,9 @@
     unpack_frame(unpack_ref, recv_ref, old_ref, got)
     grid[:, 1:9, 1:9, :] = hidden_ref[...].astype(f32).reshape(3, 8, 8, 256)
     fill_ghosts(grid, got, links)
-    states = field_ref[...].astype(f32).reshape(192, 256) + convolve(grid, weights)
-    state_ref[...] = states.reshape(3, 8, 8, 256).astype(bf16)
-    misfit = states - goal_ref[...].astype(f32).reshape(192, 256)
+    states = field_ref[...].astype(f32) + convolve(grid, weights)
+    state_ref[...] = states.astype(bf16)
+    misfit = states - goal_ref[...].astype(f32)
     misfit_ref[...] = misfit
     low = misfit.astype(bf16)
     flatten_grid(grid, flat)
@@ -323,8 +324,8 @@
     out_ref[...] = grid[:, 1:9, 1:9, :]
 
 
-vmem = pl.BlockSpec(memory_space=pltpu.VMEM)
 smem = pl.BlockSpec(memory_space=pltpu.SMEM)
+vmem = pl.BlockSpec(memory_space=pltpu.HBM)
 left = pl.BlockSpec(memory_space=pl.ANY)
 grid_shape = pltpu.VMEM((3, 10, 10, 256), f32)
 frame_shape = pltpu.VMEM((128, 256), f32)
@@ -337,16 +338,54 @@
 
 
 def run(kernel, name, args, specs, outs, scratch, flops):
-    return pl.pallas_call(
-        kernel,
+    single = not isinstance(outs, tuple)
+    outs = (outs,) if single else outs
+    moved = [i for i, spec in enumerate(specs) if spec is vmem]
+    buffers = [pltpu.VMEM(args[i].shape, args[i].dtype) for i in moved]
+    results = [pltpu.VMEM(out.shape, out.dtype) for out in outs]
+
+    def body(*refs):
+        ins, refs = refs[: len(args)], refs[len(args) :]
+        targets, refs = refs[: len(outs)], refs[len(outs) :]
+        held, refs = refs[: len(moved)], refs[len(moved) :]
+        made, refs = refs[: len(outs)], refs[len(outs) :]
+        arrived, left_for, refs = refs[0], refs[1], refs[2:]
+        copies = [
+            pltpu.make_async_copy(ins[i], held[n], arrived.at[n]) for n, i in enumerate(moved)
+        ]
+        for copy in copies:
+            copy.start()
+        for copy in copies:
+            copy.wait()
+        given = list(ins)
+        for n, i in enumerate(moved):
+            given[i] = held[n]
+        kernel(*given, *made, *refs)
+        copies = [
+            pltpu.make_async_copy(made[n], targets[n], left_for.at[n]) for n in range(len(outs))
+        ]
+        for copy in copies:
+            copy.start()
+        for copy in copies:
+            copy.wait()
+
+    made = pl.pallas_call(
+        body,
         out_shape=outs,
         in_specs=specs,
-        out_specs=jax.tree.map(lambda _: vmem, outs),
-        scratch_shapes=scratch,
+        out_specs=tuple(vmem for _ in outs),
+        scratch_shapes=[
+            *buffers,
+            *results,
+            pltpu.SemaphoreType.DMA((max(1, len(moved)),)),
+            pltpu.SemaphoreType.DMA((len(outs),)),
+            *scratch,
+        ],
         compiler_params=pltpu.CompilerParams(vmem_limit_bytes=40 * 2**20),
         cost_estimate=pl.CostEstimate(flops=flops, bytes_accessed=3000000, transcendentals=0),
         name=name,
     )(*args)
+    return made[0] if single else made
 
 
 def slope_kernel(split, place, *refs):
@@ -373,13 +412,13 @@
             tap = (3 * down + across) * 64
             total[0, tap : tap + 64] = jnp.where(low, out[:64], out[64:])
             total[1, tap : tap + 64] = jnp.where(low, out[64:], out[:64])
-    for j in range(32):
-        kept_ref[j] = total[0, 18 * j : 18 * j + 18]
-        sent_ref[j] = total[1, 18 * j : 18 * j + 18]
+    for j in range(4):
+        kept_ref[j] = total[0, 144 * j : 144 * j + 144]
+        sent_ref[j] = total[1, 144 * j : 144 * j + 144]
 
 
 def slope_terms(parts, place, split):
-    shape = like(32, 18, 128, dtype=f32)
+    shape = like(4, 144, 128, dtype=f32)
 
     def kernel(*refs):
         slope_kernel(split, *refs)
@@ -403,59 +442,90 @@
     return [shifted(part, axis, k) if k else part for k, part in enumerate(parts)]
 
 
-def spread_kernel(place, *refs):
-    parts = refs[:8]
-    first_ref, second_ref, total = refs[8:]
-    x, core = place[1], place[2]
+def pair_kernel(place, kept0, got0, kept1, got1, held, *chunks):
     for k in range(4):
-        quarter = lax.rem(x + 4 - k, 4)
-        column = pl.multiple_of(lax.rem(quarter, 2) * 128, 128)
-        for other in range(2):
-            side = core if other == 0 else 1 - core
-            row = pl.multiple_of((quarter // 2) * 128 + side * 64, 64)
-            for j in range(32):
-                piece = parts[4 * other + k][j].astype(jnp.float32)
-                total[0, 18 * j : 18 * j + 18] = piece[:18]
-                total[1, 18 * j : 18 * j + 18] = piece[18:36]
-            first_ref[:, pl.ds(row, 64), pl.ds(column, 128)] = total[0].reshape(9, 64, 128)
-            second_ref[:, pl.ds(row, 64), pl.ds(column, 128)] = total[1].reshape(9, 64, 128)
-
-
-def spread_slopes(parts, place):
+        at = lax.rem(place[3] + k, 4)
+        chunks[k][:144] = kept0[at] + got0[at]
+        chunks[k][144:] = kept1[at] + got1[at]
+
+
+def plane_kernel(own, part1, part2, part3, out, total):
+    total[...] = (own[...] + part1[...]) + (part2[...] + part3[...])
+    for j in range(8):
+        out[j] = total[36 * j : 36 * j + 36]
+
+
+def spread_kernel(place, own, other, first_ref, second_ref):
+    low = place[2] == 0
+    for x in range(4):
+        row, column = 128 * (x // 2), 128 * (x % 2)
+        for n, out in enumerate((first_ref, second_ref)):
+            at = slice(144 * n, 144 * n + 144)
+            pair = [
+                jnp.concatenate(
+                    [part[4 * x + y, at].astype(f32) for y in range(4)], axis=0
+                ).reshape(9, 64, 128)
+                for part in (own, other)
+            ]
+            out[:, row : row + 64, column : column + 128] = jnp.where(low, pair[0], pair[1])
+            out[:, row + 64 : row + 128, column : column + 128] = jnp.where(low, pair[1], pair[0])
+
+
+def groups(along):
+    axes = ("x", "y", "z", "core")
+    out = []
+    for fixed in itertools.product(*[range(1 if a in along else sizes[a]) for a in axes]):
+        group = []
+        for moving in itertools.product(*[range(sizes[a]) for a in along]):
+            at = dict(zip(axes, fixed)) | dict(zip(along, moving))
+            group.append(place_of(**at))
+        out.append(group)
+    return out
+
+
+def trade(values, *along):
+    return lax.all_to_all(
+        values, ("tile", "ens"), 0, 0, axis_index_groups=groups(along), tiled=True
+    )
+
+
+def copies_of(values, count):
+    return jnp.broadcast_to(values[None], (count,) + values.shape)
+
+
+def finish_slopes(first, second, held, scale, place):
+    chunk = like(288, 128, dtype=f32)
+    chunks = run(
+        pair_kernel,
+        "pair_sum",
+        (place, first[0], shifted(first[1], "core", 1), *second, held),
+        [smem] + [vmem] * 4 + [left],
+        (chunk,) * 4,
+        [],
+        1000,
+    )
+    terms = run(
+        plane_kernel,
+        "row_sum",
+        tuple(ring(chunks, "y")),
+        [vmem] * 4,
+        like(8, 36, 128, dtype=f32),
+        [pltpu.VMEM((288, 128), f32)],
+        1000,
+    )
+    mine = (jnp.sum(trade(terms, "z"), axis=0) * scale).astype(bf16)
+    line = trade(copies_of(mine, 8), "z").reshape(288, 128)
+    plane = trade(copies_of(line, 16), "x", "y")
     shape = like(9, 256, 256, dtype=f32)
     return run(
         spread_kernel,
         "spread_slopes",
-        (place, *parts),
-        [smem] + [vmem] * 8,
+        (place, plane, shifted(plane, "core", 1)),
+        [smem, vmem, vmem],
         (shape, shape),
-        [pltpu.VMEM((2, 576, 128), f32)],
+        [],
         1000,
     )
-
-
-def plane_groups():
-    return [
-        [place_of(x, y, z, core) for y in range(4) for z in range(8)]
-        for x in range(4)
-        for core in range(2)
-    ]
-
-
-def plane_exchange(values):
-    return lax.all_to_all(
-        values, ("tile", "ens"), 0, 0, axis_index_groups=plane_groups(), tiled=True
-    )
-
-
-def finish_slopes(first, second, scale, place):
-    terms = plane_exchange(jnp.concatenate([first, second], axis=-1))
-    mine = jnp.sum(terms, axis=0) * scale
-    mine = jnp.concatenate([mine[:, :128], mine[:, 128:]], axis=0).astype(jnp.bfloat16)
-    plane = plane_exchange(jnp.broadcast_to(mine[None], (32,) + mine.shape))
-    own = [plane] + [shifted(plane, "x", k) for k in range(1, 4)]
-    other = [shifted(part, "core", 1) for part in own]
-    return spread_slopes(own + other, place)
 
 
 def exchange(values):
@@ -463,11 +533,12 @@
 
 
 def per_device(network_conditions, subsequent_targets, w_first, w_second, tile_links):
-    field, goal = network_conditions[0], subsequent_targets[0]
+    field = network_conditions.reshape(192, 256)
+    goal = subsequent_targets.reshape(192, 256)
     first_weights, second_weights = w_first.reshape(9, 256, 256), w_second.reshape(9, 256, 256)
     scale = 1.0 / math.sqrt(lax.axis_size("ens") * lax.axis_size("tile") * 192)
     where = coordinates()
-    place = jnp.stack([lax.axis_index("tile"), where["x"], where["core"]])
+    place = jnp.stack([lax.axis_index("tile"), where["x"], where["core"], where["y"]])
     frame_like, sent_like, rows_like = like(128, 256), like(send_rows, 256), like(192, 256)
     inner_like = like(3, 8, 8, 256, dtype=f32)
     conv_flops = 2 * 9 * 192 * 256 * 256
@@ -501,24 +572,25 @@
             *field_parts[1:],
         ),
         [smem, smem] + [vmem] * 8 + [left] * 3,
-        (like(3, 8, 8, 256), like(192, 256, dtype=f32), inner_like, frame_like, sent_like)
+        (rows_like, like(192, 256, dtype=f32), inner_like, frame_like, sent_like)
         + (like(496, 128),) * 4,
         [grid_shape, frame_shape, frame_shape, flat_shape, column_shape],
         2 * conv_flops,
     )
     recv = exchange(sent)
     closing, sent_closing = slope_terms(ring(parts, "x"), place, True)
+    got_closing = shifted(sent_closing, "core", 1)
     last, frame, sent, *parts = run(
         third_kernel,
         "first_gradient",
-        (tile_links, place, inner, pre_first, recv, frame, pack, unpack, first_weights, closing),
+        (tile_links, place, inner, pre_first, recv, frame, pack, unpack, first_weights, got_closing),
         [smem, smem] + [vmem] * 7 + [left],
         (inner_like, frame_like, sent_like) + (like(192, 128),) * 4,
         [grid_shape, frame_shape, frame_shape, column_shape],
         conv_flops,
     )
     recv = exchange(sent)
-    opening, sent_opening = slope_terms(field_parts + ring(parts, "x"), place, False)
+    opening = slope_terms(field_parts + ring(parts, "x"), place, False)
     condition_derivative = run(
         last_kernel,
         "last_gradient",
@@ -528,14 +600,9 @@
         [grid_shape, frame_shape],
         1000,
     )
-    slopes = finish_slopes(
-        opening + shifted(sent_opening, "core", 1),
-        closing + shifted(sent_closing, "core", 1),
-        scale,
-        place,
-    )
+    slopes = finish_slopes(opening, (closing, got_closing), recv, scale, place)
     return (
-        states[None],
+        states.reshape(network_conditions.shape),
         condition_derivative[None],
         slopes[0].reshape(w_first.shape),
         slopes[1].reshape(w_second.shape),

time: 192 us -> 184 us (0.958)
  local copies, waits for them, and re-layouts: 26.5 us -> 16.3 us
  Pallas kernels: 17.4 us -> 27.4 us
  starting transfers between devices: 52.5 us -> 47.3 us
  blocking collectives: 66.4 us -> 62.2 us
  waiting for transfers between devices: 26.7 us -> 29.2 us
    unnamed x86 -> x62, local copies, waits for them, and re-layouts: 26.4 us -> 16.1 us
    pallas_call x8 -> x10, Pallas kernels: 17.4 us -> 27.4 us  [run(): pl.pallas_call(body, out_shape=outs, in_specs=specs, out_specs=tuple((vme...]
    all_to_all x2 -> x3, blocking collectives: 47.4 us -> 43.3 us  [trade(): lax.all_to_all(values, ('tile', 'ens'), 0, 0, axis_index_groups=groups(al...]
    ppermute x18 -> x15, starting transfers between devices: 32 us -> 29.3 us  [shifted(): return lax.ppermute(values, ('tile', 'ens'), pairs)]
    ppermute x18 -> x15, waiting for transfers between devices: 26.6 us -> 29.2 us  [shifted(): return lax.ppermute(values, ('tile', 'ens'), pairs)]
    all_to_all x3, starting transfers between devices: 20.5 us -> 18 us  [exchange(): return lax.all_to_all(values, 'tile', 0, 0, tiled=True)]
  transfers between devices with their start and end apart: 21 -> 18, of which waited for: 8 -> 11; matrix products, arithmetic and copies ran while one was open for 0% -> 0% of each run, Pallas kernels for 2% -> 3%
where the time goes in v2:
time: 184 us
  blocking collectives  62.2 us (34%)
  starting transfers between devices  47.3 us (26%)
  waiting for transfers between devices  29.2 us (16%)
  Pallas kernels  27.4 us (15%)
  local copies, waits for them, and re-layouts  16.3 us (9%)
    all_to_all x3, blocking collectives, trade(): lax.all_to_all(values, ('tile', 'ens'), 0, 0, axis_index_groups=groups(al...  43.3 us
    ppermute x15, starting transfers between devices, shifted(): return lax.ppermute(values, ('tile', 'ens'), pairs)  29.3 us
    ppermute x15, waiting for transfers between devices, shifted(): return lax.ppermute(values, ('tile', 'ens'), pairs)  29.2 us
    pallas_call x10, Pallas kernels, run(): pl.pallas_call(body, out_shape=outs, in_specs=specs, out_specs=tuple((vme...  27.4 us
    all_to_all x1, blocking collectives, exchange(): return lax.all_to_all(values, 'tile', 0, 0, tiled=True)  18.9 us
    all_to_all x3, starting transfers between devices, exchange(): return lax.all_to_all(values, 'tile', 0, 0, tiled=True)  18 us
    unnamed x62, local copies, waits for them, and re-layouts  16.1 us
  transfers between devices with their start and end apart: 18, of which 11 were waited for; matrix products, arithmetic and copies ran while one was open for 0% of the time, Pallas kernels for 3%

profile of v2, /device:TPU:1, one launch (start us, length us, event | category | flops | bytes accessed | tf_op | source)
XLA Modules:
  0.0 183.5 jit_solution(4591702180516479228)
XLA Ops:
  0.7 1.0 copy-done.2
  2.4 2.5 %routes.1 = (bf16[1024,128]{1,0:T(8,128)(2,1)S(1)}, bf16[128,1152]{1,0:T(8,128)(2,1)S(1)}, bf16[128,256]{1,0:T(8,128)(2,1)S(1)}, bf16[1024,256]{1,0:T(8,128)(2,1)S(1)}) custom-call(s32[3,16]{1,0:T(4,128)S(1)} %copy-done.18, s32[4]{0:T(128)S(1)} %pad_add_fusion.refs_1_.refs_0_, bf16[192,256]{1,0:T(8,128)(2,1)S(1)} %bitcast.29), custom_call_target="tpu_custom_call" | custom-call | flops 67108864 | bytes 3000000 | tf_op jit(solution)/shard_map/routes/pallas_call | solution.py:372
  4.9 18.9 %all_to_all.59 = bf16[32,32,256]{2,1,0:T(8,128)(2,1)S(1)} all-to-all(bf16[32,32,256]{2,1,0:T(8,128)(2,1)S(1)} %bitcast.28), channel_id=1, replica_groups=mesh['tile'=32,'ens'=8] {'tile'}, dimensions={0} | all-to-all | bytes 1048576 | tf_op jit(solution)/shard_map/all_to_all | solution.py:532
  23.9 3.9 %first_layer.1 = (bf16[192,256]{1,0:T(8,128)(2,1)S(1)}, f32[192,256]{1,0:T(8,128)S(1)}, bf16[128,256]{1,0:T(8,128)(2,1)S(1)}, bf16[1024,256]{1,0:T(8,128)(2,1)},...) custom-call(s32[3,16]{1,0:T(4,128)S(1)} %copy-done.18, ...), custom_call_target="tpu_custom_call" | custom-call | flops 226492416 | bytes 3000000 | tf_op jit(solution)/shard_map/first_layer/pallas_call | solution.py:372
  28.4 5.8 %all-to-all-start.1 = ((bf16[32,32,256]{2,1,0:T(8,128)(2,1)}), bf16[32,32,256]{2,1,0:T(8,128)(2,1)S(1)}, u32[]{:S(2)}, u32[]{:S(2)}) async-start(bf16[32,32,256]{2,1,0:T(8,128)(2,1)} %bitcast.9), calls=%async_computation.1 | async-start | bytes 1048576 | tf_op jit(solution)/shard_map/all_to_all | solution.py:532
  34.2 1.3 collective-permute-start
  35.5 2.4 %collective-permute-start.1 = (bf16[304,128]{1,0:T(8,128)(2,1)S(1)}, bf16[304,128]{1,0:T(8,128)(2,1)S(1)}, u32[]{:S(2)}, u32[]{:S(2)}) collective-permute-start(bf16[304,128]{1,0:T(8,128)(2,1)S(1)} %get-tuple-element.50), channel_id=1, source_target_pairs={{0,16},{1,17},{32,48},{33,49},{2,18},{3,19},{34,50},{35,51},{4,20}... | collective-permute-start | bytes 233480 | tf_op jit(solution)/shard_map/ppermute | solution.py:50
  37.9 1.2 collective-permute-start.2
  39.0 5.4 %collective-permute-done.refs_10_.refs_2_ = bf16[304,128]{1,0:T(8,128)(2,1)S(1)} collective-permute-done((bf16[304,128]{1,0:T(8,128)(2,1)S(1)}, bf16[304,128]{1,0:T(8,128)(2,1)S(1)}, u32[]{:S(2)}, u32[]{:S(2)}) %collective-permute-start) | collective-permute-done | bytes 77856 | tf_op jit(solution)/shard_map/ppermute | solution.py:50
  44.5 1.2 collective-permute-done.1.refs_11_.refs_3_
  45.7 1.3 copy-done.1
  47.0 4.9 %second_layer.1 = (bf16[192,256]{1,0:T(8,128)(2,1)}, f32[192,256]{1,0:T(8,128)S(1)}, f32[3,8,8,256]{3,2,1,0:T(8,128)S(1)}, bf16[128,256]{1,0:T(8,128)(2,1)S(1)},...) custom-call(s32[3,16]{1,0:T(4,128)S(1)} %copy-done.19, ...), custom_call_target="tpu_custom_call" | custom-call | flops 452984832 | bytes 3000000 | tf_op jit(solution)/shard_map/second_layer/pallas_call | solution.py:372
  54.5 6.4 %all-to-all-start.2 = ((bf16[32,32,256]{2,1,0:T(8,128)(2,1)}), bf16[32,32,256]{2,1,0:T(8,128)(2,1)S(1)}, u32[]{:S(2)}, u32[]{:S(2)}) async-start(bf16[32,32,256]{2,1,0:T(8,128)(2,1)} %bitcast.13), calls=%async_computation.2 | async-start | bytes 1048576 | tf_op jit(solution)/shard_map/all_to_all | solution.py:532
  60.9 1.3 collective-permute-start.3
  62.2 2.4 %collective-permute-start.4 = (bf16[496,128]{1,0:T(8,128)(2,1)}, bf16[496,128]{1,0:T(8,128)(2,1)S(1)}, u32[]{:S(2)}, u32[]{:S(2)}) collective-permute-start(bf16[496,128]{1,0:T(8,128)(2,1)} %copy-done.22), channel_id=1, source_target_pairs={{0,16},{1,17},{32,48},{33,49},{2,18},{3,19},{34,50},{35,51},{4,20}... | collective-permute-start | bytes 380936 | tf_op jit(solution)/shard_map/ppermute | solution.py:50
  64.6 1.2 collective-permute-start.5
  65.8 7.0 %collective-permute-done.3.refs_2_ = bf16[496,128]{1,0:T(8,128)(2,1)S(1)} collective-permute-done((bf16[496,128]{1,0:T(8,128)(2,1)}, bf16[496,128]{1,0:T(8,128)(2,1)S(1)}, u32[]{:S(2)}, u32[]{:S(2)}) %collective-permute-start.3) | collective-permute-done | bytes 127008 | tf_op jit(solution)/shard_map/ppermute | solution.py:50
  72.8 0.9 collective-permute-done.4.refs_3_
  73.7 0.9 copy-done.21
  74.6 2.1 %slope_terms.2 = (f32[4,144,128]{2,1,0:T(8,128)S(1)}, f32[4,144,128]{2,1,0:T(8,128)S(1)}) custom-call(s32[4]{0:T(128)S(1)} %pad_add_fusion.refs_1_.refs_0_, bf16[496,128]{1,0:T(8,128)(2,1)S(1)} %copy-done.21, bf16[496,128]{1,0:T(8,128)(2,1)S(1)} %collective-permute-done.3.refs_2_, bf16[496,128]{1,0:T(8,128)(2,1)S(1)} %collective-permute-done.4.refs_3_, ...), custom_call_target="tpu_custom_call" | custom-call | flops 226492416 | bytes 3000000 | tf_op jit(solution)/shard_map/slope_terms/pallas_call | solution.py:372
  76.7 3.0 %collective-permute-start.6 = (f32[4,144,128]{2,1,0:T(8,128)S(1)}, f32[4,144,128]{2,1,0:T(8,128)S(1)}, u32[]{:S(2)}, u32[]{:S(2)}) collective-permute-start(f32[4,144,128]{2,1,0:T(8,128)S(1)} %get-tuple-element.61), channel_id=1, source_target_pairs={{0,1},{1,0},{32,33},{33,32},{2,3},{3,2},{34,35},{35,34},{4,5},{5,4... | collective-permute-start | bytes 884744 | tf_op jit(solution)/shard_map/ppermute | solution.py:50
  79.7 1.2 collective-permute-done.6.refs_9_.refs_4_
  81.8 4.1 %first_gradient.1 = (f32[3,8,8,256]{3,2,1,0:T(8,128)S(1)}, bf16[128,256]{1,0:T(8,128)(2,1)S(1)}, bf16[1024,256]{1,0:T(8,128)(2,1)}, bf16[192,128]{1,0:T(8,128)(2...) custom-call(s32[3,16]{1,0:T(4,128)S(1)} %copy-done.19, ...), custom_call_target="tpu_custom_call" | custom-call | flops 226492416 | bytes 3000000 | tf_op jit(solution)/shard_map/first_gradient/pallas_call | solution.py:372
  89.6 5.9 %all-to-all-start.3 = ((bf16[32,32,256]{2,1,0:T(8,128)(2,1)}), bf16[32,32,256]{2,1,0:T(8,128)(2,1)S(1)}, u32[]{:S(2)}, u32[]{:S(2)}) async-start(bf16[32,32,256]{2,1,0:T(8,128)(2,1)} %bitcast.15), calls=%async_computation.3 | async-start | bytes 1048576 | tf_op jit(solution)/shard_map/all_to_all | solution.py:532
  95.5 1.3 collective-permute-start.7
  96.8 2.4 %collective-permute-start.8 = (bf16[192,128]{1,0:T(8,128)(2,1)}, bf16[192,128]{1,0:T(8,128)(2,1)S(1)}, u32[]{:S(2)}, u32[]{:S(2)}) collective-permute-start(bf16[192,128]{1,0:T(8,128)(2,1)} %copy-done.29), channel_id=1, source_target_pairs={{0,16},{1,17},{32,48},{33,49},{2,18},{3,19},{34,50},{35,51},{4,20}... | collective-permute-start | bytes 147464 | tf_op jit(solution)/shard_map/ppermute | solution.py:50
  99.2 1.2 collective-permute-start.9
  100.4 5.1 %collective-permute-done.7.refs_6_ = bf16[192,128]{1,0:T(8,128)(2,1)S(1)} collective-permute-done((bf16[192,128]{1,0:T(8,128)(2,1)}, bf16[192,128]{1,0:T(8,128)(2,1)S(1)}, u32[]{:S(2)}, u32[]{:S(2)}) %collective-permute-start.7) | collective-permute-done | bytes 49184 | tf_op jit(solution)/shard_map/ppermute | solution.py:50
  106.3 0.9 copy-done.9
  107.2 0.9 copy-done.11
  108.1 0.9 copy-done.13
  108.9 0.9 copy-done.25
  110.6 2.1 %slope_terms.3 = (f32[4,144,128]{2,1,0:T(8,128)S(1)}, f32[4,144,128]{2,1,0:T(8,128)S(1)}) custom-call(s32[4]{0:T(128)S(1)} %pad_add_fusion.refs_1_.refs_0_, bf16[304,128]{1,0:T(8,128)(2,1)S(1)} %copy-done.25, bf16[304,128]{1,0:T(8,128)(2,1)S(1)} %copy-done.9, bf16[304,128]{1,0:T(8,128)(2,1)S(1)} %copy-done.11, bf16[304,128]{1,0:T(8,128)(2,1)S(1)} %copy-done.13, ...), custom_call_target="tpu_custom_call" | custom-call | flops 226492416 | bytes 3000000 | tf_op jit(solution)/shard_map/slope_terms/pallas_call | solution.py:372
  112.7 1.5 collective-permute-start.10
  114.2 1.2 collective-permute-done.10.refs_2_
  115.4 1.7 pair_sum.1
  117.1 1.3 collective-permute-start.11
  118.4 2.4 %collective-permute-start.12 = (f32[288,128]{1,0:T(8,128)S(1)}, f32[288,128]{1,0:T(8,128)S(1)}, u32[]{:S(2)}, u32[]{:S(2)}) collective-permute-start(f32[288,128]{1,0:T(8,128)S(1)} %get-tuple-element.76), channel_id=1, source_target_pairs={{0,128},{1,129},{32,160},{33,161},{2,130},{3,131},{34,162},{35,163... | collective-permute-start | bytes 442376 | tf_op jit(solution)/shard_map/ppermute | solution.py:50
  120.9 1.1 collective-permute-start.13
  122.0 1.5 collective-permute-done.11.refs_1_
  123.5 4.1 %collective-permute-done.12.refs_2_ = f32[288,128]{1,0:T(8,128)S(1)} collective-permute-done((f32[288,128]{1,0:T(8,128)S(1)}, f32[288,128]{1,0:T(8,128)S(1)}, u32[]{:S(2)}, u32[]{:S(2)}) %collective-permute-start.12) | collective-permute-done | bytes 147488 | tf_op jit(solution)/shard_map/ppermute | solution.py:50
  127.6 0.9 row_sum.1
  128.5 15.4 %all_to_all.60 = f32[8,36,128]{2,1,0:T(8,128)S(1)} all-to-all(f32[8,36,128]{2,1,0:T(8,128)S(1)} %row_sum.1), channel_id=1, replica_groups={{0,32,2,34,4,36,6,38},{1,33,3,35,5,37,7,39},{64,96,66,98,68,100,70,102}..., dimensions={0} | all-to-all | bytes 294912 | tf_op jit(solution)/shard_map/all_to_all | solution.py:487
  144.0 9.8 %all_to_all.61 = bf16[8,36,128]{2,1,0:T(8,128)(2,1)S(1)} all-to-all(bf16[8,36,128]{2,1,0:T(8,128)(2,1)S(1)} %broadcast_in_dim.17), channel_id=1, replica_groups={{0,32,2,34,4,36,6,38},{1,33,3,35,5,37,7,39},{64,96,66,98,68,100,70,102}..., dimensions={0} | all-to-all | bytes 147456 | tf_op jit(solution)/shard_map/all_to_all | solution.py:487
  154.0 18.1 %all_to_all.62.refs_1_ = bf16[16,288,128]{2,1,0:T(8,128)(2,1)S(1)} all-to-all(bf16[16,288,128]{2,1,0:T(8,128)(2,1)S(1)} %broadcast_in_dim.19), channel_id=1, replica_groups={{0,64,128,192,8,72,136,200,16,80,144,208,24,88,152,216},{1,65,129,193,9..., dimensions={0} | all-to-all | bytes 2359296 | tf_op jit(solution)/shard_map/all_to_all | solution.py:487
  172.0 5.3 %collective-permute-start.14 = (bf16[16,288,128]{2,1,0:T(8,128)(2,1)S(1)}, bf16[16,288,128]{2,1,0:T(8,128)(2,1)S(1)}, u32[]{:S(2)}, u32[]{:S(2)}) collective-permute-start(bf16[16,288,128]{2,1,0:T(8,128)(2,1)S(1)} %all_to_all.62.refs_1_), channel_id=1, source_target_pairs={{0,1},{1,0},{32,33},{33,32},{2,3},{3,2},{34,35},{35,34},{4,5},{5,4... | collective-permute-start | bytes 3538952 | tf_op jit(solution)/shard_map/ppermute | solution.py:50
  177.4 1.7 last_gradient.1
  179.8 3.5 %spread_slopes.1 = (f32[9,256,256]{2,1,0:T(8,128)}, f32[9,256,256]{2,1,0:T(8,128)}) custom-call(s32[4]{0:T(128)S(1)} %pad_add_fusion.refs_1_.refs_0_, bf16[16,288,128]{2,1,0:T(8,128)(2,1)S(1)} %all_to_all.62.refs_1_, bf16[16,288,128]{2,1,0:T(8,128)(2,1)S(1)} %collective-permute-done.14.refs_2_), custom_call_target="tpu_custom_call" | custom-call | flops 1000 | bytes 3000000 | tf_op jit(solution)/shard_map/spread_slopes/pallas_call | solution.py:372
  (70 shorter events, 11.2 us)
Async XLA Ops:
  0.6 23.2 %copy-start = (bf16[3,3,256,256]{3,2,1,0:T(8,128)(2,1)S(1)}, bf16[3,3,256,256]{3,2,1,0:T(8,128)(2,1)}, u32[]{:S(2)}) copy-start(bf16[3,3,256,256]{3,2,1,0:T(8,128)(2,1)} %param.7) | copy-start | bytes 3538948
  0.7 1.0 copy-start.2
  1.7 0.7 copy-start.18
  23.9 21.8 %copy-start.7 = (bf16[1,3,8,8,256]{4,3,2,1,0:T(8,128)(2,1)S(1)}, bf16[1,3,8,8,256]{4,3,2,1,0:T(8,128)(2,1)}, u32[]{:S(2)}) copy-start(bf16[1,3,8,8,256]{4,3,2,1,0:T(8,128)(2,1)} %param.6) | copy-start | bytes 294916
  23.9 21.8 %copy-start.19 = (s32[3,16]{1,0:T(4,128)S(1)}, s32[3,16]{1,0:T(4,128)}, u32[]{:S(2)}) copy-start(s32[3,16]{1,0:T(4,128)} %refs_0_.7) | copy-start | bytes 580
  27.8 0.6 copy-start.24
  28.4 17.2 %all-to-all-start.1 = ((bf16[32,32,256]{2,1,0:T(8,128)(2,1)}), bf16[32,32,256]{2,1,0:T(8,128)(2,1)S(1)}, u32[]{:S(2)}, u32[]{:S(2)}) async-start(bf16[32,32,256]{2,1,0:T(8,128)(2,1)} %bitcast.9), calls=%async_computation.1 | async-start | bytes 1048576 | tf_op jit(solution)/shard_map/all_to_all | solution.py:532
  34.2 10.3 %collective-permute-start = (bf16[304,128]{1,0:T(8,128)(2,1)S(1)}, bf16[304,128]{1,0:T(8,128)(2,1)S(1)}, u32[]{:S(2)}, u32[]{:S(2)}) collective-permute-start(bf16[304,128]{1,0:T(8,128)(2,1)S(1)} %get-tuple-element.49), channel_id=1, source_target_pairs={{0,8},{1,9},{32,40},{33,41},{2,10},{3,11},{34,42},{35,43},{4,12},{... | collective-permute-start | bytes 233480 | tf_op jit(solution)/shard_map/ppermute | solution.py:50
  35.5 10.2 %collective-permute-start.1 = (bf16[304,128]{1,0:T(8,128)(2,1)S(1)}, bf16[304,128]{1,0:T(8,128)(2,1)S(1)}, u32[]{:S(2)}, u32[]{:S(2)}) collective-permute-start(bf16[304,128]{1,0:T(8,128)(2,1)S(1)} %get-tuple-element.50), channel_id=1, source_target_pairs={{0,16},{1,17},{32,48},{33,49},{2,18},{3,19},{34,50},{35,51},{4,20}... | collective-permute-start | bytes 233480 | tf_op jit(solution)/shard_map/ppermute | solution.py:50
  37.9 7.8 %collective-permute-start.2 = (bf16[304,128]{1,0:T(8,128)(2,1)S(1)}, bf16[304,128]{1,0:T(8,128)(2,1)S(1)}, u32[]{:S(2)}, u32[]{:S(2)}) collective-permute-start(bf16[304,128]{1,0:T(8,128)(2,1)S(1)} %get-tuple-element.51), channel_id=1, source_target_pairs={{0,24},{1,25},{32,56},{33,57},{2,26},{3,27},{34,58},{35,59},{4,28}... | collective-permute-start | bytes 233480 | tf_op jit(solution)/shard_map/ppermute | solution.py:50
  44.5 7.4 %copy-start.8 = (bf16[304,128]{1,0:T(8,128)(2,1)}, bf16[304,128]{1,0:T(8,128)(2,1)S(1)}, u32[]{:S(2)}) copy-start(bf16[304,128]{1,0:T(8,128)(2,1)S(1)} %collective-permute-done.refs_10_.refs_2_) | copy-start | bytes 233476
  45.6 6.2 %copy-start.10 = (bf16[304,128]{1,0:T(8,128)(2,1)}, bf16[304,128]{1,0:T(8,128)(2,1)S(1)}, u32[]{:S(2)}) copy-start(bf16[304,128]{1,0:T(8,128)(2,1)S(1)} %collective-permute-done.1.refs_11_.refs_3_) | copy-start | bytes 233476
  45.6 6.2 %copy-start.12 = (bf16[304,128]{1,0:T(8,128)(2,1)}, bf16[304,128]{1,0:T(8,128)(2,1)S(1)}, u32[]{:S(2)}) copy-start(bf16[304,128]{1,0:T(8,128)(2,1)S(1)} %collective-permute-done.2.refs_12_.refs_4_) | copy-start | bytes 233476
  45.7 1.3 copy-start.1
  51.9 0.7 copy-start.3
  52.6 0.6 copy-start.20
  53.2 0.6 copy-start.22
  53.9 0.6 copy-start.23
  54.5 26.4 %copy-start.16 = (bf16[128,256]{1,0:T(8,128)(2,1)}, bf16[128,256]{1,0:T(8,128)(2,1)S(1)}, u32[]{:S(2)}) copy-start(bf16[128,256]{1,0:T(8,128)(2,1)S(1)} %get-tuple-element.56.refs_5_) | copy-start | bytes 196612
  54.5 26.4 %all-to-all-start.2 = ((bf16[32,32,256]{2,1,0:T(8,128)(2,1)}), bf16[32,32,256]{2,1,0:T(8,128)(2,1)S(1)}, u32[]{:S(2)}, u32[]{:S(2)}) async-start(bf16[32,32,256]{2,1,0:T(8,128)(2,1)} %bitcast.13), calls=%async_computation.2 | async-start | bytes 1048576 | tf_op jit(solution)/shard_map/all_to_all | solution.py:532
  60.9 11.9 %collective-permute-start.3 = (bf16[496,128]{1,0:T(8,128)(2,1)}, bf16[496,128]{1,0:T(8,128)(2,1)S(1)}, u32[]{:S(2)}, u32[]{:S(2)}) collective-permute-start(bf16[496,128]{1,0:T(8,128)(2,1)} %copy-done.23), channel_id=1, source_target_pairs={{0,8},{1,9},{32,40},{33,41},{2,10},{3,11},{34,42},{35,43},{4,12},{... | collective-permute-start | bytes 380936 | tf_op jit(solution)/shard_map/ppermute | solution.py:50
  62.2 11.5 %collective-permute-start.4 = (bf16[496,128]{1,0:T(8,128)(2,1)}, bf16[496,128]{1,0:T(8,128)(2,1)S(1)}, u32[]{:S(2)}, u32[]{:S(2)}) collective-permute-start(bf16[496,128]{1,0:T(8,128)(2,1)} %copy-done.22), channel_id=1, source_target_pairs={{0,16},{1,17},{32,48},{33,49},{2,18},{3,19},{34,50},{35,51},{4,20}... | collective-permute-start | bytes 380936 | tf_op jit(solution)/shard_map/ppermute | solution.py:50
  64.6 9.1 %collective-permute-start.5 = (bf16[496,128]{1,0:T(8,128)(2,1)S(1)}, bf16[496,128]{1,0:T(8,128)(2,1)S(1)}, u32[]{:S(2)}, u32[]{:S(2)}) collective-permute-start(bf16[496,128]{1,0:T(8,128)(2,1)S(1)} %get-tuple-element.60), channel_id=1, source_target_pairs={{0,24},{1,25},{32,56},{33,57},{2,26},{3,27},{34,58},{35,59},{4,28}... | collective-permute-start | bytes 380936 | tf_op jit(solution)/shard_map/ppermute | solution.py:50
  73.7 0.9 copy-start.21
  76.7 4.2 %collective-permute-start.6 = (f32[4,144,128]{2,1,0:T(8,128)S(1)}, f32[4,144,128]{2,1,0:T(8,128)S(1)}, u32[]{:S(2)}, u32[]{:S(2)}) collective-permute-start(f32[4,144,128]{2,1,0:T(8,128)S(1)} %get-tuple-element.61), channel_id=1, source_target_pairs={{0,1},{1,0},{32,33},{33,32},{2,3},{3,2},{34,35},{35,34},{4,5},{5,4... | collective-permute-start | bytes 884744 | tf_op jit(solution)/shard_map/ppermute | solution.py:50
  80.9 0.8 copy-start.17
  85.8 0.7 copy-start.5
  86.5 0.6 copy-start.14
  87.2 0.6 copy-start.26
  88.4 0.6 copy-start.29
  89.0 0.6 copy-start.30
  89.6 25.8 %all-to-all-start.3 = ((bf16[32,32,256]{2,1,0:T(8,128)(2,1)}), bf16[32,32,256]{2,1,0:T(8,128)(2,1)S(1)}, u32[]{:S(2)}, u32[]{:S(2)}) async-start(bf16[32,32,256]{2,1,0:T(8,128)(2,1)} %bitcast.15), calls=%async_computation.3 | async-start | bytes 1048576 | tf_op jit(solution)/shard_map/all_to_all | solution.py:532
  95.5 10.0 %collective-permute-start.7 = (bf16[192,128]{1,0:T(8,128)(2,1)}, bf16[192,128]{1,0:T(8,128)(2,1)S(1)}, u32[]{:S(2)}, u32[]{:S(2)}) collective-permute-start(bf16[192,128]{1,0:T(8,128)(2,1)} %copy-done.30), channel_id=1, source_target_pairs={{0,8},{1,9},{32,40},{33,41},{2,10},{3,11},{34,42},{35,43},{4,12},{... | collective-permute-start | bytes 147464 | tf_op jit(solution)/shard_map/ppermute | solution.py:50
  96.8 9.5 %collective-permute-start.8 = (bf16[192,128]{1,0:T(8,128)(2,1)}, bf16[192,128]{1,0:T(8,128)(2,1)S(1)}, u32[]{:S(2)}, u32[]{:S(2)}) collective-permute-start(bf16[192,128]{1,0:T(8,128)(2,1)} %copy-done.29), channel_id=1, source_target_pairs={{0,16},{1,17},{32,48},{33,49},{2,18},{3,19},{34,50},{35,51},{4,20}... | collective-permute-start | bytes 147464 | tf_op jit(solution)/shard_map/ppermute | solution.py:50
  99.2 7.1 %collective-permute-start.9 = (bf16[192,128]{1,0:T(8,128)(2,1)}, bf16[192,128]{1,0:T(8,128)(2,1)S(1)}, u32[]{:S(2)}, u32[]{:S(2)}) collective-permute-start(bf16[192,128]{1,0:T(8,128)(2,1)} %copy-done.28), channel_id=1, source_target_pairs={{0,24},{1,25},{32,56},{33,57},{2,26},{3,27},{34,58},{35,59},{4,28}... | collective-permute-start | bytes 147464 | tf_op jit(solution)/shard_map/ppermute | solution.py:50
  106.3 0.9 copy-start.9
  107.2 0.9 copy-start.11
  108.0 0.9 copy-start.13
  108.9 0.9 copy-start.25
  109.8 0.8 copy-start.27
  112.7 2.7 %collective-permute-start.10 = (f32[4,144,128]{2,1,0:T(8,128)S(1)}, f32[4,144,128]{2,1,0:T(8,128)S(1)}, u32[]{:S(2)}, u32[]{:S(2)}) collective-permute-start(f32[4,144,128]{2,1,0:T(8,128)S(1)} %get-tuple-element.72), channel_id=1, source_target_pairs={{0,1},{1,0},{32,33},{33,32},{2,3},{3,2},{34,35},{35,34},{4,5},{5,4... | collective-permute-start | bytes 884744 | tf_op jit(solution)/shard_map/ppermute | solution.py:50
  117.1 6.3 %collective-permute-start.11 = (f32[288,128]{1,0:T(8,128)S(1)}, f32[288,128]{1,0:T(8,128)S(1)}, u32[]{:S(2)}, u32[]{:S(2)}) collective-permute-start(f32[288,128]{1,0:T(8,128)S(1)} %get-tuple-element.75), channel_id=1, source_target_pairs={{0,64},{1,65},{32,96},{33,97},{2,66},{3,67},{34,98},{35,99},{4,68}... | collective-permute-start | bytes 442376 | tf_op jit(solution)/shard_map/ppermute | solution.py:50
  118.4 9.2 %collective-permute-start.12 = (f32[288,128]{1,0:T(8,128)S(1)}, f32[288,128]{1,0:T(8,128)S(1)}, u32[]{:S(2)}, u32[]{:S(2)}) collective-permute-start(f32[288,128]{1,0:T(8,128)S(1)} %get-tuple-element.76), channel_id=1, source_target_pairs={{0,128},{1,129},{32,160},{33,161},{2,130},{3,131},{34,162},{35,163... | collective-permute-start | bytes 442376 | tf_op jit(solution)/shard_map/ppermute | solution.py:50
  120.9 6.8 %collective-permute-start.13 = (f32[288,128]{1,0:T(8,128)S(1)}, f32[288,128]{1,0:T(8,128)S(1)}, u32[]{:S(2)}, u32[]{:S(2)}) collective-permute-start(f32[288,128]{1,0:T(8,128)S(1)} %get-tuple-element.77), channel_id=1, source_target_pairs={{0,192},{1,193},{32,224},{33,225},{2,194},{3,195},{34,226},{35,227... | collective-permute-start | bytes 442376 | tf_op jit(solution)/shard_map/ppermute | solution.py:50
  153.9 23.4 %copy-start.4 = (f32[192,256]{1,0:T(8,128)S(1)}, f32[192,256]{1,0:T(8,128)}, u32[]{:S(2)}) copy-start(f32[192,256]{1,0:T(8,128)} %copy-done.3) | copy-start | bytes 589828
  153.9 23.4 %copy-start.6 = (f32[3,8,8,256]{3,2,1,0:T(8,128)S(1)}, f32[3,8,8,256]{3,2,1,0:T(8,128)}, u32[]{:S(2)}) copy-start(f32[3,8,8,256]{3,2,1,0:T(8,128)} %copy-done.5) | copy-start | bytes 589828
  153.9 23.4 %copy-start.15 = (bf16[128,256]{1,0:T(8,128)(2,1)S(1)}, bf16[128,256]{1,0:T(8,128)(2,1)}, u32[]{:S(2)}) copy-start(bf16[128,256]{1,0:T(8,128)(2,1)} %copy-done.14) | copy-start | bytes 196612
  172.0 7.8 %collective-permute-start.14 = (bf16[16,288,128]{2,1,0:T(8,128)(2,1)S(1)}, bf16[16,288,128]{2,1,0:T(8,128)(2,1)S(1)}, u32[]{:S(2)}, u32[]{:S(2)}) collective-permute-start(bf16[16,288,128]{2,1,0:T(8,128)(2,1)S(1)} %all_to_all.62.refs_1_), channel_id=1, source_target_pairs={{0,1},{1,0},{32,33},{33,32},{2,3},{3,2},{34,35},{35,34},{4,5},{5,4... | collective-permute-start | bytes 3538952 | tf_op jit(solution)/shard_map/ppermute | solution.py:50
  (1 other events, 0.6 us)

commit v3 on v2

--- a/solution.py
+++ b/solution.py
@@ -50,15 +50,9 @@
     return lax.ppermute(values, ("tile", "ens"), pairs)
 
 
-def coordinates():
-    tile = lax.axis_index("tile")
-    ens = lax.axis_index("ens")
-    return {
-        "x": tile % 4,
-        "y": tile // 8,
-        "z": (ens // 2) * 2 + (tile // 4) % 2,
-        "core": ens % 2,
-    }
+def placing():
+    tile, ens = lax.axis_index("tile"), lax.axis_index("ens")
+    return tile, lax.rem(tile, 4), lax.rem(ens, 2), tile // 8
 
 
 edge_starts = ((0, 3), (0, 1), (1, 2), (2, 3))
@@ -186,7 +180,7 @@
             flat[at : at + 10] = grid[tile, row]
 
 
-def route_kernel(links, place, field_ref, pack_ref, unpack_ref, frame_ref, sent_ref, grid, frame):
+def route_kernel(place, links, field_ref, pack_ref, unpack_ref, frame_ref, sent_ref, grid, frame):
     here = place[0]
 
     def rows_of(tiles, sides, valid, base, width, local_base):
@@ -250,7 +244,7 @@
 
 
 def first_kernel(
-    links, place, field_ref, recv_ref, old_ref, pack_ref, unpack_ref, weights,
+    place, links, field_ref, recv_ref, old_ref, pack_ref, unpack_ref, weights,
     hidden_ref, pre_ref, frame_ref, sent_ref, part0, part1, part2, part3,
     grid, frame, got, flat,
 ):
@@ -271,7 +265,7 @@
 
 
 def second_kernel(
-    links, place, field_ref, goal_ref, hidden_ref, recv_ref, old_ref, pack_ref, unpack_ref, weights,
+    place, links, field_ref, goal_ref, hidden_ref, recv_ref, old_ref, pack_ref, unpack_ref, weights,
     held0, held1, held2,
     state_ref, misfit_ref, inner_ref, frame_ref, sent_ref, part0, part1, part2, part3,
     grid, frame, got, flat, column,
@@ -298,10 +292,9 @@
 
 
 def third_kernel(
-    links, place, inner_ref, pre_ref, recv_ref, old_ref, pack_ref, unpack_ref, weights, held,
-    last_ref, frame_ref, sent_ref, part0, part1, part2, part3,
-    grid, frame, got, column,
+    place, links, inner_ref, pre_ref, recv_ref, old_ref, unpack_ref, weights, *refs,
 ):
+    last_ref, frame_ref, part0, part1, part2, part3, grid, frame, got, column = refs[3:]
     unpack_frame(unpack_ref, recv_ref, old_ref, got)
     grid[:, 1:9, 1:9, :] = inner_ref[...]
     add_returns(grid, got)
@@ -313,20 +306,20 @@
     spread_back(low, weights, grid, column)
     split_corners(grid, links)
     take_frame(grid, frame, links, 0, 9, True)
-    pack_frame(pack_ref, frame, frame_ref, sent_ref)
+    frame_ref[...] = frame[...].astype(bf16)
     last_ref[...] = grid[:, 1:9, 1:9, :]
 
 
-def last_kernel(last_ref, misfit_ref, recv_ref, old_ref, unpack_ref, out_ref, grid, got):
+def last_kernel(place, last_ref, misfit_ref, recv_ref, old_ref, unpack_ref, out_ref, grid, got):
     unpack_frame(unpack_ref, recv_ref, old_ref, got)
     grid[:, 1:9, 1:9, :] = last_ref[...] + misfit_ref[...].reshape(3, 8, 8, 256)
     add_returns(grid, got)
     out_ref[...] = grid[:, 1:9, 1:9, :]
 
 
-smem = pl.BlockSpec(memory_space=pltpu.SMEM)
-vmem = pl.BlockSpec(memory_space=pltpu.HBM)
-left = pl.BlockSpec(memory_space=pl.ANY)
+moved_in = pl.BlockSpec(memory_space=pltpu.HBM)
+landed = pl.BlockSpec(memory_space=pl.ANY)
+left = pl.BlockSpec()
 grid_shape = pltpu.VMEM((3, 10, 10, 256), f32)
 frame_shape = pltpu.VMEM((128, 256), f32)
 flat_shape = pltpu.VMEM((304, 256), f32)
@@ -340,8 +333,11 @@
 def run(kernel, name, args, specs, outs, scratch, flops):
     single = not isinstance(outs, tuple)
     outs = (outs,) if single else outs
-    moved = [i for i, spec in enumerate(specs) if spec is vmem]
-    buffers = [pltpu.VMEM(args[i].shape, args[i].dtype) for i in moved]
+    moved = [i for i, spec in enumerate(specs) if spec is not left]
+    buffers = [
+        (pltpu.SMEM if args[i].dtype == jnp.int32 else pltpu.VMEM)(args[i].shape, args[i].dtype)
+        for i in moved
+    ]
     results = [pltpu.VMEM(out.shape, out.dtype) for out in outs]
 
     def body(*refs):
@@ -358,9 +354,10 @@
         for copy in copies:
             copy.wait()
         given = list(ins)
+        place = placing()
         for n, i in enumerate(moved):
             given[i] = held[n]
-        kernel(*given, *made, *refs)
+        kernel(place, *given, *made, *refs)
         copies = [
             pltpu.make_async_copy(made[n], targets[n], left_for.at[n]) for n in range(len(outs))
         ]
@@ -371,9 +368,9 @@
 
     made = pl.pallas_call(
         body,
-        out_shape=outs,
-        in_specs=specs,
-        out_specs=tuple(vmem for _ in outs),
+        out_shape=tuple(pltpu.HBM(out.shape, out.dtype) for out in outs),
+        in_specs=[landed if spec is left else spec for spec in specs],
+        out_specs=tuple(moved_in for _ in outs),
         scratch_shapes=[
             *buffers,
             *results,
@@ -384,7 +381,12 @@
         compiler_params=pltpu.CompilerParams(vmem_limit_bytes=40 * 2**20),
         cost_estimate=pl.CostEstimate(flops=flops, bytes_accessed=3000000, transcendentals=0),
         name=name,
-    )(*args)
+    )(
+        *[
+            pltpu.with_memory_space_constraint(arg, pltpu.HBM) if spec is moved_in else arg
+            for arg, spec in zip(args, specs)
+        ]
+    )
     return made[0] if single else made
 
 
@@ -417,18 +419,26 @@
         sent_ref[j] = total[1, 144 * j : 144 * j + 144]
 
 
-def slope_terms(parts, place, split):
+def slope_terms(parts, split, *packing):
     shape = like(4, 144, 128, dtype=f32)
-
-    def kernel(*refs):
-        slope_kernel(split, *refs)
+    count = len(parts)
+    outs = (shape, shape) + ((like(send_rows, 256),) if packing else ())
+
+    def kernel(place, *refs):
+        ins, refs = refs[: count + len(packing)], refs[count + len(packing) :]
+        if packing:
+            pack_ref, frame_ref = ins[count:]
+            refs[2][...] = jnp.dot(
+                pack_ref[...], frame_ref[...], preferred_element_type=f32
+            ).astype(bf16)
+        slope_kernel(split, place, *ins[:count], *refs[:2], *refs[len(outs) :])
 
     return run(
         kernel,
         "slope_terms",
-        (place, *parts),
-        [smem] + [vmem] * len(parts),
-        (shape, shape),
+        (*parts, *packing),
+        ([moved_in] + [landed] * 3) * (count // 4) + [moved_in] * len(packing),
+        outs,
         [
             pltpu.VMEM((1216, 128), f32),
             pltpu.VMEM((12, 10, 8, 128), f32),
@@ -442,14 +452,14 @@
     return [shifted(part, axis, k) if k else part for k, part in enumerate(parts)]
 
 
-def pair_kernel(place, kept0, got0, kept1, got1, held, *chunks):
+def pair_kernel(place, kept0, got0, kept1, got1, *chunks):
     for k in range(4):
         at = lax.rem(place[3] + k, 4)
         chunks[k][:144] = kept0[at] + got0[at]
         chunks[k][144:] = kept1[at] + got1[at]
 
 
-def plane_kernel(own, part1, part2, part3, out, total):
+def plane_kernel(place, own, part1, part2, part3, held, out, total):
     total[...] = (own[...] + part1[...]) + (part2[...] + part3[...])
     for j in range(8):
         out[j] = total[36 * j : 36 * j + 36]
@@ -493,22 +503,12 @@
     return jnp.broadcast_to(values[None], (count,) + values.shape)
 
 
-def finish_slopes(first, second, held, scale, place):
-    chunk = like(288, 128, dtype=f32)
-    chunks = run(
-        pair_kernel,
-        "pair_sum",
-        (place, first[0], shifted(first[1], "core", 1), *second, held),
-        [smem] + [vmem] * 4 + [left],
-        (chunk,) * 4,
-        [],
-        1000,
-    )
+def finish_slopes(chunks, held, scale):
     terms = run(
         plane_kernel,
         "row_sum",
-        tuple(ring(chunks, "y")),
-        [vmem] * 4,
+        (*ring(chunks, "y"), held),
+        [moved_in] + [landed] * 3 + [left],
         like(8, 36, 128, dtype=f32),
         [pltpu.VMEM((288, 128), f32)],
         1000,
@@ -520,8 +520,8 @@
     return run(
         spread_kernel,
         "spread_slopes",
-        (place, plane, shifted(plane, "core", 1)),
-        [smem, vmem, vmem],
+        (plane, shifted(plane, "core", 1)),
+        [landed, landed],
         (shape, shape),
         [],
         1000,
@@ -537,8 +537,6 @@
     goal = subsequent_targets.reshape(192, 256)
     first_weights, second_weights = w_first.reshape(9, 256, 256), w_second.reshape(9, 256, 256)
     scale = 1.0 / math.sqrt(lax.axis_size("ens") * lax.axis_size("tile") * 192)
-    where = coordinates()
-    place = jnp.stack([lax.axis_index("tile"), where["x"], where["core"], where["y"]])
     frame_like, sent_like, rows_like = like(128, 256), like(send_rows, 256), like(192, 256)
     inner_like = like(3, 8, 8, 256, dtype=f32)
     conv_flops = 2 * 9 * 192 * 256 * 256
@@ -546,8 +544,8 @@
     pack, unpack, frame, sent = run(
         route_kernel,
         "routes",
-        (tile_links, place, field),
-        [smem, smem, vmem],
+        (tile_links, field),
+        [moved_in, moved_in],
         (like(send_rows, 128), like(128, send_rows + 128), frame_like, sent_like),
         [grid_shape, frame_shape],
         2 * send_rows * 128 * 256,
@@ -556,8 +554,8 @@
     hidden, pre_first, frame, sent, *parts = run(
         first_kernel,
         "first_layer",
-        (tile_links, place, field, recv, frame, pack, unpack, first_weights),
-        [smem, smem] + [vmem] * 6,
+        (tile_links, field, recv, frame, pack, unpack, first_weights),
+        [moved_in] * 2 + [landed] + [moved_in] * 4,
         (rows_like, like(192, 256, dtype=f32), frame_like, sent_like) + (like(304, 128),) * 4,
         [grid_shape, frame_shape, frame_shape, flat_shape],
         conv_flops,
@@ -568,39 +566,49 @@
         second_kernel,
         "second_layer",
         (
-            tile_links, place, field, goal, hidden, recv, frame, pack, unpack, second_weights,
+            tile_links, field, goal, hidden, recv, frame, pack, unpack, second_weights,
             *field_parts[1:],
         ),
-        [smem, smem] + [vmem] * 8 + [left] * 3,
+        [moved_in] * 4 + [landed] + [moved_in] * 4 + [left] * 3,
         (rows_like, like(192, 256, dtype=f32), inner_like, frame_like, sent_like)
         + (like(496, 128),) * 4,
         [grid_shape, frame_shape, frame_shape, flat_shape, column_shape],
         2 * conv_flops,
     )
     recv = exchange(sent)
-    closing, sent_closing = slope_terms(ring(parts, "x"), place, True)
-    got_closing = shifted(sent_closing, "core", 1)
-    last, frame, sent, *parts = run(
+    closing_parts = ring(parts, "x")
+    closing = slope_terms(closing_parts, True)
+    last, frame, *parts = run(
         third_kernel,
         "first_gradient",
-        (tile_links, place, inner, pre_first, recv, frame, pack, unpack, first_weights, got_closing),
-        [smem, smem] + [vmem] * 7 + [left],
-        (inner_like, frame_like, sent_like) + (like(192, 128),) * 4,
+        (tile_links, inner, pre_first, recv, frame, unpack, first_weights, *closing_parts[1:]),
+        [moved_in] * 3 + [landed] + [moved_in] * 3 + [left] * 3,
+        (inner_like, frame_like) + (like(192, 128),) * 4,
         [grid_shape, frame_shape, frame_shape, column_shape],
         conv_flops,
     )
+    got_closing = shifted(closing[1], "core", 1)
+    *opening, sent = slope_terms(field_parts + ring(parts, "x"), False, pack, frame)
     recv = exchange(sent)
-    opening = slope_terms(field_parts + ring(parts, "x"), place, False)
+    chunks = run(
+        pair_kernel,
+        "pair_sum",
+        (opening[0], shifted(opening[1], "core", 1), closing[0], got_closing),
+        [moved_in, landed, moved_in, landed],
+        (like(288, 128, dtype=f32),) * 4,
+        [],
+        1000,
+    )
     condition_derivative = run(
         last_kernel,
         "last_gradient",
         (last, misfit, recv, frame, unpack),
-        [vmem] * 5,
+        [moved_in] * 2 + [landed] + [moved_in] * 2,
         inner_like,
         [grid_shape, frame_shape],
         1000,
     )
-    slopes = finish_slopes(opening, (closing, got_closing), recv, scale, place)
+    slopes = finish_slopes(chunks, recv, scale)
     return (
         states.reshape(network_conditions.shape),
         condition_derivative[None],

time: 184 us -> 169 us (0.918)
  local copies, waits for them, and re-layouts: 16.3 us -> 0.19 us
  waiting for transfers between devices: 29.2 us -> 24.9 us
  Pallas kernels: 27.4 us -> 30.1 us
  blocking collectives: 62.2 us -> 64.3 us
    unnamed x62 -> x2, local copies, waits for them, and re-layouts: 16.1 us -> 0.01 us
    ppermute x15, waiting for transfers between devices: 29.2 us -> 24.9 us  [shifted(): return lax.ppermute(values, ('tile', 'ens'), pairs)]
    pallas_call x10, Pallas kernels: 27.4 us -> 30.1 us  [run(): pl.pallas_call(body, out_shape=tuple((pltpu.HBM(out.shape, out.dtype) for...]
    all_to_all x3, blocking collectives: 43.3 us -> 45.2 us  [trade(): lax.all_to_all(values, ('tile', 'ens'), 0, 0, axis_index_groups=groups(al...]
  transfers between devices with their start and end apart: 18 -> 18, of which waited for: 11 -> 11; matrix products, arithmetic and copies ran while one was open for 0% -> 0% of each run, Pallas kernels for 3% -> 4%
where the time goes in v3:
time: 169 us; the launch traced here: 168 us
  blocking collectives  64.3 us (38%)
  starting transfers between devices  47.3 us (28%)
  Pallas kernels  30.1 us (18%)
  waiting for transfers between devices  24.9 us (15%)
    all_to_all x3, blocking collectives, trade(): lax.all_to_all(values, ('tile', 'ens'), 0, 0, axis_index_groups=groups(al...  45.2 us
    pallas_call x10, Pallas kernels, run(): pl.pallas_call(body, out_shape=tuple((pltpu.HBM(out.shape, out.dtype) for...  30.1 us
    ppermute x15, starting transfers between devices, shifted(): return lax.ppermute(values, ('tile', 'ens'), pairs)  28.4 us
    ppermute x15, waiting for transfers between devices, shifted(): return lax.ppermute(values, ('tile', 'ens'), pairs)  24.9 us
    all_to_all x1, blocking collectives, exchange(): return lax.all_to_all(values, 'tile', 0, 0, tiled=True)  19.1 us
    all_to_all x3, starting transfers between devices, exchange(): return lax.all_to_all(values, 'tile', 0, 0, tiled=True)  19 us
  transfers between devices with their start and end apart: 18, of which 11 were waited for; matrix products, arithmetic and copies ran while one was open for 0% of the time, Pallas kernels for 4%

profile of v3, /device:TPU:1, one launch (start us, length us, event | category | flops | bytes accessed | tf_op | source)
XLA Modules:
  0.0 167.8 jit_solution(811060412309575286)
XLA Ops:
  0.6 3.4 %routes.1 = (bf16[1024,128]{1,0:T(8,128)(2,1)}, bf16[128,1152]{1,0:T(8,128)(2,1)}, bf16[128,256]{1,0:T(8,128)(2,1)}, bf16[1024,256]{1,0:T(8,128)(2,1)}) custom-call(s32[3,16]{1,0:T(4,128)} %refs_0_.7, bf16[192,256]{1,0:T(8,128)(2,1)} %bitcast.28), custom_call_target="tpu_custom_call" | custom-call | flops 67108864 | bytes 3000000 | tf_op jit(solution)/shard_map/routes/pallas_call | solution.py:369
  4.1 19.1 %all_to_all.59 = bf16[32,32,256]{2,1,0:T(8,128)(2,1)S(1)} all-to-all(bf16[32,32,256]{2,1,0:T(8,128)(2,1)} %bitcast.27), channel_id=1, replica_groups=mesh['tile'=32,'ens'=8] {'tile'}, dimensions={0} | all-to-all | bytes 1048576 | tf_op jit(solution)/shard_map/all_to_all | solution.py:532
  23.2 3.9 %first_layer.1 = (bf16[192,256]{1,0:T(8,128)(2,1)}, f32[192,256]{1,0:T(8,128)}, bf16[128,256]{1,0:T(8,128)(2,1)}, bf16[1024,256]{1,0:T(8,128)(2,1)}, bf16[304,12...) custom-call(s32[3,16]{1,0:T(4,128)} %refs_0_.7, ...), custom_call_target="tpu_custom_call" | custom-call | flops 226492416 | bytes 3000000 | tf_op jit(solution)/shard_map/first_layer/pallas_call | solution.py:369
  27.1 5.8 %all-to-all-start.1 = ((bf16[32,32,256]{2,1,0:T(8,128)(2,1)}), bf16[32,32,256]{2,1,0:T(8,128)(2,1)S(1)}, u32[]{:S(2)}, u32[]{:S(2)}) async-start(bf16[32,32,256]{2,1,0:T(8,128)(2,1)} %bitcast.26), calls=%async_computation.1 | async-start | bytes 1048576 | tf_op jit(solution)/shard_map/all_to_all | solution.py:532
  32.9 1.3 collective-permute-start
  34.2 2.4 %collective-permute-start.1 = (bf16[304,128]{1,0:T(8,128)(2,1)}, bf16[304,128]{1,0:T(8,128)(2,1)S(1)}, u32[]{:S(2)}, u32[]{:S(2)}) collective-permute-start(bf16[304,128]{1,0:T(8,128)(2,1)} %get-tuple-element.50), channel_id=1, source_target_pairs={{0,16},{1,17},{32,48},{33,49},{2,18},{3,19},{34,50},{35,51},{4,20}... | collective-permute-start | bytes 233480 | tf_op jit(solution)/shard_map/ppermute | solution.py:50
  36.6 1.2 collective-permute-start.2
  37.8 5.4 %collective-permute-done.refs_9_.refs_1_ = bf16[304,128]{1,0:T(8,128)(2,1)S(1)} collective-permute-done((bf16[304,128]{1,0:T(8,128)(2,1)}, bf16[304,128]{1,0:T(8,128)(2,1)S(1)}, u32[]{:S(2)}, u32[]{:S(2)}) %collective-permute-start) | collective-permute-done | bytes 77856 | tf_op jit(solution)/shard_map/ppermute | solution.py:50
  43.2 1.2 collective-permute-done.1.refs_10_.refs_2_
  44.4 0.0 collective-permute-done.2.refs_11_.refs_3_
  44.4 0.0 all-to-all-done.1
  44.4 4.6 %second_layer.1 = (bf16[192,256]{1,0:T(8,128)(2,1)}, f32[192,256]{1,0:T(8,128)}, f32[3,8,8,256]{3,2,1,0:T(8,128)}, bf16[128,256]{1,0:T(8,128)(2,1)}, bf16[1024,2...) custom-call(s32[3,16]{1,0:T(4,128)} %refs_0_.7, ...), custom_call_target="tpu_custom_call" | custom-call | flops 452984832 | bytes 3000000 | tf_op jit(solution)/shard_map/second_layer/pallas_call | solution.py:369
  49.0 6.4 %all-to-all-start.2 = ((bf16[32,32,256]{2,1,0:T(8,128)(2,1)}), bf16[32,32,256]{2,1,0:T(8,128)(2,1)S(1)}, u32[]{:S(2)}, u32[]{:S(2)}) async-start(bf16[32,32,256]{2,1,0:T(8,128)(2,1)} %bitcast.25), calls=%async_computation.2 | async-start | bytes 1048576 | tf_op jit(solution)/shard_map/all_to_all | solution.py:532
  55.4 1.3 collective-permute-start.3
  56.7 2.4 %collective-permute-start.4 = (bf16[496,128]{1,0:T(8,128)(2,1)}, bf16[496,128]{1,0:T(8,128)(2,1)S(1)}, u32[]{:S(2)}, u32[]{:S(2)}) collective-permute-start(bf16[496,128]{1,0:T(8,128)(2,1)} %get-tuple-element.58), channel_id=1, source_target_pairs={{0,16},{1,17},{32,48},{33,49},{2,18},{3,19},{34,50},{35,51},{4,20}... | collective-permute-start | bytes 380936 | tf_op jit(solution)/shard_map/ppermute | solution.py:50
  59.1 1.2 collective-permute-start.5
  60.3 7.0 %collective-permute-done.3.refs_7_.refs_1_ = bf16[496,128]{1,0:T(8,128)(2,1)S(1)} collective-permute-done((bf16[496,128]{1,0:T(8,128)(2,1)}, bf16[496,128]{1,0:T(8,128)(2,1)S(1)}, u32[]{:S(2)}, u32[]{:S(2)}) %collective-permute-start.3) | collective-permute-done | bytes 127008 | tf_op jit(solution)/shard_map/ppermute | solution.py:50
  67.3 1.0 collective-permute-done.4.refs_8_.refs_2_
  68.2 0.0 collective-permute-done.5.refs_9_.refs_3_
  68.2 0.0 all-to-all-done.2
  68.3 3.5 %first_gradient.1 = (f32[3,8,8,256]{3,2,1,0:T(8,128)}, bf16[128,256]{1,0:T(8,128)(2,1)}, bf16[192,128]{1,0:T(8,128)(2,1)}, bf16[192,128]{1,0:T(8,128)(2,1)}, bf1...) custom-call(s32[3,16]{1,0:T(4,128)} %refs_0_.7, f32[3,8,8,256]{3,2,1,0:T(8,128)} %get-tuple-element.53.refs_1_, ...), custom_call_target="tpu_custom_call" | custom-call | flops 226492416 | bytes 3000000 | tf_op jit(solution)/shard_map/first_gradient/pallas_call | solution.py:369
  71.7 1.8 %collective-permute-start.6 = (bf16[192,128]{1,0:T(8,128)(2,1)}, bf16[192,128]{1,0:T(8,128)(2,1)S(1)}, u32[]{:S(2)}, u32[]{:S(2)}) collective-permute-start(bf16[192,128]{1,0:T(8,128)(2,1)} %get-tuple-element.64), channel_id=1, source_target_pairs={{0,8},{1,9},{32,40},{33,41},{2,10},{3,11},{34,42},{35,43},{4,12},{... | collective-permute-start | bytes 147464 | tf_op jit(solution)/shard_map/ppermute | solution.py:50
  73.6 2.0 %collective-permute-start.7 = (bf16[192,128]{1,0:T(8,128)(2,1)}, bf16[192,128]{1,0:T(8,128)(2,1)S(1)}, u32[]{:S(2)}, u32[]{:S(2)}) collective-permute-start(bf16[192,128]{1,0:T(8,128)(2,1)} %get-tuple-element.65), channel_id=1, source_target_pairs={{0,16},{1,17},{32,48},{33,49},{2,18},{3,19},{34,50},{35,51},{4,20}... | collective-permute-start | bytes 147464 | tf_op jit(solution)/shard_map/ppermute | solution.py:50
  75.6 0.6 collective-permute-start.8
  76.3 2.3 %collective-permute-done.7.refs_6_ = bf16[192,128]{1,0:T(8,128)(2,1)S(1)} collective-permute-done((bf16[192,128]{1,0:T(8,128)(2,1)}, bf16[192,128]{1,0:T(8,128)(2,1)S(1)}, u32[]{:S(2)}, u32[]{:S(2)}) %collective-permute-start.7) | collective-permute-done | bytes 49184 | tf_op jit(solution)/shard_map/ppermute | solution.py:50
  78.5 0.5 collective-permute-done.8.refs_7_
  79.1 3.3 %slope_terms.2 = (f32[4,144,128]{2,1,0:T(8,128)}, f32[4,144,128]{2,1,0:T(8,128)}, bf16[1024,256]{1,0:T(8,128)(2,1)}) custom-call(bf16[304,128]{1,0:T(8,128)(2,1)} %get-tuple-element.62.refs_0_, bf16[304,128]{1,0:T(8,128)(2,1)S(1)} %collective-permute-done.refs_9_.refs_1_, bf16[304,128]{1,0:T(8,128)(2,1)S(1)} %collective-permute-done.1.refs_10_.refs_2_, ...), custom_call_target="tpu_custom_call" | custom-call | flops 226492416 | bytes 3000000 | tf_op jit(solution)/shard_map/slope_terms/pallas_call | solution.py:369
  82.4 6.8 %all-to-all-start.3 = ((bf16[32,32,256]{2,1,0:T(8,128)(2,1)}), bf16[32,32,256]{2,1,0:T(8,128)(2,1)S(1)}, u32[]{:S(2)}, u32[]{:S(2)}) async-start(bf16[32,32,256]{2,1,0:T(8,128)(2,1)} %bitcast.24), calls=%async_computation.3 | async-start | bytes 1048576 | tf_op jit(solution)/shard_map/all_to_all | solution.py:532
  89.2 2.5 %slope_terms.3 = (f32[4,144,128]{2,1,0:T(8,128)}, f32[4,144,128]{2,1,0:T(8,128)}) custom-call(bf16[496,128]{1,0:T(8,128)(2,1)} %get-tuple-element.71.refs_0_, bf16[496,128]{1,0:T(8,128)(2,1)S(1)} %collective-permute-done.3.refs_7_.refs_1_, bf16[496,128]{1,0:T(8,128)(2,1)S(1)} %collective-permute-done.4.refs_8_.refs_2_, ...), custom_call_target="tpu_custom_call" | custom-call | flops 226492416 | bytes 3000000 | tf_op jit(solution)/shard_map/slope_terms/pallas_call | solution.py:369
  91.7 3.5 %collective-permute-start.10 = (f32[4,144,128]{2,1,0:T(8,128)}, f32[4,144,128]{2,1,0:T(8,128)S(1)}, u32[]{:S(2)}, u32[]{:S(2)}) collective-permute-start(f32[4,144,128]{2,1,0:T(8,128)} %get-tuple-element.73), channel_id=1, source_target_pairs={{0,1},{1,0},{32,33},{33,32},{2,3},{3,2},{34,35},{35,34},{4,5},{5,4... | collective-permute-start | bytes 884744 | tf_op jit(solution)/shard_map/ppermute | solution.py:50
  95.1 0.1 collective-permute-start.9
  95.2 1.3 collective-permute-done.10.refs_3_
  96.6 0.2 collective-permute-done.9.refs_1_
  96.8 2.0 %pair_sum.1 = (f32[288,128]{1,0:T(8,128)}, f32[288,128]{1,0:T(8,128)}, f32[288,128]{1,0:T(8,128)}, f32[288,128]{1,0:T(8,128)}) custom-call(f32[4,144,128]{2,1,0:T(8,128)} %get-tuple-element.69.refs_0_, f32[4,144,128]{2,1,0:T(8,128)S(1)} %collective-permute-done.9.refs_1_, f32[4,144,128]{2,1,0:T(8,128)} %get-tuple-element.72.refs_2_, ...), custom_call_target="tpu_custom_call" | custom-call | flops 1000 | bytes 3000000 | tf_op jit(solution)/shard_map/pair_sum/pallas_call | solution.py:369
  98.7 1.6 collective-permute-start.11
  100.3 2.4 %collective-permute-start.12 = (f32[288,128]{1,0:T(8,128)}, f32[288,128]{1,0:T(8,128)S(1)}, u32[]{:S(2)}, u32[]{:S(2)}) collective-permute-start(f32[288,128]{1,0:T(8,128)} %get-tuple-element.76), channel_id=1, source_target_pairs={{0,128},{1,129},{32,160},{33,161},{2,130},{3,131},{34,162},{35,163... | collective-permute-start | bytes 442376 | tf_op jit(solution)/shard_map/ppermute | solution.py:50
  102.8 1.1 collective-permute-start.13
  103.9 1.6 collective-permute-done.11.refs_1_
  105.5 4.2 %collective-permute-done.12.refs_2_ = f32[288,128]{1,0:T(8,128)S(1)} collective-permute-done((f32[288,128]{1,0:T(8,128)}, f32[288,128]{1,0:T(8,128)S(1)}, u32[]{:S(2)}, u32[]{:S(2)}) %collective-permute-start.12) | collective-permute-done | bytes 147488 | tf_op jit(solution)/shard_map/ppermute | solution.py:50
  109.7 1.7 row_sum.1
  111.4 15.6 %all_to_all.60 = f32[8,36,128]{2,1,0:T(8,128)S(1)} all-to-all(f32[8,36,128]{2,1,0:T(8,128)} %row_sum.1), channel_id=1, replica_groups={{0,32,2,34,4,36,6,38},{1,33,3,35,5,37,7,39},{64,96,66,98,68,100,70,102}..., dimensions={0} | all-to-all | bytes 294912 | tf_op jit(solution)/shard_map/all_to_all | solution.py:497
  127.1 9.8 %all_to_all.61 = bf16[8,36,128]{2,1,0:T(8,128)(2,1)S(1)} all-to-all(bf16[8,36,128]{2,1,0:T(8,128)(2,1)S(1)} %broadcast_in_dim.17), channel_id=1, replica_groups={{0,32,2,34,4,36,6,38},{1,33,3,35,5,37,7,39},{64,96,66,98,68,100,70,102}..., dimensions={0} | all-to-all | bytes 147456 | tf_op jit(solution)/shard_map/all_to_all | solution.py:497
  136.9 0.2 broadcast_in_dim.19
  137.1 19.8 %all_to_all.62.refs_0_ = bf16[16,288,128]{2,1,0:T(8,128)(2,1)S(1)} all-to-all(bf16[16,288,128]{2,1,0:T(8,128)(2,1)S(1)} %broadcast_in_dim.19), channel_id=1, replica_groups={{0,64,128,192,8,72,136,200,16,80,144,208,24,88,152,216},{1,65,129,193,9..., dimensions={0} | all-to-all | bytes 2359296 | tf_op jit(solution)/shard_map/all_to_all | solution.py:497
  156.8 5.3 %collective-permute-start.14 = (bf16[16,288,128]{2,1,0:T(8,128)(2,1)S(1)}, bf16[16,288,128]{2,1,0:T(8,128)(2,1)S(1)}, u32[]{:S(2)}, u32[]{:S(2)}) collective-permute-start(bf16[16,288,128]{2,1,0:T(8,128)(2,1)S(1)} %all_to_all.62.refs_0_), channel_id=1, source_target_pairs={{0,1},{1,0},{32,33},{33,32},{2,3},{3,2},{34,35},{35,34},{4,5},{5,4... | collective-permute-start | bytes 3538952 | tf_op jit(solution)/shard_map/ppermute | solution.py:50
  162.2 2.3 %last_gradient.1 = f32[3,8,8,256]{3,2,1,0:T(8,128)} custom-call(f32[3,8,8,256]{3,2,1,0:T(8,128)} %get-tuple-element.60.refs_0_, f32[192,256]{1,0:T(8,128)} %get-tuple-element.61.refs_1_, bf16[1024,256]{1,0:T(8,128)(2,1)S(1)} %bitcast.17, bf16[128,256]{1,0:T(8,128)(2,1)} %get-tuple-element.67.refs_9_.refs_3_, ...), custom_call_target="tpu_custom_call" | custom-call | flops 1000 | bytes 3000000 | tf_op jit(solution)/shard_map/last_gradient/pallas_call | solution.py:369
  164.4 0.2 collective-permute-done.14.refs_1_
  164.7 3.0 %spread_slopes.1 = (f32[9,256,256]{2,1,0:T(8,128)}, f32[9,256,256]{2,1,0:T(8,128)}) custom-call(bf16[16,288,128]{2,1,0:T(8,128)(2,1)S(1)} %all_to_all.62.refs_0_, bf16[16,288,128]{2,1,0:T(8,128)(2,1)S(1)} %collective-permute-done.14.refs_1_), custom_call_target="tpu_custom_call" | custom-call | flops 1000 | bytes 3000000 | tf_op jit(solution)/shard_map/spread_slopes/pallas_call | solution.py:369
  (9 shorter events, 0.1 us)
Async XLA Ops:
  27.1 17.3 %all-to-all-start.1 = ((bf16[32,32,256]{2,1,0:T(8,128)(2,1)}), bf16[32,32,256]{2,1,0:T(8,128)(2,1)S(1)}, u32[]{:S(2)}, u32[]{:S(2)}) async-start(bf16[32,32,256]{2,1,0:T(8,128)(2,1)} %bitcast.26), calls=%async_computation.1 | async-start | bytes 1048576 | tf_op jit(solution)/shard_map/all_to_all | solution.py:532
  32.9 10.3 %collective-permute-start = (bf16[304,128]{1,0:T(8,128)(2,1)}, bf16[304,128]{1,0:T(8,128)(2,1)S(1)}, u32[]{:S(2)}, u32[]{:S(2)}) collective-permute-start(bf16[304,128]{1,0:T(8,128)(2,1)} %get-tuple-element.49), channel_id=1, source_target_pairs={{0,8},{1,9},{32,40},{33,41},{2,10},{3,11},{34,42},{35,43},{4,12},{... | collective-permute-start | bytes 233480 | tf_op jit(solution)/shard_map/ppermute | solution.py:50
  34.2 10.2 %collective-permute-start.1 = (bf16[304,128]{1,0:T(8,128)(2,1)}, bf16[304,128]{1,0:T(8,128)(2,1)S(1)}, u32[]{:S(2)}, u32[]{:S(2)}) collective-permute-start(bf16[304,128]{1,0:T(8,128)(2,1)} %get-tuple-element.50), channel_id=1, source_target_pairs={{0,16},{1,17},{32,48},{33,49},{2,18},{3,19},{34,50},{35,51},{4,20}... | collective-permute-start | bytes 233480 | tf_op jit(solution)/shard_map/ppermute | solution.py:50
  36.6 7.8 %collective-permute-start.2 = (bf16[304,128]{1,0:T(8,128)(2,1)}, bf16[304,128]{1,0:T(8,128)(2,1)S(1)}, u32[]{:S(2)}, u32[]{:S(2)}) collective-permute-start(bf16[304,128]{1,0:T(8,128)(2,1)} %get-tuple-element.51), channel_id=1, source_target_pairs={{0,24},{1,25},{32,56},{33,57},{2,26},{3,27},{34,58},{35,59},{4,28}... | collective-permute-start | bytes 233480 | tf_op jit(solution)/shard_map/ppermute | solution.py:50
  49.0 19.3 %all-to-all-start.2 = ((bf16[32,32,256]{2,1,0:T(8,128)(2,1)}), bf16[32,32,256]{2,1,0:T(8,128)(2,1)S(1)}, u32[]{:S(2)}, u32[]{:S(2)}) async-start(bf16[32,32,256]{2,1,0:T(8,128)(2,1)} %bitcast.25), calls=%async_computation.2 | async-start | bytes 1048576 | tf_op jit(solution)/shard_map/all_to_all | solution.py:532
  55.4 11.9 %collective-permute-start.3 = (bf16[496,128]{1,0:T(8,128)(2,1)}, bf16[496,128]{1,0:T(8,128)(2,1)S(1)}, u32[]{:S(2)}, u32[]{:S(2)}) collective-permute-start(bf16[496,128]{1,0:T(8,128)(2,1)} %get-tuple-element.57), channel_id=1, source_target_pairs={{0,8},{1,9},{32,40},{33,41},{2,10},{3,11},{34,42},{35,43},{4,12},{... | collective-permute-start | bytes 380936 | tf_op jit(solution)/shard_map/ppermute | solution.py:50
  56.7 11.5 %collective-permute-start.4 = (bf16[496,128]{1,0:T(8,128)(2,1)}, bf16[496,128]{1,0:T(8,128)(2,1)S(1)}, u32[]{:S(2)}, u32[]{:S(2)}) collective-permute-start(bf16[496,128]{1,0:T(8,128)(2,1)} %get-tuple-element.58), channel_id=1, source_target_pairs={{0,16},{1,17},{32,48},{33,49},{2,18},{3,19},{34,50},{35,51},{4,20}... | collective-permute-start | bytes 380936 | tf_op jit(solution)/shard_map/ppermute | solution.py:50
  59.1 9.1 %collective-permute-start.5 = (bf16[496,128]{1,0:T(8,128)(2,1)}, bf16[496,128]{1,0:T(8,128)(2,1)S(1)}, u32[]{:S(2)}, u32[]{:S(2)}) collective-permute-start(bf16[496,128]{1,0:T(8,128)(2,1)} %get-tuple-element.59), channel_id=1, source_target_pairs={{0,24},{1,25},{32,56},{33,57},{2,26},{3,27},{34,58},{35,59},{4,28}... | collective-permute-start | bytes 380936 | tf_op jit(solution)/shard_map/ppermute | solution.py:50
  71.7 4.5 %collective-permute-start.6 = (bf16[192,128]{1,0:T(8,128)(2,1)}, bf16[192,128]{1,0:T(8,128)(2,1)S(1)}, u32[]{:S(2)}, u32[]{:S(2)}) collective-permute-start(bf16[192,128]{1,0:T(8,128)(2,1)} %get-tuple-element.64), channel_id=1, source_target_pairs={{0,8},{1,9},{32,40},{33,41},{2,10},{3,11},{34,42},{35,43},{4,12},{... | collective-permute-start | bytes 147464 | tf_op jit(solution)/shard_map/ppermute | solution.py:50
  73.6 5.0 %collective-permute-start.7 = (bf16[192,128]{1,0:T(8,128)(2,1)}, bf16[192,128]{1,0:T(8,128)(2,1)S(1)}, u32[]{:S(2)}, u32[]{:S(2)}) collective-permute-start(bf16[192,128]{1,0:T(8,128)(2,1)} %get-tuple-element.65), channel_id=1, source_target_pairs={{0,16},{1,17},{32,48},{33,49},{2,18},{3,19},{34,50},{35,51},{4,20}... | collective-permute-start | bytes 147464 | tf_op jit(solution)/shard_map/ppermute | solution.py:50
  75.6 3.4 %collective-permute-start.8 = (bf16[192,128]{1,0:T(8,128)(2,1)}, bf16[192,128]{1,0:T(8,128)(2,1)S(1)}, u32[]{:S(2)}, u32[]{:S(2)}) collective-permute-start(bf16[192,128]{1,0:T(8,128)(2,1)} %get-tuple-element.66), channel_id=1, source_target_pairs={{0,24},{1,25},{32,56},{33,57},{2,26},{3,27},{34,58},{35,59},{4,28}... | collective-permute-start | bytes 147464 | tf_op jit(solution)/shard_map/ppermute | solution.py:50
  82.4 12.7 %copy-start = (f32[4,144,128]{2,1,0:T(8,128)S(1)}, f32[4,144,128]{2,1,0:T(8,128)}, u32[]{:S(2)}) copy-start(f32[4,144,128]{2,1,0:T(8,128)} %get-tuple-element.70) | copy-start | bytes 884740
  82.4 27.3 %all-to-all-start.3 = ((bf16[32,32,256]{2,1,0:T(8,128)(2,1)}), bf16[32,32,256]{2,1,0:T(8,128)(2,1)S(1)}, u32[]{:S(2)}, u32[]{:S(2)}) async-start(bf16[32,32,256]{2,1,0:T(8,128)(2,1)} %bitcast.24), calls=%async_computation.3 | async-start | bytes 1048576 | tf_op jit(solution)/shard_map/all_to_all | solution.py:532
  91.7 4.9 %collective-permute-start.10 = (f32[4,144,128]{2,1,0:T(8,128)}, f32[4,144,128]{2,1,0:T(8,128)S(1)}, u32[]{:S(2)}, u32[]{:S(2)}) collective-permute-start(f32[4,144,128]{2,1,0:T(8,128)} %get-tuple-element.73), channel_id=1, source_target_pairs={{0,1},{1,0},{32,33},{33,32},{2,3},{3,2},{34,35},{35,34},{4,5},{5,4... | collective-permute-start | bytes 884744 | tf_op jit(solution)/shard_map/ppermute | solution.py:50
  95.1 1.6 collective-permute-start.9
  98.7 6.8 %collective-permute-start.11 = (f32[288,128]{1,0:T(8,128)}, f32[288,128]{1,0:T(8,128)S(1)}, u32[]{:S(2)}, u32[]{:S(2)}) collective-permute-start(f32[288,128]{1,0:T(8,128)} %get-tuple-element.75), channel_id=1, source_target_pairs={{0,64},{1,65},{32,96},{33,97},{2,66},{3,67},{34,98},{35,99},{4,68}... | collective-permute-start | bytes 442376 | tf_op jit(solution)/shard_map/ppermute | solution.py:50
  100.3 9.4 %collective-permute-start.12 = (f32[288,128]{1,0:T(8,128)}, f32[288,128]{1,0:T(8,128)S(1)}, u32[]{:S(2)}, u32[]{:S(2)}) collective-permute-start(f32[288,128]{1,0:T(8,128)} %get-tuple-element.76), channel_id=1, source_target_pairs={{0,128},{1,129},{32,160},{33,161},{2,130},{3,131},{34,162},{35,163... | collective-permute-start | bytes 442376 | tf_op jit(solution)/shard_map/ppermute | solution.py:50
  102.8 7.0 %collective-permute-start.13 = (f32[288,128]{1,0:T(8,128)}, f32[288,128]{1,0:T(8,128)S(1)}, u32[]{:S(2)}, u32[]{:S(2)}) collective-permute-start(f32[288,128]{1,0:T(8,128)} %get-tuple-element.77), channel_id=1, source_target_pairs={{0,192},{1,193},{32,224},{33,225},{2,194},{3,195},{34,226},{35,227... | collective-permute-start | bytes 442376 | tf_op jit(solution)/shard_map/ppermute | solution.py:50
  156.8 7.8 %collective-permute-start.14 = (bf16[16,288,128]{2,1,0:T(8,128)(2,1)S(1)}, bf16[16,288,128]{2,1,0:T(8,128)(2,1)S(1)}, u32[]{:S(2)}, u32[]{:S(2)}) collective-permute-start(bf16[16,288,128]{2,1,0:T(8,128)(2,1)S(1)} %all_to_all.62.refs_0_), channel_id=1, source_target_pairs={{0,1},{1,0},{32,33},{33,32},{2,3},{3,2},{34,35},{35,34},{4,5},{5,4... | collective-permute-start | bytes 3538952 | tf_op jit(solution)/shard_map/ppermute | solution.py:50

commit v4 on v3

--- a/solution.py
+++ b/solution.py
@@ -320,6 +320,7 @@
 moved_in = pl.BlockSpec(memory_space=pltpu.HBM)
 landed = pl.BlockSpec(memory_space=pl.ANY)
 left = pl.BlockSpec()
+resting = pl.BlockSpec(memory_space=pltpu.HBM)
 grid_shape = pltpu.VMEM((3, 10, 10, 256), f32)
 frame_shape = pltpu.VMEM((128, 256), f32)
 flat_shape = pltpu.VMEM((304, 256), f32)
@@ -330,15 +331,47 @@
     return jax.ShapeDtypeStruct(shape, dtype)
 
 
+class Arriving:
+    def __init__(self, ref, copy):
+        self.ref, self.copy = ref, copy
+
+    def settle(self):
+        if self.copy is not None:
+            self.copy.wait()
+            self.copy = None
+
+    def __getitem__(self, at):
+        self.settle()
+        return self.ref[at]
+
+
+class Leaving:
+    def __init__(self, ref, copy):
+        self.ref, self.copy, self.started = ref, copy, False
+
+    def send(self):
+        if not self.started:
+            self.copy.start()
+            self.started = True
+
+    def __getitem__(self, at):
+        return self.ref[at]
+
+    def __setitem__(self, at, value):
+        self.ref[at] = value
+        if at is Ellipsis:
+            self.send()
+
+
 def run(kernel, name, args, specs, outs, scratch, flops):
     single = not isinstance(outs, tuple)
     outs = (outs,) if single else outs
-    moved = [i for i, spec in enumerate(specs) if spec is not left]
+    moved = [i for i, spec in enumerate(specs) if spec is not left and spec is not resting]
     buffers = [
         (pltpu.SMEM if args[i].dtype == jnp.int32 else pltpu.VMEM)(args[i].shape, args[i].dtype)
         for i in moved
     ]
-    results = [pltpu.VMEM(out.shape, out.dtype) for out in outs]
+    stores = [pltpu.VMEM(out.shape, out.dtype) for out in outs]
 
     def body(*refs):
         ins, refs = refs[: len(args)], refs[len(args) :]
@@ -351,20 +384,20 @@
         ]
         for copy in copies:
             copy.start()
-        for copy in copies:
-            copy.wait()
         given = list(ins)
-        place = placing()
         for n, i in enumerate(moved):
-            given[i] = held[n]
-        kernel(place, *given, *made, *refs)
-        copies = [
-            pltpu.make_async_copy(made[n], targets[n], left_for.at[n]) for n in range(len(outs))
+            given[i] = Arriving(held[n], copies[n])
+        results = [
+            Leaving(made[n], pltpu.make_async_copy(made[n], targets[n], left_for.at[n]))
+            for n in range(len(outs))
         ]
-        for copy in copies:
-            copy.start()
-        for copy in copies:
-            copy.wait()
+        kernel(placing(), *given, *results, *refs)
+        for n in range(len(moved)):
+            given[moved[n]].settle()
+        for result in results:
+            result.send()
+        for result in results:
+            result.copy.wait()
 
     made = pl.pallas_call(
         body,
@@ -373,7 +406,7 @@
         out_specs=tuple(moved_in for _ in outs),
         scratch_shapes=[
             *buffers,
-            *results,
+            *stores,
             pltpu.SemaphoreType.DMA((max(1, len(moved)),)),
             pltpu.SemaphoreType.DMA((len(outs),)),
             *scratch,
@@ -383,7 +416,9 @@
         name=name,
     )(
         *[
-            pltpu.with_memory_space_constraint(arg, pltpu.HBM) if spec is moved_in else arg
+            pltpu.with_memory_space_constraint(arg, pltpu.HBM)
+            if spec is moved_in or spec is resting
+            else arg
             for arg, spec in zip(args, specs)
         ]
     )
@@ -419,13 +454,13 @@
         sent_ref[j] = total[1, 144 * j : 144 * j + 144]
 
 
-def slope_terms(parts, split, *packing):
+def slope_terms(parts, split, packing=(), held=()):
     shape = like(4, 144, 128, dtype=f32)
     count = len(parts)
     outs = (shape, shape) + ((like(send_rows, 256),) if packing else ())
 
     def kernel(place, *refs):
-        ins, refs = refs[: count + len(packing)], refs[count + len(packing) :]
+        ins, refs = refs[: count + len(packing)], refs[count + len(packing) + len(held) :]
         if packing:
             pack_ref, frame_ref = ins[count:]
             refs[2][...] = jnp.dot(
@@ -436,8 +471,8 @@
     return run(
         kernel,
         "slope_terms",
-        (*parts, *packing),
-        ([moved_in] + [landed] * 3) * (count // 4) + [moved_in] * len(packing),
+        (*parts, *packing, *held),
+        ([moved_in] + [landed] * 3) * (count // 4) + [moved_in] * len(packing) + [resting] * len(held),
         outs,
         [
             pltpu.VMEM((1216, 128), f32),
@@ -467,10 +502,10 @@
 
 def spread_kernel(place, own, other, first_ref, second_ref):
     low = place[2] == 0
-    for x in range(4):
-        row, column = 128 * (x // 2), 128 * (x % 2)
-        for n, out in enumerate((first_ref, second_ref)):
-            at = slice(144 * n, 144 * n + 144)
+    for n, out in enumerate((first_ref, second_ref)):
+        at = slice(144 * n, 144 * n + 144)
+        for x in range(4):
+            row, column = 128 * (x // 2), 128 * (x % 2)
             pair = [
                 jnp.concatenate(
                     [part[4 * x + y, at].astype(f32) for y in range(4)], axis=0
@@ -479,6 +514,7 @@
             ]
             out[:, row : row + 64, column : column + 128] = jnp.where(low, pair[0], pair[1])
             out[:, row + 64 : row + 128, column : column + 128] = jnp.where(low, pair[1], pair[0])
+        out.send()
 
 
 def groups(along):
@@ -588,7 +624,9 @@
         conv_flops,
     )
     got_closing = shifted(closing[1], "core", 1)
-    *opening, sent = slope_terms(field_parts + ring(parts, "x"), False, pack, frame)
+    *opening, sent = slope_terms(
+        field_parts + ring(parts, "x"), False, (pack, frame), (closing[0],)
+    )
     recv = exchange(sent)
     chunks = run(
         pair_kernel,

time: 169 us -> 166 us (0.982)
  waiting for transfers between devices: 24.9 us -> 22.8 us
    ppermute x15, waiting for transfers between devices: 24.9 us -> 22.8 us  [shifted(): return lax.ppermute(values, ('tile', 'ens'), pairs)]
  transfers between devices with their start and end apart: 18 -> 18, of which waited for: 11 -> 10; matrix products, arithmetic and copies ran while one was open for 0% -> 0% of each run, Pallas kernels for 4% -> 4%
where the time goes in v4:
time: 166 us; the launch traced here: 165 us
  blocking collectives  64 us (39%)
  starting transfers between devices  47.2 us (28%)
  Pallas kernels  30.1 us (18%)
  waiting for transfers between devices  22.8 us (14%)
    all_to_all x3, blocking collectives, trade(): lax.all_to_all(values, ('tile', 'ens'), 0, 0, axis_index_groups=groups(al...  44.8 us
    pallas_call x10, Pallas kernels, run(): pl.pallas_call(body, out_shape=tuple((pltpu.HBM(out.shape, out.dtype) for...  30.1 us
    ppermute x15, starting transfers between devices, shifted(): return lax.ppermute(values, ('tile', 'ens'), pairs)  28.4 us
    ppermute x15, waiting for transfers between devices, shifted(): return lax.ppermute(values, ('tile', 'ens'), pairs)  22.8 us
    all_to_all x1, blocking collectives, exchange(): return lax.all_to_all(values, 'tile', 0, 0, tiled=True)  19.1 us
    all_to_all x3, starting transfers between devices, exchange(): return lax.all_to_all(values, 'tile', 0, 0, tiled=True)  18.8 us
  transfers between devices with their start and end apart: 18, of which 10 were waited for; matrix products, arithmetic and copies ran while one was open for 0% of the time, Pallas kernels for 4%

profile of v4, /device:TPU:1, one launch (start us, length us, event | category | flops | bytes accessed | tf_op | source)
XLA Modules:
  0.0 165.3 jit_solution(8421980423967009374)
XLA Ops:
  0.6 3.4 %routes.1 = (bf16[1024,128]{1,0:T(8,128)(2,1)}, bf16[128,1152]{1,0:T(8,128)(2,1)}, bf16[128,256]{1,0:T(8,128)(2,1)}, bf16[1024,256]{1,0:T(8,128)(2,1)}) custom-call(s32[3,16]{1,0:T(4,128)} %refs_0_.7, bf16[192,256]{1,0:T(8,128)(2,1)} %bitcast.28), custom_call_target="tpu_custom_call" | custom-call | flops 67108864 | bytes 3000000 | tf_op jit(solution)/shard_map/routes/pallas_call | solution.py:402
  4.1 19.1 %all_to_all.59 = bf16[32,32,256]{2,1,0:T(8,128)(2,1)S(1)} all-to-all(bf16[32,32,256]{2,1,0:T(8,128)(2,1)} %bitcast.27), channel_id=1, replica_groups=mesh['tile'=32,'ens'=8] {'tile'}, dimensions={0} | all-to-all | bytes 1048576 | tf_op jit(solution)/shard_map/all_to_all | solution.py:568
  23.2 3.7 %first_layer.1 = (bf16[192,256]{1,0:T(8,128)(2,1)}, f32[192,256]{1,0:T(8,128)}, bf16[128,256]{1,0:T(8,128)(2,1)}, bf16[1024,256]{1,0:T(8,128)(2,1)}, bf16[304,12...) custom-call(s32[3,16]{1,0:T(4,128)} %refs_0_.7, ...), custom_call_target="tpu_custom_call" | custom-call | flops 226492416 | bytes 3000000 | tf_op jit(solution)/shard_map/first_layer/pallas_call | solution.py:402
  26.9 5.8 %all-to-all-start.1 = ((bf16[32,32,256]{2,1,0:T(8,128)(2,1)}), bf16[32,32,256]{2,1,0:T(8,128)(2,1)S(1)}, u32[]{:S(2)}, u32[]{:S(2)}) async-start(bf16[32,32,256]{2,1,0:T(8,128)(2,1)} %bitcast.26), calls=%async_computation.1 | async-start | bytes 1048576 | tf_op jit(solution)/shard_map/all_to_all | solution.py:568
  32.7 1.3 collective-permute-start
  34.0 2.4 %collective-permute-start.1 = (bf16[304,128]{1,0:T(8,128)(2,1)}, bf16[304,128]{1,0:T(8,128)(2,1)S(1)}, u32[]{:S(2)}, u32[]{:S(2)}) collective-permute-start(bf16[304,128]{1,0:T(8,128)(2,1)} %get-tuple-element.50), channel_id=1, source_target_pairs={{0,16},{1,17},{32,48},{33,49},{2,18},{3,19},{34,50},{35,51},{4,20}... | collective-permute-start | bytes 233480 | tf_op jit(solution)/shard_map/ppermute | solution.py:50
  36.4 1.2 collective-permute-start.2
  37.5 5.4 %collective-permute-done.refs_9_.refs_1_ = bf16[304,128]{1,0:T(8,128)(2,1)S(1)} collective-permute-done((bf16[304,128]{1,0:T(8,128)(2,1)}, bf16[304,128]{1,0:T(8,128)(2,1)S(1)}, u32[]{:S(2)}, u32[]{:S(2)}) %collective-permute-start) | collective-permute-done | bytes 77856 | tf_op jit(solution)/shard_map/ppermute | solution.py:50
  43.0 1.2 collective-permute-done.1.refs_10_.refs_2_
  44.1 0.0 collective-permute-done.2.refs_11_.refs_3_
  44.1 0.0 all-to-all-done.1
  44.1 4.5 %second_layer.1 = (bf16[192,256]{1,0:T(8,128)(2,1)}, f32[192,256]{1,0:T(8,128)}, f32[3,8,8,256]{3,2,1,0:T(8,128)}, bf16[128,256]{1,0:T(8,128)(2,1)}, bf16[1024,2...) custom-call(s32[3,16]{1,0:T(4,128)} %refs_0_.7, ...), custom_call_target="tpu_custom_call" | custom-call | flops 452984832 | bytes 3000000 | tf_op jit(solution)/shard_map/second_layer/pallas_call | solution.py:402
  48.7 6.4 %all-to-all-start.2 = ((bf16[32,32,256]{2,1,0:T(8,128)(2,1)}), bf16[32,32,256]{2,1,0:T(8,128)(2,1)S(1)}, u32[]{:S(2)}, u32[]{:S(2)}) async-start(bf16[32,32,256]{2,1,0:T(8,128)(2,1)} %bitcast.25), calls=%async_computation.2 | async-start | bytes 1048576 | tf_op jit(solution)/shard_map/all_to_all | solution.py:568
  55.1 1.3 collective-permute-start.3
  56.4 2.4 %collective-permute-start.4 = (bf16[496,128]{1,0:T(8,128)(2,1)}, bf16[496,128]{1,0:T(8,128)(2,1)S(1)}, u32[]{:S(2)}, u32[]{:S(2)}) collective-permute-start(bf16[496,128]{1,0:T(8,128)(2,1)} %get-tuple-element.58), channel_id=1, source_target_pairs={{0,16},{1,17},{32,48},{33,49},{2,18},{3,19},{34,50},{35,51},{4,20}... | collective-permute-start | bytes 380936 | tf_op jit(solution)/shard_map/ppermute | solution.py:50
  58.8 1.2 collective-permute-start.5
  60.0 7.0 %collective-permute-done.3.refs_7_.refs_1_ = bf16[496,128]{1,0:T(8,128)(2,1)S(1)} collective-permute-done((bf16[496,128]{1,0:T(8,128)(2,1)}, bf16[496,128]{1,0:T(8,128)(2,1)S(1)}, u32[]{:S(2)}, u32[]{:S(2)}) %collective-permute-start.3) | collective-permute-done | bytes 127008 | tf_op jit(solution)/shard_map/ppermute | solution.py:50
  67.0 1.0 collective-permute-done.4.refs_8_.refs_2_
  67.9 0.0 collective-permute-done.5.refs_9_.refs_3_
  67.9 0.0 all-to-all-done.2
  67.9 3.4 %first_gradient.1 = (f32[3,8,8,256]{3,2,1,0:T(8,128)}, bf16[128,256]{1,0:T(8,128)(2,1)}, bf16[192,128]{1,0:T(8,128)(2,1)}, bf16[192,128]{1,0:T(8,128)(2,1)}, bf1...) custom-call(s32[3,16]{1,0:T(4,128)} %refs_0_.7, f32[3,8,8,256]{3,2,1,0:T(8,128)} %get-tuple-element.53.refs_1_, ...), custom_call_target="tpu_custom_call" | custom-call | flops 226492416 | bytes 3000000 | tf_op jit(solution)/shard_map/first_gradient/pallas_call | solution.py:402
  71.4 1.8 %collective-permute-start.6 = (bf16[192,128]{1,0:T(8,128)(2,1)}, bf16[192,128]{1,0:T(8,128)(2,1)S(1)}, u32[]{:S(2)}, u32[]{:S(2)}) collective-permute-start(bf16[192,128]{1,0:T(8,128)(2,1)} %get-tuple-element.64), channel_id=1, source_target_pairs={{0,8},{1,9},{32,40},{33,41},{2,10},{3,11},{34,42},{35,43},{4,12},{... | collective-permute-start | bytes 147464 | tf_op jit(solution)/shard_map/ppermute | solution.py:50
  73.2 2.1 %collective-permute-start.7 = (bf16[192,128]{1,0:T(8,128)(2,1)}, bf16[192,128]{1,0:T(8,128)(2,1)S(1)}, u32[]{:S(2)}, u32[]{:S(2)}) collective-permute-start(bf16[192,128]{1,0:T(8,128)(2,1)} %get-tuple-element.65), channel_id=1, source_target_pairs={{0,16},{1,17},{32,48},{33,49},{2,18},{3,19},{34,50},{35,51},{4,20}... | collective-permute-start | bytes 147464 | tf_op jit(solution)/shard_map/ppermute | solution.py:50
  75.2 0.6 collective-permute-start.8
  75.9 2.5 %slope_terms.2 = (f32[4,144,128]{2,1,0:T(8,128)}, f32[4,144,128]{2,1,0:T(8,128)}) custom-call(bf16[496,128]{1,0:T(8,128)(2,1)} %get-tuple-element.68.refs_0_, bf16[496,128]{1,0:T(8,128)(2,1)S(1)} %collective-permute-done.3.refs_7_.refs_1_, bf16[496,128]{1,0:T(8,128)(2,1)S(1)} %collective-permute-done.4.refs_8_.refs_2_, ...), custom_call_target="tpu_custom_call" | custom-call | flops 226492416 | bytes 3000000 | tf_op jit(solution)/shard_map/slope_terms/pallas_call | solution.py:402
  78.5 0.2 collective-permute-done.8.refs_7_
  78.7 3.6 %slope_terms.3 = (f32[4,144,128]{2,1,0:T(8,128)}, f32[4,144,128]{2,1,0:T(8,128)}, bf16[1024,256]{1,0:T(8,128)(2,1)}) custom-call(bf16[304,128]{1,0:T(8,128)(2,1)} %get-tuple-element.62.refs_0_, bf16[304,128]{1,0:T(8,128)(2,1)S(1)} %collective-permute-done.refs_9_.refs_1_, bf16[304,128]{1,0:T(8,128)(2,1)S(1)} %collective-permute-done.1.refs_10_.refs_2_, ...), custom_call_target="tpu_custom_call" | custom-call | flops 226492416 | bytes 3000000 | tf_op jit(solution)/shard_map/slope_terms/pallas_call | solution.py:402
  82.3 6.6 %all-to-all-start.3 = ((bf16[32,32,256]{2,1,0:T(8,128)(2,1)}), bf16[32,32,256]{2,1,0:T(8,128)(2,1)S(1)}, u32[]{:S(2)}, u32[]{:S(2)}) async-start(bf16[32,32,256]{2,1,0:T(8,128)(2,1)} %bitcast.24), calls=%async_computation.3 | async-start | bytes 1048576 | tf_op jit(solution)/shard_map/all_to_all | solution.py:568
  88.9 3.5 %collective-permute-start.10 = (f32[4,144,128]{2,1,0:T(8,128)S(1)}, f32[4,144,128]{2,1,0:T(8,128)S(1)}, u32[]{:S(2)}, u32[]{:S(2)}) collective-permute-start(f32[4,144,128]{2,1,0:T(8,128)S(1)} %copy-done), channel_id=1, source_target_pairs={{0,1},{1,0},{32,33},{33,32},{2,3},{3,2},{34,35},{35,34},{4,5},{5,4... | collective-permute-start | bytes 884744 | tf_op jit(solution)/shard_map/ppermute | solution.py:50
  92.4 0.1 collective-permute-start.9
  92.5 1.1 collective-permute-done.10.refs_3_
  93.6 0.6 collective-permute-done.9.refs_1_
  94.3 2.0 %pair_sum.1 = (f32[288,128]{1,0:T(8,128)}, f32[288,128]{1,0:T(8,128)}, f32[288,128]{1,0:T(8,128)}, f32[288,128]{1,0:T(8,128)}) custom-call(f32[4,144,128]{2,1,0:T(8,128)} %get-tuple-element.71.refs_0_, f32[4,144,128]{2,1,0:T(8,128)S(1)} %collective-permute-done.9.refs_1_, f32[4,144,128]{2,1,0:T(8,128)} %get-tuple-element.69.refs_10_.refs_2_, ...), custom_call_target="tpu_custom_call" | custom-call | flops 1000 | bytes 3000000 | tf_op jit(solution)/shard_map/pair_sum/pallas_call | solution.py:402
  96.2 1.6 collective-permute-start.11
  97.8 2.4 %collective-permute-start.12 = (f32[288,128]{1,0:T(8,128)}, f32[288,128]{1,0:T(8,128)S(1)}, u32[]{:S(2)}, u32[]{:S(2)}) collective-permute-start(f32[288,128]{1,0:T(8,128)} %get-tuple-element.76), channel_id=1, source_target_pairs={{0,128},{1,129},{32,160},{33,161},{2,130},{3,131},{34,162},{35,163... | collective-permute-start | bytes 442376 | tf_op jit(solution)/shard_map/ppermute | solution.py:50
  100.3 1.1 collective-permute-start.13
  101.4 2.6 %collective-permute-done.11.refs_1_ = f32[288,128]{1,0:T(8,128)S(1)} collective-permute-done((f32[288,128]{1,0:T(8,128)}, f32[288,128]{1,0:T(8,128)S(1)}, u32[]{:S(2)}, u32[]{:S(2)}) %collective-permute-start.11) | collective-permute-done | bytes 147488 | tf_op jit(solution)/shard_map/ppermute | solution.py:50
  104.0 3.6 %collective-permute-done.12.refs_2_ = f32[288,128]{1,0:T(8,128)S(1)} collective-permute-done((f32[288,128]{1,0:T(8,128)}, f32[288,128]{1,0:T(8,128)S(1)}, u32[]{:S(2)}, u32[]{:S(2)}) %collective-permute-start.12) | collective-permute-done | bytes 147488 | tf_op jit(solution)/shard_map/ppermute | solution.py:50
  107.6 0.0 all-to-all-done.3
  107.6 1.7 %row_sum.1 = f32[8,36,128]{2,1,0:T(8,128)} custom-call(f32[288,128]{1,0:T(8,128)} %get-tuple-element.74.refs_0_, f32[288,128]{1,0:T(8,128)S(1)} %collective-permute-done.11.refs_1_, f32[288,128]{1,0:T(8,128)S(1)} %collective-permute-done.12.refs_2_, f32[288,128]{1,0:T(8,128)S(1)} %collective-permute-done.13.refs_3_, bf16[1024,256]{1,0:T(8,128)(2,1)S(1)} %bitcast.16), custom_call_target="tpu_custom_call" | custom-call | flops 1000 | bytes 3000000 | tf_op jit(solution)/shard_map/row_sum/pallas_call | solution.py:402
  109.3 15.4 %all_to_all.60 = f32[8,36,128]{2,1,0:T(8,128)S(1)} all-to-all(f32[8,36,128]{2,1,0:T(8,128)} %row_sum.1), channel_id=1, replica_groups={{0,32,2,34,4,36,6,38},{1,33,3,35,5,37,7,39},{64,96,66,98,68,100,70,102}..., dimensions={0} | all-to-all | bytes 294912 | tf_op jit(solution)/shard_map/all_to_all | solution.py:533
  124.7 9.8 %all_to_all.61 = bf16[8,36,128]{2,1,0:T(8,128)(2,1)S(1)} all-to-all(bf16[8,36,128]{2,1,0:T(8,128)(2,1)S(1)} %broadcast_in_dim.17), channel_id=1, replica_groups={{0,32,2,34,4,36,6,38},{1,33,3,35,5,37,7,39},{64,96,66,98,68,100,70,102}..., dimensions={0} | all-to-all | bytes 147456 | tf_op jit(solution)/shard_map/all_to_all | solution.py:533
  134.5 0.2 broadcast_in_dim.19
  134.7 19.7 %all_to_all.62.refs_0_ = bf16[16,288,128]{2,1,0:T(8,128)(2,1)S(1)} all-to-all(bf16[16,288,128]{2,1,0:T(8,128)(2,1)S(1)} %broadcast_in_dim.19), channel_id=1, replica_groups={{0,64,128,192,8,72,136,200,16,80,144,208,24,88,152,216},{1,65,129,193,9..., dimensions={0} | all-to-all | bytes 2359296 | tf_op jit(solution)/shard_map/all_to_all | solution.py:533
  154.4 5.3 %collective-permute-start.14 = (bf16[16,288,128]{2,1,0:T(8,128)(2,1)S(1)}, bf16[16,288,128]{2,1,0:T(8,128)(2,1)S(1)}, u32[]{:S(2)}, u32[]{:S(2)}) collective-permute-start(bf16[16,288,128]{2,1,0:T(8,128)(2,1)S(1)} %all_to_all.62.refs_0_), channel_id=1, source_target_pairs={{0,1},{1,0},{32,33},{33,32},{2,3},{3,2},{34,35},{35,34},{4,5},{5,4... | collective-permute-start | bytes 3538952 | tf_op jit(solution)/shard_map/ppermute | solution.py:50
  159.7 2.4 %last_gradient.1 = f32[3,8,8,256]{3,2,1,0:T(8,128)} custom-call(f32[3,8,8,256]{3,2,1,0:T(8,128)} %get-tuple-element.60.refs_0_, f32[192,256]{1,0:T(8,128)} %get-tuple-element.61.refs_1_, bf16[1024,256]{1,0:T(8,128)(2,1)S(1)} %bitcast.17, bf16[128,256]{1,0:T(8,128)(2,1)} %get-tuple-element.67.refs_9_.refs_3_, ...), custom_call_target="tpu_custom_call" | custom-call | flops 1000 | bytes 3000000 | tf_op jit(solution)/shard_map/last_gradient/pallas_call | solution.py:402
  162.0 0.1 collective-permute-done.14.refs_1_
  162.2 3.0 %spread_slopes.1 = (f32[9,256,256]{2,1,0:T(8,128)}, f32[9,256,256]{2,1,0:T(8,128)}) custom-call(bf16[16,288,128]{2,1,0:T(8,128)(2,1)S(1)} %all_to_all.62.refs_0_, bf16[16,288,128]{2,1,0:T(8,128)(2,1)S(1)} %collective-permute-done.14.refs_1_), custom_call_target="tpu_custom_call" | custom-call | flops 1000 | bytes 3000000 | tf_op jit(solution)/shard_map/spread_slopes/pallas_call | solution.py:402
  (9 shorter events, 0.1 us)
Async XLA Ops:
  26.9 17.3 %all-to-all-start.1 = ((bf16[32,32,256]{2,1,0:T(8,128)(2,1)}), bf16[32,32,256]{2,1,0:T(8,128)(2,1)S(1)}, u32[]{:S(2)}, u32[]{:S(2)}) async-start(bf16[32,32,256]{2,1,0:T(8,128)(2,1)} %bitcast.26), calls=%async_computation.1 | async-start | bytes 1048576 | tf_op jit(solution)/shard_map/all_to_all | solution.py:568
  32.7 10.3 %collective-permute-start = (bf16[304,128]{1,0:T(8,128)(2,1)}, bf16[304,128]{1,0:T(8,128)(2,1)S(1)}, u32[]{:S(2)}, u32[]{:S(2)}) collective-permute-start(bf16[304,128]{1,0:T(8,128)(2,1)} %get-tuple-element.49), channel_id=1, source_target_pairs={{0,8},{1,9},{32,40},{33,41},{2,10},{3,11},{34,42},{35,43},{4,12},{... | collective-permute-start | bytes 233480 | tf_op jit(solution)/shard_map/ppermute | solution.py:50
  34.0 10.2 %collective-permute-start.1 = (bf16[304,128]{1,0:T(8,128)(2,1)}, bf16[304,128]{1,0:T(8,128)(2,1)S(1)}, u32[]{:S(2)}, u32[]{:S(2)}) collective-permute-start(bf16[304,128]{1,0:T(8,128)(2,1)} %get-tuple-element.50), channel_id=1, source_target_pairs={{0,16},{1,17},{32,48},{33,49},{2,18},{3,19},{34,50},{35,51},{4,20}... | collective-permute-start | bytes 233480 | tf_op jit(solution)/shard_map/ppermute | solution.py:50
  36.4 7.8 %collective-permute-start.2 = (bf16[304,128]{1,0:T(8,128)(2,1)}, bf16[304,128]{1,0:T(8,128)(2,1)S(1)}, u32[]{:S(2)}, u32[]{:S(2)}) collective-permute-start(bf16[304,128]{1,0:T(8,128)(2,1)} %get-tuple-element.51), channel_id=1, source_target_pairs={{0,24},{1,25},{32,56},{33,57},{2,26},{3,27},{34,58},{35,59},{4,28}... | collective-permute-start | bytes 233480 | tf_op jit(solution)/shard_map/ppermute | solution.py:50
  48.7 19.3 %all-to-all-start.2 = ((bf16[32,32,256]{2,1,0:T(8,128)(2,1)}), bf16[32,32,256]{2,1,0:T(8,128)(2,1)S(1)}, u32[]{:S(2)}, u32[]{:S(2)}) async-start(bf16[32,32,256]{2,1,0:T(8,128)(2,1)} %bitcast.25), calls=%async_computation.2 | async-start | bytes 1048576 | tf_op jit(solution)/shard_map/all_to_all | solution.py:568
  55.1 11.9 %collective-permute-start.3 = (bf16[496,128]{1,0:T(8,128)(2,1)}, bf16[496,128]{1,0:T(8,128)(2,1)S(1)}, u32[]{:S(2)}, u32[]{:S(2)}) collective-permute-start(bf16[496,128]{1,0:T(8,128)(2,1)} %get-tuple-element.57), channel_id=1, source_target_pairs={{0,8},{1,9},{32,40},{33,41},{2,10},{3,11},{34,42},{35,43},{4,12},{... | collective-permute-start | bytes 380936 | tf_op jit(solution)/shard_map/ppermute | solution.py:50
  56.4 11.5 %collective-permute-start.4 = (bf16[496,128]{1,0:T(8,128)(2,1)}, bf16[496,128]{1,0:T(8,128)(2,1)S(1)}, u32[]{:S(2)}, u32[]{:S(2)}) collective-permute-start(bf16[496,128]{1,0:T(8,128)(2,1)} %get-tuple-element.58), channel_id=1, source_target_pairs={{0,16},{1,17},{32,48},{33,49},{2,18},{3,19},{34,50},{35,51},{4,20}... | collective-permute-start | bytes 380936 | tf_op jit(solution)/shard_map/ppermute | solution.py:50
  58.8 9.1 %collective-permute-start.5 = (bf16[496,128]{1,0:T(8,128)(2,1)}, bf16[496,128]{1,0:T(8,128)(2,1)S(1)}, u32[]{:S(2)}, u32[]{:S(2)}) collective-permute-start(bf16[496,128]{1,0:T(8,128)(2,1)} %get-tuple-element.59), channel_id=1, source_target_pairs={{0,24},{1,25},{32,56},{33,57},{2,26},{3,27},{34,58},{35,59},{4,28}... | collective-permute-start | bytes 380936 | tf_op jit(solution)/shard_map/ppermute | solution.py:50
  71.4 7.1 %collective-permute-start.6 = (bf16[192,128]{1,0:T(8,128)(2,1)}, bf16[192,128]{1,0:T(8,128)(2,1)S(1)}, u32[]{:S(2)}, u32[]{:S(2)}) collective-permute-start(bf16[192,128]{1,0:T(8,128)(2,1)} %get-tuple-element.64), channel_id=1, source_target_pairs={{0,8},{1,9},{32,40},{33,41},{2,10},{3,11},{34,42},{35,43},{4,12},{... | collective-permute-start | bytes 147464 | tf_op jit(solution)/shard_map/ppermute | solution.py:50
  73.2 5.3 %collective-permute-start.7 = (bf16[192,128]{1,0:T(8,128)(2,1)}, bf16[192,128]{1,0:T(8,128)(2,1)S(1)}, u32[]{:S(2)}, u32[]{:S(2)}) collective-permute-start(bf16[192,128]{1,0:T(8,128)(2,1)} %get-tuple-element.65), channel_id=1, source_target_pairs={{0,16},{1,17},{32,48},{33,49},{2,18},{3,19},{34,50},{35,51},{4,20}... | collective-permute-start | bytes 147464 | tf_op jit(solution)/shard_map/ppermute | solution.py:50
  75.2 3.4 %collective-permute-start.8 = (bf16[192,128]{1,0:T(8,128)(2,1)}, bf16[192,128]{1,0:T(8,128)(2,1)S(1)}, u32[]{:S(2)}, u32[]{:S(2)}) collective-permute-start(bf16[192,128]{1,0:T(8,128)(2,1)} %get-tuple-element.66), channel_id=1, source_target_pairs={{0,24},{1,25},{32,56},{33,57},{2,26},{3,27},{34,58},{35,59},{4,28}... | collective-permute-start | bytes 147464 | tf_op jit(solution)/shard_map/ppermute | solution.py:50
  78.4 10.5 %copy-start = (f32[4,144,128]{2,1,0:T(8,128)S(1)}, f32[4,144,128]{2,1,0:T(8,128)}, u32[]{:S(2)}) copy-start(f32[4,144,128]{2,1,0:T(8,128)} %get-tuple-element.73) | copy-start | bytes 884740
  82.3 25.3 %all-to-all-start.3 = ((bf16[32,32,256]{2,1,0:T(8,128)(2,1)}), bf16[32,32,256]{2,1,0:T(8,128)(2,1)S(1)}, u32[]{:S(2)}, u32[]{:S(2)}) async-start(bf16[32,32,256]{2,1,0:T(8,128)(2,1)} %bitcast.24), calls=%async_computation.3 | async-start | bytes 1048576 | tf_op jit(solution)/shard_map/all_to_all | solution.py:568
  88.9 4.7 %collective-permute-start.10 = (f32[4,144,128]{2,1,0:T(8,128)S(1)}, f32[4,144,128]{2,1,0:T(8,128)S(1)}, u32[]{:S(2)}, u32[]{:S(2)}) collective-permute-start(f32[4,144,128]{2,1,0:T(8,128)S(1)} %copy-done), channel_id=1, source_target_pairs={{0,1},{1,0},{32,33},{33,32},{2,3},{3,2},{34,35},{35,34},{4,5},{5,4... | collective-permute-start | bytes 884744 | tf_op jit(solution)/shard_map/ppermute | solution.py:50
  92.4 1.8 %collective-permute-start.9 = (f32[4,144,128]{2,1,0:T(8,128)}, f32[4,144,128]{2,1,0:T(8,128)S(1)}, u32[]{:S(2)}, u32[]{:S(2)}) collective-permute-start(f32[4,144,128]{2,1,0:T(8,128)} %get-tuple-element.72), channel_id=1, source_target_pairs={{0,1},{1,0},{32,33},{33,32},{2,3},{3,2},{34,35},{35,34},{4,5},{5,4... | collective-permute-start | bytes 884744 | tf_op jit(solution)/shard_map/ppermute | solution.py:50
  96.2 7.8 %collective-permute-start.11 = (f32[288,128]{1,0:T(8,128)}, f32[288,128]{1,0:T(8,128)S(1)}, u32[]{:S(2)}, u32[]{:S(2)}) collective-permute-start(f32[288,128]{1,0:T(8,128)} %get-tuple-element.75), channel_id=1, source_target_pairs={{0,64},{1,65},{32,96},{33,97},{2,66},{3,67},{34,98},{35,99},{4,68}... | collective-permute-start | bytes 442376 | tf_op jit(solution)/shard_map/ppermute | solution.py:50
  97.8 9.8 %collective-permute-start.12 = (f32[288,128]{1,0:T(8,128)}, f32[288,128]{1,0:T(8,128)S(1)}, u32[]{:S(2)}, u32[]{:S(2)}) collective-permute-start(f32[288,128]{1,0:T(8,128)} %get-tuple-element.76), channel_id=1, source_target_pairs={{0,128},{1,129},{32,160},{33,161},{2,130},{3,131},{34,162},{35,163... | collective-permute-start | bytes 442376 | tf_op jit(solution)/shard_map/ppermute | solution.py:50
  100.3 7.3 %collective-permute-start.13 = (f32[288,128]{1,0:T(8,128)}, f32[288,128]{1,0:T(8,128)S(1)}, u32[]{:S(2)}, u32[]{:S(2)}) collective-permute-start(f32[288,128]{1,0:T(8,128)} %get-tuple-element.77), channel_id=1, source_target_pairs={{0,192},{1,193},{32,224},{33,225},{2,194},{3,195},{34,226},{35,227... | collective-permute-start | bytes 442376 | tf_op jit(solution)/shard_map/ppermute | solution.py:50
  154.4 7.8 %collective-permute-start.14 = (bf16[16,288,128]{2,1,0:T(8,128)(2,1)S(1)}, bf16[16,288,128]{2,1,0:T(8,128)(2,1)S(1)}, u32[]{:S(2)}, u32[]{:S(2)}) collective-permute-start(bf16[16,288,128]{2,1,0:T(8,128)(2,1)S(1)} %all_to_all.62.refs_0_), channel_id=1, source_target_pairs={{0,1},{1,0},{32,33},{33,32},{2,3},{3,2},{34,35},{35,34},{4,5},{5,4... | collective-permute-start | bytes 3538952 | tf_op jit(solution)/shard_map/ppermute | solution.py:50

commit v5 on v4

--- a/solution.py
+++ b/solution.py
@@ -320,6 +320,7 @@
 moved_in = pl.BlockSpec(memory_space=pltpu.HBM)
 landed = pl.BlockSpec(memory_space=pl.ANY)
 left = pl.BlockSpec()
+near = pl.BlockSpec(memory_space=pltpu.VMEM)
 resting = pl.BlockSpec(memory_space=pltpu.HBM)
 grid_shape = pltpu.VMEM((3, 10, 10, 256), f32)
 frame_shape = pltpu.VMEM((128, 256), f32)
@@ -363,21 +364,22 @@
             self.send()
 
 
-def run(kernel, name, args, specs, outs, scratch, flops):
+def run(kernel, name, args, specs, outs, scratch, flops, kept=()):
     single = not isinstance(outs, tuple)
     outs = (outs,) if single else outs
-    moved = [i for i, spec in enumerate(specs) if spec is not left and spec is not resting]
+    moved = [i for i, spec in enumerate(specs) if spec is moved_in or spec is landed]
     buffers = [
         (pltpu.SMEM if args[i].dtype == jnp.int32 else pltpu.VMEM)(args[i].shape, args[i].dtype)
         for i in moved
     ]
-    stores = [pltpu.VMEM(out.shape, out.dtype) for out in outs]
+    away = [n for n in range(len(outs)) if n not in kept]
+    stores = [pltpu.VMEM(outs[n].shape, outs[n].dtype) for n in away]
 
     def body(*refs):
         ins, refs = refs[: len(args)], refs[len(args) :]
         targets, refs = refs[: len(outs)], refs[len(outs) :]
         held, refs = refs[: len(moved)], refs[len(moved) :]
-        made, refs = refs[: len(outs)], refs[len(outs) :]
+        made, refs = refs[: len(away)], refs[len(away) :]
         arrived, left_for, refs = refs[0], refs[1], refs[2:]
         copies = [
             pltpu.make_async_copy(ins[i], held[n], arrived.at[n]) for n, i in enumerate(moved)
@@ -387,28 +389,30 @@
         given = list(ins)
         for n, i in enumerate(moved):
             given[i] = Arriving(held[n], copies[n])
-        results = [
-            Leaving(made[n], pltpu.make_async_copy(made[n], targets[n], left_for.at[n]))
-            for n in range(len(outs))
-        ]
+        results = list(targets)
+        for m, n in enumerate(away):
+            copy = pltpu.make_async_copy(made[m], targets[n], left_for.at[m])
+            results[n] = Leaving(made[m], copy)
         kernel(placing(), *given, *results, *refs)
         for n in range(len(moved)):
             given[moved[n]].settle()
-        for result in results:
-            result.send()
-        for result in results:
-            result.copy.wait()
+        for n in away:
+            results[n].send()
+        for n in away:
+            results[n].copy.wait()
 
     made = pl.pallas_call(
         body,
-        out_shape=tuple(pltpu.HBM(out.shape, out.dtype) for out in outs),
+        out_shape=tuple(
+            pltpu.HBM(out.shape, out.dtype) if n in away else out for n, out in enumerate(outs)
+        ),
         in_specs=[landed if spec is left else spec for spec in specs],
-        out_specs=tuple(moved_in for _ in outs),
+        out_specs=tuple(moved_in if n in away else near for n in range(len(outs))),
         scratch_shapes=[
             *buffers,
             *stores,
             pltpu.SemaphoreType.DMA((max(1, len(moved)),)),
-            pltpu.SemaphoreType.DMA((len(outs),)),
+            pltpu.SemaphoreType.DMA((max(1, len(away)),)),
             *scratch,
         ],
         compiler_params=pltpu.CompilerParams(vmem_limit_bytes=40 * 2**20),
@@ -472,7 +476,10 @@
         kernel,
         "slope_terms",
         (*parts, *packing, *held),
-        ([moved_in] + [landed] * 3) * (count // 4) + [moved_in] * len(packing) + [resting] * len(held),
+        ([moved_in] + [landed] * 3) * (count // 4 - 1)
+        + [near] * 4
+        + [near] * len(packing)
+        + [near] * len(held),
         outs,
         [
             pltpu.VMEM((1216, 128), f32),
@@ -480,6 +487,7 @@
             pltpu.VMEM((2, 576, 128), f32),
         ],
         2 * 9 * 768 * 128 * 128,
+        tuple(range(len(outs))),
     )
 
 
@@ -544,10 +552,11 @@
         plane_kernel,
         "row_sum",
         (*ring(chunks, "y"), held),
-        [moved_in] + [landed] * 3 + [left],
+        [near] * 4 + [left],
         like(8, 36, 128, dtype=f32),
         [pltpu.VMEM((288, 128), f32)],
         1000,
+        (0,),
     )
     mine = (jnp.sum(trade(terms, "z"), axis=0) * scale).astype(bf16)
     line = trade(copies_of(mine, 8), "z").reshape(288, 128)
@@ -585,16 +594,18 @@
         (like(send_rows, 128), like(128, send_rows + 128), frame_like, sent_like),
         [grid_shape, frame_shape],
         2 * send_rows * 128 * 256,
+        (0,1,2,3),
     )
     recv = exchange(sent)
     hidden, pre_first, frame, sent, *parts = run(
         first_kernel,
         "first_layer",
         (tile_links, field, recv, frame, pack, unpack, first_weights),
-        [moved_in] * 2 + [landed] + [moved_in] * 4,
+        [moved_in] * 2 + [near] * 4 + [moved_in],
         (rows_like, like(192, 256, dtype=f32), frame_like, sent_like) + (like(304, 128),) * 4,
         [grid_shape, frame_shape, frame_shape, flat_shape],
         conv_flops,
+        (0,2,3,5,6,7),
     )
     recv = exchange(sent)
     field_parts = ring(parts, "x")
@@ -605,11 +616,12 @@
             tile_links, field, goal, hidden, recv, frame, pack, unpack, second_weights,
             *field_parts[1:],
         ),
-        [moved_in] * 4 + [landed] + [moved_in] * 4 + [left] * 3,
+        [moved_in] * 3 + [near] * 5 + [moved_in] + [left] * 3,
         (rows_like, like(192, 256, dtype=f32), inner_like, frame_like, sent_like)
         + (like(496, 128),) * 4,
         [grid_shape, frame_shape, frame_shape, flat_shape, column_shape],
         2 * conv_flops,
+        (2,3,4,5,6,7,8),
     )
     recv = exchange(sent)
     closing_parts = ring(parts, "x")
@@ -618,10 +630,11 @@
         third_kernel,
         "first_gradient",
         (tile_links, inner, pre_first, recv, frame, unpack, first_weights, *closing_parts[1:]),
-        [moved_in] * 3 + [landed] + [moved_in] * 3 + [left] * 3,
+        [moved_in, near, moved_in] + [near] * 3 + [moved_in] + [left] * 3,
         (inner_like, frame_like) + (like(192, 128),) * 4,
         [grid_shape, frame_shape, frame_shape, column_shape],
         conv_flops,
+        (1,2,3,4,5),
     )
     got_closing = shifted(closing[1], "core", 1)
     *opening, sent = slope_terms(
@@ -632,16 +645,17 @@
         pair_kernel,
         "pair_sum",
         (opening[0], shifted(opening[1], "core", 1), closing[0], got_closing),
-        [moved_in, landed, moved_in, landed],
+        [near] * 4,
         (like(288, 128, dtype=f32),) * 4,
         [],
         1000,
+        (0, 1, 2, 3),
     )
     condition_derivative = run(
         last_kernel,
         "last_gradient",
         (last, misfit, recv, frame, unpack),
-        [moved_in] * 2 + [landed] + [moved_in] * 2,
+        [moved_in] * 2 + [near] * 3,
         inner_like,
         [grid_shape, frame_shape],
         1000,

time: 166 us -> 158 us (0.952)
  Pallas kernels: 30.1 us -> 21.5 us
  waiting for transfers between devices: 22.8 us -> 26 us
  blocking collectives: 64 us -> 62 us
    pallas_call x10, Pallas kernels: 30.1 us -> 21.5 us  [run(): pl.pallas_call(body, out_shape=tuple((pltpu.HBM(out.shape, out.dtype) if...]
    ppermute x15, waiting for transfers between devices: 22.8 us -> 26 us  [shifted(): return lax.ppermute(values, ('tile', 'ens'), pairs)]
    all_to_all x3, blocking collectives: 44.8 us -> 43.1 us  [trade(): lax.all_to_all(values, ('tile', 'ens'), 0, 0, axis_index_groups=groups(al...]
  transfers between devices with their start and end apart: 18 -> 18, of which waited for: 10 -> 11; matrix products, arithmetic and copies ran while one was open for 0% -> 0% of each run, Pallas kernels for 4% -> 2%
where the time goes in v5:
time: 158 us
  blocking collectives  62 us (39%)
  starting transfers between devices  47.1 us (30%)
  waiting for transfers between devices  26 us (16%)
  Pallas kernels  21.5 us (14%)
    all_to_all x3, blocking collectives, trade(): lax.all_to_all(values, ('tile', 'ens'), 0, 0, axis_index_groups=groups(al...  43.1 us
    ppermute x15, starting transfers between devices, shifted(): return lax.ppermute(values, ('tile', 'ens'), pairs)  28.3 us
    ppermute x15, waiting for transfers between devices, shifted(): return lax.ppermute(values, ('tile', 'ens'), pairs)  26 us
    pallas_call x10, Pallas kernels, run(): pl.pallas_call(body, out_shape=tuple((pltpu.HBM(out.shape, out.dtype) if...  21.5 us
    all_to_all x1, blocking collectives, exchange(): return lax.all_to_all(values, 'tile', 0, 0, tiled=True)  18.9 us
    all_to_all x3, starting transfers between devices, exchange(): return lax.all_to_all(values, 'tile', 0, 0, tiled=True)  18.8 us
  transfers between devices with their start and end apart: 18, of which 11 were waited for; matrix products, arithmetic and copies ran while one was open for 0% of the time, Pallas kernels for 2%

profile of v5, /device:TPU:1, one launch (start us, length us, event | category | flops | bytes accessed | tf_op | source)
XLA Modules:
  0.0 157.8 jit_solution(771948607104225867)
XLA Ops:
  0.6 2.5 %routes.1 = (bf16[1024,128]{1,0:T(8,128)(2,1)S(1)}, bf16[128,1152]{1,0:T(8,128)(2,1)S(1)}, bf16[128,256]{1,0:T(8,128)(2,1)S(1)}, bf16[1024,256]{1,0:T(8,128)(2,1)S(1)}) custom-call(s32[3,16]{1,0:T(4,128)} %refs_0_.7, bf16[192,256]{1,0:T(8,128)(2,1)} %bitcast.25), custom_call_target="tpu_custom_call" | custom-call | flops 67108864 | bytes 3000000 | tf_op jit(solution)/shard_map/routes/pallas_call | solution.py:404
  3.1 18.9 %all_to_all.59 = bf16[32,32,256]{2,1,0:T(8,128)(2,1)S(1)} all-to-all(bf16[32,32,256]{2,1,0:T(8,128)(2,1)S(1)} %bitcast.21), channel_id=1, replica_groups=mesh['tile'=32,'ens'=8] {'tile'}, dimensions={0} | all-to-all | bytes 1048576 | tf_op jit(solution)/shard_map/all_to_all | solution.py:577
  22.1 3.9 %first_layer.1 = (bf16[192,256]{1,0:T(8,128)(2,1)S(1)}, f32[192,256]{1,0:T(8,128)}, bf16[128,256]{1,0:T(8,128)(2,1)S(1)}, bf16[1024,256]{1,0:T(8,128)(2,1)}, bf1...) custom-call(s32[3,16]{1,0:T(4,128)} %refs_0_.7, ...), custom_call_target="tpu_custom_call" | custom-call | flops 226492416 | bytes 3000000 | tf_op jit(solution)/shard_map/first_layer/pallas_call | solution.py:404
  25.9 5.8 %all-to-all-start.1 = ((bf16[32,32,256]{2,1,0:T(8,128)(2,1)}), bf16[32,32,256]{2,1,0:T(8,128)(2,1)S(1)}, u32[]{:S(2)}, u32[]{:S(2)}) async-start(bf16[32,32,256]{2,1,0:T(8,128)(2,1)} %bitcast.5), calls=%async_computation.1 | async-start | bytes 1048576 | tf_op jit(solution)/shard_map/all_to_all | solution.py:577
  31.7 1.3 collective-permute-start
  33.0 2.4 %collective-permute-start.1 = (bf16[304,128]{1,0:T(8,128)(2,1)S(1)}, bf16[304,128]{1,0:T(8,128)(2,1)S(1)}, u32[]{:S(2)}, u32[]{:S(2)}) collective-permute-start(bf16[304,128]{1,0:T(8,128)(2,1)S(1)} %get-tuple-element.50), channel_id=1, source_target_pairs={{0,16},{1,17},{32,48},{33,49},{2,18},{3,19},{34,50},{35,51},{4,20}... | collective-permute-start | bytes 233480 | tf_op jit(solution)/shard_map/ppermute | solution.py:50
  35.4 1.2 collective-permute-start.2
  36.6 5.4 %collective-permute-done.refs_9_.refs_1_ = bf16[304,128]{1,0:T(8,128)(2,1)S(1)} collective-permute-done((bf16[304,128]{1,0:T(8,128)(2,1)S(1)}, bf16[304,128]{1,0:T(8,128)(2,1)S(1)}, u32[]{:S(2)}, u32[]{:S(2)}) %collective-permute-start) | collective-permute-done | bytes 77856 | tf_op jit(solution)/shard_map/ppermute | solution.py:50
  42.0 1.2 collective-permute-done.1.refs_10_.refs_2_
  43.2 0.0 collective-permute-done.2.refs_11_.refs_3_
  43.2 0.0 all-to-all-done.1
  43.2 4.6 %second_layer.1 = (bf16[192,256]{1,0:T(8,128)(2,1)}, f32[192,256]{1,0:T(8,128)}, f32[3,8,8,256]{3,2,1,0:T(8,128)S(1)}, bf16[128,256]{1,0:T(8,128)(2,1)S(1)}, bf1...) custom-call(s32[3,16]{1,0:T(4,128)} %refs_0_.7, ...), custom_call_target="tpu_custom_call" | custom-call | flops 452984832 | bytes 3000000 | tf_op jit(solution)/shard_map/second_layer/pallas_call | solution.py:404
  47.8 6.4 %all-to-all-start.2 = ((bf16[32,32,256]{2,1,0:T(8,128)(2,1)}), bf16[32,32,256]{2,1,0:T(8,128)(2,1)S(1)}, u32[]{:S(2)}, u32[]{:S(2)}) async-start(bf16[32,32,256]{2,1,0:T(8,128)(2,1)} %bitcast.9), calls=%async_computation.2 | async-start | bytes 1048576 | tf_op jit(solution)/shard_map/all_to_all | solution.py:577
  54.2 1.3 collective-permute-start.3
  55.5 2.4 %collective-permute-start.4 = (bf16[496,128]{1,0:T(8,128)(2,1)S(1)}, bf16[496,128]{1,0:T(8,128)(2,1)S(1)}, u32[]{:S(2)}, u32[]{:S(2)}) collective-permute-start(bf16[496,128]{1,0:T(8,128)(2,1)S(1)} %get-tuple-element.58), channel_id=1, source_target_pairs={{0,16},{1,17},{32,48},{33,49},{2,18},{3,19},{34,50},{35,51},{4,20}... | collective-permute-start | bytes 380936 | tf_op jit(solution)/shard_map/ppermute | solution.py:50
  57.9 1.2 collective-permute-start.5
  59.1 7.0 %collective-permute-done.3.refs_7_.refs_1_ = bf16[496,128]{1,0:T(8,128)(2,1)S(1)} collective-permute-done((bf16[496,128]{1,0:T(8,128)(2,1)S(1)}, bf16[496,128]{1,0:T(8,128)(2,1)S(1)}, u32[]{:S(2)}, u32[]{:S(2)}) %collective-permute-start.3) | collective-permute-done | bytes 127008 | tf_op jit(solution)/shard_map/ppermute | solution.py:50
  66.1 1.0 collective-permute-done.4.refs_8_.refs_2_
  67.0 0.0 collective-permute-done.5.refs_9_.refs_3_
  67.0 3.0 %first_gradient.1 = (f32[3,8,8,256]{3,2,1,0:T(8,128)}, bf16[128,256]{1,0:T(8,128)(2,1)S(1)}, bf16[192,128]{1,0:T(8,128)(2,1)S(1)}, bf16[192,128]{1,0:T(8,128)(2,...) custom-call(s32[3,16]{1,0:T(4,128)} %refs_0_.7, f32[3,8,8,256]{3,2,1,0:T(8,128)S(1)} %get-tuple-element.53.refs_1_, ...), custom_call_target="tpu_custom_call" | custom-call | flops 226492416 | bytes 3000000 | tf_op jit(solution)/shard_map/first_gradient/pallas_call | solution.py:404
  70.1 1.7 %collective-permute-start.6 = (bf16[192,128]{1,0:T(8,128)(2,1)S(1)}, bf16[192,128]{1,0:T(8,128)(2,1)S(1)}, u32[]{:S(2)}, u32[]{:S(2)}) collective-permute-start(bf16[192,128]{1,0:T(8,128)(2,1)S(1)} %get-tuple-element.64), channel_id=1, source_target_pairs={{0,8},{1,9},{32,40},{33,41},{2,10},{3,11},{34,42},{35,43},{4,12},{... | collective-permute-start | bytes 147464 | tf_op jit(solution)/shard_map/ppermute | solution.py:50
  71.8 2.2 %collective-permute-start.7 = (bf16[192,128]{1,0:T(8,128)(2,1)S(1)}, bf16[192,128]{1,0:T(8,128)(2,1)S(1)}, u32[]{:S(2)}, u32[]{:S(2)}) collective-permute-start(bf16[192,128]{1,0:T(8,128)(2,1)S(1)} %get-tuple-element.65), channel_id=1, source_target_pairs={{0,16},{1,17},{32,48},{33,49},{2,18},{3,19},{34,50},{35,51},{4,20}... | collective-permute-start | bytes 147464 | tf_op jit(solution)/shard_map/ppermute | solution.py:50
  74.0 0.5 collective-permute-start.8
  74.5 0.7 slope_terms.2
  75.2 1.3 collective-permute-done.7.refs_6_
  76.5 0.7 collective-permute-done.8.refs_7_
  77.2 1.8 %slope_terms.3 = (f32[4,144,128]{2,1,0:T(8,128)S(1)}, f32[4,144,128]{2,1,0:T(8,128)S(1)}, bf16[1024,256]{1,0:T(8,128)(2,1)}) custom-call(bf16[304,128]{1,0:T(8,128)(2,1)} %get-tuple-element.62.refs_0_, bf16[304,128]{1,0:T(8,128)(2,1)S(1)} %collective-permute-done.refs_9_.refs_1_, bf16[304,128]{1,0:T(8,128)(2,1)S(1)} %collective-permute-done.1.refs_10_.refs_2_, ...), custom_call_target="tpu_custom_call" | custom-call | flops 226492416 | bytes 3000000 | tf_op jit(solution)/shard_map/slope_terms/pallas_call | solution.py:404
  79.0 6.6 %all-to-all-start.3 = ((bf16[32,32,256]{2,1,0:T(8,128)(2,1)}), bf16[32,32,256]{2,1,0:T(8,128)(2,1)S(1)}, u32[]{:S(2)}, u32[]{:S(2)}) async-start(bf16[32,32,256]{2,1,0:T(8,128)(2,1)} %bitcast.11), calls=%async_computation.3 | async-start | bytes 1048576 | tf_op jit(solution)/shard_map/all_to_all | solution.py:577
  85.6 3.5 %collective-permute-start.10 = (f32[4,144,128]{2,1,0:T(8,128)S(1)}, f32[4,144,128]{2,1,0:T(8,128)S(1)}, u32[]{:S(2)}, u32[]{:S(2)}) collective-permute-start(f32[4,144,128]{2,1,0:T(8,128)S(1)} %get-tuple-element.73), channel_id=1, source_target_pairs={{0,1},{1,0},{32,33},{33,32},{2,3},{3,2},{34,35},{35,34},{4,5},{5,4... | collective-permute-start | bytes 884744 | tf_op jit(solution)/shard_map/ppermute | solution.py:50
  89.1 0.1 collective-permute-start.9
  89.2 1.1 collective-permute-done.10.refs_3_
  90.3 0.4 collective-permute-done.9.refs_1_
  90.7 0.1 pair_sum.1
  90.8 1.6 %collective-permute-start.11 = (f32[288,128]{1,0:T(8,128)S(1)}, f32[288,128]{1,0:T(8,128)S(1)}, u32[]{:S(2)}, u32[]{:S(2)}) collective-permute-start(f32[288,128]{1,0:T(8,128)S(1)} %get-tuple-element.75), channel_id=1, source_target_pairs={{0,64},{1,65},{32,96},{33,97},{2,66},{3,67},{34,98},{35,99},{4,68}... | collective-permute-start | bytes 442376 | tf_op jit(solution)/shard_map/ppermute | solution.py:50
  92.4 2.4 %collective-permute-start.12 = (f32[288,128]{1,0:T(8,128)S(1)}, f32[288,128]{1,0:T(8,128)S(1)}, u32[]{:S(2)}, u32[]{:S(2)}) collective-permute-start(f32[288,128]{1,0:T(8,128)S(1)} %get-tuple-element.76), channel_id=1, source_target_pairs={{0,128},{1,129},{32,160},{33,161},{2,130},{3,131},{34,162},{35,163... | collective-permute-start | bytes 442376 | tf_op jit(solution)/shard_map/ppermute | solution.py:50
  94.8 1.1 collective-permute-start.13
  96.0 4.0 %collective-permute-done.11.refs_1_ = f32[288,128]{1,0:T(8,128)S(1)} collective-permute-done((f32[288,128]{1,0:T(8,128)S(1)}, f32[288,128]{1,0:T(8,128)S(1)}, u32[]{:S(2)}, u32[]{:S(2)}) %collective-permute-start.11) | collective-permute-done | bytes 147488 | tf_op jit(solution)/shard_map/ppermute | solution.py:50
  100.0 3.4 %collective-permute-done.12.refs_2_ = f32[288,128]{1,0:T(8,128)S(1)} collective-permute-done((f32[288,128]{1,0:T(8,128)S(1)}, f32[288,128]{1,0:T(8,128)S(1)}, u32[]{:S(2)}, u32[]{:S(2)}) %collective-permute-start.12) | collective-permute-done | bytes 147488 | tf_op jit(solution)/shard_map/ppermute | solution.py:50
  103.4 0.0 all-to-all-done.3
  103.4 0.1 row_sum.1
  103.5 15.7 %all_to_all.60 = f32[8,36,128]{2,1,0:T(8,128)S(1)} all-to-all(f32[8,36,128]{2,1,0:T(8,128)S(1)} %row_sum.1), channel_id=1, replica_groups={{0,32,2,34,4,36,6,38},{1,33,3,35,5,37,7,39},{64,96,66,98,68,100,70,102}..., dimensions={0} | all-to-all | bytes 294912 | tf_op jit(solution)/shard_map/all_to_all | solution.py:541
  119.3 10.1 %all_to_all.61 = bf16[8,36,128]{2,1,0:T(8,128)(2,1)S(1)} all-to-all(bf16[8,36,128]{2,1,0:T(8,128)(2,1)S(1)} %broadcast_in_dim.17), channel_id=1, replica_groups={{0,32,2,34,4,36,6,38},{1,33,3,35,5,37,7,39},{64,96,66,98,68,100,70,102}..., dimensions={0} | all-to-all | bytes 147456 | tf_op jit(solution)/shard_map/all_to_all | solution.py:541
  129.4 0.2 broadcast_in_dim.19
  129.5 17.3 %all_to_all.62.refs_0_ = bf16[16,288,128]{2,1,0:T(8,128)(2,1)S(1)} all-to-all(bf16[16,288,128]{2,1,0:T(8,128)(2,1)S(1)} %broadcast_in_dim.19), channel_id=1, replica_groups={{0,64,128,192,8,72,136,200,16,80,144,208,24,88,152,216},{1,65,129,193,9..., dimensions={0} | all-to-all | bytes 2359296 | tf_op jit(solution)/shard_map/all_to_all | solution.py:541
  146.8 5.3 %collective-permute-start.14 = (bf16[16,288,128]{2,1,0:T(8,128)(2,1)S(1)}, bf16[16,288,128]{2,1,0:T(8,128)(2,1)S(1)}, u32[]{:S(2)}, u32[]{:S(2)}) collective-permute-start(bf16[16,288,128]{2,1,0:T(8,128)(2,1)S(1)} %all_to_all.62.refs_0_), channel_id=1, source_target_pairs={{0,1},{1,0},{32,33},{33,32},{2,3},{3,2},{34,35},{35,34},{4,5},{5,4... | collective-permute-start | bytes 3538952 | tf_op jit(solution)/shard_map/ppermute | solution.py:50
  152.2 1.9 %last_gradient.1 = f32[3,8,8,256]{3,2,1,0:T(8,128)} custom-call(f32[3,8,8,256]{3,2,1,0:T(8,128)} %get-tuple-element.60.refs_0_, f32[192,256]{1,0:T(8,128)} %get-tuple-element.61.refs_1_, bf16[1024,256]{1,0:T(8,128)(2,1)S(1)} %bitcast.17, bf16[128,256]{1,0:T(8,128)(2,1)S(1)} %get-tuple-element.67.refs_9_.refs_3_, ...), custom_call_target="tpu_custom_call" | custom-call | flops 1000 | bytes 3000000 | tf_op jit(solution)/shard_map/last_gradient/pallas_call | solution.py:404
  154.1 0.5 collective-permute-done.14.refs_1_
  154.6 3.0 %spread_slopes.1 = (f32[9,256,256]{2,1,0:T(8,128)}, f32[9,256,256]{2,1,0:T(8,128)}) custom-call(bf16[16,288,128]{2,1,0:T(8,128)(2,1)S(1)} %all_to_all.62.refs_0_, bf16[16,288,128]{2,1,0:T(8,128)(2,1)S(1)} %collective-permute-done.14.refs_1_), custom_call_target="tpu_custom_call" | custom-call | flops 1000 | bytes 3000000 | tf_op jit(solution)/shard_map/spread_slopes/pallas_call | solution.py:404
  (7 shorter events, 0.1 us)
Async XLA Ops:
  25.9 17.3 %all-to-all-start.1 = ((bf16[32,32,256]{2,1,0:T(8,128)(2,1)}), bf16[32,32,256]{2,1,0:T(8,128)(2,1)S(1)}, u32[]{:S(2)}, u32[]{:S(2)}) async-start(bf16[32,32,256]{2,1,0:T(8,128)(2,1)} %bitcast.5), calls=%async_computation.1 | async-start | bytes 1048576 | tf_op jit(solution)/shard_map/all_to_all | solution.py:577
  31.7 10.3 %collective-permute-start = (bf16[304,128]{1,0:T(8,128)(2,1)S(1)}, bf16[304,128]{1,0:T(8,128)(2,1)S(1)}, u32[]{:S(2)}, u32[]{:S(2)}) collective-permute-start(bf16[304,128]{1,0:T(8,128)(2,1)S(1)} %get-tuple-element.49), channel_id=1, source_target_pairs={{0,8},{1,9},{32,40},{33,41},{2,10},{3,11},{34,42},{35,43},{4,12},{... | collective-permute-start | bytes 233480 | tf_op jit(solution)/shard_map/ppermute | solution.py:50
  33.0 10.2 %collective-permute-start.1 = (bf16[304,128]{1,0:T(8,128)(2,1)S(1)}, bf16[304,128]{1,0:T(8,128)(2,1)S(1)}, u32[]{:S(2)}, u32[]{:S(2)}) collective-permute-start(bf16[304,128]{1,0:T(8,128)(2,1)S(1)} %get-tuple-element.50), channel_id=1, source_target_pairs={{0,16},{1,17},{32,48},{33,49},{2,18},{3,19},{34,50},{35,51},{4,20}... | collective-permute-start | bytes 233480 | tf_op jit(solution)/shard_map/ppermute | solution.py:50
  35.4 7.8 %collective-permute-start.2 = (bf16[304,128]{1,0:T(8,128)(2,1)S(1)}, bf16[304,128]{1,0:T(8,128)(2,1)S(1)}, u32[]{:S(2)}, u32[]{:S(2)}) collective-permute-start(bf16[304,128]{1,0:T(8,128)(2,1)S(1)} %get-tuple-element.51), channel_id=1, source_target_pairs={{0,24},{1,25},{32,56},{33,57},{2,26},{3,27},{34,58},{35,59},{4,28}... | collective-permute-start | bytes 233480 | tf_op jit(solution)/shard_map/ppermute | solution.py:50
  47.8 19.3 %all-to-all-start.2 = ((bf16[32,32,256]{2,1,0:T(8,128)(2,1)}), bf16[32,32,256]{2,1,0:T(8,128)(2,1)S(1)}, u32[]{:S(2)}, u32[]{:S(2)}) async-start(bf16[32,32,256]{2,1,0:T(8,128)(2,1)} %bitcast.9), calls=%async_computation.2 | async-start | bytes 1048576 | tf_op jit(solution)/shard_map/all_to_all | solution.py:577
  54.2 11.9 %collective-permute-start.3 = (bf16[496,128]{1,0:T(8,128)(2,1)S(1)}, bf16[496,128]{1,0:T(8,128)(2,1)S(1)}, u32[]{:S(2)}, u32[]{:S(2)}) collective-permute-start(bf16[496,128]{1,0:T(8,128)(2,1)S(1)} %get-tuple-element.57), channel_id=1, source_target_pairs={{0,8},{1,9},{32,40},{33,41},{2,10},{3,11},{34,42},{35,43},{4,12},{... | collective-permute-start | bytes 380936 | tf_op jit(solution)/shard_map/ppermute | solution.py:50
  55.5 11.5 %collective-permute-start.4 = (bf16[496,128]{1,0:T(8,128)(2,1)S(1)}, bf16[496,128]{1,0:T(8,128)(2,1)S(1)}, u32[]{:S(2)}, u32[]{:S(2)}) collective-permute-start(bf16[496,128]{1,0:T(8,128)(2,1)S(1)} %get-tuple-element.58), channel_id=1, source_target_pairs={{0,16},{1,17},{32,48},{33,49},{2,18},{3,19},{34,50},{35,51},{4,20}... | collective-permute-start | bytes 380936 | tf_op jit(solution)/shard_map/ppermute | solution.py:50
  57.9 9.1 %collective-permute-start.5 = (bf16[496,128]{1,0:T(8,128)(2,1)S(1)}, bf16[496,128]{1,0:T(8,128)(2,1)S(1)}, u32[]{:S(2)}, u32[]{:S(2)}) collective-permute-start(bf16[496,128]{1,0:T(8,128)(2,1)S(1)} %get-tuple-element.59), channel_id=1, source_target_pairs={{0,24},{1,25},{32,56},{33,57},{2,26},{3,27},{34,58},{35,59},{4,28}... | collective-permute-start | bytes 380936 | tf_op jit(solution)/shard_map/ppermute | solution.py:50
  70.1 5.1 %collective-permute-start.6 = (bf16[192,128]{1,0:T(8,128)(2,1)S(1)}, bf16[192,128]{1,0:T(8,128)(2,1)S(1)}, u32[]{:S(2)}, u32[]{:S(2)}) collective-permute-start(bf16[192,128]{1,0:T(8,128)(2,1)S(1)} %get-tuple-element.64), channel_id=1, source_target_pairs={{0,8},{1,9},{32,40},{33,41},{2,10},{3,11},{34,42},{35,43},{4,12},{... | collective-permute-start | bytes 147464 | tf_op jit(solution)/shard_map/ppermute | solution.py:50
  71.8 4.7 %collective-permute-start.7 = (bf16[192,128]{1,0:T(8,128)(2,1)S(1)}, bf16[192,128]{1,0:T(8,128)(2,1)S(1)}, u32[]{:S(2)}, u32[]{:S(2)}) collective-permute-start(bf16[192,128]{1,0:T(8,128)(2,1)S(1)} %get-tuple-element.65), channel_id=1, source_target_pairs={{0,16},{1,17},{32,48},{33,49},{2,18},{3,19},{34,50},{35,51},{4,20}... | collective-permute-start | bytes 147464 | tf_op jit(solution)/shard_map/ppermute | solution.py:50
  74.0 3.2 %collective-permute-start.8 = (bf16[192,128]{1,0:T(8,128)(2,1)S(1)}, bf16[192,128]{1,0:T(8,128)(2,1)S(1)}, u32[]{:S(2)}, u32[]{:S(2)}) collective-permute-start(bf16[192,128]{1,0:T(8,128)(2,1)S(1)} %get-tuple-element.66), channel_id=1, source_target_pairs={{0,24},{1,25},{32,56},{33,57},{2,26},{3,27},{34,58},{35,59},{4,28}... | collective-permute-start | bytes 147464 | tf_op jit(solution)/shard_map/ppermute | solution.py:50
  79.0 24.4 %all-to-all-start.3 = ((bf16[32,32,256]{2,1,0:T(8,128)(2,1)}), bf16[32,32,256]{2,1,0:T(8,128)(2,1)S(1)}, u32[]{:S(2)}, u32[]{:S(2)}) async-start(bf16[32,32,256]{2,1,0:T(8,128)(2,1)} %bitcast.11), calls=%async_computation.3 | async-start | bytes 1048576 | tf_op jit(solution)/shard_map/all_to_all | solution.py:577
  85.6 4.7 %collective-permute-start.10 = (f32[4,144,128]{2,1,0:T(8,128)S(1)}, f32[4,144,128]{2,1,0:T(8,128)S(1)}, u32[]{:S(2)}, u32[]{:S(2)}) collective-permute-start(f32[4,144,128]{2,1,0:T(8,128)S(1)} %get-tuple-element.73), channel_id=1, source_target_pairs={{0,1},{1,0},{32,33},{33,32},{2,3},{3,2},{34,35},{35,34},{4,5},{5,4... | collective-permute-start | bytes 884744 | tf_op jit(solution)/shard_map/ppermute | solution.py:50
  89.1 1.6 %collective-permute-start.9 = (f32[4,144,128]{2,1,0:T(8,128)S(1)}, f32[4,144,128]{2,1,0:T(8,128)S(1)}, u32[]{:S(2)}, u32[]{:S(2)}) collective-permute-start(f32[4,144,128]{2,1,0:T(8,128)S(1)} %get-tuple-element.72), channel_id=1, source_target_pairs={{0,1},{1,0},{32,33},{33,32},{2,3},{3,2},{34,35},{35,34},{4,5},{5,4... | collective-permute-start | bytes 884744 | tf_op jit(solution)/shard_map/ppermute | solution.py:50
  90.8 9.2 %collective-permute-start.11 = (f32[288,128]{1,0:T(8,128)S(1)}, f32[288,128]{1,0:T(8,128)S(1)}, u32[]{:S(2)}, u32[]{:S(2)}) collective-permute-start(f32[288,128]{1,0:T(8,128)S(1)} %get-tuple-element.75), channel_id=1, source_target_pairs={{0,64},{1,65},{32,96},{33,97},{2,66},{3,67},{34,98},{35,99},{4,68}... | collective-permute-start | bytes 442376 | tf_op jit(solution)/shard_map/ppermute | solution.py:50
  92.4 11.0 %collective-permute-start.12 = (f32[288,128]{1,0:T(8,128)S(1)}, f32[288,128]{1,0:T(8,128)S(1)}, u32[]{:S(2)}, u32[]{:S(2)}) collective-permute-start(f32[288,128]{1,0:T(8,128)S(1)} %get-tuple-element.76), channel_id=1, source_target_pairs={{0,128},{1,129},{32,160},{33,161},{2,130},{3,131},{34,162},{35,163... | collective-permute-start | bytes 442376 | tf_op jit(solution)/shard_map/ppermute | solution.py:50
  94.8 8.6 %collective-permute-start.13 = (f32[288,128]{1,0:T(8,128)S(1)}, f32[288,128]{1,0:T(8,128)S(1)}, u32[]{:S(2)}, u32[]{:S(2)}) collective-permute-start(f32[288,128]{1,0:T(8,128)S(1)} %get-tuple-element.77), channel_id=1, source_target_pairs={{0,192},{1,193},{32,224},{33,225},{2,194},{3,195},{34,226},{35,227... | collective-permute-start | bytes 442376 | tf_op jit(solution)/shard_map/ppermute | solution.py:50
  146.8 7.8 %collective-permute-start.14 = (bf16[16,288,128]{2,1,0:T(8,128)(2,1)S(1)}, bf16[16,288,128]{2,1,0:T(8,128)(2,1)S(1)}, u32[]{:S(2)}, u32[]{:S(2)}) collective-permute-start(bf16[16,288,128]{2,1,0:T(8,128)(2,1)S(1)} %all_to_all.62.refs_0_), channel_id=1, source_target_pairs={{0,1},{1,0},{32,33},{33,32},{2,3},{3,2},{34,35},{35,34},{4,5},{5,4... | collective-permute-start | bytes 3538952 | tf_op jit(solution)/shard_map/ppermute | solution.py:50

commit v6 on v5

--- a/solution.py
+++ b/solution.py
@@ -1,3 +1,4 @@
+import functools
 import itertools
 import math
 
@@ -37,7 +38,7 @@
     return ((y * 2 + z % 2) * 4 + x) * 8 + (z // 2) * 2 + core
 
 
-def shifted(values, axis, by):
+def moved_to(values, axis, target):
     pairs = []
     for x in range(4):
         for y in range(4):
@@ -45,14 +46,23 @@
                 for core in range(2):
                     at = {"x": x, "y": y, "z": z, "core": core}
                     to = dict(at)
-                    to[axis] = (at[axis] + by) % sizes[axis]
+                    to[axis] = target(at[axis])
                     pairs.append((place_of(**at), place_of(**to)))
     return lax.ppermute(values, ("tile", "ens"), pairs)
 
 
+def shifted(values, axis, by):
+    return moved_to(values, axis, lambda at: (at + by) % sizes[axis])
+
+
+def mirrored(values, bit):
+    return moved_to(values, "z", lambda at: at ^ (1 << bit))
+
+
 def placing():
     tile, ens = lax.axis_index("tile"), lax.axis_index("ens")
-    return tile, lax.rem(tile, 4), lax.rem(ens, 2), tile // 8
+    z = (ens // 2) * 2 + lax.rem(tile // 4, 2)
+    return tile, lax.rem(tile, 4), lax.rem(ens, 2), tile // 8, z
 
 
 edge_starts = ((0, 3), (0, 1), (1, 2), (2, 3))
@@ -346,6 +356,18 @@
         return self.ref[at]
 
 
+class ArrivingTaps:
+    def __init__(self, ref, copies):
+        self.taps = [Arriving(ref.at[tap], copies[tap]) for tap in range(9)]
+
+    def settle(self):
+        for tap in self.taps:
+            tap.settle()
+
+    def __getitem__(self, tap):
+        return self.taps[tap][...]
+
+
 class Leaving:
     def __init__(self, ref, copy):
         self.ref, self.copy, self.started = ref, copy, False
@@ -380,15 +402,25 @@
         targets, refs = refs[: len(outs)], refs[len(outs) :]
         held, refs = refs[: len(moved)], refs[len(moved) :]
         made, refs = refs[: len(away)], refs[len(away) :]
-        arrived, left_for, refs = refs[0], refs[1], refs[2:]
-        copies = [
-            pltpu.make_async_copy(ins[i], held[n], arrived.at[n]) for n, i in enumerate(moved)
-        ]
-        for copy in copies:
-            copy.start()
+        arrived, left_for, by_tap, refs = refs[0], refs[1], refs[2], refs[3:]
+        copies = {}
+        for n, i in enumerate(moved):
+            if args[i].shape[0] != 9:
+                copies[n] = pltpu.make_async_copy(ins[i], held[n], arrived.at[n])
+                copies[n].start()
+        for n, i in enumerate(moved):
+            if args[i].shape[0] == 9:
+                copies[n] = {}
+                for across in range(3):
+                    for tap in range(across, 9, 3):
+                        copies[n][tap] = pltpu.make_async_copy(
+                            ins[i].at[tap], held[n].at[tap], by_tap.at[tap]
+                        )
+                        copies[n][tap].start()
         given = list(ins)
         for n, i in enumerate(moved):
-            given[i] = Arriving(held[n], copies[n])
+            kind = ArrivingTaps if args[i].shape[0] == 9 else Arriving
+            given[i] = kind(held[n], copies[n])
         results = list(targets)
         for m, n in enumerate(away):
             copy = pltpu.make_async_copy(made[m], targets[n], left_for.at[m])
@@ -413,6 +445,7 @@
             *stores,
             pltpu.SemaphoreType.DMA((max(1, len(moved)),)),
             pltpu.SemaphoreType.DMA((max(1, len(away)),)),
+            pltpu.SemaphoreType.DMA((9,)),
             *scratch,
         ],
         compiler_params=pltpu.CompilerParams(vmem_limit_bytes=40 * 2**20),
@@ -502,10 +535,37 @@
         chunks[k][144:] = kept1[at] + got1[at]
 
 
-def plane_kernel(place, own, part1, part2, part3, held, out, total):
-    total[...] = (own[...] + part1[...]) + (part2[...] + part3[...])
-    for j in range(8):
-        out[j] = total[36 * j : 36 * j + 36]
+def bit_of(place, bit):
+    return lax.rem(place[4] // (1 << bit), 2) == 0
+
+
+def plane_kernel(place, own, part1, part2, part3, held, kept, sent):
+    total = (own[...] + part1[...]) + (part2[...] + part3[...])
+    low = bit_of(place, 0)
+    kept[...] = jnp.where(low, total[:144], total[144:])
+    sent[...] = jnp.where(low, total[144:], total[:144])
+
+
+def halve_kernel(bit, place, own, got, kept, sent, total):
+    half = own.shape[0] // 2
+    total[...] = own[...] + got[...]
+    low = bit_of(place, bit)
+    first, second = total[:half], total[half : 2 * half]
+    kept[...] = jnp.where(low, first, second)
+    sent[...] = jnp.where(low, second, first)
+
+
+def round_kernel(scale, place, own, got, out):
+    out[...] = ((own[...] + got[...]) * scale).astype(bf16)
+
+
+def join_kernel(bit, place, own, got, out, total):
+    size = own.shape[0]
+    low = bit_of(place, bit)
+    mine, other = own[...].astype(f32), got[...].astype(f32)
+    total[:size] = jnp.where(low, mine, other)
+    total[size:] = jnp.where(low, other, mine)
+    out[...] = total[...].astype(bf16)
 
 
 def spread_kernel(place, own, other, first_ref, second_ref):
@@ -548,18 +608,45 @@
 
 
 def finish_slopes(chunks, held, scale):
-    terms = run(
+    def small(kernel, name, args, outs, scratch=()):
+        specs = [near] * len(args)
+        return run(kernel, name, args, specs, outs, scratch, 1000, tuple(range(len(outs))))
+
+    def rows(count, dtype=f32):
+        return like(count, 128, dtype=dtype)
+
+    kept, sent = run(
         plane_kernel,
         "row_sum",
         (*ring(chunks, "y"), held),
         [near] * 4 + [left],
-        like(8, 36, 128, dtype=f32),
-        [pltpu.VMEM((288, 128), f32)],
+        (rows(144), rows(144)),
+        [],
         1000,
-        (0,),
-    )
-    mine = (jnp.sum(trade(terms, "z"), axis=0) * scale).astype(bf16)
-    line = trade(copies_of(mine, 8), "z").reshape(288, 128)
+        (0, 1),
+    )
+    for bit, count in ((1, 144), (2, 72)):
+        kept, sent = small(
+            functools.partial(halve_kernel, bit),
+            "halve_sum",
+            (kept, mirrored(sent, bit - 1)),
+            (rows(count // 2),) * 2,
+            [pltpu.VMEM((count, 128), f32)],
+        )
+    (line,) = small(
+        functools.partial(round_kernel, scale),
+        "round_sum",
+        (kept, mirrored(sent, 2)),
+        (rows(36, bf16),),
+    )
+    for bit, count in ((2, 72), (1, 144), (0, 288)):
+        (line,) = small(
+            functools.partial(join_kernel, bit),
+            "join_rows",
+            (line, mirrored(line, bit)),
+            (rows(count, bf16),),
+            [pltpu.VMEM((count, 128), f32)],
+        )
     plane = trade(copies_of(line, 16), "x", "y")
     shape = like(9, 256, 256, dtype=f32)
     return run(

time: 158 us -> 167 us (1.057)
  blocking collectives: 62 us -> 35.5 us
  starting transfers between devices: 47.1 us -> 70.1 us
  waiting for transfers between devices: 26 us -> 34.4 us
  Pallas kernels: 21.5 us -> 24.9 us
    all_to_all x3 -> x1, blocking collectives: 43.1 us -> 16.5 us  [trade(): lax.all_to_all(values, ('tile', 'ens'), 0, 0, axis_index_groups=groups(al...]
    ppermute x15 -> x21, starting transfers between devices: 28.3 us -> 51.3 us  [moved_to(): return lax.ppermute(values, ('tile', 'ens'), pairs)]
    ppermute x15 -> x21, waiting for transfers between devices: 26 us -> 34.3 us  [moved_to(): return lax.ppermute(values, ('tile', 'ens'), pairs)]
    pallas_call x10 -> x16, Pallas kernels: 21.5 us -> 24.9 us  [run(): pl.pallas_call(body, out_shape=tuple((pltpu.HBM(out.shape, out.dtype) if...]
  transfers between devices with their start and end apart: 18 -> 24, of which waited for: 11 -> 17; matrix products, arithmetic and copies ran while one was open for 0% -> 0% of each run, Pallas kernels for 2% -> 2%
where the time goes in v6:
time: 167 us; the launch traced here: 166 us
  starting transfers between devices  70.1 us (42%)
  blocking collectives  35.5 us (21%)
  waiting for transfers between devices  34.4 us (21%)
  Pallas kernels  24.9 us (15%)
    ppermute x21, starting transfers between devices, moved_to(): return lax.ppermute(values, ('tile', 'ens'), pairs)  51.3 us
    ppermute x21, waiting for transfers between devices, moved_to(): return lax.ppermute(values, ('tile', 'ens'), pairs)  34.3 us
    pallas_call x16, Pallas kernels, run(): pl.pallas_call(body, out_shape=tuple((pltpu.HBM(out.shape, out.dtype) if...  24.9 us
    all_to_all x1, blocking collectives, exchange(): return lax.all_to_all(values, 'tile', 0, 0, tiled=True)  18.9 us
    all_to_all x3, starting transfers between devices, exchange(): return lax.all_to_all(values, 'tile', 0, 0, tiled=True)  18.8 us
    all_to_all x1, blocking collectives, trade(): lax.all_to_all(values, ('tile', 'ens'), 0, 0, axis_index_groups=groups(al...  16.5 us
  transfers between devices with their start and end apart: 24, of which 17 were waited for; matrix products, arithmetic and copies ran while one was open for 0% of the time, Pallas kernels for 2%

profile of v6, /device:TPU:1, one launch (start us, length us, event | category | flops | bytes accessed | tf_op | source)
XLA Modules:
  0.0 165.9 jit_solution(16611462956422145466)
XLA Ops:
  0.6 2.6 %routes.1 = (bf16[1024,128]{1,0:T(8,128)(2,1)S(1)}, bf16[128,1152]{1,0:T(8,128)(2,1)S(1)}, bf16[128,256]{1,0:T(8,128)(2,1)S(1)}, bf16[1024,256]{1,0:T(8,128)(2,1)S(1)}) custom-call(s32[3,16]{1,0:T(4,128)} %refs_0_.7, bf16[192,256]{1,0:T(8,128)(2,1)} %bitcast.25), custom_call_target="tpu_custom_call" | custom-call | flops 67108864 | bytes 3000000 | tf_op jit(solution)/shard_map/routes/pallas_call | solution.py:436
  3.2 18.9 %all_to_all.49 = bf16[32,32,256]{2,1,0:T(8,128)(2,1)S(1)} all-to-all(bf16[32,32,256]{2,1,0:T(8,128)(2,1)S(1)} %bitcast.21), channel_id=1, replica_groups=mesh['tile'=32,'ens'=8] {'tile'}, dimensions={0} | all-to-all | bytes 1048576 | tf_op jit(solution)/shard_map/all_to_all | solution.py:664
  22.1 4.1 %first_layer.1 = (bf16[192,256]{1,0:T(8,128)(2,1)S(1)}, f32[192,256]{1,0:T(8,128)}, bf16[128,256]{1,0:T(8,128)(2,1)S(1)}, bf16[1024,256]{1,0:T(8,128)(2,1)}, bf1...) custom-call(s32[3,16]{1,0:T(4,128)} %refs_0_.7, ...), custom_call_target="tpu_custom_call" | custom-call | flops 226492416 | bytes 3000000 | tf_op jit(solution)/shard_map/first_layer/pallas_call | solution.py:436
  26.2 5.8 %all-to-all-start.1 = ((bf16[32,32,256]{2,1,0:T(8,128)(2,1)}), bf16[32,32,256]{2,1,0:T(8,128)(2,1)S(1)}, u32[]{:S(2)}, u32[]{:S(2)}) async-start(bf16[32,32,256]{2,1,0:T(8,128)(2,1)} %bitcast.5), calls=%async_computation.1 | async-start | bytes 1048576 | tf_op jit(solution)/shard_map/all_to_all | solution.py:664
  32.0 1.3 collective-permute-start
  33.3 2.4 %collective-permute-start.1 = (bf16[304,128]{1,0:T(8,128)(2,1)S(1)}, bf16[304,128]{1,0:T(8,128)(2,1)S(1)}, u32[]{:S(2)}, u32[]{:S(2)}) collective-permute-start(bf16[304,128]{1,0:T(8,128)(2,1)S(1)} %get-tuple-element.56), channel_id=1, source_target_pairs={{0,16},{1,17},{32,48},{33,49},{2,18},{3,19},{34,50},{35,51},{4,20}... | collective-permute-start | bytes 233480 | tf_op jit(solution)/shard_map/ppermute | solution.py:51
  35.7 1.2 collective-permute-start.2
  36.9 5.4 %collective-permute-done.refs_9_.refs_1_ = bf16[304,128]{1,0:T(8,128)(2,1)S(1)} collective-permute-done((bf16[304,128]{1,0:T(8,128)(2,1)S(1)}, bf16[304,128]{1,0:T(8,128)(2,1)S(1)}, u32[]{:S(2)}, u32[]{:S(2)}) %collective-permute-start) | collective-permute-done | bytes 77856 | tf_op jit(solution)/shard_map/ppermute | solution.py:51
  42.3 1.2 collective-permute-done.1.refs_10_.refs_2_
  43.5 4.8 %second_layer.1 = (bf16[192,256]{1,0:T(8,128)(2,1)}, f32[192,256]{1,0:T(8,128)}, f32[3,8,8,256]{3,2,1,0:T(8,128)S(1)}, bf16[128,256]{1,0:T(8,128)(2,1)S(1)}, bf1...) custom-call(s32[3,16]{1,0:T(4,128)} %refs_0_.7, ...), custom_call_target="tpu_custom_call" | custom-call | flops 452984832 | bytes 3000000 | tf_op jit(solution)/shard_map/second_layer/pallas_call | solution.py:436
  48.3 6.4 %all-to-all-start.2 = ((bf16[32,32,256]{2,1,0:T(8,128)(2,1)}), bf16[32,32,256]{2,1,0:T(8,128)(2,1)S(1)}, u32[]{:S(2)}, u32[]{:S(2)}) async-start(bf16[32,32,256]{2,1,0:T(8,128)(2,1)} %bitcast.9), calls=%async_computation.2 | async-start | bytes 1048576 | tf_op jit(solution)/shard_map/all_to_all | solution.py:664
  54.7 1.3 collective-permute-start.3
  56.1 2.4 %collective-permute-start.4 = (bf16[496,128]{1,0:T(8,128)(2,1)S(1)}, bf16[496,128]{1,0:T(8,128)(2,1)S(1)}, u32[]{:S(2)}, u32[]{:S(2)}) collective-permute-start(bf16[496,128]{1,0:T(8,128)(2,1)S(1)} %get-tuple-element.64), channel_id=1, source_target_pairs={{0,16},{1,17},{32,48},{33,49},{2,18},{3,19},{34,50},{35,51},{4,20}... | collective-permute-start | bytes 380936 | tf_op jit(solution)/shard_map/ppermute | solution.py:51
  58.4 1.2 collective-permute-start.5
  59.6 7.0 %collective-permute-done.3.refs_7_.refs_1_ = bf16[496,128]{1,0:T(8,128)(2,1)S(1)} collective-permute-done((bf16[496,128]{1,0:T(8,128)(2,1)S(1)}, bf16[496,128]{1,0:T(8,128)(2,1)S(1)}, u32[]{:S(2)}, u32[]{:S(2)}) %collective-permute-start.3) | collective-permute-done | bytes 127008 | tf_op jit(solution)/shard_map/ppermute | solution.py:51
  66.6 1.0 collective-permute-done.4.refs_8_.refs_2_
  67.6 4.7 %first_gradient.1 = (f32[3,8,8,256]{3,2,1,0:T(8,128)}, bf16[128,256]{1,0:T(8,128)(2,1)S(1)}, bf16[192,128]{1,0:T(8,128)(2,1)S(1)}, bf16[192,128]{1,0:T(8,128)(2,...) custom-call(s32[3,16]{1,0:T(4,128)} %refs_0_.7, f32[3,8,8,256]{3,2,1,0:T(8,128)S(1)} %get-tuple-element.59.refs_1_, ...), custom_call_target="tpu_custom_call" | custom-call | flops 226492416 | bytes 3000000 | tf_op jit(solution)/shard_map/first_gradient/pallas_call | solution.py:436
  72.3 1.9 %collective-permute-start.6 = (bf16[192,128]{1,0:T(8,128)(2,1)S(1)}, bf16[192,128]{1,0:T(8,128)(2,1)S(1)}, u32[]{:S(2)}, u32[]{:S(2)}) collective-permute-start(bf16[192,128]{1,0:T(8,128)(2,1)S(1)} %get-tuple-element.70), channel_id=1, source_target_pairs={{0,8},{1,9},{32,40},{33,41},{2,10},{3,11},{34,42},{35,43},{4,12},{... | collective-permute-start | bytes 147464 | tf_op jit(solution)/shard_map/ppermute | solution.py:51
  74.2 2.2 %collective-permute-start.7 = (bf16[192,128]{1,0:T(8,128)(2,1)S(1)}, bf16[192,128]{1,0:T(8,128)(2,1)S(1)}, u32[]{:S(2)}, u32[]{:S(2)}) collective-permute-start(bf16[192,128]{1,0:T(8,128)(2,1)S(1)} %get-tuple-element.71), channel_id=1, source_target_pairs={{0,16},{1,17},{32,48},{33,49},{2,18},{3,19},{34,50},{35,51},{4,20}... | collective-permute-start | bytes 147464 | tf_op jit(solution)/shard_map/ppermute | solution.py:51
  76.4 0.5 collective-permute-start.8
  76.9 0.8 slope_terms.2
  77.7 1.2 collective-permute-done.7.refs_6_
  78.9 0.7 collective-permute-done.8.refs_7_
  79.6 1.9 %slope_terms.3 = (f32[4,144,128]{2,1,0:T(8,128)S(1)}, f32[4,144,128]{2,1,0:T(8,128)S(1)}, bf16[1024,256]{1,0:T(8,128)(2,1)}) custom-call(bf16[304,128]{1,0:T(8,128)(2,1)} %get-tuple-element.68.refs_0_, bf16[304,128]{1,0:T(8,128)(2,1)S(1)} %collective-permute-done.refs_9_.refs_1_, bf16[304,128]{1,0:T(8,128)(2,1)S(1)} %collective-permute-done.1.refs_10_.refs_2_, ...), custom_call_target="tpu_custom_call" | custom-call | flops 226492416 | bytes 3000000 | tf_op jit(solution)/shard_map/slope_terms/pallas_call | solution.py:436
  81.5 6.6 %all-to-all-start.3 = ((bf16[32,32,256]{2,1,0:T(8,128)(2,1)}), bf16[32,32,256]{2,1,0:T(8,128)(2,1)S(1)}, u32[]{:S(2)}, u32[]{:S(2)}) async-start(bf16[32,32,256]{2,1,0:T(8,128)(2,1)} %bitcast.11), calls=%async_computation.3 | async-start | bytes 1048576 | tf_op jit(solution)/shard_map/all_to_all | solution.py:664
  88.1 3.5 %collective-permute-start.10 = (f32[4,144,128]{2,1,0:T(8,128)S(1)}, f32[4,144,128]{2,1,0:T(8,128)S(1)}, u32[]{:S(2)}, u32[]{:S(2)}) collective-permute-start(f32[4,144,128]{2,1,0:T(8,128)S(1)} %get-tuple-element.79), channel_id=1, source_target_pairs={{0,1},{1,0},{32,33},{33,32},{2,3},{3,2},{34,35},{35,34},{4,5},{5,4... | collective-permute-start | bytes 884744 | tf_op jit(solution)/shard_map/ppermute | solution.py:51
  91.7 1.1 collective-permute-done.10.refs_3_
  93.3 1.6 collective-permute-start.11
  94.9 2.4 %collective-permute-start.12 = (f32[288,128]{1,0:T(8,128)S(1)}, f32[288,128]{1,0:T(8,128)S(1)}, u32[]{:S(2)}, u32[]{:S(2)}) collective-permute-start(f32[288,128]{1,0:T(8,128)S(1)} %get-tuple-element.82), channel_id=1, source_target_pairs={{0,128},{1,129},{32,160},{33,161},{2,130},{3,131},{34,162},{35,163... | collective-permute-start | bytes 442376 | tf_op jit(solution)/shard_map/ppermute | solution.py:51
  97.4 1.1 collective-permute-start.13
  98.5 4.0 %collective-permute-done.11.refs_1_ = f32[288,128]{1,0:T(8,128)S(1)} collective-permute-done((f32[288,128]{1,0:T(8,128)S(1)}, f32[288,128]{1,0:T(8,128)S(1)}, u32[]{:S(2)}, u32[]{:S(2)}) %collective-permute-start.11) | collective-permute-done | bytes 147488 | tf_op jit(solution)/shard_map/ppermute | solution.py:51
  102.5 3.4 %collective-permute-done.12.refs_2_ = f32[288,128]{1,0:T(8,128)S(1)} collective-permute-done((f32[288,128]{1,0:T(8,128)S(1)}, f32[288,128]{1,0:T(8,128)S(1)}, u32[]{:S(2)}, u32[]{:S(2)}) %collective-permute-start.12) | collective-permute-done | bytes 147488 | tf_op jit(solution)/shard_map/ppermute | solution.py:51
  106.0 1.5 collective-permute-start.14
  107.6 1.7 %collective-permute-done.14.refs_1_ = f32[144,128]{1,0:T(8,128)S(1)} collective-permute-done((f32[144,128]{1,0:T(8,128)S(1)}, f32[144,128]{1,0:T(8,128)S(1)}, u32[]{:S(2)}, u32[]{:S(2)}) %collective-permute-start.14) | collective-permute-done | bytes 73760 | tf_op jit(solution)/shard_map/ppermute | solution.py:51
  109.4 3.1 %collective-permute-start.15 = (f32[72,128]{1,0:T(8,128)S(1)}, f32[72,128]{1,0:T(8,128)S(1)}, u32[]{:S(2)}, u32[]{:S(2)}) collective-permute-start(f32[72,128]{1,0:T(8,128)S(1)} %get-tuple-element.87), channel_id=1, source_target_pairs={{0,2},{1,3},{32,34},{33,35},{2,0},{3,1},{34,32},{35,33},{4,6},{5,7... | collective-permute-start | bytes 110600 | tf_op jit(solution)/shard_map/ppermute | solution.py:51
  112.5 1.3 collective-permute-done.15.refs_1_
  114.0 5.5 %collective-permute-start.16 = (f32[36,128]{1,0:T(8,128)S(1)}, f32[36,128]{1,0:T(8,128)S(1)}, u32[]{:S(2)}, u32[]{:S(2)}) collective-permute-start(f32[36,128]{1,0:T(8,128)S(1)} %get-tuple-element.89), channel_id=1, source_target_pairs={{0,4},{1,5},{32,36},{33,37},{2,6},{3,7},{34,38},{35,39},{4,0},{5,1... | collective-permute-start | bytes 55304 | tf_op jit(solution)/shard_map/ppermute | solution.py:51
  119.4 1.3 collective-permute-done.16.refs_1_
  120.8 5.4 %collective-permute-start.17 = (bf16[36,128]{1,0:T(8,128)(2,1)S(1)}, bf16[36,128]{1,0:T(8,128)(2,1)S(1)}, u32[]{:S(2)}, u32[]{:S(2)}) collective-permute-start(bf16[36,128]{1,0:T(8,128)(2,1)S(1)} %round_sum.1.refs_0_), channel_id=1, source_target_pairs={{0,4},{1,5},{32,36},{33,37},{2,6},{3,7},{34,38},{35,39},{4,0},{5,1... | collective-permute-start | bytes 27656 | tf_op jit(solution)/shard_map/ppermute | solution.py:51
  126.2 1.2 collective-permute-done.17.refs_1_
  127.4 2.7 %collective-permute-start.18 = (bf16[72,128]{1,0:T(8,128)(2,1)S(1)}, bf16[72,128]{1,0:T(8,128)(2,1)S(1)}, u32[]{:S(2)}, u32[]{:S(2)}) collective-permute-start(bf16[72,128]{1,0:T(8,128)(2,1)S(1)} %join_rows.3.refs_0_), channel_id=1, source_target_pairs={{0,2},{1,3},{32,34},{33,35},{2,0},{3,1},{34,32},{35,33},{4,6},{5,7... | collective-permute-start | bytes 55304 | tf_op jit(solution)/shard_map/ppermute | solution.py:51
  130.2 1.4 collective-permute-done.18.refs_1_
  131.7 1.3 collective-permute-start.19
  133.0 1.6 collective-permute-done.19.refs_1_
  134.9 16.5 %all_to_all.50.refs_0_ = bf16[16,288,128]{2,1,0:T(8,128)(2,1)S(1)} all-to-all(bf16[16,288,128]{2,1,0:T(8,128)(2,1)S(1)} %broadcast_in_dim.10), channel_id=1, replica_groups={{0,64,128,192,8,72,136,200,16,80,144,208,24,88,152,216},{1,65,129,193,9..., dimensions={0} | all-to-all | bytes 2359296 | tf_op jit(solution)/shard_map/all_to_all | solution.py:601
  151.5 8.8 %collective-permute-start.20 = (bf16[16,288,128]{2,1,0:T(8,128)(2,1)S(1)}, bf16[16,288,128]{2,1,0:T(8,128)(2,1)S(1)}, u32[]{:S(2)}, u32[]{:S(2)}) collective-permute-start(bf16[16,288,128]{2,1,0:T(8,128)(2,1)S(1)} %all_to_all.50.refs_0_), channel_id=1, source_target_pairs={{0,1},{1,0},{32,33},{33,32},{2,3},{3,2},{34,35},{35,34},{4,5},{5,4... | collective-permute-start | bytes 3538952 | tf_op jit(solution)/shard_map/ppermute | solution.py:51
  160.2 2.0 %last_gradient.1 = f32[3,8,8,256]{3,2,1,0:T(8,128)} custom-call(f32[3,8,8,256]{3,2,1,0:T(8,128)} %get-tuple-element.66.refs_0_, f32[192,256]{1,0:T(8,128)} %get-tuple-element.67.refs_1_, bf16[1024,256]{1,0:T(8,128)(2,1)S(1)} %bitcast.17, bf16[128,256]{1,0:T(8,128)(2,1)S(1)} %get-tuple-element.73.refs_9_.refs_3_, ...), custom_call_target="tpu_custom_call" | custom-call | flops 1000 | bytes 3000000 | tf_op jit(solution)/shard_map/last_gradient/pallas_call | solution.py:436
  162.7 3.1 %spread_slopes.1 = (f32[9,256,256]{2,1,0:T(8,128)}, f32[9,256,256]{2,1,0:T(8,128)}) custom-call(bf16[16,288,128]{2,1,0:T(8,128)(2,1)S(1)} %all_to_all.50.refs_0_, bf16[16,288,128]{2,1,0:T(8,128)(2,1)S(1)} %collective-permute-done.20.refs_1_), custom_call_target="tpu_custom_call" | custom-call | flops 1000 | bytes 3000000 | tf_op jit(solution)/shard_map/spread_slopes/pallas_call | solution.py:436
  (19 shorter events, 2.1 us)
Async XLA Ops:
  26.2 17.3 %all-to-all-start.1 = ((bf16[32,32,256]{2,1,0:T(8,128)(2,1)}), bf16[32,32,256]{2,1,0:T(8,128)(2,1)S(1)}, u32[]{:S(2)}, u32[]{:S(2)}) async-start(bf16[32,32,256]{2,1,0:T(8,128)(2,1)} %bitcast.5), calls=%async_computation.1 | async-start | bytes 1048576 | tf_op jit(solution)/shard_map/all_to_all | solution.py:664
  32.0 10.3 %collective-permute-start = (bf16[304,128]{1,0:T(8,128)(2,1)S(1)}, bf16[304,128]{1,0:T(8,128)(2,1)S(1)}, u32[]{:S(2)}, u32[]{:S(2)}) collective-permute-start(bf16[304,128]{1,0:T(8,128)(2,1)S(1)} %get-tuple-element.55), channel_id=1, source_target_pairs={{0,8},{1,9},{32,40},{33,41},{2,10},{3,11},{34,42},{35,43},{4,12},{... | collective-permute-start | bytes 233480 | tf_op jit(solution)/shard_map/ppermute | solution.py:51
  33.3 10.2 %collective-permute-start.1 = (bf16[304,128]{1,0:T(8,128)(2,1)S(1)}, bf16[304,128]{1,0:T(8,128)(2,1)S(1)}, u32[]{:S(2)}, u32[]{:S(2)}) collective-permute-start(bf16[304,128]{1,0:T(8,128)(2,1)S(1)} %get-tuple-element.56), channel_id=1, source_target_pairs={{0,16},{1,17},{32,48},{33,49},{2,18},{3,19},{34,50},{35,51},{4,20}... | collective-permute-start | bytes 233480 | tf_op jit(solution)/shard_map/ppermute | solution.py:51
  35.7 7.8 %collective-permute-start.2 = (bf16[304,128]{1,0:T(8,128)(2,1)S(1)}, bf16[304,128]{1,0:T(8,128)(2,1)S(1)}, u32[]{:S(2)}, u32[]{:S(2)}) collective-permute-start(bf16[304,128]{1,0:T(8,128)(2,1)S(1)} %get-tuple-element.57), channel_id=1, source_target_pairs={{0,24},{1,25},{32,56},{33,57},{2,26},{3,27},{34,58},{35,59},{4,28}... | collective-permute-start | bytes 233480 | tf_op jit(solution)/shard_map/ppermute | solution.py:51
  48.3 19.3 %all-to-all-start.2 = ((bf16[32,32,256]{2,1,0:T(8,128)(2,1)}), bf16[32,32,256]{2,1,0:T(8,128)(2,1)S(1)}, u32[]{:S(2)}, u32[]{:S(2)}) async-start(bf16[32,32,256]{2,1,0:T(8,128)(2,1)} %bitcast.9), calls=%async_computation.2 | async-start | bytes 1048576 | tf_op jit(solution)/shard_map/all_to_all | solution.py:664
  54.7 11.9 %collective-permute-start.3 = (bf16[496,128]{1,0:T(8,128)(2,1)S(1)}, bf16[496,128]{1,0:T(8,128)(2,1)S(1)}, u32[]{:S(2)}, u32[]{:S(2)}) collective-permute-start(bf16[496,128]{1,0:T(8,128)(2,1)S(1)} %get-tuple-element.63), channel_id=1, source_target_pairs={{0,8},{1,9},{32,40},{33,41},{2,10},{3,11},{34,42},{35,43},{4,12},{... | collective-permute-start | bytes 380936 | tf_op jit(solution)/shard_map/ppermute | solution.py:51
  56.1 11.5 %collective-permute-start.4 = (bf16[496,128]{1,0:T(8,128)(2,1)S(1)}, bf16[496,128]{1,0:T(8,128)(2,1)S(1)}, u32[]{:S(2)}, u32[]{:S(2)}) collective-permute-start(bf16[496,128]{1,0:T(8,128)(2,1)S(1)} %get-tuple-element.64), channel_id=1, source_target_pairs={{0,16},{1,17},{32,48},{33,49},{2,18},{3,19},{34,50},{35,51},{4,20}... | collective-permute-start | bytes 380936 | tf_op jit(solution)/shard_map/ppermute | solution.py:51
  58.4 9.1 %collective-permute-start.5 = (bf16[496,128]{1,0:T(8,128)(2,1)S(1)}, bf16[496,128]{1,0:T(8,128)(2,1)S(1)}, u32[]{:S(2)}, u32[]{:S(2)}) collective-permute-start(bf16[496,128]{1,0:T(8,128)(2,1)S(1)} %get-tuple-element.65), channel_id=1, source_target_pairs={{0,24},{1,25},{32,56},{33,57},{2,26},{3,27},{34,58},{35,59},{4,28}... | collective-permute-start | bytes 380936 | tf_op jit(solution)/shard_map/ppermute | solution.py:51
  72.3 5.4 %collective-permute-start.6 = (bf16[192,128]{1,0:T(8,128)(2,1)S(1)}, bf16[192,128]{1,0:T(8,128)(2,1)S(1)}, u32[]{:S(2)}, u32[]{:S(2)}) collective-permute-start(bf16[192,128]{1,0:T(8,128)(2,1)S(1)} %get-tuple-element.70), channel_id=1, source_target_pairs={{0,8},{1,9},{32,40},{33,41},{2,10},{3,11},{34,42},{35,43},{4,12},{... | collective-permute-start | bytes 147464 | tf_op jit(solution)/shard_map/ppermute | solution.py:51
  74.2 4.7 %collective-permute-start.7 = (bf16[192,128]{1,0:T(8,128)(2,1)S(1)}, bf16[192,128]{1,0:T(8,128)(2,1)S(1)}, u32[]{:S(2)}, u32[]{:S(2)}) collective-permute-start(bf16[192,128]{1,0:T(8,128)(2,1)S(1)} %get-tuple-element.71), channel_id=1, source_target_pairs={{0,16},{1,17},{32,48},{33,49},{2,18},{3,19},{34,50},{35,51},{4,20}... | collective-permute-start | bytes 147464 | tf_op jit(solution)/shard_map/ppermute | solution.py:51
  76.4 3.2 %collective-permute-start.8 = (bf16[192,128]{1,0:T(8,128)(2,1)S(1)}, bf16[192,128]{1,0:T(8,128)(2,1)S(1)}, u32[]{:S(2)}, u32[]{:S(2)}) collective-permute-start(bf16[192,128]{1,0:T(8,128)(2,1)S(1)} %get-tuple-element.72), channel_id=1, source_target_pairs={{0,24},{1,25},{32,56},{33,57},{2,26},{3,27},{34,58},{35,59},{4,28}... | collective-permute-start | bytes 147464 | tf_op jit(solution)/shard_map/ppermute | solution.py:51
  81.5 24.4 %all-to-all-start.3 = ((bf16[32,32,256]{2,1,0:T(8,128)(2,1)}), bf16[32,32,256]{2,1,0:T(8,128)(2,1)S(1)}, u32[]{:S(2)}, u32[]{:S(2)}) async-start(bf16[32,32,256]{2,1,0:T(8,128)(2,1)} %bitcast.11), calls=%async_computation.3 | async-start | bytes 1048576 | tf_op jit(solution)/shard_map/all_to_all | solution.py:664
  88.1 4.7 %collective-permute-start.10 = (f32[4,144,128]{2,1,0:T(8,128)S(1)}, f32[4,144,128]{2,1,0:T(8,128)S(1)}, u32[]{:S(2)}, u32[]{:S(2)}) collective-permute-start(f32[4,144,128]{2,1,0:T(8,128)S(1)} %get-tuple-element.79), channel_id=1, source_target_pairs={{0,1},{1,0},{32,33},{33,32},{2,3},{3,2},{34,35},{35,34},{4,5},{5,4... | collective-permute-start | bytes 884744 | tf_op jit(solution)/shard_map/ppermute | solution.py:51
  91.6 1.6 collective-permute-start.9
  93.3 9.1 %collective-permute-start.11 = (f32[288,128]{1,0:T(8,128)S(1)}, f32[288,128]{1,0:T(8,128)S(1)}, u32[]{:S(2)}, u32[]{:S(2)}) collective-permute-start(f32[288,128]{1,0:T(8,128)S(1)} %get-tuple-element.81), channel_id=1, source_target_pairs={{0,64},{1,65},{32,96},{33,97},{2,66},{3,67},{34,98},{35,99},{4,68}... | collective-permute-start | bytes 442376 | tf_op jit(solution)/shard_map/ppermute | solution.py:51
  94.9 10.9 %collective-permute-start.12 = (f32[288,128]{1,0:T(8,128)S(1)}, f32[288,128]{1,0:T(8,128)S(1)}, u32[]{:S(2)}, u32[]{:S(2)}) collective-permute-start(f32[288,128]{1,0:T(8,128)S(1)} %get-tuple-element.82), channel_id=1, source_target_pairs={{0,128},{1,129},{32,160},{33,161},{2,130},{3,131},{34,162},{35,163... | collective-permute-start | bytes 442376 | tf_op jit(solution)/shard_map/ppermute | solution.py:51
  97.4 8.5 %collective-permute-start.13 = (f32[288,128]{1,0:T(8,128)S(1)}, f32[288,128]{1,0:T(8,128)S(1)}, u32[]{:S(2)}, u32[]{:S(2)}) collective-permute-start(f32[288,128]{1,0:T(8,128)S(1)} %get-tuple-element.83), channel_id=1, source_target_pairs={{0,192},{1,193},{32,224},{33,225},{2,194},{3,195},{34,226},{35,227... | collective-permute-start | bytes 442376 | tf_op jit(solution)/shard_map/ppermute | solution.py:51
  106.0 3.3 %collective-permute-start.14 = (f32[144,128]{1,0:T(8,128)S(1)}, f32[144,128]{1,0:T(8,128)S(1)}, u32[]{:S(2)}, u32[]{:S(2)}) collective-permute-start(f32[144,128]{1,0:T(8,128)S(1)} %get-tuple-element.85), channel_id=1, source_target_pairs={{0,32},{1,33},{32,0},{33,1},{2,34},{3,35},{34,2},{35,3},{4,36},{5,... | collective-permute-start | bytes 221192 | tf_op jit(solution)/shard_map/ppermute | solution.py:51
  109.4 4.4 %collective-permute-start.15 = (f32[72,128]{1,0:T(8,128)S(1)}, f32[72,128]{1,0:T(8,128)S(1)}, u32[]{:S(2)}, u32[]{:S(2)}) collective-permute-start(f32[72,128]{1,0:T(8,128)S(1)} %get-tuple-element.87), channel_id=1, source_target_pairs={{0,2},{1,3},{32,34},{33,35},{2,0},{3,1},{34,32},{35,33},{4,6},{5,7... | collective-permute-start | bytes 110600 | tf_op jit(solution)/shard_map/ppermute | solution.py:51
  114.0 6.7 %collective-permute-start.16 = (f32[36,128]{1,0:T(8,128)S(1)}, f32[36,128]{1,0:T(8,128)S(1)}, u32[]{:S(2)}, u32[]{:S(2)}) collective-permute-start(f32[36,128]{1,0:T(8,128)S(1)} %get-tuple-element.89), channel_id=1, source_target_pairs={{0,4},{1,5},{32,36},{33,37},{2,6},{3,7},{34,38},{35,39},{4,0},{5,1... | collective-permute-start | bytes 55304 | tf_op jit(solution)/shard_map/ppermute | solution.py:51
  120.8 6.5 %collective-permute-start.17 = (bf16[36,128]{1,0:T(8,128)(2,1)S(1)}, bf16[36,128]{1,0:T(8,128)(2,1)S(1)}, u32[]{:S(2)}, u32[]{:S(2)}) collective-permute-start(bf16[36,128]{1,0:T(8,128)(2,1)S(1)} %round_sum.1.refs_0_), channel_id=1, source_target_pairs={{0,4},{1,5},{32,36},{33,37},{2,6},{3,7},{34,38},{35,39},{4,0},{5,1... | collective-permute-start | bytes 27656 | tf_op jit(solution)/shard_map/ppermute | solution.py:51
  127.4 4.2 %collective-permute-start.18 = (bf16[72,128]{1,0:T(8,128)(2,1)S(1)}, bf16[72,128]{1,0:T(8,128)(2,1)S(1)}, u32[]{:S(2)}, u32[]{:S(2)}) collective-permute-start(bf16[72,128]{1,0:T(8,128)(2,1)S(1)} %join_rows.3.refs_0_), channel_id=1, source_target_pairs={{0,2},{1,3},{32,34},{33,35},{2,0},{3,1},{34,32},{35,33},{4,6},{5,7... | collective-permute-start | bytes 55304 | tf_op jit(solution)/shard_map/ppermute | solution.py:51
  131.7 2.9 %collective-permute-start.19 = (bf16[144,128]{1,0:T(8,128)(2,1)S(1)}, bf16[144,128]{1,0:T(8,128)(2,1)S(1)}, u32[]{:S(2)}, u32[]{:S(2)}) collective-permute-start(bf16[144,128]{1,0:T(8,128)(2,1)S(1)} %join_rows.4.refs_0_), channel_id=1, source_target_pairs={{0,32},{1,33},{32,0},{33,1},{2,34},{3,35},{34,2},{35,3},{4,36},{5,... | collective-permute-start | bytes 110600 | tf_op jit(solution)/shard_map/ppermute | solution.py:51
  151.5 11.3 %collective-permute-start.20 = (bf16[16,288,128]{2,1,0:T(8,128)(2,1)S(1)}, bf16[16,288,128]{2,1,0:T(8,128)(2,1)S(1)}, u32[]{:S(2)}, u32[]{:S(2)}) collective-permute-start(bf16[16,288,128]{2,1,0:T(8,128)(2,1)S(1)} %all_to_all.50.refs_0_), channel_id=1, source_target_pairs={{0,1},{1,0},{32,33},{33,32},{2,3},{3,2},{34,35},{35,34},{4,5},{5,4... | collective-permute-start | bytes 3538952 | tf_op jit(solution)/shard_map/ppermute | solution.py:51

commit v7 on v5

--- a/solution.py
+++ b/solution.py
@@ -141,13 +141,16 @@
 
 
 def convolve(grid, weights):
-    total = jnp.zeros((192, 256), f32)
-    for across in range(3):
-        columns = grid[:, :, across : across + 8, :]
-        for down in range(3):
-            window = columns[:, down : down + 8].reshape(192, 256).astype(bf16)
-            total += jnp.dot(window, weights[3 * down + across], preferred_element_type=f32)
-    return total
+    windows = []
+    for down in range(3):
+        for across in range(3):
+            window = grid[:, down : down + 8, across : across + 8, :]
+            windows.append(window.reshape(192, 256).astype(bf16))
+    return jnp.dot(
+        jnp.concatenate(windows, axis=1),
+        weights[...].reshape(2304, 256),
+        preferred_element_type=f32,
+    )
 
 
 def spread_back(gradient, weights, grid, column):
@@ -601,7 +604,7 @@
         first_kernel,
         "first_layer",
         (tile_links, field, recv, frame, pack, unpack, first_weights),
-        [moved_in] * 2 + [near] * 4 + [moved_in],
+        [moved_in] + [near] * 6,
         (rows_like, like(192, 256, dtype=f32), frame_like, sent_like) + (like(304, 128),) * 4,
         [grid_shape, frame_shape, frame_shape, flat_shape],
         conv_flops,
@@ -616,7 +619,7 @@
             tile_links, field, goal, hidden, recv, frame, pack, unpack, second_weights,
             *field_parts[1:],
         ),
-        [moved_in] * 3 + [near] * 5 + [moved_in] + [left] * 3,
+        [moved_in] * 3 + [near] * 6 + [left] * 3,
         (rows_like, like(192, 256, dtype=f32), inner_like, frame_like, sent_like)
         + (like(496, 128),) * 4,
         [grid_shape, frame_shape, frame_shape, flat_shape, column_shape],

time: 158 us -> 158 us (level)
  no operation moved by 1% of the time
where the time goes in v7:
time: 158 us
  blocking collectives  62.1 us (39%)
  starting transfers between devices  47 us (30%)
  waiting for transfers between devices  26 us (16%)
  Pallas kernels  20.6 us (13%)
    all_to_all x3, blocking collectives, trade(): lax.all_to_all(values, ('tile', 'ens'), 0, 0, axis_index_groups=groups(al...  43.2 us
    ppermute x15, starting transfers between devices, shifted(): return lax.ppermute(values, ('tile', 'ens'), pairs)  28.3 us
    ppermute x15, waiting for transfers between devices, shifted(): return lax.ppermute(values, ('tile', 'ens'), pairs)  26 us
    pallas_call x10, Pallas kernels, run(): pl.pallas_call(body, out_shape=tuple((pltpu.HBM(out.shape, out.dtype) if...  20.6 us
    all_to_all x1, blocking collectives, exchange(): return lax.all_to_all(values, 'tile', 0, 0, tiled=True)  18.9 us
    all_to_all x3, starting transfers between devices, exchange(): return lax.all_to_all(values, 'tile', 0, 0, tiled=True)  18.8 us
  transfers between devices with their start and end apart: 18, of which 11 were waited for; matrix products, arithmetic and copies ran while one was open for 0% of the time, Pallas kernels for 2%

profile of v7, /device:TPU:1, one launch (start us, length us, event | category | flops | bytes accessed | tf_op | source)
XLA Modules:
  0.0 157.6 jit_solution(2244683620516892390)
XLA Ops:
  0.6 0.0 copy-start.2
  0.6 0.0 copy-start
  0.7 2.6 %routes.1 = (bf16[1024,128]{1,0:T(8,128)(2,1)S(1)}, bf16[128,1152]{1,0:T(8,128)(2,1)S(1)}, bf16[128,256]{1,0:T(8,128)(2,1)S(1)}, bf16[1024,256]{1,0:T(8,128)(2,1)S(1)}) custom-call(s32[3,16]{1,0:T(4,128)} %refs_0_.7, bf16[192,256]{1,0:T(8,128)(2,1)} %bitcast.25), custom_call_target="tpu_custom_call" | custom-call | flops 67108864 | bytes 3000000 | tf_op jit(solution)/shard_map/routes/pallas_call | solution.py:407
  3.3 18.9 %all_to_all.59 = bf16[32,32,256]{2,1,0:T(8,128)(2,1)S(1)} all-to-all(bf16[32,32,256]{2,1,0:T(8,128)(2,1)S(1)} %bitcast.24), channel_id=1, replica_groups=mesh['tile'=32,'ens'=8] {'tile'}, dimensions={0} | all-to-all | bytes 1048576 | tf_op jit(solution)/shard_map/all_to_all | solution.py:580
  22.2 3.4 %first_layer.1 = (bf16[192,256]{1,0:T(8,128)(2,1)S(1)}, f32[192,256]{1,0:T(8,128)}, bf16[128,256]{1,0:T(8,128)(2,1)S(1)}, bf16[1024,256]{1,0:T(8,128)(2,1)}, bf1...) custom-call(s32[3,16]{1,0:T(4,128)} %refs_0_.7, ...), custom_call_target="tpu_custom_call" | custom-call | flops 226492416 | bytes 3000000 | tf_op jit(solution)/shard_map/first_layer/pallas_call | solution.py:407
  25.6 5.8 %all-to-all-start.1 = ((bf16[32,32,256]{2,1,0:T(8,128)(2,1)}), bf16[32,32,256]{2,1,0:T(8,128)(2,1)S(1)}, u32[]{:S(2)}, u32[]{:S(2)}) async-start(bf16[32,32,256]{2,1,0:T(8,128)(2,1)} %bitcast.5), calls=%async_computation.1 | async-start | bytes 1048576 | tf_op jit(solution)/shard_map/all_to_all | solution.py:580
  31.4 1.3 collective-permute-start
  32.7 2.4 %collective-permute-start.1 = (bf16[304,128]{1,0:T(8,128)(2,1)S(1)}, bf16[304,128]{1,0:T(8,128)(2,1)S(1)}, u32[]{:S(2)}, u32[]{:S(2)}) collective-permute-start(bf16[304,128]{1,0:T(8,128)(2,1)S(1)} %get-tuple-element.50), channel_id=1, source_target_pairs={{0,16},{1,17},{32,48},{33,49},{2,18},{3,19},{34,50},{35,51},{4,20}... | collective-permute-start | bytes 233480 | tf_op jit(solution)/shard_map/ppermute | solution.py:50
  35.1 1.2 collective-permute-start.2
  36.2 5.4 %collective-permute-done.refs_9_.refs_1_ = bf16[304,128]{1,0:T(8,128)(2,1)S(1)} collective-permute-done((bf16[304,128]{1,0:T(8,128)(2,1)S(1)}, bf16[304,128]{1,0:T(8,128)(2,1)S(1)}, u32[]{:S(2)}, u32[]{:S(2)}) %collective-permute-start) | collective-permute-done | bytes 77856 | tf_op jit(solution)/shard_map/ppermute | solution.py:50
  41.7 1.2 collective-permute-done.1.refs_10_.refs_2_
  42.8 0.0 collective-permute-done.2.refs_11_.refs_3_
  42.8 4.1 %second_layer.1 = (bf16[192,256]{1,0:T(8,128)(2,1)}, f32[192,256]{1,0:T(8,128)}, f32[3,8,8,256]{3,2,1,0:T(8,128)S(1)}, bf16[128,256]{1,0:T(8,128)(2,1)S(1)}, bf1...) custom-call(s32[3,16]{1,0:T(4,128)} %refs_0_.7, ...), custom_call_target="tpu_custom_call" | custom-call | flops 452984832 | bytes 3000000 | tf_op jit(solution)/shard_map/second_layer/pallas_call | solution.py:407
  46.9 0.6 copy-done.3
  47.6 6.4 %all-to-all-start.2 = ((bf16[32,32,256]{2,1,0:T(8,128)(2,1)}), bf16[32,32,256]{2,1,0:T(8,128)(2,1)S(1)}, u32[]{:S(2)}, u32[]{:S(2)}) async-start(bf16[32,32,256]{2,1,0:T(8,128)(2,1)} %bitcast.9), calls=%async_computation.2 | async-start | bytes 1048576 | tf_op jit(solution)/shard_map/all_to_all | solution.py:580
  54.0 1.3 collective-permute-start.3
  55.3 2.4 %collective-permute-start.4 = (bf16[496,128]{1,0:T(8,128)(2,1)S(1)}, bf16[496,128]{1,0:T(8,128)(2,1)S(1)}, u32[]{:S(2)}, u32[]{:S(2)}) collective-permute-start(bf16[496,128]{1,0:T(8,128)(2,1)S(1)} %get-tuple-element.58), channel_id=1, source_target_pairs={{0,16},{1,17},{32,48},{33,49},{2,18},{3,19},{34,50},{35,51},{4,20}... | collective-permute-start | bytes 380936 | tf_op jit(solution)/shard_map/ppermute | solution.py:50
  57.7 1.2 collective-permute-start.5
  58.9 7.0 %collective-permute-done.3.refs_7_.refs_1_ = bf16[496,128]{1,0:T(8,128)(2,1)S(1)} collective-permute-done((bf16[496,128]{1,0:T(8,128)(2,1)}, bf16[496,128]{1,0:T(8,128)(2,1)S(1)}, u32[]{:S(2)}, u32[]{:S(2)}) %collective-permute-start.3) | collective-permute-done | bytes 127008 | tf_op jit(solution)/shard_map/ppermute | solution.py:50
  65.8 1.0 collective-permute-done.4.refs_8_.refs_2_
  66.8 3.0 %first_gradient.1 = (f32[3,8,8,256]{3,2,1,0:T(8,128)}, bf16[128,256]{1,0:T(8,128)(2,1)S(1)}, bf16[192,128]{1,0:T(8,128)(2,1)S(1)}, bf16[192,128]{1,0:T(8,128)(2,...) custom-call(s32[3,16]{1,0:T(4,128)} %refs_0_.7, f32[3,8,8,256]{3,2,1,0:T(8,128)S(1)} %get-tuple-element.53.refs_1_, ...), custom_call_target="tpu_custom_call" | custom-call | flops 226492416 | bytes 3000000 | tf_op jit(solution)/shard_map/first_gradient/pallas_call | solution.py:407
  69.8 1.7 %collective-permute-start.6 = (bf16[192,128]{1,0:T(8,128)(2,1)S(1)}, bf16[192,128]{1,0:T(8,128)(2,1)S(1)}, u32[]{:S(2)}, u32[]{:S(2)}) collective-permute-start(bf16[192,128]{1,0:T(8,128)(2,1)S(1)} %get-tuple-element.64), channel_id=1, source_target_pairs={{0,8},{1,9},{32,40},{33,41},{2,10},{3,11},{34,42},{35,43},{4,12},{... | collective-permute-start | bytes 147464 | tf_op jit(solution)/shard_map/ppermute | solution.py:50
  71.5 2.2 %collective-permute-start.7 = (bf16[192,128]{1,0:T(8,128)(2,1)S(1)}, bf16[192,128]{1,0:T(8,128)(2,1)S(1)}, u32[]{:S(2)}, u32[]{:S(2)}) collective-permute-start(bf16[192,128]{1,0:T(8,128)(2,1)S(1)} %get-tuple-element.65), channel_id=1, source_target_pairs={{0,16},{1,17},{32,48},{33,49},{2,18},{3,19},{34,50},{35,51},{4,20}... | collective-permute-start | bytes 147464 | tf_op jit(solution)/shard_map/ppermute | solution.py:50
  73.7 0.5 collective-permute-start.8
  74.2 0.7 slope_terms.2
  75.0 1.3 collective-permute-done.7.refs_6_
  76.2 0.7 collective-permute-done.8.refs_7_
  77.0 1.8 %slope_terms.3 = (f32[4,144,128]{2,1,0:T(8,128)S(1)}, f32[4,144,128]{2,1,0:T(8,128)S(1)}, bf16[1024,256]{1,0:T(8,128)(2,1)}) custom-call(bf16[304,128]{1,0:T(8,128)(2,1)} %get-tuple-element.62.refs_0_, bf16[304,128]{1,0:T(8,128)(2,1)S(1)} %collective-permute-done.refs_9_.refs_1_, bf16[304,128]{1,0:T(8,128)(2,1)S(1)} %collective-permute-done.1.refs_10_.refs_2_, ...), custom_call_target="tpu_custom_call" | custom-call | flops 226492416 | bytes 3000000 | tf_op jit(solution)/shard_map/slope_terms/pallas_call | solution.py:407
  78.8 6.6 %all-to-all-start.3 = ((bf16[32,32,256]{2,1,0:T(8,128)(2,1)}), bf16[32,32,256]{2,1,0:T(8,128)(2,1)S(1)}, u32[]{:S(2)}, u32[]{:S(2)}) async-start(bf16[32,32,256]{2,1,0:T(8,128)(2,1)} %bitcast.11), calls=%async_computation.3 | async-start | bytes 1048576 | tf_op jit(solution)/shard_map/all_to_all | solution.py:580
  85.3 3.5 %collective-permute-start.10 = (f32[4,144,128]{2,1,0:T(8,128)S(1)}, f32[4,144,128]{2,1,0:T(8,128)S(1)}, u32[]{:S(2)}, u32[]{:S(2)}) collective-permute-start(f32[4,144,128]{2,1,0:T(8,128)S(1)} %get-tuple-element.73), channel_id=1, source_target_pairs={{0,1},{1,0},{32,33},{33,32},{2,3},{3,2},{34,35},{35,34},{4,5},{5,4... | collective-permute-start | bytes 884744 | tf_op jit(solution)/shard_map/ppermute | solution.py:50
  88.8 0.1 collective-permute-start.9
  88.9 1.1 collective-permute-done.10.refs_3_
  90.1 0.4 collective-permute-done.9.refs_1_
  90.5 0.1 pair_sum.1
  90.6 1.6 %collective-permute-start.11 = (f32[288,128]{1,0:T(8,128)S(1)}, f32[288,128]{1,0:T(8,128)S(1)}, u32[]{:S(2)}, u32[]{:S(2)}) collective-permute-start(f32[288,128]{1,0:T(8,128)S(1)} %get-tuple-element.75), channel_id=1, source_target_pairs={{0,64},{1,65},{32,96},{33,97},{2,66},{3,67},{34,98},{35,99},{4,68}... | collective-permute-start | bytes 442376 | tf_op jit(solution)/shard_map/ppermute | solution.py:50
  92.1 2.4 %collective-permute-start.12 = (f32[288,128]{1,0:T(8,128)S(1)}, f32[288,128]{1,0:T(8,128)S(1)}, u32[]{:S(2)}, u32[]{:S(2)}) collective-permute-start(f32[288,128]{1,0:T(8,128)S(1)} %get-tuple-element.76), channel_id=1, source_target_pairs={{0,128},{1,129},{32,160},{33,161},{2,130},{3,131},{34,162},{35,163... | collective-permute-start | bytes 442376 | tf_op jit(solution)/shard_map/ppermute | solution.py:50
  94.6 1.1 collective-permute-start.13
  95.7 4.0 %collective-permute-done.11.refs_1_ = f32[288,128]{1,0:T(8,128)S(1)} collective-permute-done((f32[288,128]{1,0:T(8,128)S(1)}, f32[288,128]{1,0:T(8,128)S(1)}, u32[]{:S(2)}, u32[]{:S(2)}) %collective-permute-start.11) | collective-permute-done | bytes 147488 | tf_op jit(solution)/shard_map/ppermute | solution.py:50
  99.8 3.4 %collective-permute-done.12.refs_2_ = f32[288,128]{1,0:T(8,128)S(1)} collective-permute-done((f32[288,128]{1,0:T(8,128)S(1)}, f32[288,128]{1,0:T(8,128)S(1)}, u32[]{:S(2)}, u32[]{:S(2)}) %collective-permute-start.12) | collective-permute-done | bytes 147488 | tf_op jit(solution)/shard_map/ppermute | solution.py:50
  103.2 0.1 row_sum.1
  103.3 15.8 %all_to_all.60 = f32[8,36,128]{2,1,0:T(8,128)S(1)} all-to-all(f32[8,36,128]{2,1,0:T(8,128)S(1)} %row_sum.1), channel_id=1, replica_groups={{0,32,2,34,4,36,6,38},{1,33,3,35,5,37,7,39},{64,96,66,98,68,100,70,102}..., dimensions={0} | all-to-all | bytes 294912 | tf_op jit(solution)/shard_map/all_to_all | solution.py:544
  119.1 10.1 %all_to_all.61 = bf16[8,36,128]{2,1,0:T(8,128)(2,1)S(1)} all-to-all(bf16[8,36,128]{2,1,0:T(8,128)(2,1)S(1)} %broadcast_in_dim.17), channel_id=1, replica_groups={{0,32,2,34,4,36,6,38},{1,33,3,35,5,37,7,39},{64,96,66,98,68,100,70,102}..., dimensions={0} | all-to-all | bytes 147456 | tf_op jit(solution)/shard_map/all_to_all | solution.py:544
  129.2 0.2 broadcast_in_dim.19
  129.3 17.3 %all_to_all.62.refs_0_ = bf16[16,288,128]{2,1,0:T(8,128)(2,1)S(1)} all-to-all(bf16[16,288,128]{2,1,0:T(8,128)(2,1)S(1)} %broadcast_in_dim.19), channel_id=1, replica_groups={{0,64,128,192,8,72,136,200,16,80,144,208,24,88,152,216},{1,65,129,193,9..., dimensions={0} | all-to-all | bytes 2359296 | tf_op jit(solution)/shard_map/all_to_all | solution.py:544
  146.7 5.3 %collective-permute-start.14 = (bf16[16,288,128]{2,1,0:T(8,128)(2,1)S(1)}, bf16[16,288,128]{2,1,0:T(8,128)(2,1)S(1)}, u32[]{:S(2)}, u32[]{:S(2)}) collective-permute-start(bf16[16,288,128]{2,1,0:T(8,128)(2,1)S(1)} %all_to_all.62.refs_0_), channel_id=1, source_target_pairs={{0,1},{1,0},{32,33},{33,32},{2,3},{3,2},{34,35},{35,34},{4,5},{5,4... | collective-permute-start | bytes 3538952 | tf_op jit(solution)/shard_map/ppermute | solution.py:50
  152.0 1.9 %last_gradient.1 = f32[3,8,8,256]{3,2,1,0:T(8,128)} custom-call(f32[3,8,8,256]{3,2,1,0:T(8,128)} %get-tuple-element.60.refs_0_, f32[192,256]{1,0:T(8,128)} %get-tuple-element.61.refs_1_, bf16[1024,256]{1,0:T(8,128)(2,1)S(1)} %bitcast.17, bf16[128,256]{1,0:T(8,128)(2,1)S(1)} %get-tuple-element.67.refs_9_.refs_3_, ...), custom_call_target="tpu_custom_call" | custom-call | flops 1000 | bytes 3000000 | tf_op jit(solution)/shard_map/last_gradient/pallas_call | solution.py:407
  153.9 0.5 collective-permute-done.14.refs_1_
  154.5 3.0 %spread_slopes.1 = (f32[9,256,256]{2,1,0:T(8,128)}, f32[9,256,256]{2,1,0:T(8,128)}) custom-call(bf16[16,288,128]{2,1,0:T(8,128)(2,1)S(1)} %all_to_all.62.refs_0_, bf16[16,288,128]{2,1,0:T(8,128)(2,1)S(1)} %collective-permute-done.14.refs_1_), custom_call_target="tpu_custom_call" | custom-call | flops 1000 | bytes 3000000 | tf_op jit(solution)/shard_map/spread_slopes/pallas_call | solution.py:407
  (15 shorter events, 0.1 us)
Async XLA Ops:
  0.6 21.6 %copy-start.2 = (bf16[1,3,8,8,256]{4,3,2,1,0:T(8,128)(2,1)S(1)}, bf16[1,3,8,8,256]{4,3,2,1,0:T(8,128)(2,1)}, u32[]{:S(2)}) copy-start(bf16[1,3,8,8,256]{4,3,2,1,0:T(8,128)(2,1)} %param.5) | copy-start | bytes 294916
  0.6 21.6 %copy-start = (bf16[3,3,256,256]{3,2,1,0:T(8,128)(2,1)S(1)}, bf16[3,3,256,256]{3,2,1,0:T(8,128)(2,1)}, u32[]{:S(2)}) copy-start(bf16[3,3,256,256]{3,2,1,0:T(8,128)(2,1)} %param.7) | copy-start | bytes 3538948
  22.2 20.6 %copy-start.1 = (bf16[3,3,256,256]{3,2,1,0:T(8,128)(2,1)S(1)}, bf16[3,3,256,256]{3,2,1,0:T(8,128)(2,1)}, u32[]{:S(2)}) copy-start(bf16[3,3,256,256]{3,2,1,0:T(8,128)(2,1)} %param.8) | copy-start | bytes 3538948
  25.6 17.3 %all-to-all-start.1 = ((bf16[32,32,256]{2,1,0:T(8,128)(2,1)}), bf16[32,32,256]{2,1,0:T(8,128)(2,1)S(1)}, u32[]{:S(2)}, u32[]{:S(2)}) async-start(bf16[32,32,256]{2,1,0:T(8,128)(2,1)} %bitcast.5), calls=%async_computation.1 | async-start | bytes 1048576 | tf_op jit(solution)/shard_map/all_to_all | solution.py:580
  31.4 10.3 %collective-permute-start = (bf16[304,128]{1,0:T(8,128)(2,1)S(1)}, bf16[304,128]{1,0:T(8,128)(2,1)S(1)}, u32[]{:S(2)}, u32[]{:S(2)}) collective-permute-start(bf16[304,128]{1,0:T(8,128)(2,1)S(1)} %get-tuple-element.49), channel_id=1, source_target_pairs={{0,8},{1,9},{32,40},{33,41},{2,10},{3,11},{34,42},{35,43},{4,12},{... | collective-permute-start | bytes 233480 | tf_op jit(solution)/shard_map/ppermute | solution.py:50
  32.7 10.2 %collective-permute-start.1 = (bf16[304,128]{1,0:T(8,128)(2,1)S(1)}, bf16[304,128]{1,0:T(8,128)(2,1)S(1)}, u32[]{:S(2)}, u32[]{:S(2)}) collective-permute-start(bf16[304,128]{1,0:T(8,128)(2,1)S(1)} %get-tuple-element.50), channel_id=1, source_target_pairs={{0,16},{1,17},{32,48},{33,49},{2,18},{3,19},{34,50},{35,51},{4,20}... | collective-permute-start | bytes 233480 | tf_op jit(solution)/shard_map/ppermute | solution.py:50
  35.1 7.8 %collective-permute-start.2 = (bf16[304,128]{1,0:T(8,128)(2,1)S(1)}, bf16[304,128]{1,0:T(8,128)(2,1)S(1)}, u32[]{:S(2)}, u32[]{:S(2)}) collective-permute-start(bf16[304,128]{1,0:T(8,128)(2,1)S(1)} %get-tuple-element.51), channel_id=1, source_target_pairs={{0,24},{1,25},{32,56},{33,57},{2,26},{3,27},{34,58},{35,59},{4,28}... | collective-permute-start | bytes 233480 | tf_op jit(solution)/shard_map/ppermute | solution.py:50
  46.9 0.7 copy-start.3
  47.6 19.2 %all-to-all-start.2 = ((bf16[32,32,256]{2,1,0:T(8,128)(2,1)}), bf16[32,32,256]{2,1,0:T(8,128)(2,1)S(1)}, u32[]{:S(2)}, u32[]{:S(2)}) async-start(bf16[32,32,256]{2,1,0:T(8,128)(2,1)} %bitcast.9), calls=%async_computation.2 | async-start | bytes 1048576 | tf_op jit(solution)/shard_map/all_to_all | solution.py:580
  54.0 11.9 %collective-permute-start.3 = (bf16[496,128]{1,0:T(8,128)(2,1)}, bf16[496,128]{1,0:T(8,128)(2,1)S(1)}, u32[]{:S(2)}, u32[]{:S(2)}) collective-permute-start(bf16[496,128]{1,0:T(8,128)(2,1)} %copy-done.3), channel_id=1, source_target_pairs={{0,8},{1,9},{32,40},{33,41},{2,10},{3,11},{34,42},{35,43},{4,12},{... | collective-permute-start | bytes 380936 | tf_op jit(solution)/shard_map/ppermute | solution.py:50
  55.3 11.5 %collective-permute-start.4 = (bf16[496,128]{1,0:T(8,128)(2,1)S(1)}, bf16[496,128]{1,0:T(8,128)(2,1)S(1)}, u32[]{:S(2)}, u32[]{:S(2)}) collective-permute-start(bf16[496,128]{1,0:T(8,128)(2,1)S(1)} %get-tuple-element.58), channel_id=1, source_target_pairs={{0,16},{1,17},{32,48},{33,49},{2,18},{3,19},{34,50},{35,51},{4,20}... | collective-permute-start | bytes 380936 | tf_op jit(solution)/shard_map/ppermute | solution.py:50
  57.7 9.1 %collective-permute-start.5 = (bf16[496,128]{1,0:T(8,128)(2,1)S(1)}, bf16[496,128]{1,0:T(8,128)(2,1)S(1)}, u32[]{:S(2)}, u32[]{:S(2)}) collective-permute-start(bf16[496,128]{1,0:T(8,128)(2,1)S(1)} %get-tuple-element.59), channel_id=1, source_target_pairs={{0,24},{1,25},{32,56},{33,57},{2,26},{3,27},{34,58},{35,59},{4,28}... | collective-permute-start | bytes 380936 | tf_op jit(solution)/shard_map/ppermute | solution.py:50
  69.8 5.1 %collective-permute-start.6 = (bf16[192,128]{1,0:T(8,128)(2,1)S(1)}, bf16[192,128]{1,0:T(8,128)(2,1)S(1)}, u32[]{:S(2)}, u32[]{:S(2)}) collective-permute-start(bf16[192,128]{1,0:T(8,128)(2,1)S(1)} %get-tuple-element.64), channel_id=1, source_target_pairs={{0,8},{1,9},{32,40},{33,41},{2,10},{3,11},{34,42},{35,43},{4,12},{... | collective-permute-start | bytes 147464 | tf_op jit(solution)/shard_map/ppermute | solution.py:50
  71.5 4.7 %collective-permute-start.7 = (bf16[192,128]{1,0:T(8,128)(2,1)S(1)}, bf16[192,128]{1,0:T(8,128)(2,1)S(1)}, u32[]{:S(2)}, u32[]{:S(2)}) collective-permute-start(bf16[192,128]{1,0:T(8,128)(2,1)S(1)} %get-tuple-element.65), channel_id=1, source_target_pairs={{0,16},{1,17},{32,48},{33,49},{2,18},{3,19},{34,50},{35,51},{4,20}... | collective-permute-start | bytes 147464 | tf_op jit(solution)/shard_map/ppermute | solution.py:50
  73.7 3.2 %collective-permute-start.8 = (bf16[192,128]{1,0:T(8,128)(2,1)S(1)}, bf16[192,128]{1,0:T(8,128)(2,1)S(1)}, u32[]{:S(2)}, u32[]{:S(2)}) collective-permute-start(bf16[192,128]{1,0:T(8,128)(2,1)S(1)} %get-tuple-element.66), channel_id=1, source_target_pairs={{0,24},{1,25},{32,56},{33,57},{2,26},{3,27},{34,58},{35,59},{4,28}... | collective-permute-start | bytes 147464 | tf_op jit(solution)/shard_map/ppermute | solution.py:50
  78.8 24.4 %all-to-all-start.3 = ((bf16[32,32,256]{2,1,0:T(8,128)(2,1)}), bf16[32,32,256]{2,1,0:T(8,128)(2,1)S(1)}, u32[]{:S(2)}, u32[]{:S(2)}) async-start(bf16[32,32,256]{2,1,0:T(8,128)(2,1)} %bitcast.11), calls=%async_computation.3 | async-start | bytes 1048576 | tf_op jit(solution)/shard_map/all_to_all | solution.py:580
  85.3 4.7 %collective-permute-start.10 = (f32[4,144,128]{2,1,0:T(8,128)S(1)}, f32[4,144,128]{2,1,0:T(8,128)S(1)}, u32[]{:S(2)}, u32[]{:S(2)}) collective-permute-start(f32[4,144,128]{2,1,0:T(8,128)S(1)} %get-tuple-element.73), channel_id=1, source_target_pairs={{0,1},{1,0},{32,33},{33,32},{2,3},{3,2},{34,35},{35,34},{4,5},{5,4... | collective-permute-start | bytes 884744 | tf_op jit(solution)/shard_map/ppermute | solution.py:50
  88.8 1.6 %collective-permute-start.9 = (f32[4,144,128]{2,1,0:T(8,128)S(1)}, f32[4,144,128]{2,1,0:T(8,128)S(1)}, u32[]{:S(2)}, u32[]{:S(2)}) collective-permute-start(f32[4,144,128]{2,1,0:T(8,128)S(1)} %get-tuple-element.72), channel_id=1, source_target_pairs={{0,1},{1,0},{32,33},{33,32},{2,3},{3,2},{34,35},{35,34},{4,5},{5,4... | collective-permute-start | bytes 884744 | tf_op jit(solution)/shard_map/ppermute | solution.py:50
  90.6 9.2 %collective-permute-start.11 = (f32[288,128]{1,0:T(8,128)S(1)}, f32[288,128]{1,0:T(8,128)S(1)}, u32[]{:S(2)}, u32[]{:S(2)}) collective-permute-start(f32[288,128]{1,0:T(8,128)S(1)} %get-tuple-element.75), channel_id=1, source_target_pairs={{0,64},{1,65},{32,96},{33,97},{2,66},{3,67},{34,98},{35,99},{4,68}... | collective-permute-start | bytes 442376 | tf_op jit(solution)/shard_map/ppermute | solution.py:50
  92.1 11.0 %collective-permute-start.12 = (f32[288,128]{1,0:T(8,128)S(1)}, f32[288,128]{1,0:T(8,128)S(1)}, u32[]{:S(2)}, u32[]{:S(2)}) collective-permute-start(f32[288,128]{1,0:T(8,128)S(1)} %get-tuple-element.76), channel_id=1, source_target_pairs={{0,128},{1,129},{32,160},{33,161},{2,130},{3,131},{34,162},{35,163... | collective-permute-start | bytes 442376 | tf_op jit(solution)/shard_map/ppermute | solution.py:50
  94.6 8.6 %collective-permute-start.13 = (f32[288,128]{1,0:T(8,128)S(1)}, f32[288,128]{1,0:T(8,128)S(1)}, u32[]{:S(2)}, u32[]{:S(2)}) collective-permute-start(f32[288,128]{1,0:T(8,128)S(1)} %get-tuple-element.77), channel_id=1, source_target_pairs={{0,192},{1,193},{32,224},{33,225},{2,194},{3,195},{34,226},{35,227... | collective-permute-start | bytes 442376 | tf_op jit(solution)/shard_map/ppermute | solution.py:50
  146.7 7.8 %collective-permute-start.14 = (bf16[16,288,128]{2,1,0:T(8,128)(2,1)S(1)}, bf16[16,288,128]{2,1,0:T(8,128)(2,1)S(1)}, u32[]{:S(2)}, u32[]{:S(2)}) collective-permute-start(bf16[16,288,128]{2,1,0:T(8,128)(2,1)S(1)} %all_to_all.62.refs_0_), channel_id=1, source_target_pairs={{0,1},{1,0},{32,33},{33,32},{2,3},{3,2},{34,35},{35,34},{4,5},{5,4... | collective-permute-start | bytes 3538952 | tf_op jit(solution)/shard_map/ppermute | solution.py:50

commit v8 on v7

--- a/solution.py
+++ b/solution.py
@@ -297,7 +297,7 @@
 def third_kernel(
     place, links, inner_ref, pre_ref, recv_ref, old_ref, unpack_ref, weights, *refs,
 ):
-    last_ref, frame_ref, part0, part1, part2, part3, grid, frame, got, column = refs[3:]
+    last_ref, frame_ref, part0, part1, part2, part3, grid, frame, got, column = refs
     unpack_frame(unpack_ref, recv_ref, old_ref, got)
     grid[:, 1:9, 1:9, :] = inner_ref[...]
     add_returns(grid, got)
@@ -632,8 +632,8 @@
     last, frame, *parts = run(
         third_kernel,
         "first_gradient",
-        (tile_links, inner, pre_first, recv, frame, unpack, first_weights, *closing_parts[1:]),
-        [moved_in, near, moved_in] + [near] * 3 + [moved_in] + [left] * 3,
+        (tile_links, inner, pre_first, recv, frame, unpack, first_weights),
+        [moved_in, near, moved_in] + [near] * 3 + [moved_in],
         (inner_like, frame_like) + (like(192, 128),) * 4,
         [grid_shape, frame_shape, frame_shape, column_shape],
         conv_flops,

time: 158 us -> 154 us (0.975)
  waiting for transfers between devices: 26 us -> 20.9 us
    ppermute x15, waiting for transfers between devices: 26 us -> 16.6 us  [shifted(): return lax.ppermute(values, ('tile', 'ens'), pairs)]
    all_to_all x3, waiting for transfers between devices: 0.01 us -> 4.34 us  [exchange(): return lax.all_to_all(values, 'tile', 0, 0, tiled=True)]
    ppermute x15, starting transfers between devices: 28.3 us -> 30 us  [shifted(): return lax.ppermute(values, ('tile', 'ens'), pairs)]
  transfers between devices with their start and end apart: 18 -> 18, of which waited for: 11 -> 9; matrix products, arithmetic and copies ran while one was open for 0% -> 0% of each run, Pallas kernels for 2% -> 4%
where the time goes in v8:
time: 154 us; the launch traced here: 153 us
  blocking collectives  62.1 us (40%)
  starting transfers between devices  48.2 us (31%)
  waiting for transfers between devices  20.9 us (14%)
  Pallas kernels  20.6 us (13%)
    all_to_all x3, blocking collectives, trade(): lax.all_to_all(values, ('tile', 'ens'), 0, 0, axis_index_groups=groups(al...  43.2 us
    ppermute x15, starting transfers between devices, shifted(): return lax.ppermute(values, ('tile', 'ens'), pairs)  30 us
    pallas_call x10, Pallas kernels, run(): pl.pallas_call(body, out_shape=tuple((pltpu.HBM(out.shape, out.dtype) if...  20.6 us
    all_to_all x1, blocking collectives, exchange(): return lax.all_to_all(values, 'tile', 0, 0, tiled=True)  18.9 us
    all_to_all x3, starting transfers between devices, exchange(): return lax.all_to_all(values, 'tile', 0, 0, tiled=True)  18.1 us
    ppermute x15, waiting for transfers between devices, shifted(): return lax.ppermute(values, ('tile', 'ens'), pairs)  16.6 us
    all_to_all x3, waiting for transfers between devices, exchange(): return lax.all_to_all(values, 'tile', 0, 0, tiled=True)  4.34 us
  transfers between devices with their start and end apart: 18, of which 9 were waited for; matrix products, arithmetic and copies ran while one was open for 0% of the time, Pallas kernels for 4%

profile of v8, /device:TPU:1, one launch (start us, length us, event | category | flops | bytes accessed | tf_op | source)
XLA Modules:
  0.0 153.0 jit_solution(13861069268652044034)
XLA Ops:
  0.6 0.0 copy-start.2
  0.6 0.0 copy-start
  0.7 2.6 %routes.1 = (bf16[1024,128]{1,0:T(8,128)(2,1)S(1)}, bf16[128,1152]{1,0:T(8,128)(2,1)S(1)}, bf16[128,256]{1,0:T(8,128)(2,1)S(1)}, bf16[1024,256]{1,0:T(8,128)(2,1)S(1)}) custom-call(s32[3,16]{1,0:T(4,128)} %refs_0_.7, bf16[192,256]{1,0:T(8,128)(2,1)} %bitcast.25), custom_call_target="tpu_custom_call" | custom-call | flops 67108864 | bytes 3000000 | tf_op jit(solution)/shard_map/routes/pallas_call | solution.py:407
  3.3 18.9 %all_to_all.59 = bf16[32,32,256]{2,1,0:T(8,128)(2,1)S(1)} all-to-all(bf16[32,32,256]{2,1,0:T(8,128)(2,1)S(1)} %bitcast.24), channel_id=1, replica_groups=mesh['tile'=32,'ens'=8] {'tile'}, dimensions={0} | all-to-all | bytes 1048576 | tf_op jit(solution)/shard_map/all_to_all | solution.py:580
  22.2 3.4 %first_layer.1 = (bf16[192,256]{1,0:T(8,128)(2,1)S(1)}, f32[192,256]{1,0:T(8,128)}, bf16[128,256]{1,0:T(8,128)(2,1)S(1)}, bf16[1024,256]{1,0:T(8,128)(2,1)}, bf1...) custom-call(s32[3,16]{1,0:T(4,128)} %refs_0_.7, ...), custom_call_target="tpu_custom_call" | custom-call | flops 226492416 | bytes 3000000 | tf_op jit(solution)/shard_map/first_layer/pallas_call | solution.py:407
  25.6 5.8 %all-to-all-start.1 = ((bf16[32,32,256]{2,1,0:T(8,128)(2,1)}), bf16[32,32,256]{2,1,0:T(8,128)(2,1)S(1)}, u32[]{:S(2)}, u32[]{:S(2)}) async-start(bf16[32,32,256]{2,1,0:T(8,128)(2,1)} %bitcast.5), calls=%async_computation.1 | async-start | bytes 1048576 | tf_op jit(solution)/shard_map/all_to_all | solution.py:580
  31.4 1.3 collective-permute-start
  32.7 2.4 %collective-permute-start.1 = (bf16[304,128]{1,0:T(8,128)(2,1)S(1)}, bf16[304,128]{1,0:T(8,128)(2,1)S(1)}, u32[]{:S(2)}, u32[]{:S(2)}) collective-permute-start(bf16[304,128]{1,0:T(8,128)(2,1)S(1)} %get-tuple-element.50), channel_id=1, source_target_pairs={{0,16},{1,17},{32,48},{33,49},{2,18},{3,19},{34,50},{35,51},{4,20}... | collective-permute-start | bytes 233480 | tf_op jit(solution)/shard_map/ppermute | solution.py:50
  35.1 1.2 collective-permute-start.2
  36.2 5.4 %collective-permute-done.refs_9_.refs_1_ = bf16[304,128]{1,0:T(8,128)(2,1)S(1)} collective-permute-done((bf16[304,128]{1,0:T(8,128)(2,1)S(1)}, bf16[304,128]{1,0:T(8,128)(2,1)S(1)}, u32[]{:S(2)}, u32[]{:S(2)}) %collective-permute-start) | collective-permute-done | bytes 77856 | tf_op jit(solution)/shard_map/ppermute | solution.py:50
  41.7 1.2 collective-permute-done.1.refs_10_.refs_2_
  42.8 4.1 %second_layer.1 = (bf16[192,256]{1,0:T(8,128)(2,1)}, f32[192,256]{1,0:T(8,128)}, f32[3,8,8,256]{3,2,1,0:T(8,128)S(1)}, bf16[128,256]{1,0:T(8,128)(2,1)S(1)}, bf1...) custom-call(s32[3,16]{1,0:T(4,128)} %refs_0_.7, ...), custom_call_target="tpu_custom_call" | custom-call | flops 452984832 | bytes 3000000 | tf_op jit(solution)/shard_map/second_layer/pallas_call | solution.py:407
  46.9 6.4 %all-to-all-start.2 = ((bf16[32,32,256]{2,1,0:T(8,128)(2,1)}), bf16[32,32,256]{2,1,0:T(8,128)(2,1)S(1)}, u32[]{:S(2)}, u32[]{:S(2)}) async-start(bf16[32,32,256]{2,1,0:T(8,128)(2,1)} %bitcast.9), calls=%async_computation.2 | async-start | bytes 1048576 | tf_op jit(solution)/shard_map/all_to_all | solution.py:580
  53.3 1.3 collective-permute-start.6
  54.6 2.4 %collective-permute-start.7 = (bf16[496,128]{1,0:T(8,128)(2,1)S(1)}, bf16[496,128]{1,0:T(8,128)(2,1)S(1)}, u32[]{:S(2)}, u32[]{:S(2)}) collective-permute-start(bf16[496,128]{1,0:T(8,128)(2,1)S(1)} %get-tuple-element.67), channel_id=1, source_target_pairs={{0,16},{1,17},{32,48},{33,49},{2,18},{3,19},{34,50},{35,51},{4,20}... | collective-permute-start | bytes 380936 | tf_op jit(solution)/shard_map/ppermute | solution.py:50
  57.0 1.2 collective-permute-start.8
  58.2 4.3 %all-to-all-done.2 = bf16[32,32,256]{2,1,0:T(8,128)(2,1)S(1)} async-done(((bf16[32,32,256]{2,1,0:T(8,128)(2,1)}), bf16[32,32,256]{2,1,0:T(8,128)(2,1)S(1)}, u32[]{:S(2)}, u32[]{:S(2)}) %all-to-all-start.2) | async-done | bytes 524320 | tf_op jit(solution)/shard_map/all_to_all | solution.py:580
  62.6 3.0 %first_gradient.1 = (f32[3,8,8,256]{3,2,1,0:T(8,128)}, bf16[128,256]{1,0:T(8,128)(2,1)S(1)}, bf16[192,128]{1,0:T(8,128)(2,1)S(1)}, bf16[192,128]{1,0:T(8,128)(2,...) custom-call(s32[3,16]{1,0:T(4,128)} %refs_0_.7, f32[3,8,8,256]{3,2,1,0:T(8,128)S(1)} %get-tuple-element.53.refs_1_, ...), custom_call_target="tpu_custom_call" | custom-call | flops 226492416 | bytes 3000000 | tf_op jit(solution)/shard_map/first_gradient/pallas_call | solution.py:407
  65.6 1.2 collective-permute-start.3
  66.8 1.4 collective-permute-start.4
  68.2 0.0 collective-permute-done.6.refs_1_
  68.2 1.8 %collective-permute-start.5 = (bf16[192,128]{1,0:T(8,128)(2,1)S(1)}, bf16[192,128]{1,0:T(8,128)(2,1)S(1)}, u32[]{:S(2)}, u32[]{:S(2)}) collective-permute-start(bf16[192,128]{1,0:T(8,128)(2,1)S(1)} %get-tuple-element.63), channel_id=1, source_target_pairs={{0,24},{1,25},{32,56},{33,57},{2,26},{3,27},{34,58},{35,59},{4,28}... | collective-permute-start | bytes 147464 | tf_op jit(solution)/shard_map/ppermute | solution.py:50
  70.0 0.0 collective-permute-done.7.refs_2_
  70.0 0.0 collective-permute-done.8.refs_3_
  70.0 0.7 slope_terms.2
  70.7 0.0 collective-permute-done.3.refs_5_
  70.7 0.5 collective-permute-done.4.refs_6_
  71.2 1.8 %slope_terms.3 = (f32[4,144,128]{2,1,0:T(8,128)S(1)}, f32[4,144,128]{2,1,0:T(8,128)S(1)}, bf16[1024,256]{1,0:T(8,128)(2,1)}) custom-call(bf16[304,128]{1,0:T(8,128)(2,1)} %get-tuple-element.59.refs_0_, bf16[304,128]{1,0:T(8,128)(2,1)S(1)} %collective-permute-done.refs_9_.refs_1_, bf16[304,128]{1,0:T(8,128)(2,1)S(1)} %collective-permute-done.1.refs_10_.refs_2_, ...), custom_call_target="tpu_custom_call" | custom-call | flops 226492416 | bytes 3000000 | tf_op jit(solution)/shard_map/slope_terms/pallas_call | solution.py:407
  73.0 5.9 %all-to-all-start.3 = ((bf16[32,32,256]{2,1,0:T(8,128)(2,1)}), bf16[32,32,256]{2,1,0:T(8,128)(2,1)S(1)}, u32[]{:S(2)}, u32[]{:S(2)}) async-start(bf16[32,32,256]{2,1,0:T(8,128)(2,1)} %bitcast.11), calls=%async_computation.3 | async-start | bytes 1048576 | tf_op jit(solution)/shard_map/all_to_all | solution.py:580
  79.0 5.2 %collective-permute-start.10 = (f32[4,144,128]{2,1,0:T(8,128)S(1)}, f32[4,144,128]{2,1,0:T(8,128)S(1)}, u32[]{:S(2)}, u32[]{:S(2)}) collective-permute-start(f32[4,144,128]{2,1,0:T(8,128)S(1)} %get-tuple-element.73), channel_id=1, source_target_pairs={{0,1},{1,0},{32,33},{33,32},{2,3},{3,2},{34,35},{35,34},{4,5},{5,4... | collective-permute-start | bytes 884744 | tf_op jit(solution)/shard_map/ppermute | solution.py:50
  84.2 0.1 collective-permute-start.9
  84.3 1.1 collective-permute-done.10.refs_3_
  85.4 0.4 collective-permute-done.9.refs_1_
  85.8 0.1 pair_sum.1
  85.9 1.6 %collective-permute-start.11 = (f32[288,128]{1,0:T(8,128)S(1)}, f32[288,128]{1,0:T(8,128)S(1)}, u32[]{:S(2)}, u32[]{:S(2)}) collective-permute-start(f32[288,128]{1,0:T(8,128)S(1)} %get-tuple-element.75), channel_id=1, source_target_pairs={{0,64},{1,65},{32,96},{33,97},{2,66},{3,67},{34,98},{35,99},{4,68}... | collective-permute-start | bytes 442376 | tf_op jit(solution)/shard_map/ppermute | solution.py:50
  87.5 2.4 %collective-permute-start.12 = (f32[288,128]{1,0:T(8,128)S(1)}, f32[288,128]{1,0:T(8,128)S(1)}, u32[]{:S(2)}, u32[]{:S(2)}) collective-permute-start(f32[288,128]{1,0:T(8,128)S(1)} %get-tuple-element.76), channel_id=1, source_target_pairs={{0,128},{1,129},{32,160},{33,161},{2,130},{3,131},{34,162},{35,163... | collective-permute-start | bytes 442376 | tf_op jit(solution)/shard_map/ppermute | solution.py:50
  89.9 1.1 collective-permute-start.13
  91.1 3.9 %collective-permute-done.11.refs_1_ = f32[288,128]{1,0:T(8,128)S(1)} collective-permute-done((f32[288,128]{1,0:T(8,128)S(1)}, f32[288,128]{1,0:T(8,128)S(1)}, u32[]{:S(2)}, u32[]{:S(2)}) %collective-permute-start.11) | collective-permute-done | bytes 147488 | tf_op jit(solution)/shard_map/ppermute | solution.py:50
  95.0 3.5 %collective-permute-done.12.refs_2_ = f32[288,128]{1,0:T(8,128)S(1)} collective-permute-done((f32[288,128]{1,0:T(8,128)S(1)}, f32[288,128]{1,0:T(8,128)S(1)}, u32[]{:S(2)}, u32[]{:S(2)}) %collective-permute-start.12) | collective-permute-done | bytes 147488 | tf_op jit(solution)/shard_map/ppermute | solution.py:50
  98.6 0.1 row_sum.1
  98.6 15.8 %all_to_all.60 = f32[8,36,128]{2,1,0:T(8,128)S(1)} all-to-all(f32[8,36,128]{2,1,0:T(8,128)S(1)} %row_sum.1), channel_id=1, replica_groups={{0,32,2,34,4,36,6,38},{1,33,3,35,5,37,7,39},{64,96,66,98,68,100,70,102}..., dimensions={0} | all-to-all | bytes 294912 | tf_op jit(solution)/shard_map/all_to_all | solution.py:544
  114.4 10.1 %all_to_all.61 = bf16[8,36,128]{2,1,0:T(8,128)(2,1)S(1)} all-to-all(bf16[8,36,128]{2,1,0:T(8,128)(2,1)S(1)} %broadcast_in_dim.17), channel_id=1, replica_groups={{0,32,2,34,4,36,6,38},{1,33,3,35,5,37,7,39},{64,96,66,98,68,100,70,102}..., dimensions={0} | all-to-all | bytes 147456 | tf_op jit(solution)/shard_map/all_to_all | solution.py:544
  124.5 0.2 broadcast_in_dim.19
  124.7 17.3 %all_to_all.62.refs_0_ = bf16[16,288,128]{2,1,0:T(8,128)(2,1)S(1)} all-to-all(bf16[16,288,128]{2,1,0:T(8,128)(2,1)S(1)} %broadcast_in_dim.19), channel_id=1, replica_groups={{0,64,128,192,8,72,136,200,16,80,144,208,24,88,152,216},{1,65,129,193,9..., dimensions={0} | all-to-all | bytes 2359296 | tf_op jit(solution)/shard_map/all_to_all | solution.py:544
  142.0 5.3 %collective-permute-start.14 = (bf16[16,288,128]{2,1,0:T(8,128)(2,1)S(1)}, bf16[16,288,128]{2,1,0:T(8,128)(2,1)S(1)}, u32[]{:S(2)}, u32[]{:S(2)}) collective-permute-start(bf16[16,288,128]{2,1,0:T(8,128)(2,1)S(1)} %all_to_all.62.refs_0_), channel_id=1, source_target_pairs={{0,1},{1,0},{32,33},{33,32},{2,3},{3,2},{34,35},{35,34},{4,5},{5,4... | collective-permute-start | bytes 3538952 | tf_op jit(solution)/shard_map/ppermute | solution.py:50
  147.4 1.9 %last_gradient.1 = f32[3,8,8,256]{3,2,1,0:T(8,128)} custom-call(f32[3,8,8,256]{3,2,1,0:T(8,128)} %get-tuple-element.57.refs_0_, f32[192,256]{1,0:T(8,128)} %get-tuple-element.58.refs_1_, bf16[1024,256]{1,0:T(8,128)(2,1)S(1)} %bitcast.17, bf16[128,256]{1,0:T(8,128)(2,1)S(1)} %get-tuple-element.64.refs_9_.refs_3_, ...), custom_call_target="tpu_custom_call" | custom-call | flops 1000 | bytes 3000000 | tf_op jit(solution)/shard_map/last_gradient/pallas_call | solution.py:407
  149.3 0.5 collective-permute-done.14.refs_1_
  149.8 3.0 %spread_slopes.1 = (f32[9,256,256]{2,1,0:T(8,128)}, f32[9,256,256]{2,1,0:T(8,128)}) custom-call(bf16[16,288,128]{2,1,0:T(8,128)(2,1)S(1)} %all_to_all.62.refs_0_, bf16[16,288,128]{2,1,0:T(8,128)(2,1)S(1)} %collective-permute-done.14.refs_1_), custom_call_target="tpu_custom_call" | custom-call | flops 1000 | bytes 3000000 | tf_op jit(solution)/shard_map/spread_slopes/pallas_call | solution.py:407
  (13 shorter events, 0.1 us)
Async XLA Ops:
  0.6 21.6 %copy-start.2 = (bf16[1,3,8,8,256]{4,3,2,1,0:T(8,128)(2,1)S(1)}, bf16[1,3,8,8,256]{4,3,2,1,0:T(8,128)(2,1)}, u32[]{:S(2)}) copy-start(bf16[1,3,8,8,256]{4,3,2,1,0:T(8,128)(2,1)} %param.5) | copy-start | bytes 294916
  0.6 21.6 %copy-start = (bf16[3,3,256,256]{3,2,1,0:T(8,128)(2,1)S(1)}, bf16[3,3,256,256]{3,2,1,0:T(8,128)(2,1)}, u32[]{:S(2)}) copy-start(bf16[3,3,256,256]{3,2,1,0:T(8,128)(2,1)} %param.7) | copy-start | bytes 3538948
  22.2 20.6 %copy-start.1 = (bf16[3,3,256,256]{3,2,1,0:T(8,128)(2,1)S(1)}, bf16[3,3,256,256]{3,2,1,0:T(8,128)(2,1)}, u32[]{:S(2)}) copy-start(bf16[3,3,256,256]{3,2,1,0:T(8,128)(2,1)} %param.8) | copy-start | bytes 3538948
  25.6 17.3 %all-to-all-start.1 = ((bf16[32,32,256]{2,1,0:T(8,128)(2,1)}), bf16[32,32,256]{2,1,0:T(8,128)(2,1)S(1)}, u32[]{:S(2)}, u32[]{:S(2)}) async-start(bf16[32,32,256]{2,1,0:T(8,128)(2,1)} %bitcast.5), calls=%async_computation.1 | async-start | bytes 1048576 | tf_op jit(solution)/shard_map/all_to_all | solution.py:580
  31.4 10.3 %collective-permute-start = (bf16[304,128]{1,0:T(8,128)(2,1)S(1)}, bf16[304,128]{1,0:T(8,128)(2,1)S(1)}, u32[]{:S(2)}, u32[]{:S(2)}) collective-permute-start(bf16[304,128]{1,0:T(8,128)(2,1)S(1)} %get-tuple-element.49), channel_id=1, source_target_pairs={{0,8},{1,9},{32,40},{33,41},{2,10},{3,11},{34,42},{35,43},{4,12},{... | collective-permute-start | bytes 233480 | tf_op jit(solution)/shard_map/ppermute | solution.py:50
  32.7 10.2 %collective-permute-start.1 = (bf16[304,128]{1,0:T(8,128)(2,1)S(1)}, bf16[304,128]{1,0:T(8,128)(2,1)S(1)}, u32[]{:S(2)}, u32[]{:S(2)}) collective-permute-start(bf16[304,128]{1,0:T(8,128)(2,1)S(1)} %get-tuple-element.50), channel_id=1, source_target_pairs={{0,16},{1,17},{32,48},{33,49},{2,18},{3,19},{34,50},{35,51},{4,20}... | collective-permute-start | bytes 233480 | tf_op jit(solution)/shard_map/ppermute | solution.py:50
  35.1 7.8 %collective-permute-start.2 = (bf16[304,128]{1,0:T(8,128)(2,1)S(1)}, bf16[304,128]{1,0:T(8,128)(2,1)S(1)}, u32[]{:S(2)}, u32[]{:S(2)}) collective-permute-start(bf16[304,128]{1,0:T(8,128)(2,1)S(1)} %get-tuple-element.51), channel_id=1, source_target_pairs={{0,24},{1,25},{32,56},{33,57},{2,26},{3,27},{34,58},{35,59},{4,28}... | collective-permute-start | bytes 233480 | tf_op jit(solution)/shard_map/ppermute | solution.py:50
  46.9 15.6 %all-to-all-start.2 = ((bf16[32,32,256]{2,1,0:T(8,128)(2,1)}), bf16[32,32,256]{2,1,0:T(8,128)(2,1)S(1)}, u32[]{:S(2)}, u32[]{:S(2)}) async-start(bf16[32,32,256]{2,1,0:T(8,128)(2,1)} %bitcast.9), calls=%async_computation.2 | async-start | bytes 1048576 | tf_op jit(solution)/shard_map/all_to_all | solution.py:580
  53.3 14.9 %collective-permute-start.6 = (bf16[496,128]{1,0:T(8,128)(2,1)S(1)}, bf16[496,128]{1,0:T(8,128)(2,1)S(1)}, u32[]{:S(2)}, u32[]{:S(2)}) collective-permute-start(bf16[496,128]{1,0:T(8,128)(2,1)S(1)} %get-tuple-element.66), channel_id=1, source_target_pairs={{0,8},{1,9},{32,40},{33,41},{2,10},{3,11},{34,42},{35,43},{4,12},{... | collective-permute-start | bytes 380936 | tf_op jit(solution)/shard_map/ppermute | solution.py:50
  54.6 15.3 %collective-permute-start.7 = (bf16[496,128]{1,0:T(8,128)(2,1)S(1)}, bf16[496,128]{1,0:T(8,128)(2,1)S(1)}, u32[]{:S(2)}, u32[]{:S(2)}) collective-permute-start(bf16[496,128]{1,0:T(8,128)(2,1)S(1)} %get-tuple-element.67), channel_id=1, source_target_pairs={{0,16},{1,17},{32,48},{33,49},{2,18},{3,19},{34,50},{35,51},{4,20}... | collective-permute-start | bytes 380936 | tf_op jit(solution)/shard_map/ppermute | solution.py:50
  57.0 13.0 %collective-permute-start.8 = (bf16[496,128]{1,0:T(8,128)(2,1)S(1)}, bf16[496,128]{1,0:T(8,128)(2,1)S(1)}, u32[]{:S(2)}, u32[]{:S(2)}) collective-permute-start(bf16[496,128]{1,0:T(8,128)(2,1)S(1)} %get-tuple-element.68), channel_id=1, source_target_pairs={{0,24},{1,25},{32,56},{33,57},{2,26},{3,27},{34,58},{35,59},{4,28}... | collective-permute-start | bytes 380936 | tf_op jit(solution)/shard_map/ppermute | solution.py:50
  65.6 5.2 %collective-permute-start.3 = (bf16[192,128]{1,0:T(8,128)(2,1)S(1)}, bf16[192,128]{1,0:T(8,128)(2,1)S(1)}, u32[]{:S(2)}, u32[]{:S(2)}) collective-permute-start(bf16[192,128]{1,0:T(8,128)(2,1)S(1)} %get-tuple-element.61), channel_id=1, source_target_pairs={{0,8},{1,9},{32,40},{33,41},{2,10},{3,11},{34,42},{35,43},{4,12},{... | collective-permute-start | bytes 147464 | tf_op jit(solution)/shard_map/ppermute | solution.py:50
  66.8 4.4 %collective-permute-start.4 = (bf16[192,128]{1,0:T(8,128)(2,1)S(1)}, bf16[192,128]{1,0:T(8,128)(2,1)S(1)}, u32[]{:S(2)}, u32[]{:S(2)}) collective-permute-start(bf16[192,128]{1,0:T(8,128)(2,1)S(1)} %get-tuple-element.62), channel_id=1, source_target_pairs={{0,16},{1,17},{32,48},{33,49},{2,18},{3,19},{34,50},{35,51},{4,20}... | collective-permute-start | bytes 147464 | tf_op jit(solution)/shard_map/ppermute | solution.py:50
  68.2 3.1 %collective-permute-start.5 = (bf16[192,128]{1,0:T(8,128)(2,1)S(1)}, bf16[192,128]{1,0:T(8,128)(2,1)S(1)}, u32[]{:S(2)}, u32[]{:S(2)}) collective-permute-start(bf16[192,128]{1,0:T(8,128)(2,1)S(1)} %get-tuple-element.63), channel_id=1, source_target_pairs={{0,24},{1,25},{32,56},{33,57},{2,26},{3,27},{34,58},{35,59},{4,28}... | collective-permute-start | bytes 147464 | tf_op jit(solution)/shard_map/ppermute | solution.py:50
  73.0 25.5 %all-to-all-start.3 = ((bf16[32,32,256]{2,1,0:T(8,128)(2,1)}), bf16[32,32,256]{2,1,0:T(8,128)(2,1)S(1)}, u32[]{:S(2)}, u32[]{:S(2)}) async-start(bf16[32,32,256]{2,1,0:T(8,128)(2,1)} %bitcast.11), calls=%async_computation.3 | async-start | bytes 1048576 | tf_op jit(solution)/shard_map/all_to_all | solution.py:580
  79.0 6.4 %collective-permute-start.10 = (f32[4,144,128]{2,1,0:T(8,128)S(1)}, f32[4,144,128]{2,1,0:T(8,128)S(1)}, u32[]{:S(2)}, u32[]{:S(2)}) collective-permute-start(f32[4,144,128]{2,1,0:T(8,128)S(1)} %get-tuple-element.73), channel_id=1, source_target_pairs={{0,1},{1,0},{32,33},{33,32},{2,3},{3,2},{34,35},{35,34},{4,5},{5,4... | collective-permute-start | bytes 884744 | tf_op jit(solution)/shard_map/ppermute | solution.py:50
  84.2 1.6 %collective-permute-start.9 = (f32[4,144,128]{2,1,0:T(8,128)S(1)}, f32[4,144,128]{2,1,0:T(8,128)S(1)}, u32[]{:S(2)}, u32[]{:S(2)}) collective-permute-start(f32[4,144,128]{2,1,0:T(8,128)S(1)} %get-tuple-element.72), channel_id=1, source_target_pairs={{0,1},{1,0},{32,33},{33,32},{2,3},{3,2},{34,35},{35,34},{4,5},{5,4... | collective-permute-start | bytes 884744 | tf_op jit(solution)/shard_map/ppermute | solution.py:50
  85.9 9.1 %collective-permute-start.11 = (f32[288,128]{1,0:T(8,128)S(1)}, f32[288,128]{1,0:T(8,128)S(1)}, u32[]{:S(2)}, u32[]{:S(2)}) collective-permute-start(f32[288,128]{1,0:T(8,128)S(1)} %get-tuple-element.75), channel_id=1, source_target_pairs={{0,64},{1,65},{32,96},{33,97},{2,66},{3,67},{34,98},{35,99},{4,68}... | collective-permute-start | bytes 442376 | tf_op jit(solution)/shard_map/ppermute | solution.py:50
  87.5 11.0 %collective-permute-start.12 = (f32[288,128]{1,0:T(8,128)S(1)}, f32[288,128]{1,0:T(8,128)S(1)}, u32[]{:S(2)}, u32[]{:S(2)}) collective-permute-start(f32[288,128]{1,0:T(8,128)S(1)} %get-tuple-element.76), channel_id=1, source_target_pairs={{0,128},{1,129},{32,160},{33,161},{2,130},{3,131},{34,162},{35,163... | collective-permute-start | bytes 442376 | tf_op jit(solution)/shard_map/ppermute | solution.py:50
  89.9 8.6 %collective-permute-start.13 = (f32[288,128]{1,0:T(8,128)S(1)}, f32[288,128]{1,0:T(8,128)S(1)}, u32[]{:S(2)}, u32[]{:S(2)}) collective-permute-start(f32[288,128]{1,0:T(8,128)S(1)} %get-tuple-element.77), channel_id=1, source_target_pairs={{0,192},{1,193},{32,224},{33,225},{2,194},{3,195},{34,226},{35,227... | collective-permute-start | bytes 442376 | tf_op jit(solution)/shard_map/ppermute | solution.py:50
  142.0 7.8 %collective-permute-start.14 = (bf16[16,288,128]{2,1,0:T(8,128)(2,1)S(1)}, bf16[16,288,128]{2,1,0:T(8,128)(2,1)S(1)}, u32[]{:S(2)}, u32[]{:S(2)}) collective-permute-start(bf16[16,288,128]{2,1,0:T(8,128)(2,1)S(1)} %all_to_all.62.refs_0_), channel_id=1, source_target_pairs={{0,1},{1,0},{32,33},{33,32},{2,3},{3,2},{34,35},{35,34},{4,5},{5,4... | collective-permute-start | bytes 3538952 | tf_op jit(solution)/shard_map/ppermute | solution.py:50

commit v9 on v7

--- a/solution.py
+++ b/solution.py
@@ -269,7 +269,6 @@
 
 def second_kernel(
     place, links, field_ref, goal_ref, hidden_ref, recv_ref, old_ref, pack_ref, unpack_ref, weights,
-    held0, held1, held2,
     state_ref, misfit_ref, inner_ref, frame_ref, sent_ref, part0, part1, part2, part3,
     grid, frame, got, flat, column,
 ):
@@ -617,9 +616,8 @@
         "second_layer",
         (
             tile_links, field, goal, hidden, recv, frame, pack, unpack, second_weights,
-            *field_parts[1:],
         ),
-        [moved_in] * 3 + [near] * 6 + [left] * 3,
+        [moved_in] * 3 + [near] * 6,
         (rows_like, like(192, 256, dtype=f32), inner_like, frame_like, sent_like)
         + (like(496, 128),) * 4,
         [grid_shape, frame_shape, frame_shape, flat_shape, column_shape],
@@ -632,7 +630,7 @@
     last, frame, *parts = run(
         third_kernel,
         "first_gradient",
-        (tile_links, inner, pre_first, recv, frame, unpack, first_weights, *closing_parts[1:]),
+        (tile_links, inner, pre_first, recv, frame, unpack, first_weights, *field_parts[1:]),
         [moved_in, near, moved_in] + [near] * 3 + [moved_in] + [left] * 3,
         (inner_like, frame_like) + (like(192, 128),) * 4,
         [grid_shape, frame_shape, frame_shape, column_shape],

time: 158 us -> 156 us (0.987)
  blocking collectives: 62.1 us -> 77.4 us
  starting transfers between devices: 47 us -> 38.1 us
  waiting for transfers between devices: 26 us -> 18.7 us
    all_to_all x1 -> x2, blocking collectives: 18.9 us -> 34.2 us  [exchange(): return lax.all_to_all(values, 'tile', 0, 0, tiled=True)]
    ppermute x15, waiting for transfers between devices: 26 us -> 18.7 us  [shifted(): return lax.ppermute(values, ('tile', 'ens'), pairs)]
    all_to_all x3 -> x2, starting transfers between devices: 18.8 us -> 13.3 us  [exchange(): return lax.all_to_all(values, 'tile', 0, 0, tiled=True)]
    ppermute x15, starting transfers between devices: 28.3 us -> 24.8 us  [shifted(): return lax.ppermute(values, ('tile', 'ens'), pairs)]
  transfers between devices with their start and end apart: 18 -> 17, of which waited for: 11 -> 10; matrix products, arithmetic and copies ran while one was open for 0% -> 0% of each run, Pallas kernels for 2% -> 4%
where the time goes in v9:
time: 156 us; the launch traced here: 155 us
  blocking collectives  77.4 us (50%)
  starting transfers between devices  38.1 us (24%)
  Pallas kernels  19.8 us (13%)
  waiting for transfers between devices  18.7 us (12%)
    all_to_all x3, blocking collectives, trade(): lax.all_to_all(values, ('tile', 'ens'), 0, 0, axis_index_groups=groups(al...  43.1 us
    all_to_all x2, blocking collectives, exchange(): return lax.all_to_all(values, 'tile', 0, 0, tiled=True)  34.2 us
    ppermute x15, starting transfers between devices, shifted(): return lax.ppermute(values, ('tile', 'ens'), pairs)  24.8 us
    pallas_call x10, Pallas kernels, run(): pl.pallas_call(body, out_shape=tuple((pltpu.HBM(out.shape, out.dtype) if...  19.8 us
    ppermute x15, waiting for transfers between devices, shifted(): return lax.ppermute(values, ('tile', 'ens'), pairs)  18.7 us
    all_to_all x2, starting transfers between devices, exchange(): return lax.all_to_all(values, 'tile', 0, 0, tiled=True)  13.3 us
  transfers between devices with their start and end apart: 17, of which 10 were waited for; matrix products, arithmetic and copies ran while one was open for 0% of the time, Pallas kernels for 4%

profile of v9, /device:TPU:1, one launch (start us, length us, event | category | flops | bytes accessed | tf_op | source)
XLA Modules:
  0.0 155.1 jit_solution(14781022353929602820)
XLA Ops:
  0.6 0.0 copy-start.2
  0.6 0.0 copy-start
  0.7 2.6 %routes.1 = (bf16[1024,128]{1,0:T(8,128)(2,1)S(1)}, bf16[128,1152]{1,0:T(8,128)(2,1)S(1)}, bf16[128,256]{1,0:T(8,128)(2,1)S(1)}, bf16[1024,256]{1,0:T(8,128)(2,1)S(1)}) custom-call(s32[3,16]{1,0:T(4,128)} %refs_0_.7, bf16[192,256]{1,0:T(8,128)(2,1)} %bitcast.26), custom_call_target="tpu_custom_call" | custom-call | flops 67108864 | bytes 3000000 | tf_op jit(solution)/shard_map/routes/pallas_call | solution.py:406
  3.3 18.9 %all_to_all.59 = bf16[32,32,256]{2,1,0:T(8,128)(2,1)S(1)} all-to-all(bf16[32,32,256]{2,1,0:T(8,128)(2,1)S(1)} %bitcast.25), channel_id=1, replica_groups=mesh['tile'=32,'ens'=8] {'tile'}, dimensions={0} | all-to-all | bytes 1048576 | tf_op jit(solution)/shard_map/all_to_all | solution.py:579
  22.2 2.5 %first_layer.1 = (bf16[192,256]{1,0:T(8,128)(2,1)S(1)}, f32[192,256]{1,0:T(8,128)}, bf16[128,256]{1,0:T(8,128)(2,1)S(1)}, bf16[1024,256]{1,0:T(8,128)(2,1)S(1)},...) custom-call(s32[3,16]{1,0:T(4,128)} %refs_0_.7, ...), custom_call_target="tpu_custom_call" | custom-call | flops 226492416 | bytes 3000000 | tf_op jit(solution)/shard_map/first_layer/pallas_call | solution.py:406
  24.7 15.3 %all_to_all.60 = bf16[32,32,256]{2,1,0:T(8,128)(2,1)S(1)} all-to-all(bf16[32,32,256]{2,1,0:T(8,128)(2,1)S(1)} %bitcast.24), channel_id=1, replica_groups=mesh['tile'=32,'ens'=8] {'tile'}, dimensions={0} | all-to-all | bytes 1048576 | tf_op jit(solution)/shard_map/all_to_all | solution.py:579
  40.0 4.1 %second_layer.1 = (bf16[192,256]{1,0:T(8,128)(2,1)}, f32[192,256]{1,0:T(8,128)}, f32[3,8,8,256]{3,2,1,0:T(8,128)S(1)}, bf16[128,256]{1,0:T(8,128)(2,1)S(1)}, bf1...) custom-call(s32[3,16]{1,0:T(4,128)} %refs_0_.7, ...), custom_call_target="tpu_custom_call" | custom-call | flops 452984832 | bytes 3000000 | tf_op jit(solution)/shard_map/second_layer/pallas_call | solution.py:406
  44.1 5.8 %all-to-all-start.2 = ((bf16[32,32,256]{2,1,0:T(8,128)(2,1)}), bf16[32,32,256]{2,1,0:T(8,128)(2,1)S(1)}, u32[]{:S(2)}, u32[]{:S(2)}) async-start(bf16[32,32,256]{2,1,0:T(8,128)(2,1)} %bitcast.9), calls=%async_computation.2 | async-start | bytes 1048576 | tf_op jit(solution)/shard_map/all_to_all | solution.py:579
  49.9 1.3 collective-permute-start
  51.2 1.2 collective-permute-start.6
  52.4 1.4 collective-permute-start.1
  53.8 1.8 %collective-permute-start.2 = (bf16[304,128]{1,0:T(8,128)(2,1)S(1)}, bf16[304,128]{1,0:T(8,128)(2,1)S(1)}, u32[]{:S(2)}, u32[]{:S(2)}) collective-permute-start(bf16[304,128]{1,0:T(8,128)(2,1)S(1)} %get-tuple-element.56), channel_id=1, source_target_pairs={{0,24},{1,25},{32,56},{33,57},{2,26},{3,27},{34,58},{35,59},{4,28}... | collective-permute-start | bytes 233480 | tf_op jit(solution)/shard_map/ppermute | solution.py:50
  55.6 0.6 collective-permute-start.7
  56.2 3.3 %collective-permute-done.refs_7_.refs_1_ = bf16[304,128]{1,0:T(8,128)(2,1)S(1)} collective-permute-done((bf16[304,128]{1,0:T(8,128)(2,1)S(1)}, bf16[304,128]{1,0:T(8,128)(2,1)S(1)}, u32[]{:S(2)}, u32[]{:S(2)}) %collective-permute-start) | collective-permute-done | bytes 77856 | tf_op jit(solution)/shard_map/ppermute | solution.py:50
  59.5 0.0 collective-permute-start.8
  59.5 4.1 %collective-permute-done.1.refs_8_.refs_2_ = bf16[304,128]{1,0:T(8,128)(2,1)S(1)} collective-permute-done((bf16[304,128]{1,0:T(8,128)(2,1)S(1)}, bf16[304,128]{1,0:T(8,128)(2,1)S(1)}, u32[]{:S(2)}, u32[]{:S(2)}) %collective-permute-start.1) | collective-permute-done | bytes 77856 | tf_op jit(solution)/shard_map/ppermute | solution.py:50
  63.6 0.0 collective-permute-done.2.refs_9_.refs_3_
  63.6 0.0 all-to-all-done.2
  63.6 3.0 %first_gradient.1 = (f32[3,8,8,256]{3,2,1,0:T(8,128)}, bf16[128,256]{1,0:T(8,128)(2,1)S(1)}, bf16[192,128]{1,0:T(8,128)(2,1)S(1)}, bf16[192,128]{1,0:T(8,128)(2,...) custom-call(s32[3,16]{1,0:T(4,128)} %refs_0_.7, f32[3,8,8,256]{3,2,1,0:T(8,128)S(1)} %get-tuple-element.50.refs_1_, ...), custom_call_target="tpu_custom_call" | custom-call | flops 226492416 | bytes 3000000 | tf_op jit(solution)/shard_map/first_gradient/pallas_call | solution.py:406
  66.6 0.1 collective-permute-start.3
  66.7 0.9 collective-permute-start.4
  67.6 0.0 collective-permute-done.6.refs_1_
  67.6 1.8 %collective-permute-start.5 = (bf16[192,128]{1,0:T(8,128)(2,1)S(1)}, bf16[192,128]{1,0:T(8,128)(2,1)S(1)}, u32[]{:S(2)}, u32[]{:S(2)}) collective-permute-start(bf16[192,128]{1,0:T(8,128)(2,1)S(1)} %get-tuple-element.63), channel_id=1, source_target_pairs={{0,24},{1,25},{32,56},{33,57},{2,26},{3,27},{34,58},{35,59},{4,28}... | collective-permute-start | bytes 147464 | tf_op jit(solution)/shard_map/ppermute | solution.py:50
  69.4 0.7 slope_terms.2
  70.2 0.7 collective-permute-done.3.refs_5_
  70.8 0.6 collective-permute-done.4.refs_6_
  71.4 0.5 collective-permute-done.5.refs_7_
  71.9 1.8 %slope_terms.3 = (f32[4,144,128]{2,1,0:T(8,128)S(1)}, f32[4,144,128]{2,1,0:T(8,128)S(1)}, bf16[1024,256]{1,0:T(8,128)(2,1)}) custom-call(bf16[304,128]{1,0:T(8,128)(2,1)} %get-tuple-element.59.refs_0_, bf16[304,128]{1,0:T(8,128)(2,1)S(1)} %collective-permute-done.refs_7_.refs_1_, bf16[304,128]{1,0:T(8,128)(2,1)S(1)} %collective-permute-done.1.refs_8_.refs_2_, ...), custom_call_target="tpu_custom_call" | custom-call | flops 226492416 | bytes 3000000 | tf_op jit(solution)/shard_map/slope_terms/pallas_call | solution.py:406
  73.7 7.5 %all-to-all-start.3 = ((bf16[32,32,256]{2,1,0:T(8,128)(2,1)}), bf16[32,32,256]{2,1,0:T(8,128)(2,1)S(1)}, u32[]{:S(2)}, u32[]{:S(2)}) async-start(bf16[32,32,256]{2,1,0:T(8,128)(2,1)} %bitcast.11), calls=%async_computation.3 | async-start | bytes 1048576 | tf_op jit(solution)/shard_map/all_to_all | solution.py:579
  81.3 5.1 %collective-permute-start.10 = (f32[4,144,128]{2,1,0:T(8,128)S(1)}, f32[4,144,128]{2,1,0:T(8,128)S(1)}, u32[]{:S(2)}, u32[]{:S(2)}) collective-permute-start(f32[4,144,128]{2,1,0:T(8,128)S(1)} %get-tuple-element.73), channel_id=1, source_target_pairs={{0,1},{1,0},{32,33},{33,32},{2,3},{3,2},{34,35},{35,34},{4,5},{5,4... | collective-permute-start | bytes 884744 | tf_op jit(solution)/shard_map/ppermute | solution.py:50
  86.3 0.1 collective-permute-start.9
  86.4 1.1 collective-permute-done.10.refs_3_
  87.5 0.4 collective-permute-done.9.refs_1_
  88.0 0.1 pair_sum.1
  88.1 1.6 %collective-permute-start.11 = (f32[288,128]{1,0:T(8,128)S(1)}, f32[288,128]{1,0:T(8,128)S(1)}, u32[]{:S(2)}, u32[]{:S(2)}) collective-permute-start(f32[288,128]{1,0:T(8,128)S(1)} %get-tuple-element.75), channel_id=1, source_target_pairs={{0,64},{1,65},{32,96},{33,97},{2,66},{3,67},{34,98},{35,99},{4,68}... | collective-permute-start | bytes 442376 | tf_op jit(solution)/shard_map/ppermute | solution.py:50
  89.6 2.4 %collective-permute-start.12 = (f32[288,128]{1,0:T(8,128)S(1)}, f32[288,128]{1,0:T(8,128)S(1)}, u32[]{:S(2)}, u32[]{:S(2)}) collective-permute-start(f32[288,128]{1,0:T(8,128)S(1)} %get-tuple-element.76), channel_id=1, source_target_pairs={{0,128},{1,129},{32,160},{33,161},{2,130},{3,131},{34,162},{35,163... | collective-permute-start | bytes 442376 | tf_op jit(solution)/shard_map/ppermute | solution.py:50
  92.1 1.1 collective-permute-start.13
  93.2 3.9 %collective-permute-done.11.refs_1_ = f32[288,128]{1,0:T(8,128)S(1)} collective-permute-done((f32[288,128]{1,0:T(8,128)S(1)}, f32[288,128]{1,0:T(8,128)S(1)}, u32[]{:S(2)}, u32[]{:S(2)}) %collective-permute-start.11) | collective-permute-done | bytes 147488 | tf_op jit(solution)/shard_map/ppermute | solution.py:50
  97.2 3.5 %collective-permute-done.12.refs_2_ = f32[288,128]{1,0:T(8,128)S(1)} collective-permute-done((f32[288,128]{1,0:T(8,128)S(1)}, f32[288,128]{1,0:T(8,128)S(1)}, u32[]{:S(2)}, u32[]{:S(2)}) %collective-permute-start.12) | collective-permute-done | bytes 147488 | tf_op jit(solution)/shard_map/ppermute | solution.py:50
  100.7 0.1 row_sum.1
  100.8 15.8 %all_to_all.61 = f32[8,36,128]{2,1,0:T(8,128)S(1)} all-to-all(f32[8,36,128]{2,1,0:T(8,128)S(1)} %row_sum.1), channel_id=1, replica_groups={{0,32,2,34,4,36,6,38},{1,33,3,35,5,37,7,39},{64,96,66,98,68,100,70,102}..., dimensions={0} | all-to-all | bytes 294912 | tf_op jit(solution)/shard_map/all_to_all | solution.py:543
  116.6 10.1 %all_to_all.62 = bf16[8,36,128]{2,1,0:T(8,128)(2,1)S(1)} all-to-all(bf16[8,36,128]{2,1,0:T(8,128)(2,1)S(1)} %broadcast_in_dim.17), channel_id=1, replica_groups={{0,32,2,34,4,36,6,38},{1,33,3,35,5,37,7,39},{64,96,66,98,68,100,70,102}..., dimensions={0} | all-to-all | bytes 147456 | tf_op jit(solution)/shard_map/all_to_all | solution.py:543
  126.7 0.2 broadcast_in_dim.19
  126.8 17.3 %all_to_all.63.refs_0_ = bf16[16,288,128]{2,1,0:T(8,128)(2,1)S(1)} all-to-all(bf16[16,288,128]{2,1,0:T(8,128)(2,1)S(1)} %broadcast_in_dim.19), channel_id=1, replica_groups={{0,64,128,192,8,72,136,200,16,80,144,208,24,88,152,216},{1,65,129,193,9..., dimensions={0} | all-to-all | bytes 2359296 | tf_op jit(solution)/shard_map/all_to_all | solution.py:543
  144.2 5.3 %collective-permute-start.14 = (bf16[16,288,128]{2,1,0:T(8,128)(2,1)S(1)}, bf16[16,288,128]{2,1,0:T(8,128)(2,1)S(1)}, u32[]{:S(2)}, u32[]{:S(2)}) collective-permute-start(bf16[16,288,128]{2,1,0:T(8,128)(2,1)S(1)} %all_to_all.63.refs_0_), channel_id=1, source_target_pairs={{0,1},{1,0},{32,33},{33,32},{2,3},{3,2},{34,35},{35,34},{4,5},{5,4... | collective-permute-start | bytes 3538952 | tf_op jit(solution)/shard_map/ppermute | solution.py:50
  149.5 1.9 %last_gradient.1 = f32[3,8,8,256]{3,2,1,0:T(8,128)} custom-call(f32[3,8,8,256]{3,2,1,0:T(8,128)} %get-tuple-element.57.refs_0_, f32[192,256]{1,0:T(8,128)} %get-tuple-element.58.refs_1_, bf16[1024,256]{1,0:T(8,128)(2,1)S(1)} %bitcast.17, bf16[128,256]{1,0:T(8,128)(2,1)S(1)} %get-tuple-element.64.refs_9_.refs_3_, ...), custom_call_target="tpu_custom_call" | custom-call | flops 1000 | bytes 3000000 | tf_op jit(solution)/shard_map/last_gradient/pallas_call | solution.py:406
  151.4 0.5 collective-permute-done.14.refs_1_
  152.0 3.0 %spread_slopes.1 = (f32[9,256,256]{2,1,0:T(8,128)}, f32[9,256,256]{2,1,0:T(8,128)}) custom-call(bf16[16,288,128]{2,1,0:T(8,128)(2,1)S(1)} %all_to_all.63.refs_0_, bf16[16,288,128]{2,1,0:T(8,128)(2,1)S(1)} %collective-permute-done.14.refs_1_), custom_call_target="tpu_custom_call" | custom-call | flops 1000 | bytes 3000000 | tf_op jit(solution)/shard_map/spread_slopes/pallas_call | solution.py:406
  (12 shorter events, 0.1 us)
Async XLA Ops:
  0.6 21.6 %copy-start.2 = (bf16[1,3,8,8,256]{4,3,2,1,0:T(8,128)(2,1)S(1)}, bf16[1,3,8,8,256]{4,3,2,1,0:T(8,128)(2,1)}, u32[]{:S(2)}) copy-start(bf16[1,3,8,8,256]{4,3,2,1,0:T(8,128)(2,1)} %param.5) | copy-start | bytes 294916
  0.6 21.6 %copy-start = (bf16[3,3,256,256]{3,2,1,0:T(8,128)(2,1)S(1)}, bf16[3,3,256,256]{3,2,1,0:T(8,128)(2,1)}, u32[]{:S(2)}) copy-start(bf16[3,3,256,256]{3,2,1,0:T(8,128)(2,1)} %param.7) | copy-start | bytes 3538948
  22.2 17.8 %copy-start.1 = (bf16[3,3,256,256]{3,2,1,0:T(8,128)(2,1)S(1)}, bf16[3,3,256,256]{3,2,1,0:T(8,128)(2,1)}, u32[]{:S(2)}) copy-start(bf16[3,3,256,256]{3,2,1,0:T(8,128)(2,1)} %param.8) | copy-start | bytes 3538948
  44.1 19.5 %all-to-all-start.2 = ((bf16[32,32,256]{2,1,0:T(8,128)(2,1)}), bf16[32,32,256]{2,1,0:T(8,128)(2,1)S(1)}, u32[]{:S(2)}, u32[]{:S(2)}) async-start(bf16[32,32,256]{2,1,0:T(8,128)(2,1)} %bitcast.9), calls=%async_computation.2 | async-start | bytes 1048576 | tf_op jit(solution)/shard_map/all_to_all | solution.py:579
  49.9 9.6 %collective-permute-start = (bf16[304,128]{1,0:T(8,128)(2,1)S(1)}, bf16[304,128]{1,0:T(8,128)(2,1)S(1)}, u32[]{:S(2)}, u32[]{:S(2)}) collective-permute-start(bf16[304,128]{1,0:T(8,128)(2,1)S(1)} %get-tuple-element.54), channel_id=1, source_target_pairs={{0,8},{1,9},{32,40},{33,41},{2,10},{3,11},{34,42},{35,43},{4,12},{... | collective-permute-start | bytes 233480 | tf_op jit(solution)/shard_map/ppermute | solution.py:50
  51.2 16.5 %collective-permute-start.6 = (bf16[496,128]{1,0:T(8,128)(2,1)S(1)}, bf16[496,128]{1,0:T(8,128)(2,1)S(1)}, u32[]{:S(2)}, u32[]{:S(2)}) collective-permute-start(bf16[496,128]{1,0:T(8,128)(2,1)S(1)} %get-tuple-element.66), channel_id=1, source_target_pairs={{0,8},{1,9},{32,40},{33,41},{2,10},{3,11},{34,42},{35,43},{4,12},{... | collective-permute-start | bytes 380936 | tf_op jit(solution)/shard_map/ppermute | solution.py:50
  52.4 11.2 %collective-permute-start.1 = (bf16[304,128]{1,0:T(8,128)(2,1)S(1)}, bf16[304,128]{1,0:T(8,128)(2,1)S(1)}, u32[]{:S(2)}, u32[]{:S(2)}) collective-permute-start(bf16[304,128]{1,0:T(8,128)(2,1)S(1)} %get-tuple-element.55), channel_id=1, source_target_pairs={{0,16},{1,17},{32,48},{33,49},{2,18},{3,19},{34,50},{35,51},{4,20}... | collective-permute-start | bytes 233480 | tf_op jit(solution)/shard_map/ppermute | solution.py:50
  53.8 9.8 %collective-permute-start.2 = (bf16[304,128]{1,0:T(8,128)(2,1)S(1)}, bf16[304,128]{1,0:T(8,128)(2,1)S(1)}, u32[]{:S(2)}, u32[]{:S(2)}) collective-permute-start(bf16[304,128]{1,0:T(8,128)(2,1)S(1)} %get-tuple-element.56), channel_id=1, source_target_pairs={{0,24},{1,25},{32,56},{33,57},{2,26},{3,27},{34,58},{35,59},{4,28}... | collective-permute-start | bytes 233480 | tf_op jit(solution)/shard_map/ppermute | solution.py:50
  55.6 13.8 %collective-permute-start.7 = (bf16[496,128]{1,0:T(8,128)(2,1)S(1)}, bf16[496,128]{1,0:T(8,128)(2,1)S(1)}, u32[]{:S(2)}, u32[]{:S(2)}) collective-permute-start(bf16[496,128]{1,0:T(8,128)(2,1)S(1)} %get-tuple-element.67), channel_id=1, source_target_pairs={{0,16},{1,17},{32,48},{33,49},{2,18},{3,19},{34,50},{35,51},{4,20}... | collective-permute-start | bytes 380936 | tf_op jit(solution)/shard_map/ppermute | solution.py:50
  59.5 9.9 %collective-permute-start.8 = (bf16[496,128]{1,0:T(8,128)(2,1)S(1)}, bf16[496,128]{1,0:T(8,128)(2,1)S(1)}, u32[]{:S(2)}, u32[]{:S(2)}) collective-permute-start(bf16[496,128]{1,0:T(8,128)(2,1)S(1)} %get-tuple-element.68), channel_id=1, source_target_pairs={{0,24},{1,25},{32,56},{33,57},{2,26},{3,27},{34,58},{35,59},{4,28}... | collective-permute-start | bytes 380936 | tf_op jit(solution)/shard_map/ppermute | solution.py:50
  66.6 4.2 %collective-permute-start.3 = (bf16[192,128]{1,0:T(8,128)(2,1)S(1)}, bf16[192,128]{1,0:T(8,128)(2,1)S(1)}, u32[]{:S(2)}, u32[]{:S(2)}) collective-permute-start(bf16[192,128]{1,0:T(8,128)(2,1)S(1)} %get-tuple-element.61), channel_id=1, source_target_pairs={{0,8},{1,9},{32,40},{33,41},{2,10},{3,11},{34,42},{35,43},{4,12},{... | collective-permute-start | bytes 147464 | tf_op jit(solution)/shard_map/ppermute | solution.py:50
  66.7 4.7 %collective-permute-start.4 = (bf16[192,128]{1,0:T(8,128)(2,1)S(1)}, bf16[192,128]{1,0:T(8,128)(2,1)S(1)}, u32[]{:S(2)}, u32[]{:S(2)}) collective-permute-start(bf16[192,128]{1,0:T(8,128)(2,1)S(1)} %get-tuple-element.62), channel_id=1, source_target_pairs={{0,16},{1,17},{32,48},{33,49},{2,18},{3,19},{34,50},{35,51},{4,20}... | collective-permute-start | bytes 147464 | tf_op jit(solution)/shard_map/ppermute | solution.py:50
  67.6 4.3 %collective-permute-start.5 = (bf16[192,128]{1,0:T(8,128)(2,1)S(1)}, bf16[192,128]{1,0:T(8,128)(2,1)S(1)}, u32[]{:S(2)}, u32[]{:S(2)}) collective-permute-start(bf16[192,128]{1,0:T(8,128)(2,1)S(1)} %get-tuple-element.63), channel_id=1, source_target_pairs={{0,24},{1,25},{32,56},{33,57},{2,26},{3,27},{34,58},{35,59},{4,28}... | collective-permute-start | bytes 147464 | tf_op jit(solution)/shard_map/ppermute | solution.py:50
  73.7 27.0 %all-to-all-start.3 = ((bf16[32,32,256]{2,1,0:T(8,128)(2,1)}), bf16[32,32,256]{2,1,0:T(8,128)(2,1)S(1)}, u32[]{:S(2)}, u32[]{:S(2)}) async-start(bf16[32,32,256]{2,1,0:T(8,128)(2,1)} %bitcast.11), calls=%async_computation.3 | async-start | bytes 1048576 | tf_op jit(solution)/shard_map/all_to_all | solution.py:579
  81.3 6.3 %collective-permute-start.10 = (f32[4,144,128]{2,1,0:T(8,128)S(1)}, f32[4,144,128]{2,1,0:T(8,128)S(1)}, u32[]{:S(2)}, u32[]{:S(2)}) collective-permute-start(f32[4,144,128]{2,1,0:T(8,128)S(1)} %get-tuple-element.73), channel_id=1, source_target_pairs={{0,1},{1,0},{32,33},{33,32},{2,3},{3,2},{34,35},{35,34},{4,5},{5,4... | collective-permute-start | bytes 884744 | tf_op jit(solution)/shard_map/ppermute | solution.py:50
  86.3 1.6 %collective-permute-start.9 = (f32[4,144,128]{2,1,0:T(8,128)S(1)}, f32[4,144,128]{2,1,0:T(8,128)S(1)}, u32[]{:S(2)}, u32[]{:S(2)}) collective-permute-start(f32[4,144,128]{2,1,0:T(8,128)S(1)} %get-tuple-element.72), channel_id=1, source_target_pairs={{0,1},{1,0},{32,33},{33,32},{2,3},{3,2},{34,35},{35,34},{4,5},{5,4... | collective-permute-start | bytes 884744 | tf_op jit(solution)/shard_map/ppermute | solution.py:50
  88.1 9.1 %collective-permute-start.11 = (f32[288,128]{1,0:T(8,128)S(1)}, f32[288,128]{1,0:T(8,128)S(1)}, u32[]{:S(2)}, u32[]{:S(2)}) collective-permute-start(f32[288,128]{1,0:T(8,128)S(1)} %get-tuple-element.75), channel_id=1, source_target_pairs={{0,64},{1,65},{32,96},{33,97},{2,66},{3,67},{34,98},{35,99},{4,68}... | collective-permute-start | bytes 442376 | tf_op jit(solution)/shard_map/ppermute | solution.py:50
  89.6 11.0 %collective-permute-start.12 = (f32[288,128]{1,0:T(8,128)S(1)}, f32[288,128]{1,0:T(8,128)S(1)}, u32[]{:S(2)}, u32[]{:S(2)}) collective-permute-start(f32[288,128]{1,0:T(8,128)S(1)} %get-tuple-element.76), channel_id=1, source_target_pairs={{0,128},{1,129},{32,160},{33,161},{2,130},{3,131},{34,162},{35,163... | collective-permute-start | bytes 442376 | tf_op jit(solution)/shard_map/ppermute | solution.py:50
  92.1 8.6 %collective-permute-start.13 = (f32[288,128]{1,0:T(8,128)S(1)}, f32[288,128]{1,0:T(8,128)S(1)}, u32[]{:S(2)}, u32[]{:S(2)}) collective-permute-start(f32[288,128]{1,0:T(8,128)S(1)} %get-tuple-element.77), channel_id=1, source_target_pairs={{0,192},{1,193},{32,224},{33,225},{2,194},{3,195},{34,226},{35,227... | collective-permute-start | bytes 442376 | tf_op jit(solution)/shard_map/ppermute | solution.py:50
  144.2 7.8 %collective-permute-start.14 = (bf16[16,288,128]{2,1,0:T(8,128)(2,1)S(1)}, bf16[16,288,128]{2,1,0:T(8,128)(2,1)S(1)}, u32[]{:S(2)}, u32[]{:S(2)}) collective-permute-start(bf16[16,288,128]{2,1,0:T(8,128)(2,1)S(1)} %all_to_all.63.refs_0_), channel_id=1, source_target_pairs={{0,1},{1,0},{32,33},{33,32},{2,3},{3,2},{34,35},{35,34},{4,5},{5,4... | collective-permute-start | bytes 3538952 | tf_op jit(solution)/shard_map/ppermute | solution.py:50
